TPU v7x, 32 devices: a whole 2x2x4 slice. The times are simulated.
32 devices in a mesh: reg: 8 (over z, core), lon: 4 (over y, x).
Axes of the slice: x: 2, y: 2, z: 4, core: 2. Of those that a mesh axis runs over, the one named last changes fastest.
Arguments:
- nodes: bfloat16 [1, 4096, 512], P(None, ('reg', 'lon')), may hold values from -6 to 6
- norm_gain: float32 [512], replicated, may hold values from 0.25 to 1.75
- w_qkv: bfloat16 [512, 1536], replicated
- w_out: bfloat16 [512, 512], replicated, may hold values from -0.25 to 0.25
- w_latent: bfloat16 [512, 512], replicated, may hold values from -0.25 to 0.25
- neighbours: int32 [32, 5], P(('reg', 'lon')), may hold values from 0 to 31, as said below
- assignment: int32 [16, 1024], P('reg', 'lon'), may hold values from 0 to 4095, as said below
- psi: float32 [9, 16, 5, 5], P(None, 'reg'), may hold values from -1.2 to 1.2
- w_dec: bfloat16 [9, 512, 84], replicated, may hold values from -0.09375 to 0.09375
Outputs:
- mesh_state: bfloat16 [1, 4096, 512], P(None, ('reg', 'lon'))
- fields: bfloat16 [1, 84, 16, 1024], P(None, None, 'reg', 'lon')
Inputs may be any that keep to these rules, and one draw needn't show every extreme that they name: neighbours[b, 0] = b; the other entries of a row are distinct blocks adjacent to b (diagonals included) on the grid of 8 x 4 blocks, where block b has row b // 4 and column b % 4; columns wrap around, rows do not. `assignment`: the node of cell (i, j) lies in block (i // 2) * 4 + j // 256.
All inputs are finite; a program needn't handle non-finite values.
Results may differ from a plain program's by a relative error of at most 0.011.
Values may be sent and summed in bfloat16 or wider, within the bound.
No kernel may reach another device: no remote copies, remote signals or barrier semaphores. Data moves between devices by JAX's collectives and lax.ppermute only.
A program may use at most 64 MiB of HBM per device.

v0:
```python
import jax
import jax.numpy as jnp
from jax import lax
from jax.sharding import PartitionSpec as P

HEADS = 16


def with_halo(array, sides, width, wrap):
    for axis, dim in sides:
        size, length = (lax.axis_size(axis), array.shape[dim])
        up = [(i, (i + 1) % size) for i in range(size if wrap else size - 1)]
        down = [(j, i) for i, j in up]
        last = lax.slice_in_dim(array, length - width, length, axis=dim)
        leading = lax.slice_in_dim(array, 0, width, axis=dim)
        before = lax.ppermute(last, axis, up)
        after = lax.ppermute(leading, axis, down)
        array = jnp.concatenate([before, array, after], axis=dim)
    return array


def layer_norm(nodes, gain):
    values = nodes.astype(jnp.float32)
    center = values - jnp.mean(values, axis=-1, keepdims=True)
    spread = jnp.mean(center * center, axis=-1, keepdims=True)
    return (center * lax.rsqrt(spread + 1e-05) * gain).astype(jnp.bfloat16)


def apply_taps(extended, psi, lat_rows, lon_cols, basis_count, out_ch):
    members = extended.shape[0]
    ext_rows = extended.shape[2]
    ext_cols = extended.shape[3]
    split = extended.reshape(members, basis_count, out_ch, ext_rows, ext_cols)
    accum = None
    for row_off in range(5):
        for col_off in range(5):
            window = split[:, :, :, row_off : row_off + lat_rows, col_off : col_off + lon_cols]
            taps = psi[:, :, row_off, col_off][None, :, None, :, None]
            contrib = jnp.sum(taps * window, axis=1)
            accum = contrib if accum is None else accum + contrib
    return accum


def shards(nodes, norm_gain, w_qkv, w_out, w_latent, neighbours, assignment, psi, w_dec):
    members, rows, width = nodes.shape
    head_dim = width // HEADS
    count = neighbours.shape[1]
    normed = layer_norm(nodes, norm_gain)
    flat = normed.reshape(-1, width)
    reg_here = lax.axis_index("reg")
    lon_here = lax.axis_index("lon")
    sectors = lax.axis_size("lon")
    listed = neighbours[0]
    step_reg = listed // sectors - reg_here
    step_lon = (listed % sectors - lon_here + 1) % sectors - 1
    slots = (step_reg + 1) * 3 + step_lon + 1
    projected = jnp.dot(flat, w_qkv, preferred_element_type=jnp.float32)
    queries = projected[:, :width].astype(jnp.bfloat16)
    keyvals = projected[:, width:].astype(jnp.bfloat16).reshape(1, 1, members, rows, 2 * width)
    wider = with_halo(keyvals, (("reg", 0),), 1, False)
    wider = with_halo(wider, (("lon", 1),), 1, True)
    candidates = wider.reshape(9, members, rows, 2 * width)
    selected = jnp.take(candidates, slots, axis=0)
    keyset = selected.transpose(1, 0, 2, 3).reshape(members, count * rows, 2 * width)
    key_part = keyset[..., :width].reshape(members, count * rows, HEADS, head_dim)
    value_part = keyset[..., width:].reshape(members, count * rows, HEADS, head_dim)
    query_part = queries.reshape(members, rows, HEADS, head_dim)
    scale = 1.0 / head_dim**0.5
    scores = (
        jnp.einsum("mqhd,mkhd->mhqk", query_part, key_part, preferred_element_type=jnp.float32)
        * scale
    )
    top = jnp.max(scores, axis=-1, keepdims=True)
    expo = jnp.exp(scores - top)
    total = jnp.sum(expo, axis=-1, keepdims=True)
    summed = jnp.einsum(
        "mhqk,mkhd->mqhd", expo.astype(jnp.bfloat16), value_part, preferred_element_type=jnp.float32
    )
    attended = (summed / total.transpose(0, 2, 1, 3)).astype(jnp.bfloat16).reshape(-1, width)
    state = (
        nodes.reshape(-1, width).astype(jnp.float32)
        + jnp.dot(attended, w_out, preferred_element_type=jnp.float32)
    ).astype(jnp.bfloat16)
    latent = jax.nn.silu(jnp.dot(state, w_latent, preferred_element_type=jnp.float32)).astype(
        jnp.bfloat16
    )
    channels = w_latent.shape[1]
    latent = latent.reshape(members, rows, channels)
    lat_rows, lon_cols = assignment.shape
    local_nodes = (assignment % rows).reshape(-1)
    grid = jnp.take(latent, local_nodes, axis=1).reshape(members, lat_rows, lon_cols, channels)
    basis_count = psi.shape[0]
    out_ch = w_dec.shape[2]
    mixing = w_dec.transpose(1, 0, 2).reshape(channels, basis_count * out_ch)
    extended = with_halo(grid, (("reg", 1),), 2, False)
    extended = with_halo(extended, (("lon", 2),), 2, True)
    mixed = jnp.einsum("mijc,cn->mnij", extended, mixing, preferred_element_type=jnp.float32)
    accum = apply_taps(mixed, psi, lat_rows, lon_cols, basis_count, out_ch)
    fields = accum.astype(jnp.bfloat16)
    return (state.reshape(members, rows, width), fields)


def solution(mesh):
    in_specs = (
        P(None, ("reg", "lon"), None),
        P(),
        P(),
        P(),
        P(),
        P(("reg", "lon"), None),
        P("reg", "lon"),
        P(None, "reg", None, None),
        P(),
    )
    out_specs = (P(None, ("reg", "lon"), None), P(None, None, "reg", "lon"))
    return jax.shard_map(shards, mesh=mesh, in_specs=in_specs, out_specs=out_specs, check_vma=False)
```

profile of v0, /device:TPU:1, one launch (start us, length us, event | category | flops | bytes accessed | tf_op | source)
XLA Modules:
  0.0 124.5 jit_solution(5737258672986852372)
XLA Ops:
  2.9 1.3 %convolution_convert_fusion = bf16[128,1536]{1,0:T(8,128)(2,1)S(1)} fusion(bf16[512,1536]{1,0:T(8,128)(2,1)S(1)} %copy-done, bf16[1,128,512]{2,1,0:T(8,128)(2,1)} %param.9, f32[512]{0:T(512)} %param.10, f32[128]{0:T(128)S(1)} %add_rsqrt_fusion, f32[128]{0:T(128)S(1)} %broadcast_multiply_fusion), kind=kOutput, calls=%fused_computation.9 | convolution fusion | flops 201850880 | bytes 2100224 | tf_op jit(solution)/shard_map/dot_general | solution.py:57
  4.3 4.6 %collective-permute-start = (bf16[1,1,1,128,1024]{4,3,2,1,0:T(8,128)(2,1)S(1)}, bf16[1,1,1,128,1024]{4,3,2,1,0:T(8,128)(2,1)S(1)}, u32[]{:S(2)}, u32[]{:S(2)}) collective-permute-start(bf16[1,1,1,128,1024]{4,3,2,1,0:T(8,128)(2,1)S(1)} %slice_bitcast_fusion), channel_id=1, source_target_pairs={{0,4},{4,8},{8,12},{12,16},{16,20},{20,24},{24,28},{1,5},{5,9},{9,... | collective-permute-start | bytes 786440 | tf_op jit(solution)/shard_map/ppermute | solution.py:16
  8.9 1.9 %collective-permute-start.1 = (bf16[1,1,1,128,1024]{4,3,2,1,0:T(8,128)(2,1)S(1)}, bf16[1,1,1,128,1024]{4,3,2,1,0:T(8,128)(2,1)S(1)}, u32[]{:S(2)}, u32[]{:S(2)}) collective-permute-start(bf16[1,1,1,128,1024]{4,3,2,1,0:T(8,128)(2,1)S(1)} %slice_bitcast_fusion), channel_id=1, source_target_pairs={{4,0},{8,4},{12,8},{16,12},{20,16},{24,20},{28,24},{5,1},{9,5},{13... | collective-permute-start | bytes 786440 | tf_op jit(solution)/shard_map/ppermute | solution.py:17
  12.2 4.4 %collective-permute-done.1 = bf16[1,1,1,128,1024]{4,3,2,1,0:T(8,128)(2,1)S(1)} collective-permute-done((bf16[1,1,1,128,1024]{4,3,2,1,0:T(8,128)(2,1)S(1)}, bf16[1,1,1,128,1024]{4,3,2,1,0:T(8,128)(2,1)S(1)}, u32[]{:S(2)}, u32[]{:S(2)}) %collective-permute-start.1) | collective-permute-done | bytes 262176 | tf_op jit(solution)/shard_map/ppermute | solution.py:17
  17.5 1.5 %collective-permute-start.2 = (bf16[3,1,1,128,1024]{4,3,2,1,0:T(8,128)(2,1)}, bf16[3,1,1,128,1024]{4,3,2,1,0:T(8,128)(2,1)S(1)}, u32[]{:S(2)}, u32[]{:S(2)}) collective-permute-start(bf16[3,1,1,128,1024]{4,3,2,1,0:T(8,128)(2,1)} %pad_maximum_fusion.1), channel_id=1, source_target_pairs={{0,1},{1,2},{2,3},{3,0},{4,5},{5,6},{6,7},{7,4},{8,9},{9,10},{10,1... | collective-permute-start | bytes 2359304 | tf_op jit(solution)/shard_map/ppermute | solution.py:16
  20.7 1.7 %copy.17 = bf16[128,512]{0,1:T(8,128)(2,1)} copy(bf16[128,512]{1,0:T(8,128)(2,1)} %slice.232) | data formatting | bytes 262144 | tf_op jit(solution)/shard_map/slice | solution.py:58
  22.5 15.6 %collective-permute-done.2 = bf16[3,1,1,128,1024]{4,3,2,1,0:T(8,128)(2,1)S(1)} collective-permute-done((bf16[3,1,1,128,1024]{4,3,2,1,0:T(8,128)(2,1)}, bf16[3,1,1,128,1024]{4,3,2,1,0:T(8,128)(2,1)S(1)}, u32[]{:S(2)}, u32[]{:S(2)}) %collective-permute-start.2) | collective-permute-done | bytes 786464 | tf_op jit(solution)/shard_map/ppermute | solution.py:16
  38.1 13.1 %collective-permute-done.3 = bf16[3,1,1,128,1024]{4,3,2,1,0:T(8,128)(2,1)} collective-permute-done((bf16[3,1,1,128,1024]{4,3,2,1,0:T(8,128)(2,1)}, bf16[3,1,1,128,1024]{4,3,2,1,0:T(8,128)(2,1)}, u32[]{:S(2)}, u32[]{:S(2)}) %collective-permute-start.3) | collective-permute-done | bytes 786464 | tf_op jit(solution)/shard_map/ppermute | solution.py:17
  51.1 2.6 %pad_maximum_fusion = bf16[3,3,1,128,1024]{4,3,2,1,0:T(8,128)(2,1)} fusion(bf16[3,1,1,128,1024]{4,3,2,1,0:T(8,128)(2,1)} %collective-permute-done.3, bf16[1,1,1,128,1024]{4,3,2,1,0:T(8,128)(2,1)S(1)} %collective-permute-done.1, bf16[1,1,1,128,1024]{4,3,2,1,0:T(8,128)(2,1)S(1)} %slice_bitcast_fusion, ...), kind=kLoop, calls=%fused_computation.10 | loop fusion | flops 4718592 | bytes 4718592 | tf_op jit(solution)/shard_map/concatenate | solution.py:18
  53.7 2.3 %gather_fusion = bf16[5,128,1024]{2,1,0:T(8,128)(2,1)S(1)} fusion(bf16[9,128,1024]{2,1,0:T(8,128)(2,1)} %bitcast.172, s32[1024]{0:T(1024)S(1)} %pad_clamp_fusion.1), kind=kCustom, calls=%fused_computation | custom fusion | bytes 2621460 | tf_op jit(solution)/shard_map/jit(_take)/gather | solution.py:63
  56.0 1.5 %copy.16 = bf16[1,640,1024]{1,2,0:T(8,128)(2,1)} copy(bf16[1,640,1024]{2,1,0:T(8,128)(2,1)S(1)} %bitcast.173) | data formatting | bytes 2621440 | tf_op jit(solution)/shard_map/jit(_take)/gather | solution.py:63
  57.5 1.5 %broadcast_select_fusion = bf16[1,640,1024]{1,2,0:T(8,128)(2,1)S(1)} fusion(bf16[1,640,1024]{1,2,0:T(8,128)(2,1)} %copy.16, pred[640]{0:T(1024)(128)(4,1)S(1)} %broadcast_bitcast_fusion), kind=kLoop, calls=%fused_computation.71 | loop fusion | flops 655360 | bytes 2622080 | tf_op jit(solution)/shard_map/jit(_take)/select_n | solution.py:63
  60.8 1.4 %fusion = f32[16,128]{1,0:T(8,128)S(1)} fusion(f32[16,128,640]{2,1,0:T(8,128)S(1)} %get-tuple-element.61, f32[16,128]{1,0:T(8,128)S(1)} %get-tuple-element.60), kind=kLoop, calls=%fused_computation.4 | loop fusion | flops 3930112 | bytes 5259264 | tf_op jit(solution)/shard_map/reduce_sum | solution.py:75
  64.7 2.0 %gather_fusion.1 = bf16[512,512]{1,0:T(8,128)(2,1)S(1)} fusion(bf16[128,512]{1,0:T(8,128)(2,1)S(1)} %multiply_convert_fusion, s32[1024]{0:T(1024)S(1)} %pad_clamp_fusion), kind=kCustom, calls=%fused_computation.1 | custom fusion | bytes 1050624 | tf_op jit(solution)/shard_map/jit(_take)/gather | solution.py:91
  66.8 6.0 %collective-permute-start.4 = (bf16[1,2,256,512]{3,2,1,0:T(8,128)(2,1)S(1)}, bf16[1,2,256,512]{3,2,1,0:T(8,128)(2,1)S(1)}, u32[]{:S(2)}, u32[]{:S(2)}) collective-permute-start(bf16[1,2,256,512]{3,2,1,0:T(8,128)(2,1)S(1)} %broadcast_select_fusion.1), channel_id=1, source_target_pairs={{0,4},{4,8},{8,12},{12,16},{16,20},{20,24},{24,28},{1,5},{5,9},{9,... | collective-permute-start | bytes 1572872 | tf_op jit(solution)/shard_map/ppermute | solution.py:16
  72.7 1.9 %collective-permute-start.5 = (bf16[1,2,256,512]{3,2,1,0:T(8,128)(2,1)S(1)}, bf16[1,2,256,512]{3,2,1,0:T(8,128)(2,1)S(1)}, u32[]{:S(2)}, u32[]{:S(2)}) collective-permute-start(bf16[1,2,256,512]{3,2,1,0:T(8,128)(2,1)S(1)} %broadcast_select_fusion.1), channel_id=1, source_target_pairs={{4,0},{8,4},{12,8},{16,12},{20,16},{24,20},{28,24},{5,1},{9,5},{13... | collective-permute-start | bytes 1572872 | tf_op jit(solution)/shard_map/ppermute | solution.py:17
  75.3 3.6 %collective-permute-done.4 = bf16[1,2,256,512]{3,2,1,0:T(8,128)(2,1)S(1)} collective-permute-done((bf16[1,2,256,512]{3,2,1,0:T(8,128)(2,1)S(1)}, bf16[1,2,256,512]{3,2,1,0:T(8,128)(2,1)S(1)}, u32[]{:S(2)}, u32[]{:S(2)}) %collective-permute-start.4) | collective-permute-done | bytes 524320 | tf_op jit(solution)/shard_map/ppermute | solution.py:16
  78.9 4.4 %collective-permute-done.5 = bf16[1,2,256,512]{3,2,1,0:T(8,128)(2,1)S(1)} collective-permute-done((bf16[1,2,256,512]{3,2,1,0:T(8,128)(2,1)S(1)}, bf16[1,2,256,512]{3,2,1,0:T(8,128)(2,1)S(1)}, u32[]{:S(2)}, u32[]{:S(2)}) %collective-permute-start.5) | collective-permute-done | bytes 524320 | tf_op jit(solution)/shard_map/ppermute | solution.py:17
  88.2 5.0 %convolution_bitcast_fusion = f32[756,6,260]{0,2,1:T(8,128)} fusion(bf16[512,756,1]{0,1,2:T(8,128)(2,1)} %reshape.701, bf16[1,6,2,512]{3,2,1,0:T(2,128)(2,1)} %collective-permute-done.7, bf16[1,2,256,512]{3,2,1,0:T(8,128)(2,1)} %copy-done.4, bf16[1,2,256,512]{3,2,1,0:T(8,128)(2,1)S(1)} %broadcast_select_fusion.1, ...), kind=kOutput, calls=%fused_computation.11 | convolution fusion | flops 1215651840 | bytes 7089024 | tf_op jit(solution)/shard_map/mijc,cn->mnij/dot_general | solution.py:97
  93.2 6.6 %copy.18 = f32[756,6,260]{2,0,1:T(8,128)} copy(f32[756,6,260]{0,2,1:T(8,128)} %convolution_bitcast_fusion) | data formatting | bytes 9434880 | tf_op jit(solution)/shard_map/mijc,cn->mnij/dot_general | solution.py:97
  99.8 7.4 %transpose.46 = f32[1,9,84,6,260]{4,2,1,3,0:T(8,128)} reshape(f32[756,6,260]{2,0,1:T(8,128)} %copy.18) | data formatting | bytes 9434880 | tf_op jit(solution)/shard_map/reshape;mijc,cn->mnij/transpose | solution.py:33
  107.2 9.0 %fusion.28 = (f32[84,2,256]{2,0,1:T(8,128)S(1)}, f32[84,2,256]{2,0,1:T(8,128)S(1)}, f32[84,2,256]{2,0,1:T(8,128)S(1)}, f32[84,2,256]{2,0,1:T(8,128)S(1)}, f32[84...) fusion(f32[1,9,84,6,260]{4,2,1,3,0:T(8,128)} %transpose.46, ...), kind=kLoop, calls=%fused_computation.57 | loop fusion | flops 5117952 | bytes 12042744 | tf_op jit(solution)/shard_map/reduce_sum | solution.py:39
  116.3 3.3 %fusion.30 = (f32[84,2,256]{2,0,1:T(8,128)S(1)}, f32[84,2,256]{2,0,1:T(8,128)S(1)}, f32[84,2,256]{2,0,1:T(8,128)S(1)}, f32[84,2,256]{2,0,1:T(8,128)S(1)}, f32[84...) fusion(f32[1,9,84,6,260]{4,2,1,3,0:T(8,128)S(1)} %copy-done.1, ...), kind=kLoop, calls=%fused_computation.61 | loop fusion | flops 6580224 | bytes 15483528 | tf_op jit(solution)/shard_map/reduce_sum | solution.py:39
  119.6 3.8 %fusion.29 = (f32[84,2,256]{2,0,1:T(8,128)S(1)}, f32[84,2,256]{2,0,1:T(8,128)S(1)}, f32[84,2,256]{2,0,1:T(8,128)S(1)}, f32[84,2,256]{2,0,1:T(8,128)S(1)}, f32[84...) fusion(f32[1,9,84,6,260]{4,2,1,3,0:T(8,128)S(1)} %copy-done.1, ...), kind=kLoop, calls=%fused_computation.59 | loop fusion | flops 6580224 | bytes 15483528 | tf_op jit(solution)/shard_map/reduce_sum | solution.py:39
  (73 shorter events, 17.2 us)
Async XLA Ops:
  0.6 2.3 %copy-start = (bf16[512,1536]{1,0:T(8,128)(2,1)S(1)}, bf16[512,1536]{1,0:T(8,128)(2,1)}, u32[]{:S(2)}) copy-start(bf16[512,1536]{1,0:T(8,128)(2,1)} %param.11) | copy-start | bytes 4718596
  0.6 10.2 %copy-start.18 = (s32[1,5]{1,0:T(1,128)S(1)}, s32[1,5]{1,0:T(1,128)}, u32[]{:S(2)}) copy-start(s32[1,5]{1,0:T(1,128)} %param.14) | copy-start | bytes 64
  0.7 10.2 %copy-start.17 = (s32[2,256]{1,0:T(2,128)S(1)}, s32[2,256]{1,0:T(2,128)}, u32[]{:S(2)}) copy-start(s32[2,256]{1,0:T(2,128)} %param.15) | copy-start | bytes 6148
  4.3 7.9 %collective-permute-start = (bf16[1,1,1,128,1024]{4,3,2,1,0:T(8,128)(2,1)S(1)}, bf16[1,1,1,128,1024]{4,3,2,1,0:T(8,128)(2,1)S(1)}, u32[]{:S(2)}, u32[]{:S(2)}) collective-permute-start(bf16[1,1,1,128,1024]{4,3,2,1,0:T(8,128)(2,1)S(1)} %slice_bitcast_fusion), channel_id=1, source_target_pairs={{0,4},{4,8},{8,12},{12,16},{16,20},{20,24},{24,28},{1,5},{5,9},{9,... | collective-permute-start | bytes 786440 | tf_op jit(solution)/shard_map/ppermute | solution.py:16
  8.9 7.7 %collective-permute-start.1 = (bf16[1,1,1,128,1024]{4,3,2,1,0:T(8,128)(2,1)S(1)}, bf16[1,1,1,128,1024]{4,3,2,1,0:T(8,128)(2,1)S(1)}, u32[]{:S(2)}, u32[]{:S(2)}) collective-permute-start(bf16[1,1,1,128,1024]{4,3,2,1,0:T(8,128)(2,1)S(1)} %slice_bitcast_fusion), channel_id=1, source_target_pairs={{4,0},{8,4},{12,8},{16,12},{20,16},{24,20},{28,24},{5,1},{9,5},{13... | collective-permute-start | bytes 786440 | tf_op jit(solution)/shard_map/ppermute | solution.py:17
  17.5 20.5 %collective-permute-start.2 = (bf16[3,1,1,128,1024]{4,3,2,1,0:T(8,128)(2,1)}, bf16[3,1,1,128,1024]{4,3,2,1,0:T(8,128)(2,1)S(1)}, u32[]{:S(2)}, u32[]{:S(2)}) collective-permute-start(bf16[3,1,1,128,1024]{4,3,2,1,0:T(8,128)(2,1)} %pad_maximum_fusion.1), channel_id=1, source_target_pairs={{0,1},{1,2},{2,3},{3,0},{4,5},{5,6},{6,7},{7,4},{8,9},{9,10},{10,1... | collective-permute-start | bytes 2359304 | tf_op jit(solution)/shard_map/ppermute | solution.py:16
  19.0 32.1 %collective-permute-start.3 = (bf16[3,1,1,128,1024]{4,3,2,1,0:T(8,128)(2,1)}, bf16[3,1,1,128,1024]{4,3,2,1,0:T(8,128)(2,1)}, u32[]{:S(2)}, u32[]{:S(2)}) collective-permute-start(bf16[3,1,1,128,1024]{4,3,2,1,0:T(8,128)(2,1)} %pad_maximum_fusion.1), channel_id=1, source_target_pairs={{1,0},{2,1},{3,2},{0,3},{5,4},{6,5},{7,6},{4,7},{9,8},{10,9},{11,1... | collective-permute-start | bytes 2359304 | tf_op jit(solution)/shard_map/ppermute | solution.py:17
  62.3 1.2 copy-start.2
  62.3 2.1 %copy-start.19 = (bf16[512,512]{1,0:T(8,128)(2,1)S(1)}, bf16[512,512]{1,0:T(8,128)(2,1)}, u32[]{:S(2)}) copy-start(bf16[512,512]{1,0:T(8,128)(2,1)} %param.13) | copy-start | bytes 1572868
  64.6 10.0 %copy-start.8 = (f32[9,2,5,5]{0,1,3,2:T(2,128)S(1)}, f32[9,2,5,5]{0,1,3,2:T(2,128)}, u32[]{:S(2)}) copy-start(f32[9,2,5,5]{0,1,3,2:T(2,128)} %param.16) | copy-start | bytes 5404
  66.6 20.5 %copy-start.3 = (bf16[9,512,84]{1,2,0:T(8,128)(2,1)S(1)}, bf16[9,512,84]{1,2,0:T(8,128)(2,1)}, u32[]{:S(2)}) copy-start(bf16[9,512,84]{1,2,0:T(8,128)(2,1)} %param.17) | copy-start | bytes 2322436
  66.8 12.1 %collective-permute-start.4 = (bf16[1,2,256,512]{3,2,1,0:T(8,128)(2,1)S(1)}, bf16[1,2,256,512]{3,2,1,0:T(8,128)(2,1)S(1)}, u32[]{:S(2)}, u32[]{:S(2)}) collective-permute-start(bf16[1,2,256,512]{3,2,1,0:T(8,128)(2,1)S(1)} %broadcast_select_fusion.1), channel_id=1, source_target_pairs={{0,4},{4,8},{8,12},{12,16},{16,20},{20,24},{24,28},{1,5},{5,9},{9,... | collective-permute-start | bytes 1572872 | tf_op jit(solution)/shard_map/ppermute | solution.py:16
  72.7 10.5 %collective-permute-start.5 = (bf16[1,2,256,512]{3,2,1,0:T(8,128)(2,1)S(1)}, bf16[1,2,256,512]{3,2,1,0:T(8,128)(2,1)S(1)}, u32[]{:S(2)}, u32[]{:S(2)}) collective-permute-start(bf16[1,2,256,512]{3,2,1,0:T(8,128)(2,1)S(1)} %broadcast_select_fusion.1), channel_id=1, source_target_pairs={{4,0},{8,4},{12,8},{16,12},{20,16},{24,20},{28,24},{5,1},{9,5},{13... | collective-permute-start | bytes 1572872 | tf_op jit(solution)/shard_map/ppermute | solution.py:17
  84.1 4.1 %collective-permute-start.6 = (bf16[1,6,2,512]{3,2,1,0:T(2,128)(2,1)S(1)}, bf16[1,6,2,512]{3,2,1,0:T(2,128)(2,1)}, u32[]{:S(2)}, u32[]{:S(2)}) collective-permute-start(bf16[1,6,2,512]{3,2,1,0:T(2,128)(2,1)S(1)} %get-tuple-element.31), channel_id=1, source_target_pairs={{0,1},{1,2},{2,3},{3,0},{4,5},{5,6},{6,7},{7,4},{8,9},{9,10},{10,1... | collective-permute-start | bytes 36872 | tf_op jit(solution)/shard_map/ppermute | solution.py:16
  85.3 2.8 %collective-permute-start.7 = (bf16[1,6,2,512]{3,2,1,0:T(2,128)(2,1)S(1)}, bf16[1,6,2,512]{3,2,1,0:T(2,128)(2,1)}, u32[]{:S(2)}, u32[]{:S(2)}) collective-permute-start(bf16[1,6,2,512]{3,2,1,0:T(2,128)(2,1)S(1)} %get-tuple-element.32), channel_id=1, source_target_pairs={{1,0},{2,1},{3,2},{0,3},{5,4},{6,5},{7,6},{4,7},{9,8},{10,9},{11,1... | collective-permute-start | bytes 36872 | tf_op jit(solution)/shard_map/ppermute | solution.py:17
  107.2 9.0 %copy-start.1 = (f32[1,9,84,6,260]{4,2,1,3,0:T(8,128)S(1)}, f32[1,9,84,6,260]{4,2,1,3,0:T(8,128)}, u32[]{:S(2)}) copy-start(f32[1,9,84,6,260]{4,2,1,3,0:T(8,128)} %transpose.46) | copy-start | bytes 14152324
  107.2 9.1 %copy-start.9 = (f32[9,2]{0,1:T(2,128)S(1)}, f32[9,2]{0,1:T(2,128)}, u32[]{:S(2)}) copy-start(f32[9,2]{0,1:T(2,128)} %get-tuple-element.46) | copy-start | bytes 220
  107.2 9.1 %copy-start.10 = (f32[9,2]{0,1:T(2,128)S(1)}, f32[9,2]{0,1:T(2,128)}, u32[]{:S(2)}) copy-start(f32[9,2]{0,1:T(2,128)} %get-tuple-element.47) | copy-start | bytes 220
  107.2 9.1 %copy-start.11 = (f32[9,2]{0,1:T(2,128)S(1)}, f32[9,2]{0,1:T(2,128)}, u32[]{:S(2)}) copy-start(f32[9,2]{0,1:T(2,128)} %get-tuple-element.48) | copy-start | bytes 220
  107.2 9.1 %copy-start.12 = (f32[9,2]{0,1:T(2,128)S(1)}, f32[9,2]{0,1:T(2,128)}, u32[]{:S(2)}) copy-start(f32[9,2]{0,1:T(2,128)} %get-tuple-element.49) | copy-start | bytes 220
  107.2 9.1 %copy-start.16 = (f32[9,2]{0,1:T(2,128)S(1)}, f32[9,2]{0,1:T(2,128)}, u32[]{:S(2)}) copy-start(f32[9,2]{0,1:T(2,128)} %get-tuple-element.57) | copy-start | bytes 220
  116.3 3.3 %copy-start.13 = (f32[9,2]{0,1:T(2,128)S(1)}, f32[9,2]{0,1:T(2,128)}, u32[]{:S(2)}) copy-start(f32[9,2]{0,1:T(2,128)} %get-tuple-element.56) | copy-start | bytes 220
  116.3 3.3 %copy-start.14 = (f32[9,2]{0,1:T(2,128)S(1)}, f32[9,2]{0,1:T(2,128)}, u32[]{:S(2)}) copy-start(f32[9,2]{0,1:T(2,128)} %get-tuple-element.58) | copy-start | bytes 220
  116.3 3.3 %copy-start.15 = (f32[9,2]{0,1:T(2,128)S(1)}, f32[9,2]{0,1:T(2,128)}, u32[]{:S(2)}) copy-start(f32[9,2]{0,1:T(2,128)} %get-tuple-element.59) | copy-start | bytes 220
  (4 other events, 3.5 us)
where the time goes:
time: 125 us; the launch traced here: 124 us
  waiting for transfers between devices  42.3 us (34%)
  local copies, waits for them, and re-layouts  27.6 us (22%)
  other arithmetic  25.3 us (20%)
  starting transfers between devices  19.3 us (15%)
  matrix products  8.92 us (7%)
    ppermute x4, waiting for transfers between devices, with_halo(): after = lax.ppermute(leading, axis, down)  21.9 us
    ppermute x4, waiting for transfers between devices, with_halo(): before = lax.ppermute(last, axis, up)  20.5 us
    reduce_sum x3, other arithmetic, apply_taps(): contrib = jnp.sum(taps * window, axis=1)  16.1 us
    ppermute x4, starting transfers between devices, with_halo(): before = lax.ppermute(last, axis, up)  13.3 us
    transpose x1, local copies, waits for them, and re-layouts, apply_taps(): split = extended.reshape(members, basis_count, out_ch, ext_rows, ext_cols)  7.42 us
    dot_general x1, local copies, waits for them, and re-layouts, shards(): jnp.einsum('mijc,cn->mnij', extended, mixing, preferred_element_type=jnp....  6.6 us
    ppermute x4, starting transfers between devices, with_halo(): after = lax.ppermute(leading, axis, down)  5.96 us
    dot_general x1, matrix products, shards(): jnp.einsum('mijc,cn->mnij', extended, mixing, preferred_element_type=jnp....  4.99 us
  transfers between devices with their start and end apart: 8, of which 6 were waited for; matrix products, arithmetic and copies ran while one was open for 4% of the time, Pallas kernels for 0%

commit v1 on v0

v1 whole, which is shorter than its diff:
```python
import functools
import math

import jax
import jax.numpy as jnp
from jax import lax
from jax.experimental import pallas as pl
from jax.experimental.pallas import tpu as pltpu
from jax.sharding import PartitionSpec as P

HEADS = 16
REACH = 2
SIDE = 8
LANES = 128
F32 = jnp.float32
BF16 = jnp.bfloat16
NT = (((1,), (1,)), ((), ()))

BANDS = (
    ((-2, (0,)), (-1, (0, 1))),
    ((0, (0, 1)), (1, (0, 1))),
    ((2, (0, 1)), (3, (1,))),
)
TAPS = 2 * REACH + 1


def band_blocks(band):
    return [
        (out_row, src - out_row + REACH, off)
        for src, out_rows in BANDS[band]
        for off in range(TAPS)
        for out_row in out_rows
    ]


def iota(shape, dim):
    return lax.broadcasted_iota(jnp.int32, shape, dim)


def normalise(rows, gain):
    values = rows.astype(F32)
    center = values - jnp.mean(values, axis=-1, keepdims=True)
    spread = jnp.mean(center * center, axis=-1, keepdims=True)
    return (center * lax.rsqrt(spread + 1e-05) * gain).astype(BF16)


def prepare_kernel(x_ref, gain_ref, wqkv_ref, psi_ref, dec_ref, query_ref, key_ref, value_ref, wvt_ref, *out):
    band_refs, taps_ref = out[:3], out[3]
    rows, width = x_ref.shape
    group, members = query_ref.shape[1], query_ref.shape[2] // rows
    head = group // members
    normed = normalise(x_ref[...], gain_ref[...])
    query = jnp.dot(normed, wqkv_ref[:, :width], preferred_element_type=F32)
    query_t = query.T.astype(BF16)
    mask = (iota((group, members * rows), 0) // head) == (iota((group, members * rows), 1) // rows)
    for part in range(width // group):
        piece = query_t[part * group : (part + 1) * group]
        wide = jnp.concatenate([piece] * members, axis=1)
        query_ref[part] = jnp.where(mask, wide, jnp.zeros_like(wide))
    key_ref[...] = jnp.dot(
        normed, wqkv_ref[:, width : 2 * width], preferred_element_type=F32
    ).astype(BF16)
    wvt = wqkv_ref[:, 2 * width :].astype(F32).T.astype(BF16)
    wvt_ref[...] = wvt
    value_ref[...] = lax.dot_general(wvt, normed, NT, preferred_element_type=F32).astype(BF16)

    groups, depth, channels = dec_ref.shape
    basis = psi_ref.shape[1]
    own = depth // basis
    padded = band_refs[0].shape[1] // groups
    spread = (iota((basis, depth), 1) // own == iota((basis, depth), 0)).astype(F32)
    expanded = jnp.dot(psi_ref[...], spread, preferred_element_type=F32)
    pick = iota((padded, depth), 1) % own == iota((padded, depth), 0)
    blocks = [(band, at) + item for band in range(3) for at, item in enumerate(band_blocks(band))]
    for at, (_, _, out_row, tap, off) in enumerate(blocks):
        source = (out_row * TAPS + tap) * TAPS + off
        line = jnp.broadcast_to(expanded[source : source + 1], (padded, depth))
        taps_ref[at * padded : (at + 1) * padded, :] = jnp.where(pick, line, 0.0).astype(BF16)
    for piece in range(groups):
        start = 0
        for band in range(3):
            count = band_refs[band].shape[0]
            mixed = jnp.dot(
                taps_ref[start * padded : (start + count) * padded, :],
                dec_ref[piece],
                preferred_element_type=F32,
            ).astype(BF16)
            band_refs[band][:, piece * padded : (piece + 1) * padded, :] = mixed.reshape(
                count, padded, channels
            )
            start += count


def attend_kernel(
    sectors,
    listed_ref, assign_ref, x_ref, left_ref, right_ref, up_ref, down_ref, upper_ref, lower_ref,
    gain_ref, wqkv_ref, query_ref, key_ref, value_ref, wvt_ref, wout_ref, wlat_ref,
    state_ref, latent_ref, west_ref, east_ref,
    near_ref, keys_ref, values_ref, attended_ref,
):
    rows, width = x_ref.shape
    count = listed_ref.shape[1]
    parts, group, lanes = query_ref.shape
    members = lanes // rows
    head = group // members
    reg_here, lon_here = lax.axis_index("reg"), lax.axis_index("lon")
    sources = (
        (upper_ref, 0), (up_ref, 0), (upper_ref, rows),
        (left_ref, 0), None, (right_ref, 0),
        (lower_ref, 0), (down_ref, 0), (lower_ref, rows),
    )
    slots = []
    for at in range(1, count):
        block = listed_ref[0, at]
        step_reg = block // sectors - reg_here
        step_lon = (block % sectors - lon_here + 1 + sectors) % sectors - 1
        slots.append((step_reg + 1) * 3 + step_lon + 1)
    for slot, source in enumerate(sources):
        if source is None:
            continue
        ref, start = source
        place = jnp.int32(-1)
        for at, value in enumerate(slots):
            place = jnp.where(value == slot, at, place)

        @pl.when(place >= 0)
        def _():
            near_ref[place] = ref[start : start + rows, :]

    normed = normalise(near_ref[...].reshape((count - 1) * rows, width), gain_ref[...])
    keys_ref[:rows] = key_ref[...]
    keys_ref[rows:] = jnp.dot(
        normed, wqkv_ref[:, width : 2 * width], preferred_element_type=F32
    ).astype(BF16)
    values_ref[:, :rows] = value_ref[...]
    values_ref[:, rows:] = lax.dot_general(
        wvt_ref[...], normed, NT, preferred_element_type=F32
    ).astype(BF16)
    scale = math.log2(math.e) / head**0.5
    owner = iota((group, rows), 0) // head
    for part in range(parts):
        span = slice(part * group, (part + 1) * group)
        scores = jnp.dot(keys_ref[:, span], query_ref[part], preferred_element_type=F32)
        top = jnp.max(scores, axis=0, keepdims=True)
        expo = jnp.exp2((scores - top) * scale)
        total = jnp.sum(expo, axis=0, keepdims=True)
        summed = jnp.dot(values_ref[span, :], expo.astype(BF16), preferred_element_type=F32)
        summed = summed * (1.0 / total)
        merged = None
        for member in range(members):
            piece = summed[:, member * rows : (member + 1) * rows]
            merged = piece if merged is None else jnp.where(owner == member, piece, merged)
        attended_ref[:, span] = merged.T.astype(BF16)
    state = (
        x_ref[...].astype(F32)
        + jnp.dot(attended_ref[...], wout_ref[...], preferred_element_type=F32)
    ).astype(BF16)
    state_ref[...] = state
    value = jnp.dot(state, wlat_ref[...], preferred_element_type=F32)
    latent = (value / (1.0 + jnp.exp(-value))).astype(BF16)
    latent_ref[...] = latent
    lat_rows, lon_cols = assign_ref.shape
    for ref, first in ((west_ref, 0), (east_ref, lon_cols - REACH)):
        cells = ref.shape[0]
        line, node = iota((cells, rows), 0), iota((cells, rows), 1)
        hit = jnp.zeros((cells, rows), F32)
        for row in range(lat_rows):
            for col in range(REACH):
                local = assign_ref[row, first + col] % rows
                hit = jnp.where((line == row * REACH + col) & (node == local), 1.0, hit)
        ref[...] = jnp.dot(hit.astype(BF16), latent, preferred_element_type=F32).astype(BF16)


def band_sum(band, latent, weights_ref, places, acc):
    blocks, outputs, channels = weights_ref.shape
    nodes = latent.shape[0]
    cols = places[0].shape[1]
    rows = nodes - 2 * SIDE
    shares = lax.dot_general(
        weights_ref[...].reshape(blocks * outputs, channels), latent, NT, preferred_element_type=F32
    ).astype(BF16)
    column = iota((8, cols), 1)
    node = iota((nodes, cols), 0).astype(F32)
    start = 0
    for line, (_, out_rows) in enumerate(BANDS[band]):
        for off in range(TAPS):
            step = off - REACH
            where = jnp.broadcast_to(places[line], (8, cols))
            if step:
                where = pltpu.roll(where, (-step) % cols, 1)
            reach = column + step
            where = jnp.where(reach < 0, (rows + REACH * line + reach + REACH).astype(F32), where)
            where = jnp.where(
                reach >= cols, (rows + SIDE + REACH * line + reach - cols).astype(F32), where
            )
            hot = jnp.where(node == where[:1], 1.0, 0.0).astype(BF16)
            size = len(out_rows) * outputs
            part = jnp.dot(shares[start : start + size], hot, preferred_element_type=F32)
            start += size
            for at, out_row in enumerate(out_rows):
                piece = part[at * outputs : (at + 1) * outputs]
                acc[out_row] = piece if acc[out_row] is None else acc[out_row] + piece
    return acc


def lines_of(line_ref, start, cols):
    values = line_ref[start : start + 16, :].astype(F32)
    return [values[:1, :cols], values[:1, cols:]]


def own_kernel(line_ref, latent_ref, weights_ref, out_ref):
    cols = out_ref.shape[2]
    acc = band_sum(1, latent_ref[...], weights_ref, lines_of(line_ref, 0, cols), [None, None])
    for row in range(2):
        out_ref[row] = acc[row]


def fields_kernel(
    begin, upper_ref, lower_ref, up_ref, down_ref, above_ref, below_ref, own_ref, out_ref
):
    cols = own_ref.shape[2]
    acc = [own_ref[0], own_ref[1]]
    acc = band_sum(0, up_ref[...], above_ref, lines_of(upper_ref, begin, cols), acc)
    acc = band_sum(2, down_ref[...], below_ref, lines_of(lower_ref, begin, cols), acc)
    out_ch = out_ref.shape[0]
    groups = 3
    padded, size = own_ref.shape[1] // groups, out_ch // groups
    for row in range(2):
        for piece in range(groups):
            out_ref[piece * size : (piece + 1) * size, row, :] = acc[row][
                piece * padded : piece * padded + size
            ].astype(BF16)


def whole(memory=pltpu.VMEM):
    return pl.BlockSpec(memory_space=memory)


def struct(*shape, dtype=BF16):
    return jax.ShapeDtypeStruct(shape, dtype)


def params(limit):
    return pltpu.CompilerParams(vmem_limit_bytes=limit << 20)


def cost(flops, moved):
    return pl.CostEstimate(flops=int(flops), bytes_accessed=int(moved), transcendentals=0)


def shards(nodes, norm_gain, w_qkv, w_out, w_latent, neighbours, assignment, psi, w_dec):
    _, rows, width = nodes.shape
    channels = w_latent.shape[1]
    lat_rows, lon_cols = assignment.shape
    basis, _, out_ch = w_dec.shape
    sectors = lax.axis_size("lon")
    count = neighbours.shape[1]
    x = nodes.reshape(rows, width)
    gain = norm_gain.reshape(1, width)

    def shifted(array, axis, step, wrap):
        size = lax.axis_size(axis)
        pairs = [(i, (i + step) % size) for i in range(size) if wrap or 0 <= i + step < size]
        return lax.ppermute(array, axis, pairs)

    left = shifted(x, "lon", 1, True)
    right = shifted(x, "lon", -1, True)
    up = shifted(x, "reg", 1, False)
    down = shifted(x, "reg", -1, False)

    line = (assignment % rows).astype(BF16).reshape(1, lat_rows * lon_cols)
    line = jnp.pad(line, ((0, 15), (0, 0)))
    both = jnp.concatenate([left, right, line], axis=0)
    upper = shifted(both, "reg", 1, False)
    lower = shifted(both, "reg", -1, False)

    groups, padded = 3, 32
    own = out_ch // groups
    depth = basis * own
    dec = w_dec.transpose(0, 2, 1).reshape(basis, groups, own, channels).transpose(1, 0, 2, 3)
    dec = dec.reshape(groups, depth, channels)
    taps = psi.transpose(1, 2, 3, 0).reshape(lat_rows * TAPS * TAPS, basis)
    head = width // HEADS
    members = LANES // head
    parts = HEADS // members
    sizes = [len(band_blocks(band)) for band in range(3)]
    query, key, value, wvt, above, middle, below = pl.pallas_call(
        prepare_kernel,
        in_specs=[whole()] * 5,
        out_specs=[whole()] * 7,
        out_shape=[
            struct(parts, LANES, members * rows),
            struct(rows, width),
            struct(width, rows),
            struct(width, width),
        ]
        + [struct(size, groups * padded, channels) for size in sizes],
        scratch_shapes=[pltpu.VMEM((sum(sizes) * padded, depth), BF16)],
        compiler_params=params(32),
        cost_estimate=cost(3e9, 1.2e7),
        name="prepare",
    )(x, gain, w_qkv, taps, dec)

    state, latent, west, east = pl.pallas_call(
        functools.partial(attend_kernel, sectors),
        in_specs=[whole(pltpu.SMEM)] * 2 + [whole()] * 15,
        out_specs=[whole()] * 4,
        out_shape=[struct(rows, width), struct(rows, channels), struct(16, channels), struct(16, channels)],
        scratch_shapes=[
            pltpu.VMEM((count - 1, rows, width), BF16),
            pltpu.VMEM((count * rows, width), BF16),
            pltpu.VMEM((width, count * rows), BF16),
            pltpu.VMEM((rows, width), BF16),
        ],
        compiler_params=params(32),
        cost_estimate=cost(4e9, 6e6),
        name="attend",
    )(
        neighbours, assignment, x, left, right, up, down, upper, lower,
        gain, w_qkv, query, key, value, wvt, w_out, w_latent,
    )

    from_left = shifted(east, "lon", 1, True)
    from_right = shifted(west, "lon", -1, True)
    extended = jnp.concatenate([latent, from_left[:SIDE], from_right[:SIDE]], axis=0)
    north = shifted(extended, "reg", 1, False)
    south = shifted(extended, "reg", -1, False)

    partial = pl.pallas_call(
        own_kernel,
        in_specs=[whole()] * 3,
        out_specs=whole(),
        out_shape=struct(lat_rows, groups * padded, lon_cols, dtype=F32),
        compiler_params=params(32),
        cost_estimate=cost(1e9, 2.5e6),
        name="own_band",
    )(line, extended, middle)
    fields = pl.pallas_call(
        functools.partial(fields_kernel, 2 * rows),
        in_specs=[whole()] * 7,
        out_specs=whole(),
        out_shape=struct(out_ch, lat_rows, lon_cols),
        compiler_params=params(32),
        cost_estimate=cost(2e9, 4e6),
        name="fields",
    )(upper, lower, north, south, above, below, partial)
    return (state.reshape(1, rows, width), fields.reshape(1, out_ch, lat_rows, lon_cols))


def solution(mesh):
    in_specs = (
        P(None, ("reg", "lon"), None),
        P(),
        P(),
        P(),
        P(),
        P(("reg", "lon"), None),
        P("reg", "lon"),
        P(None, "reg", None, None),
        P(),
    )
    out_specs = (P(None, ("reg", "lon"), None), P(None, None, "reg", "lon"))
    return jax.shard_map(shards, mesh=mesh, in_specs=in_specs, out_specs=out_specs, check_vma=False)
```

time: 125 us -> 47.5 us (0.38)
  waiting for transfers between devices: 42.3 us -> 8.67 us
  other arithmetic: 25.3 us -> 0.73 us
  local copies, waits for them, and re-layouts: 27.6 us -> 3.63 us
  Pallas kernels: 0 us -> 10.6 us
  matrix products: 8.92 us -> 0 us
  starting transfers between devices: 19.3 us -> 22.2 us
    ppermute x8 -> x10, waiting for transfers between devices: 42.3 us -> 8.67 us  [shifted(): return lax.ppermute(array, axis, pairs)]
    reduce_sum x6 -> x0, other arithmetic: 19.8 us -> none  [the longest x3 16.1 us: apply_taps(): contrib = jnp.sum(taps * window, axis=1)]
    pallas_call x0 -> x4, Pallas kernels: none -> 10.6 us  [the longest x1 5.08 us: shards(): pl.pallas_call(functools.partial(attend_kernel, sectors), in_specs=[whole...]
    dot_general x6 -> x0, matrix products: 8.92 us -> none  [the longest x1 4.99 us: shards(): jnp.einsum('mijc,cn->mnij', extended, mixing, preferred_element_type=jnp....]
    transpose x1, local copies, waits for them, and re-layouts: 7.42 us -> 0.01 us  [shards(): taps = psi.transpose(1, 2, 3, 0).reshape(lat_rows * TAPS * TAPS, basis)]
    dot_general x1 -> x0, local copies, waits for them, and re-layouts: 6.6 us -> none  [shards(): jnp.einsum('mijc,cn->mnij', extended, mixing, preferred_element_type=jnp....]
    gather x3 -> x0, local copies, waits for them, and re-layouts: 5.73 us -> none  [the longest x2 3.76 us: shards(): selected = jnp.take(candidates, slots, axis=0)]
    concatenate x2, other arithmetic: 3.53 us -> 0.03 us  [the longest x1 0.02 us: shards(): both = jnp.concatenate([left, right, line], axis=0)]
  transfers between devices with their start and end apart: 8 -> 10, of which waited for: 6 -> 4; matrix products, arithmetic and copies ran while one was open for 4% -> 9% of each run, Pallas kernels for 0% -> 7%
where the time goes in v1:
time: 47.5 us; the launch traced here: 46.7 us
  starting transfers between devices  22.2 us (47%)
  Pallas kernels  10.6 us (22%)
  waiting for transfers between devices  8.67 us (18%)
  local copies, waits for them, and re-layouts  3.63 us (8%)
  between operations  0.88 us (2%)
  other arithmetic  0.73 us (2%)
    ppermute x10, starting transfers between devices, shifted(): return lax.ppermute(array, axis, pairs)  22.2 us
    ppermute x10, waiting for transfers between devices, shifted(): return lax.ppermute(array, axis, pairs)  8.67 us
    pallas_call x1, Pallas kernels, shards(): pl.pallas_call(functools.partial(attend_kernel, sectors), in_specs=[whole...  5.08 us
    pallas_call x1, Pallas kernels, shards(): pl.pallas_call(functools.partial(fields_kernel, 2 * rows), in_specs=[whol...  2.49 us
    reshape x2, local copies, waits for them, and re-layouts, shards(): w_dec.transpose(0, 2, 1).reshape(basis, groups, own, channels)  2.19 us
    pallas_call x1, Pallas kernels, shards(): pl.pallas_call(prepare_kernel, in_specs=[whole()] * 5, out_specs=[whole()...  2.01 us
    reshape x1, local copies, waits for them, and re-layouts, shards(): dec = dec.reshape(groups, depth, channels)  1.37 us
    pallas_call x1, Pallas kernels, shards(): pl.pallas_call(own_kernel, in_specs=[whole()] * 3, out_specs=whole(), out...  1.04 us
  transfers between devices with their start and end apart: 10, of which 4 were waited for; matrix products, arithmetic and copies ran while one was open for 9% of the time, Pallas kernels for 7%

profile of v1, /device:TPU:1, one launch (start us, length us, event | category | flops | bytes accessed | tf_op | source)
XLA Modules:
  0.0 46.7 jit_solution(349157637890279161)
XLA Ops:
  0.6 2.1 %collective-permute-start = (bf16[128,512]{1,0:T(8,128)(2,1)}, bf16[128,512]{1,0:T(8,128)(2,1)S(1)}, u32[]{:S(2)}, u32[]{:S(2)}) collective-permute-start(bf16[128,512]{1,0:T(8,128)(2,1)} %bitcast.13), channel_id=1, source_target_pairs={{0,1},{1,2},{2,3},{3,0},{4,5},{5,6},{6,7},{7,4},{8,9},{9,10},{10,1... | collective-permute-start | bytes 393224 | tf_op jit(solution)/shard_map/ppermute | solution.py:264
  2.7 1.0 %collective-permute-start.1 = (bf16[128,512]{1,0:T(8,128)(2,1)}, bf16[128,512]{1,0:T(8,128)(2,1)S(1)}, u32[]{:S(2)}, u32[]{:S(2)}) collective-permute-start(bf16[128,512]{1,0:T(8,128)(2,1)} %bitcast.14), channel_id=1, source_target_pairs={{0,3},{1,0},{2,1},{3,2},{4,7},{5,4},{6,5},{7,6},{8,11},{9,8},{10,9... | collective-permute-start | bytes 393224 | tf_op jit(solution)/shard_map/ppermute | solution.py:264
  3.7 4.4 %collective-permute-start.2 = (bf16[128,512]{1,0:T(8,128)(2,1)}, bf16[128,512]{1,0:T(8,128)(2,1)S(1)}, u32[]{:S(2)}, u32[]{:S(2)}) collective-permute-start(bf16[128,512]{1,0:T(8,128)(2,1)} %bitcast.15), channel_id=1, source_target_pairs={{0,4},{4,8},{8,12},{12,16},{16,20},{20,24},{24,28},{1,5},{5,9},{9,... | collective-permute-start | bytes 393224 | tf_op jit(solution)/shard_map/ppermute | solution.py:264
  8.2 1.9 %collective-permute-start.3 = (bf16[128,512]{1,0:T(8,128)(2,1)}, bf16[128,512]{1,0:T(8,128)(2,1)S(1)}, u32[]{:S(2)}, u32[]{:S(2)}) collective-permute-start(bf16[128,512]{1,0:T(8,128)(2,1)} %bitcast.16), channel_id=1, source_target_pairs={{4,0},{8,4},{12,8},{16,12},{20,16},{24,20},{28,24},{5,1},{9,5},{13... | collective-permute-start | bytes 393224 | tf_op jit(solution)/shard_map/ppermute | solution.py:264
  10.1 0.7 %fusion.2 = bf16[1,1,2,256]{3,2,1,0:T(2,128)(2,1)S(1)} fusion(s32[2,256]{1,0:T(2,128)} %assign_ref.1), kind=kLoop, calls=%fused_computation.8 | loop fusion | flops 6144 | bytes 3072
  10.8 1.2 %reshape.32 = bf16[9,3,28,512]{3,2,1,0:T(8,128)(2,1)S(1)} reshape(bf16[9,84,512]{2,1,0:T(8,128)(2,1)} %bitcast.22) | data formatting | bytes 1548288 | tf_op jit(solution)/shard_map/reshape | solution.py:280
  12.1 1.0 %copy.17 = bf16[9,3,28,512]{3,2,0,1:T(8,128)(2,1)} copy(bf16[9,3,28,512]{3,2,1,0:T(8,128)(2,1)S(1)} %reshape.32) | data formatting | bytes 1548288 | tf_op jit(solution)/shard_map/reshape | solution.py:280
  13.1 1.4 %reshape.33.dec_ref = bf16[3,252,512]{2,1,0:T(8,128)(2,1)S(1)} reshape(bf16[3,9,28,512]{3,2,1,0:T(8,128)(2,1)} %bitcast.21) | data formatting | bytes 1548288 | tf_op jit(solution)/shard_map/reshape | solution.py:281
  14.5 3.6 %collective-permute-start.4 = (bf16[272,512]{1,0:T(8,128)(2,1)S(1)}, bf16[272,512]{1,0:T(8,128)(2,1)S(1)}, u32[]{:S(2)}, u32[]{:S(2)}) collective-permute-start(bf16[272,512]{1,0:T(8,128)(2,1)S(1)} %pad_maximum_fusion), channel_id=1, source_target_pairs={{0,4},{4,8},{8,12},{12,16},{16,20},{20,24},{24,28},{1,5},{5,9},{9,... | collective-permute-start | bytes 835592 | tf_op jit(solution)/shard_map/ppermute | solution.py:264
  18.2 1.9 %collective-permute-start.5 = (bf16[272,512]{1,0:T(8,128)(2,1)S(1)}, bf16[272,512]{1,0:T(8,128)(2,1)S(1)}, u32[]{:S(2)}, u32[]{:S(2)}) collective-permute-start(bf16[272,512]{1,0:T(8,128)(2,1)S(1)} %pad_maximum_fusion), channel_id=1, source_target_pairs={{4,0},{8,4},{12,8},{16,12},{20,16},{24,20},{28,24},{5,1},{9,5},{13... | collective-permute-start | bytes 835592 | tf_op jit(solution)/shard_map/ppermute | solution.py:264
  20.1 0.0 copy-start
  20.2 0.0 copy-start.6
  20.2 2.0 %prepare.1 = (bf16[4,128,512]{2,1,0:T(8,128)(2,1)S(1)}, bf16[128,512]{1,0:T(8,128)(2,1)S(1)}, bf16[512,128]{1,0:T(8,128)(2,1)S(1)}, bf16[512,512]{1,0:T(8,128)(2...) custom-call(bf16[128,512]{1,0:T(8,128)(2,1)S(1)} %bitcast.17, ...), custom_call_target="tpu_custom_call" | custom-call | flops 3000000000 | bytes 12000000 | tf_op jit(solution)/shard_map/prepare/pallas_call | solution.py:287
  22.2 3.8 %collective-permute-done.5.lower_ref = bf16[272,512]{1,0:T(8,128)(2,1)S(1)} collective-permute-done((bf16[272,512]{1,0:T(8,128)(2,1)S(1)}, bf16[272,512]{1,0:T(8,128)(2,1)S(1)}, u32[]{:S(2)}, u32[]{:S(2)}) %collective-permute-start.5) | collective-permute-done | bytes 278560 | tf_op jit(solution)/shard_map/ppermute | solution.py:264
  26.1 5.1 %attend.1 = (bf16[128,512]{1,0:T(8,128)(2,1)}, bf16[128,512]{1,0:T(8,128)(2,1)S(1)}, bf16[16,512]{1,0:T(8,128)(2,1)S(1)}, bf16[16,512]{1,0:T(8,128)(2,1)S(1)}) custom-call(s32[1,5]{1,0:T(1,128)S(1)} %copy-done.6, s32[2,256]{1,0:T(2,128)S(1)} %copy-done, bf16[128,512]{1,0:T(8,128)(2,1)S(1)} %bitcast.18, bf16[128,512]{1,0:T(8,128)(2,1)S(1)} %collective-permute-done.left_ref, ...), custom_call_target="tpu_custom_call" | custom-call | flops 4000000000 | bytes 6000000 | tf_op jit(solution)/shard_map/attend/pallas_call | solution.py:304
  31.2 0.3 collective-permute-start.6
  31.5 2.1 %collective-permute-start.7 = (bf16[16,512]{1,0:T(8,128)(2,1)S(1)}, bf16[16,512]{1,0:T(8,128)(2,1)S(1)}, u32[]{:S(2)}, u32[]{:S(2)}) collective-permute-start(bf16[16,512]{1,0:T(8,128)(2,1)S(1)} %get-tuple-element.20), channel_id=1, source_target_pairs={{0,3},{1,0},{2,1},{3,2},{4,7},{5,4},{6,5},{7,6},{8,11},{9,8},{10,9... | collective-permute-start | bytes 49160 | tf_op jit(solution)/shard_map/ppermute | solution.py:264
  33.5 1.1 %collective-permute-done.6 = bf16[16,512]{1,0:T(8,128)(2,1)S(1)} collective-permute-done((bf16[16,512]{1,0:T(8,128)(2,1)S(1)}, bf16[16,512]{1,0:T(8,128)(2,1)S(1)}, u32[]{:S(2)}, u32[]{:S(2)}) %collective-permute-start.6) | collective-permute-done | bytes 16416 | tf_op jit(solution)/shard_map/ppermute | solution.py:264
  34.6 0.2 collective-permute-done.7
  34.9 2.9 %collective-permute-start.8 = (bf16[144,512]{1,0:T(8,128)(2,1)S(1)}, bf16[144,512]{1,0:T(8,128)(2,1)S(1)}, u32[]{:S(2)}, u32[]{:S(2)}) collective-permute-start(bf16[144,512]{1,0:T(8,128)(2,1)S(1)} %pad_maximum_fusion.1.latent_ref), channel_id=1, source_target_pairs={{0,4},{4,8},{8,12},{12,16},{16,20},{20,24},{24,28},{1,5},{5,9},{9,... | collective-permute-start | bytes 442376 | tf_op jit(solution)/shard_map/ppermute | solution.py:264
  37.8 1.9 %collective-permute-start.9 = (bf16[144,512]{1,0:T(8,128)(2,1)S(1)}, bf16[144,512]{1,0:T(8,128)(2,1)S(1)}, u32[]{:S(2)}, u32[]{:S(2)}) collective-permute-start(bf16[144,512]{1,0:T(8,128)(2,1)S(1)} %pad_maximum_fusion.1.latent_ref), channel_id=1, source_target_pairs={{4,0},{8,4},{12,8},{16,12},{20,16},{24,20},{28,24},{5,1},{9,5},{13... | collective-permute-start | bytes 442376 | tf_op jit(solution)/shard_map/ppermute | solution.py:264
  39.7 1.0 %own_band.1.own_ref = f32[2,96,256]{2,1,0:T(8,128)S(1)} custom-call(bf16[16,512]{1,0:T(8,128)(2,1)S(1)} %pad.4.line_ref, bf16[144,512]{1,0:T(8,128)(2,1)S(1)} %pad_maximum_fusion.1.latent_ref, bf16[20,96,512]{2,1,0:T(8,128)(2,1)S(1)} %get-tuple-element.23.weights_ref), custom_call_target="tpu_custom_call" | custom-call | flops 1000000000 | bytes 2500000 | tf_op jit(solution)/shard_map/own_band/pallas_call | solution.py:329
  40.8 3.5 %collective-permute-done.9.down_ref = bf16[144,512]{1,0:T(8,128)(2,1)S(1)} collective-permute-done((bf16[144,512]{1,0:T(8,128)(2,1)S(1)}, bf16[144,512]{1,0:T(8,128)(2,1)S(1)}, u32[]{:S(2)}, u32[]{:S(2)}) %collective-permute-start.9) | collective-permute-done | bytes 147488 | tf_op jit(solution)/shard_map/ppermute | solution.py:264
  44.3 2.5 %fields.1 = bf16[84,2,256]{2,1,0:T(2,128)(2,1)} custom-call(bf16[272,512]{1,0:T(8,128)(2,1)S(1)} %collective-permute-done.4.upper_ref, bf16[272,512]{1,0:T(8,128)(2,1)S(1)} %collective-permute-done.5.lower_ref, bf16[144,512]{1,0:T(8,128)(2,1)S(1)} %collective-permute-done.8.up_ref, bf16[144,512]{1,0:T(8,128)(2,1)S(1)} %collective-permute-done.9.down_ref, ...), custom_call_target="tpu_custom_call" | custom-call | flops 2000000000 | bytes 4000000 | tf_op jit(solution)/shard_map/fields/pallas_call | solution.py:338
  (28 shorter events, 0.1 us)
Async XLA Ops:
  0.6 13.9 %collective-permute-start = (bf16[128,512]{1,0:T(8,128)(2,1)}, bf16[128,512]{1,0:T(8,128)(2,1)S(1)}, u32[]{:S(2)}, u32[]{:S(2)}) collective-permute-start(bf16[128,512]{1,0:T(8,128)(2,1)} %bitcast.13), channel_id=1, source_target_pairs={{0,1},{1,2},{2,3},{3,0},{4,5},{5,6},{6,7},{7,4},{8,9},{9,10},{10,1... | collective-permute-start | bytes 393224 | tf_op jit(solution)/shard_map/ppermute | solution.py:264
  2.7 11.8 %collective-permute-start.1 = (bf16[128,512]{1,0:T(8,128)(2,1)}, bf16[128,512]{1,0:T(8,128)(2,1)S(1)}, u32[]{:S(2)}, u32[]{:S(2)}) collective-permute-start(bf16[128,512]{1,0:T(8,128)(2,1)} %bitcast.14), channel_id=1, source_target_pairs={{0,3},{1,0},{2,1},{3,2},{4,7},{5,4},{6,5},{7,6},{8,11},{9,8},{10,9... | collective-permute-start | bytes 393224 | tf_op jit(solution)/shard_map/ppermute | solution.py:264
  3.7 18.5 %collective-permute-start.2 = (bf16[128,512]{1,0:T(8,128)(2,1)}, bf16[128,512]{1,0:T(8,128)(2,1)S(1)}, u32[]{:S(2)}, u32[]{:S(2)}) collective-permute-start(bf16[128,512]{1,0:T(8,128)(2,1)} %bitcast.15), channel_id=1, source_target_pairs={{0,4},{4,8},{8,12},{12,16},{16,20},{20,24},{24,28},{1,5},{5,9},{9,... | collective-permute-start | bytes 393224 | tf_op jit(solution)/shard_map/ppermute | solution.py:264
  8.2 14.0 %collective-permute-start.3 = (bf16[128,512]{1,0:T(8,128)(2,1)}, bf16[128,512]{1,0:T(8,128)(2,1)S(1)}, u32[]{:S(2)}, u32[]{:S(2)}) collective-permute-start(bf16[128,512]{1,0:T(8,128)(2,1)} %bitcast.16), channel_id=1, source_target_pairs={{4,0},{8,4},{12,8},{16,12},{20,16},{24,20},{28,24},{5,1},{9,5},{13... | collective-permute-start | bytes 393224 | tf_op jit(solution)/shard_map/ppermute | solution.py:264
  12.1 2.4 %copy-start.7 = (f32[9,2,5,5]{0,1,3,2:T(2,128)S(1)}, f32[9,2,5,5]{0,1,3,2:T(2,128)}, u32[]{:S(2)}) copy-start(f32[9,2,5,5]{0,1,3,2:T(2,128)} %param.16) | copy-start | bytes 5404
  13.0 7.1 %copy-start.1 = (bf16[512,1536]{1,0:T(8,128)(2,1)S(1)}, bf16[512,1536]{1,0:T(8,128)(2,1)}, u32[]{:S(2)}) copy-start(bf16[512,1536]{1,0:T(8,128)(2,1)} %wqkv_ref.3) | copy-start | bytes 4718596
  13.0 7.1 %copy-start.4 = (bf16[1,128,512]{2,1,0:T(8,128)(2,1)S(1)}, bf16[1,128,512]{2,1,0:T(8,128)(2,1)}, u32[]{:S(2)}) copy-start(bf16[1,128,512]{2,1,0:T(8,128)(2,1)} %param.9) | copy-start | bytes 393220
  13.0 7.1 %copy-start.5 = (f32[512]{0:T(512)S(1)}, f32[512]{0:T(512)}, u32[]{:S(2)}) copy-start(f32[512]{0:T(512)} %param.10) | copy-start | bytes 6148
  14.5 7.7 %collective-permute-start.4 = (bf16[272,512]{1,0:T(8,128)(2,1)S(1)}, bf16[272,512]{1,0:T(8,128)(2,1)S(1)}, u32[]{:S(2)}, u32[]{:S(2)}) collective-permute-start(bf16[272,512]{1,0:T(8,128)(2,1)S(1)} %pad_maximum_fusion), channel_id=1, source_target_pairs={{0,4},{4,8},{8,12},{12,16},{16,20},{20,24},{24,28},{1,5},{5,9},{9,... | collective-permute-start | bytes 835592 | tf_op jit(solution)/shard_map/ppermute | solution.py:264
  18.2 7.9 %collective-permute-start.5 = (bf16[272,512]{1,0:T(8,128)(2,1)S(1)}, bf16[272,512]{1,0:T(8,128)(2,1)S(1)}, u32[]{:S(2)}, u32[]{:S(2)}) collective-permute-start(bf16[272,512]{1,0:T(8,128)(2,1)S(1)} %pad_maximum_fusion), channel_id=1, source_target_pairs={{4,0},{8,4},{12,8},{16,12},{20,16},{24,20},{28,24},{5,1},{9,5},{13... | collective-permute-start | bytes 835592 | tf_op jit(solution)/shard_map/ppermute | solution.py:264
  20.1 5.9 %copy-start = (s32[2,256]{1,0:T(2,128)S(1)}, s32[2,256]{1,0:T(2,128)}, u32[]{:S(2)}) copy-start(s32[2,256]{1,0:T(2,128)} %assign_ref.1) | copy-start | bytes 6148
  20.2 5.9 %copy-start.2 = (bf16[512,512]{1,0:T(8,128)(2,1)S(1)}, bf16[512,512]{1,0:T(8,128)(2,1)}, u32[]{:S(2)}) copy-start(bf16[512,512]{1,0:T(8,128)(2,1)} %wout_ref.1) | copy-start | bytes 1572868
  20.2 5.9 %copy-start.3 = (bf16[512,512]{1,0:T(8,128)(2,1)S(1)}, bf16[512,512]{1,0:T(8,128)(2,1)}, u32[]{:S(2)}) copy-start(bf16[512,512]{1,0:T(8,128)(2,1)} %wlat_ref.1) | copy-start | bytes 1572868
  20.2 5.9 %copy-start.6 = (s32[1,5]{1,0:T(1,128)S(1)}, s32[1,5]{1,0:T(1,128)}, u32[]{:S(2)}) copy-start(s32[1,5]{1,0:T(1,128)} %listed_ref.1) | copy-start | bytes 64
  31.2 3.5 %collective-permute-start.6 = (bf16[16,512]{1,0:T(8,128)(2,1)S(1)}, bf16[16,512]{1,0:T(8,128)(2,1)S(1)}, u32[]{:S(2)}, u32[]{:S(2)}) collective-permute-start(bf16[16,512]{1,0:T(8,128)(2,1)S(1)} %get-tuple-element.19), channel_id=1, source_target_pairs={{0,1},{1,2},{2,3},{3,0},{4,5},{5,6},{6,7},{7,4},{8,9},{9,10},{10,1... | collective-permute-start | bytes 49160 | tf_op jit(solution)/shard_map/ppermute | solution.py:264
  31.5 3.4 %collective-permute-start.7 = (bf16[16,512]{1,0:T(8,128)(2,1)S(1)}, bf16[16,512]{1,0:T(8,128)(2,1)S(1)}, u32[]{:S(2)}, u32[]{:S(2)}) collective-permute-start(bf16[16,512]{1,0:T(8,128)(2,1)S(1)} %get-tuple-element.20), channel_id=1, source_target_pairs={{0,3},{1,0},{2,1},{3,2},{4,7},{5,4},{6,5},{7,6},{8,11},{9,8},{10,9... | collective-permute-start | bytes 49160 | tf_op jit(solution)/shard_map/ppermute | solution.py:264
  34.9 5.9 %collective-permute-start.8 = (bf16[144,512]{1,0:T(8,128)(2,1)S(1)}, bf16[144,512]{1,0:T(8,128)(2,1)S(1)}, u32[]{:S(2)}, u32[]{:S(2)}) collective-permute-start(bf16[144,512]{1,0:T(8,128)(2,1)S(1)} %pad_maximum_fusion.1.latent_ref), channel_id=1, source_target_pairs={{0,4},{4,8},{8,12},{12,16},{16,20},{20,24},{24,28},{1,5},{5,9},{9,... | collective-permute-start | bytes 442376 | tf_op jit(solution)/shard_map/ppermute | solution.py:264
  37.8 6.5 %collective-permute-start.9 = (bf16[144,512]{1,0:T(8,128)(2,1)S(1)}, bf16[144,512]{1,0:T(8,128)(2,1)S(1)}, u32[]{:S(2)}, u32[]{:S(2)}) collective-permute-start(bf16[144,512]{1,0:T(8,128)(2,1)S(1)} %pad_maximum_fusion.1.latent_ref), channel_id=1, source_target_pairs={{4,0},{8,4},{12,8},{16,12},{20,16},{24,20},{28,24},{5,1},{9,5},{13... | collective-permute-start | bytes 442376 | tf_op jit(solution)/shard_map/ppermute | solution.py:264

commit v2 on v1

--- a/solution.py
+++ b/solution.py
@@ -11,6 +11,7 @@
 HEADS = 16
 REACH = 2
 SIDE = 8
+ROWS = 16
 LANES = 128
 F32 = jnp.float32
 BF16 = jnp.bfloat16
@@ -64,36 +65,37 @@
     wvt_ref[...] = wvt
     value_ref[...] = lax.dot_general(wvt, normed, NT, preferred_element_type=F32).astype(BF16)
 
-    groups, depth, channels = dec_ref.shape
-    basis = psi_ref.shape[1]
-    own = depth // basis
-    padded = band_refs[0].shape[1] // groups
-    spread = (iota((basis, depth), 1) // own == iota((basis, depth), 0)).astype(F32)
+    basis, out_ch, channels = dec_ref.shape
+    depth = basis * ROWS
+    spread = (iota((basis, depth), 1) // ROWS == iota((basis, depth), 0)).astype(F32)
     expanded = jnp.dot(psi_ref[...], spread, preferred_element_type=F32)
-    pick = iota((padded, depth), 1) % own == iota((padded, depth), 0)
-    blocks = [(band, at) + item for band in range(3) for at, item in enumerate(band_blocks(band))]
-    for at, (_, _, out_row, tap, off) in enumerate(blocks):
+    pick = iota((ROWS, depth), 1) % ROWS == iota((ROWS, depth), 0)
+    blocks = [item for band in range(3) for item in band_blocks(band)]
+    for at, (out_row, tap, off) in enumerate(blocks):
         source = (out_row * TAPS + tap) * TAPS + off
-        line = jnp.broadcast_to(expanded[source : source + 1], (padded, depth))
-        taps_ref[at * padded : (at + 1) * padded, :] = jnp.where(pick, line, 0.0).astype(BF16)
-    for piece in range(groups):
+        line = jnp.broadcast_to(expanded[source : source + 1], (ROWS, depth))
+        taps_ref[at * ROWS : (at + 1) * ROWS, :] = jnp.where(pick, line, 0.0).astype(BF16)
+    for first in range(0, out_ch, ROWS):
+        size = min(ROWS, out_ch - first)
+        pieces = []
+        for base in range(basis):
+            pieces.append(dec_ref[base, first : first + size, :])
+            if size < ROWS:
+                pieces.append(jnp.zeros((ROWS - size, channels), BF16))
+        mixing = jnp.concatenate(pieces, axis=0)
         start = 0
-        for band in range(3):
-            count = band_refs[band].shape[0]
+        for band_ref in band_refs:
+            count = band_ref.shape[0]
             mixed = jnp.dot(
-                taps_ref[start * padded : (start + count) * padded, :],
-                dec_ref[piece],
-                preferred_element_type=F32,
+                taps_ref[start * ROWS : (start + count) * ROWS, :], mixing, preferred_element_type=F32
             ).astype(BF16)
-            band_refs[band][:, piece * padded : (piece + 1) * padded, :] = mixed.reshape(
-                count, padded, channels
-            )
+            band_ref[:, first : first + ROWS, :] = mixed.reshape(count, ROWS, channels)
             start += count
 
 
 def attend_kernel(
     sectors,
-    listed_ref, assign_ref, x_ref, left_ref, right_ref, up_ref, down_ref, upper_ref, lower_ref,
+    listed_ref, assign_ref, x_ref, left_ref, right_ref, inner_ref, outer_ref,
     gain_ref, wqkv_ref, query_ref, key_ref, value_ref, wvt_ref, wout_ref, wlat_ref,
     state_ref, latent_ref, west_ref, east_ref,
     near_ref, keys_ref, values_ref, attended_ref,
@@ -104,21 +106,18 @@
     members = lanes // rows
     head = group // members
     reg_here, lon_here = lax.axis_index("reg"), lax.axis_index("lon")
-    sources = (
-        (upper_ref, 0), (up_ref, 0), (upper_ref, rows),
-        (left_ref, 0), None, (right_ref, 0),
-        (lower_ref, 0), (down_ref, 0), (lower_ref, rows),
-    )
+    odd = reg_here % 2
+    inner, outer = 6 * (1 - odd), 6 * odd
+    sources = [(left_ref, 0, 3), (right_ref, 0, 5)]
+    for ref, base in ((inner_ref, inner), (outer_ref, outer)):
+        sources += [(ref, 0, base), (ref, rows, base + 1), (ref, 2 * rows, base + 2)]
     slots = []
     for at in range(1, count):
         block = listed_ref[0, at]
         step_reg = block // sectors - reg_here
         step_lon = (block % sectors - lon_here + 1 + sectors) % sectors - 1
         slots.append((step_reg + 1) * 3 + step_lon + 1)
-    for slot, source in enumerate(sources):
-        if source is None:
-            continue
-        ref, start = source
+    for ref, start, slot in sources:
         place = jnp.int32(-1)
         for at, value in enumerate(slots):
             place = jnp.where(value == slot, at, place)
@@ -171,31 +170,33 @@
         ref[...] = jnp.dot(hit.astype(BF16), latent, preferred_element_type=F32).astype(BF16)
 
 
-def band_sum(band, latent, weights_ref, places, acc):
+def hot_rows(values, rows, cols, line):
+    column = iota((8, cols), 1)
+    node = iota((rows + 2 * SIDE, cols), 0).astype(F32)
+    for off in range(TAPS):
+        step = off - REACH
+        where = jnp.broadcast_to(values, (8, cols))
+        if step:
+            where = pltpu.roll(where, (-step) % cols, 1)
+        reach = column + step
+        before = (rows + REACH * line + reach + REACH).astype(F32)
+        after = (rows + SIDE + REACH * line + reach - cols).astype(F32)
+        where = jnp.where(reach < 0, before, jnp.where(reach >= cols, after, where))
+        yield jnp.where(node == where[:1], 1.0, 0.0).astype(BF16)
+
+
+def band_sum(band, latent, weights_ref, hot, acc):
     blocks, outputs, channels = weights_ref.shape
-    nodes = latent.shape[0]
-    cols = places[0].shape[1]
-    rows = nodes - 2 * SIDE
     shares = lax.dot_general(
         weights_ref[...].reshape(blocks * outputs, channels), latent, NT, preferred_element_type=F32
     ).astype(BF16)
-    column = iota((8, cols), 1)
-    node = iota((nodes, cols), 0).astype(F32)
     start = 0
     for line, (_, out_rows) in enumerate(BANDS[band]):
         for off in range(TAPS):
-            step = off - REACH
-            where = jnp.broadcast_to(places[line], (8, cols))
-            if step:
-                where = pltpu.roll(where, (-step) % cols, 1)
-            reach = column + step
-            where = jnp.where(reach < 0, (rows + REACH * line + reach + REACH).astype(F32), where)
-            where = jnp.where(
-                reach >= cols, (rows + SIDE + REACH * line + reach - cols).astype(F32), where
+            size = len(out_rows) * outputs
+            part = jnp.dot(
+                shares[start : start + size], hot(line, off), preferred_element_type=F32
             )
-            hot = jnp.where(node == where[:1], 1.0, 0.0).astype(BF16)
-            size = len(out_rows) * outputs
-            part = jnp.dot(shares[start : start + size], hot, preferred_element_type=F32)
             start += size
             for at, out_row in enumerate(out_rows):
                 piece = part[at * outputs : (at + 1) * outputs]
@@ -204,32 +205,50 @@
 
 
 def lines_of(line_ref, start, cols):
-    values = line_ref[start : start + 16, :].astype(F32)
-    return [values[:1, :cols], values[:1, cols:]]
-
-
-def own_kernel(line_ref, latent_ref, weights_ref, out_ref):
+    values = line_ref[start : start + ROWS, :].astype(F32)
+    return values[:1, :cols], values[:1, cols:]
+
+
+def own_kernel(begin, line_ref, inner_ref, outer_ref, latent_ref, weights_ref, out_ref, hot_ref):
     cols = out_ref.shape[2]
-    acc = band_sum(1, latent_ref[...], weights_ref, lines_of(line_ref, 0, cols), [None, None])
+    rows = latent_ref.shape[0] - 2 * SIDE
+    own = lines_of(line_ref, 0, cols)
+    table = [list(hot_rows(own[line], rows, cols, line)) for line in range(2)]
+    acc = band_sum(
+        1, latent_ref[...], weights_ref, lambda line, off: table[line][off], [None, None]
+    )
     for row in range(2):
         out_ref[row] = acc[row]
-
-
-def fields_kernel(
-    begin, upper_ref, lower_ref, up_ref, down_ref, above_ref, below_ref, own_ref, out_ref
-):
-    cols = own_ref.shape[2]
+    odd = lax.axis_index("reg") % 2 == 1
+    inner, outer = lines_of(inner_ref, begin, cols), lines_of(outer_ref, begin, cols)
+    for band, (yes, no) in enumerate(((inner, outer), (outer, inner))):
+        for line in range(2):
+            values = jnp.where(odd, yes[line], no[line])
+            for off, hot in enumerate(hot_rows(values, rows, cols, line)):
+                hot_ref[(band * 2 + line) * TAPS + off] = hot
+
+
+def fields_kernel(inner_ref, outer_ref, above_ref, below_ref, own_ref, hot_ref, out_ref, up_ref, down_ref):
+    odd = lax.axis_index("reg") % 2
+
+    @pl.when(odd == 1)
+    def _():
+        up_ref[...] = inner_ref[...]
+        down_ref[...] = outer_ref[...]
+
+    @pl.when(odd == 0)
+    def _():
+        up_ref[...] = outer_ref[...]
+        down_ref[...] = inner_ref[...]
+
     acc = [own_ref[0], own_ref[1]]
-    acc = band_sum(0, up_ref[...], above_ref, lines_of(upper_ref, begin, cols), acc)
-    acc = band_sum(2, down_ref[...], below_ref, lines_of(lower_ref, begin, cols), acc)
+    acc = band_sum(0, up_ref[...], above_ref, lambda line, off: hot_ref[line * TAPS + off], acc)
+    acc = band_sum(
+        2, down_ref[...], below_ref, lambda line, off: hot_ref[(2 + line) * TAPS + off], acc
+    )
     out_ch = out_ref.shape[0]
-    groups = 3
-    padded, size = own_ref.shape[1] // groups, out_ch // groups
     for row in range(2):
-        for piece in range(groups):
-            out_ref[piece * size : (piece + 1) * size, row, :] = acc[row][
-                piece * padded : piece * padded + size
-            ].astype(BF16)
+        out_ref[:, row, :] = acc[row][:out_ch].astype(BF16)
 
 
 def whole(memory=pltpu.VMEM):
@@ -263,22 +282,20 @@
         pairs = [(i, (i + step) % size) for i in range(size) if wrap or 0 <= i + step < size]
         return lax.ppermute(array, axis, pairs)
 
+    def exchanged(array, first):
+        size = lax.axis_size("reg")
+        pairs = [(i, i + 1) for i in range(first, size - 1, 2)]
+        return lax.ppermute(array, "reg", pairs + [(j, i) for i, j in pairs])
+
     left = shifted(x, "lon", 1, True)
     right = shifted(x, "lon", -1, True)
-    up = shifted(x, "reg", 1, False)
-    down = shifted(x, "reg", -1, False)
-
-    line = (assignment % rows).astype(BF16).reshape(1, lat_rows * lon_cols)
-    line = jnp.pad(line, ((0, 15), (0, 0)))
-    both = jnp.concatenate([left, right, line], axis=0)
-    upper = shifted(both, "reg", 1, False)
-    lower = shifted(both, "reg", -1, False)
-
-    groups, padded = 3, 32
-    own = out_ch // groups
-    depth = basis * own
-    dec = w_dec.transpose(0, 2, 1).reshape(basis, groups, own, channels).transpose(1, 0, 2, 3)
-    dec = dec.reshape(groups, depth, channels)
+    line = lax.rem(assignment, rows).astype(BF16).reshape(1, lat_rows * lon_cols)
+    line = jnp.pad(line, ((0, ROWS - 1), (0, 0)))
+    column = jnp.concatenate([left, x, right, line], axis=0)
+    outer = exchanged(column, 1)
+    inner = exchanged(column, 0)
+
+    outputs = -(-out_ch // ROWS) * ROWS
     taps = psi.transpose(1, 2, 3, 0).reshape(lat_rows * TAPS * TAPS, basis)
     head = width // HEADS
     members = LANES // head
@@ -294,16 +311,16 @@
             struct(width, rows),
             struct(width, width),
         ]
-        + [struct(size, groups * padded, channels) for size in sizes],
-        scratch_shapes=[pltpu.VMEM((sum(sizes) * padded, depth), BF16)],
+        + [struct(size, outputs, channels) for size in sizes],
+        scratch_shapes=[pltpu.VMEM((sum(sizes) * ROWS, basis * ROWS), BF16)],
         compiler_params=params(32),
         cost_estimate=cost(3e9, 1.2e7),
         name="prepare",
-    )(x, gain, w_qkv, taps, dec)
+    )(x, gain, w_qkv, taps, w_dec.transpose(0, 2, 1))
 
     state, latent, west, east = pl.pallas_call(
         functools.partial(attend_kernel, sectors),
-        in_specs=[whole(pltpu.SMEM)] * 2 + [whole()] * 15,
+        in_specs=[whole(pltpu.SMEM)] * 2 + [whole()] * 13,
         out_specs=[whole()] * 4,
         out_shape=[struct(rows, width), struct(rows, channels), struct(16, channels), struct(16, channels)],
         scratch_shapes=[
@@ -316,34 +333,39 @@
         cost_estimate=cost(4e9, 6e6),
         name="attend",
     )(
-        neighbours, assignment, x, left, right, up, down, upper, lower,
+        neighbours, assignment, x, left, right, inner, outer,
         gain, w_qkv, query, key, value, wvt, w_out, w_latent,
     )
 
     from_left = shifted(east, "lon", 1, True)
     from_right = shifted(west, "lon", -1, True)
     extended = jnp.concatenate([latent, from_left[:SIDE], from_right[:SIDE]], axis=0)
-    north = shifted(extended, "reg", 1, False)
-    south = shifted(extended, "reg", -1, False)
-
-    partial = pl.pallas_call(
-        own_kernel,
-        in_specs=[whole()] * 3,
-        out_specs=whole(),
-        out_shape=struct(lat_rows, groups * padded, lon_cols, dtype=F32),
+    far = exchanged(extended, 1)
+    near = exchanged(extended, 0)
+
+    nodes_ext = rows + 2 * SIDE
+    partial, hots = pl.pallas_call(
+        functools.partial(own_kernel, 3 * rows),
+        in_specs=[whole()] * 5,
+        out_specs=[whole()] * 2,
+        out_shape=[
+            struct(lat_rows, outputs, lon_cols, dtype=F32),
+            struct(4 * TAPS, nodes_ext, lon_cols),
+        ],
         compiler_params=params(32),
         cost_estimate=cost(1e9, 2.5e6),
         name="own_band",
-    )(line, extended, middle)
+    )(line, inner, outer, extended, middle)
     fields = pl.pallas_call(
-        functools.partial(fields_kernel, 2 * rows),
-        in_specs=[whole()] * 7,
+        fields_kernel,
+        in_specs=[whole()] * 6,
         out_specs=whole(),
         out_shape=struct(out_ch, lat_rows, lon_cols),
+        scratch_shapes=[pltpu.VMEM((nodes_ext, channels), BF16)] * 2,
         compiler_params=params(32),
         cost_estimate=cost(2e9, 4e6),
         name="fields",
-    )(upper, lower, north, south, above, below, partial)
+    )(near, far, above, below, partial, hots)
     return (state.reshape(1, rows, width), fields.reshape(1, out_ch, lat_rows, lon_cols))
 
 

time: 47.5 us -> 42.1 us (0.89)
  starting transfers between devices: 22.2 us -> 14.8 us
  local copies, waits for them, and re-layouts: 3.63 us -> 4.92 us
  other arithmetic: 0.73 us -> 1.63 us
    ppermute x10 -> x4, starting transfers between devices: 22.2 us -> 5.42 us  [shifted(): return lax.ppermute(array, axis, pairs)]
    ppermute x0 -> x4, starting transfers between devices: none -> 9.4 us  [exchanged(): return lax.ppermute(array, 'reg', pairs + [(j, i) for i, j in pairs])]
    unnamed x17, local copies, waits for them, and re-layouts: 0.05 us -> 4.15 us
    reshape x3 -> x0, local copies, waits for them, and re-layouts: 3.56 us -> none  [the longest x2 2.19 us: shards(): w_dec.transpose(0, 2, 1).reshape(basis, groups, own, channels)]
    ppermute x0 -> x4, waiting for transfers between devices: none -> 1.58 us  [exchanged(): return lax.ppermute(array, 'reg', pairs + [(j, i) for i, j in pairs])]
    ppermute x10 -> x4, waiting for transfers between devices: 8.67 us -> 7.27 us  [shifted(): return lax.ppermute(array, axis, pairs)]
    concatenate x1, other arithmetic: 0.02 us -> 0.93 us  [shards(): column = jnp.concatenate([left, x, right, line], axis=0)]
    transpose x1, local copies, waits for them, and re-layouts: 0.01 us -> 0.75 us  [shards(): taps = psi.transpose(1, 2, 3, 0).reshape(lat_rows * TAPS * TAPS, basis)]
  transfers between devices with their start and end apart: 10 -> 8, of which waited for: 4 -> 5; matrix products, arithmetic and copies ran while one was open for 9% -> 3% of each run, Pallas kernels for 7% -> 8%
where the time goes in v2:
time: 42.1 us; the launch traced here: 41.8 us
  starting transfers between devices  14.8 us (35%)
  Pallas kernels  10.8 us (26%)
  waiting for transfers between devices  8.85 us (21%)
  local copies, waits for them, and re-layouts  4.92 us (12%)
  other arithmetic  1.63 us (4%)
  between operations  0.76 us (2%)
    ppermute x4, starting transfers between devices, exchanged(): return lax.ppermute(array, 'reg', pairs + [(j, i) for i, j in pairs])  9.4 us
    ppermute x4, waiting for transfers between devices, shifted(): return lax.ppermute(array, axis, pairs)  7.27 us
    ppermute x4, starting transfers between devices, shifted(): return lax.ppermute(array, axis, pairs)  5.42 us
    pallas_call x1, Pallas kernels, shards(): pl.pallas_call(functools.partial(attend_kernel, sectors), in_specs=[whole...  5.11 us
    unnamed x17, local copies, waits for them, and re-layouts  4.15 us
    pallas_call x1, Pallas kernels, shards(): pl.pallas_call(fields_kernel, in_specs=[whole()] * 6, out_specs=whole(),...  2.5 us
    pallas_call x1, Pallas kernels, shards(): pl.pallas_call(prepare_kernel, in_specs=[whole()] * 5, out_specs=[whole()...  2.05 us
    ppermute x4, waiting for transfers between devices, exchanged(): return lax.ppermute(array, 'reg', pairs + [(j, i) for i, j in pairs])  1.58 us
  transfers between devices with their start and end apart: 8, of which 5 were waited for; matrix products, arithmetic and copies ran while one was open for 3% of the time, Pallas kernels for 8%

profile of v2, /device:TPU:1, one launch (start us, length us, event | category | flops | bytes accessed | tf_op | source)
XLA Modules:
  0.0 41.8 jit_solution(3038344202498640341)
XLA Ops:
  0.6 3.0 %collective-permute-start.1 = (bf16[128,512]{1,0:T(8,128)(2,1)}, bf16[128,512]{1,0:T(8,128)(2,1)S(1)}, u32[]{:S(2)}, u32[]{:S(2)}) collective-permute-start(bf16[128,512]{1,0:T(8,128)(2,1)} %bitcast.10), channel_id=1, source_target_pairs={{0,3},{1,0},{2,1},{3,2},{4,7},{5,4},{6,5},{7,6},{8,11},{9,8},{10,9... | collective-permute-start | bytes 393224 | tf_op jit(solution)/shard_map/ppermute | solution.py:283
  3.7 0.7 %fusion.2 = bf16[1,1,2,256]{3,2,1,0:T(2,128)(2,1)S(1)} fusion(s32[2,256]{1,0:T(2,128)} %assign_ref.1), kind=kLoop, calls=%fused_computation.6 | loop fusion | flops 3584 | bytes 3072
  4.4 1.8 %collective-permute-done.1.right_ref = bf16[128,512]{1,0:T(8,128)(2,1)S(1)} collective-permute-done((bf16[128,512]{1,0:T(8,128)(2,1)}, bf16[128,512]{1,0:T(8,128)(2,1)S(1)}, u32[]{:S(2)}, u32[]{:S(2)}) %collective-permute-start.1) | collective-permute-done | bytes 131104 | tf_op jit(solution)/shard_map/ppermute | solution.py:283
  6.2 4.1 %collective-permute-done.left_ref = bf16[128,512]{1,0:T(8,128)(2,1)S(1)} collective-permute-done((bf16[128,512]{1,0:T(8,128)(2,1)}, bf16[128,512]{1,0:T(8,128)(2,1)S(1)}, u32[]{:S(2)}, u32[]{:S(2)}) %collective-permute-start) | collective-permute-done | bytes 131104 | tf_op jit(solution)/shard_map/ppermute | solution.py:283
  10.2 0.9 %pad_maximum_fusion = bf16[400,512]{1,0:T(8,128)(2,1)S(1)} fusion(bf16[16,512]{1,0:T(8,128)(2,1)S(1)} %pad.4.line_ref, bf16[128,512]{1,0:T(8,128)(2,1)S(1)} %collective-permute-done.1.right_ref, bf16[128,512]{1,0:T(8,128)(2,1)} %bitcast.12, bf16[128,512]{1,0:T(8,128)(2,1)S(1)} %collective-permute-done.left_ref), kind=kLoop, calls=%fused_computation | loop fusion | flops 1638400 | bytes 819200 | tf_op jit(solution)/shard_map/concatenate | solution.py:294
  11.2 4.3 %collective-permute-start.3 = (bf16[400,512]{1,0:T(8,128)(2,1)S(1)}, bf16[400,512]{1,0:T(8,128)(2,1)S(1)}, u32[]{:S(2)}, u32[]{:S(2)}) collective-permute-start(bf16[400,512]{1,0:T(8,128)(2,1)S(1)} %pad_maximum_fusion), channel_id=1, source_target_pairs={{4,8},{12,16},{20,24},{8,4},{16,12},{24,20},{5,9},{13,17},{21,25},... | collective-permute-start | bytes 1228808 | tf_op jit(solution)/shard_map/ppermute | solution.py:288
  15.4 0.1 collective-permute-start.2
  15.5 0.8 %copy.12 = f32[2,5,5,9]{3,2,1,0:T(8,128)S(1)} copy(f32[2,5,5,9]{3,0,2,1:T(2,128)} %bitcast.18) | data formatting | bytes 3600 | tf_op jit(solution)/shard_map/transpose | solution.py:299
  16.3 0.0 copy-start
  16.3 0.9 %copy-done = bf16[1,128,512]{2,1,0:T(8,128)(2,1)S(1)} copy-done((bf16[1,128,512]{2,1,0:T(8,128)(2,1)S(1)}, bf16[1,128,512]{2,1,0:T(8,128)(2,1)}, u32[]{:S(2)}) %copy-start) | copy-done | bytes 131096
  17.2 1.4 %copy-done.2 = bf16[512,1536]{1,0:T(8,128)(2,1)S(1)} copy-done((bf16[512,1536]{1,0:T(8,128)(2,1)S(1)}, bf16[512,1536]{1,0:T(8,128)(2,1)}, u32[]{:S(2)}) %copy-start.2) | copy-done | bytes 1572888
  18.6 1.1 %copy-done.3 = bf16[9,512,84]{1,2,0:T(8,128)(2,1)S(1)} copy-done((bf16[9,512,84]{1,2,0:T(8,128)(2,1)S(1)}, bf16[9,512,84]{1,2,0:T(8,128)(2,1)}, u32[]{:S(2)}) %copy-start.3) | copy-done | bytes 774168
  19.7 0.7 %copy-done.6 = f32[512]{0:T(512)S(1)} copy-done((f32[512]{0:T(512)S(1)}, f32[512]{0:T(512)}, u32[]{:S(2)}) %copy-start.6) | copy-done | bytes 2072
  20.4 2.1 %prepare.1 = (bf16[4,128,512]{2,1,0:T(8,128)(2,1)S(1)}, bf16[128,512]{1,0:T(8,128)(2,1)S(1)}, bf16[512,128]{1,0:T(8,128)(2,1)S(1)}, bf16[512,512]{1,0:T(8,128)(2...) custom-call(bf16[128,512]{1,0:T(8,128)(2,1)S(1)} %bitcast.13, ...), custom_call_target="tpu_custom_call" | custom-call | flops 3000000000 | bytes 12000000 | tf_op jit(solution)/shard_map/prepare/pallas_call | solution.py:304
  22.5 5.1 %attend.1 = (bf16[128,512]{1,0:T(8,128)(2,1)}, bf16[128,512]{1,0:T(8,128)(2,1)S(1)}, bf16[16,512]{1,0:T(8,128)(2,1)S(1)}, bf16[16,512]{1,0:T(8,128)(2,1)S(1)}) custom-call(s32[1,5]{1,0:T(1,128)S(1)} %copy-done.7, s32[2,256]{1,0:T(2,128)S(1)} %copy-done.1, bf16[128,512]{1,0:T(8,128)(2,1)S(1)} %bitcast.14, bf16[128,512]{1,0:T(8,128)(2,1)S(1)} %collective-permute-done.left_ref, ...), custom_call_target="tpu_custom_call" | custom-call | flops 4000000000 | bytes 6000000 | tf_op jit(solution)/shard_map/attend/pallas_call | solution.py:321
  27.7 1.2 %collective-permute-start.4 = (bf16[16,512]{1,0:T(8,128)(2,1)S(1)}, bf16[16,512]{1,0:T(8,128)(2,1)S(1)}, u32[]{:S(2)}, u32[]{:S(2)}) collective-permute-start(bf16[16,512]{1,0:T(8,128)(2,1)S(1)} %get-tuple-element.21), channel_id=1, source_target_pairs={{0,1},{1,2},{2,3},{3,0},{4,5},{5,6},{6,7},{7,4},{8,9},{9,10},{10,1... | collective-permute-start | bytes 49160 | tf_op jit(solution)/shard_map/ppermute | solution.py:283
  28.9 1.2 %collective-permute-start.5 = (bf16[16,512]{1,0:T(8,128)(2,1)S(1)}, bf16[16,512]{1,0:T(8,128)(2,1)S(1)}, u32[]{:S(2)}, u32[]{:S(2)}) collective-permute-start(bf16[16,512]{1,0:T(8,128)(2,1)S(1)} %get-tuple-element.22), channel_id=1, source_target_pairs={{0,3},{1,0},{2,1},{3,2},{4,7},{5,4},{6,5},{7,6},{8,11},{9,8},{10,9... | collective-permute-start | bytes 49160 | tf_op jit(solution)/shard_map/ppermute | solution.py:283
  30.0 1.1 %collective-permute-done.4 = bf16[16,512]{1,0:T(8,128)(2,1)S(1)} collective-permute-done((bf16[16,512]{1,0:T(8,128)(2,1)S(1)}, bf16[16,512]{1,0:T(8,128)(2,1)S(1)}, u32[]{:S(2)}, u32[]{:S(2)}) %collective-permute-start.4) | collective-permute-done | bytes 16416 | tf_op jit(solution)/shard_map/ppermute | solution.py:283
  31.1 0.3 collective-permute-done.5
  31.5 5.0 %collective-permute-start.7 = (bf16[144,512]{1,0:T(8,128)(2,1)S(1)}, bf16[144,512]{1,0:T(8,128)(2,1)S(1)}, u32[]{:S(2)}, u32[]{:S(2)}) collective-permute-start(bf16[144,512]{1,0:T(8,128)(2,1)S(1)} %pad_maximum_fusion.1.latent_ref), channel_id=1, source_target_pairs={{4,8},{12,16},{20,24},{8,4},{16,12},{24,20},{5,9},{13,17},{21,25},... | collective-permute-start | bytes 442376 | tf_op jit(solution)/shard_map/ppermute | solution.py:288
  36.5 0.1 collective-permute-start.6
  36.6 1.2 %own_band.1 = (f32[2,96,256]{2,1,0:T(8,128)S(1)}, bf16[20,144,256]{2,1,0:T(8,128)(2,1)S(1)}) custom-call(bf16[16,512]{1,0:T(8,128)(2,1)S(1)} %pad.4.line_ref, bf16[400,512]{1,0:T(8,128)(2,1)S(1)} %collective-permute-done.2.inner_ref, bf16[400,512]{1,0:T(8,128)(2,1)S(1)} %collective-permute-done.3.outer_ref, ...), custom_call_target="tpu_custom_call" | custom-call | flops 1000000000 | bytes 2500000 | tf_op jit(solution)/shard_map/own_band/pallas_call | solution.py:347
  37.7 1.6 %collective-permute-done.7.outer_ref = bf16[144,512]{1,0:T(8,128)(2,1)S(1)} collective-permute-done((bf16[144,512]{1,0:T(8,128)(2,1)S(1)}, bf16[144,512]{1,0:T(8,128)(2,1)S(1)}, u32[]{:S(2)}, u32[]{:S(2)}) %collective-permute-start.7) | collective-permute-done | bytes 147488 | tf_op jit(solution)/shard_map/ppermute | solution.py:288
  39.3 2.5 %fields.1 = bf16[84,2,256]{2,1,0:T(2,128)(2,1)} custom-call(bf16[144,512]{1,0:T(8,128)(2,1)S(1)} %collective-permute-done.6.inner_ref, bf16[144,512]{1,0:T(8,128)(2,1)S(1)} %collective-permute-done.7.outer_ref, bf16[15,96,512]{2,1,0:T(8,128)(2,1)S(1)} %get-tuple-element.23.above_ref, bf16[15,96,512]{2,1,0:T(8,128)(2,1)S(1)} %get-tuple-element.24.below_ref, ...), custom_call_target="tpu_custom_call" | custom-call | flops 2000000000 | bytes 4000000 | tf_op jit(solution)/shard_map/fields/pallas_call | solution.py:359
  (21 shorter events, 0.1 us)
Async XLA Ops:
  0.6 5.5 %collective-permute-start.1 = (bf16[128,512]{1,0:T(8,128)(2,1)}, bf16[128,512]{1,0:T(8,128)(2,1)S(1)}, u32[]{:S(2)}, u32[]{:S(2)}) collective-permute-start(bf16[128,512]{1,0:T(8,128)(2,1)} %bitcast.10), channel_id=1, source_target_pairs={{0,3},{1,0},{2,1},{3,2},{4,7},{5,4},{6,5},{7,6},{8,11},{9,8},{10,9... | collective-permute-start | bytes 393224 | tf_op jit(solution)/shard_map/ppermute | solution.py:283
  3.7 6.6 %collective-permute-start = (bf16[128,512]{1,0:T(8,128)(2,1)}, bf16[128,512]{1,0:T(8,128)(2,1)S(1)}, u32[]{:S(2)}, u32[]{:S(2)}) collective-permute-start(bf16[128,512]{1,0:T(8,128)(2,1)} %bitcast.11), channel_id=1, source_target_pairs={{0,1},{1,2},{2,3},{3,0},{4,5},{5,6},{6,7},{7,4},{8,9},{9,10},{10,1... | collective-permute-start | bytes 393224 | tf_op jit(solution)/shard_map/ppermute | solution.py:283
  11.2 11.3 %collective-permute-start.3 = (bf16[400,512]{1,0:T(8,128)(2,1)S(1)}, bf16[400,512]{1,0:T(8,128)(2,1)S(1)}, u32[]{:S(2)}, u32[]{:S(2)}) collective-permute-start(bf16[400,512]{1,0:T(8,128)(2,1)S(1)} %pad_maximum_fusion), channel_id=1, source_target_pairs={{4,8},{12,16},{20,24},{8,4},{16,12},{24,20},{5,9},{13,17},{21,25},... | collective-permute-start | bytes 1228808 | tf_op jit(solution)/shard_map/ppermute | solution.py:288
  15.4 7.1 %collective-permute-start.2 = (bf16[400,512]{1,0:T(8,128)(2,1)S(1)}, bf16[400,512]{1,0:T(8,128)(2,1)S(1)}, u32[]{:S(2)}, u32[]{:S(2)}) collective-permute-start(bf16[400,512]{1,0:T(8,128)(2,1)S(1)} %pad_maximum_fusion), channel_id=1, source_target_pairs={{0,4},{8,12},{16,20},{24,28},{4,0},{12,8},{20,16},{28,24},{1,5},{9... | collective-permute-start | bytes 1228808 | tf_op jit(solution)/shard_map/ppermute | solution.py:288
  16.3 0.9 %copy-start = (bf16[1,128,512]{2,1,0:T(8,128)(2,1)S(1)}, bf16[1,128,512]{2,1,0:T(8,128)(2,1)}, u32[]{:S(2)}) copy-start(bf16[1,128,512]{2,1,0:T(8,128)(2,1)} %param.9) | copy-start | bytes 393220
  17.2 1.4 %copy-start.2 = (bf16[512,1536]{1,0:T(8,128)(2,1)S(1)}, bf16[512,1536]{1,0:T(8,128)(2,1)}, u32[]{:S(2)}) copy-start(bf16[512,1536]{1,0:T(8,128)(2,1)} %wqkv_ref.3) | copy-start | bytes 4718596
  18.6 1.1 %copy-start.3 = (bf16[9,512,84]{1,2,0:T(8,128)(2,1)S(1)}, bf16[9,512,84]{1,2,0:T(8,128)(2,1)}, u32[]{:S(2)}) copy-start(bf16[9,512,84]{1,2,0:T(8,128)(2,1)} %param.17) | copy-start | bytes 2322436
  19.7 0.7 %copy-start.6 = (f32[512]{0:T(512)S(1)}, f32[512]{0:T(512)}, u32[]{:S(2)}) copy-start(f32[512]{0:T(512)} %param.10) | copy-start | bytes 6148
  20.4 2.1 %copy-start.1 = (s32[2,256]{1,0:T(2,128)S(1)}, s32[2,256]{1,0:T(2,128)}, u32[]{:S(2)}) copy-start(s32[2,256]{1,0:T(2,128)} %assign_ref.1) | copy-start | bytes 6148
  20.4 2.1 %copy-start.4 = (bf16[512,512]{1,0:T(8,128)(2,1)S(1)}, bf16[512,512]{1,0:T(8,128)(2,1)}, u32[]{:S(2)}) copy-start(bf16[512,512]{1,0:T(8,128)(2,1)} %wout_ref.1) | copy-start | bytes 1572868
  20.4 2.1 %copy-start.5 = (bf16[512,512]{1,0:T(8,128)(2,1)S(1)}, bf16[512,512]{1,0:T(8,128)(2,1)}, u32[]{:S(2)}) copy-start(bf16[512,512]{1,0:T(8,128)(2,1)} %wlat_ref.1) | copy-start | bytes 1572868
  20.4 2.1 %copy-start.7 = (s32[1,5]{1,0:T(1,128)S(1)}, s32[1,5]{1,0:T(1,128)}, u32[]{:S(2)}) copy-start(s32[1,5]{1,0:T(1,128)} %listed_ref.1) | copy-start | bytes 64
  27.7 3.5 %collective-permute-start.4 = (bf16[16,512]{1,0:T(8,128)(2,1)S(1)}, bf16[16,512]{1,0:T(8,128)(2,1)S(1)}, u32[]{:S(2)}, u32[]{:S(2)}) collective-permute-start(bf16[16,512]{1,0:T(8,128)(2,1)S(1)} %get-tuple-element.21), channel_id=1, source_target_pairs={{0,1},{1,2},{2,3},{3,0},{4,5},{5,6},{6,7},{7,4},{8,9},{9,10},{10,1... | collective-permute-start | bytes 49160 | tf_op jit(solution)/shard_map/ppermute | solution.py:283
  28.9 2.6 %collective-permute-start.5 = (bf16[16,512]{1,0:T(8,128)(2,1)S(1)}, bf16[16,512]{1,0:T(8,128)(2,1)S(1)}, u32[]{:S(2)}, u32[]{:S(2)}) collective-permute-start(bf16[16,512]{1,0:T(8,128)(2,1)S(1)} %get-tuple-element.22), channel_id=1, source_target_pairs={{0,3},{1,0},{2,1},{3,2},{4,7},{5,4},{6,5},{7,6},{8,11},{9,8},{10,9... | collective-permute-start | bytes 49160 | tf_op jit(solution)/shard_map/ppermute | solution.py:283
  31.5 7.8 %collective-permute-start.7 = (bf16[144,512]{1,0:T(8,128)(2,1)S(1)}, bf16[144,512]{1,0:T(8,128)(2,1)S(1)}, u32[]{:S(2)}, u32[]{:S(2)}) collective-permute-start(bf16[144,512]{1,0:T(8,128)(2,1)S(1)} %pad_maximum_fusion.1.latent_ref), channel_id=1, source_target_pairs={{4,8},{12,16},{20,24},{8,4},{16,12},{24,20},{5,9},{13,17},{21,25},... | collective-permute-start | bytes 442376 | tf_op jit(solution)/shard_map/ppermute | solution.py:288
  36.5 2.8 %collective-permute-start.6 = (bf16[144,512]{1,0:T(8,128)(2,1)S(1)}, bf16[144,512]{1,0:T(8,128)(2,1)S(1)}, u32[]{:S(2)}, u32[]{:S(2)}) collective-permute-start(bf16[144,512]{1,0:T(8,128)(2,1)S(1)} %pad_maximum_fusion.1.latent_ref), channel_id=1, source_target_pairs={{0,4},{8,12},{16,20},{24,28},{4,0},{12,8},{20,16},{28,24},{1,5},{9... | collective-permute-start | bytes 442376 | tf_op jit(solution)/shard_map/ppermute | solution.py:288

commit v3 on v2

--- a/solution.py
+++ b/solution.py
@@ -45,14 +45,22 @@
     return (center * lax.rsqrt(spread + 1e-05) * gain).astype(BF16)
 
 
-def prepare_kernel(x_ref, gain_ref, wqkv_ref, psi_ref, dec_ref, query_ref, key_ref, value_ref, wvt_ref, *out):
-    band_refs, taps_ref = out[:3], out[3]
+def prepare_kernel(
+    x_ref, gain_ref, wqkv_ref, assign_ref, psi_ref, dec_ref,
+    own_ref, query_ref, key_ref, value_ref, wvt_ref, above_ref, middle_ref, below_ref, taps_ref,
+):
+    band_refs = (above_ref, middle_ref, below_ref)
     rows, width = x_ref.shape
     group, members = query_ref.shape[1], query_ref.shape[2] // rows
     head = group // members
+    own_ref[:rows] = x_ref[...]
+    local = lax.rem(assign_ref[...], rows).astype(F32)
+    line = jnp.concatenate([local[:1], local[1:2]], axis=1)
+    line = jnp.broadcast_to(line, (ROWS, line.shape[1]))
+    own_ref[rows:] = jnp.where(iota(line.shape, 0) == 0, line, 0.0).astype(BF16)
     normed = normalise(x_ref[...], gain_ref[...])
     query = jnp.dot(normed, wqkv_ref[:, :width], preferred_element_type=F32)
-    query_t = query.T.astype(BF16)
+    query_t = (query * (math.log2(math.e) / head**0.5)).T.astype(BF16)
     mask = (iota((group, members * rows), 0) // head) == (iota((group, members * rows), 1) // rows)
     for part in range(width // group):
         piece = query_t[part * group : (part + 1) * group]
@@ -95,63 +103,59 @@
 
 def attend_kernel(
     sectors,
-    listed_ref, assign_ref, x_ref, left_ref, right_ref, inner_ref, outer_ref,
+    listed_ref, assign_ref, column_ref, inner_ref, outer_ref,
     gain_ref, wqkv_ref, query_ref, key_ref, value_ref, wvt_ref, wout_ref, wlat_ref,
     state_ref, latent_ref, west_ref, east_ref,
-    near_ref, keys_ref, values_ref, attended_ref,
+    keys_ref, values_ref, attended_ref,
 ):
-    rows, width = x_ref.shape
+    rows, width = key_ref.shape
     count = listed_ref.shape[1]
     parts, group, lanes = query_ref.shape
     members = lanes // rows
     head = group // members
     reg_here, lon_here = lax.axis_index("reg"), lax.axis_index("lon")
-    odd = reg_here % 2
-    inner, outer = 6 * (1 - odd), 6 * odd
-    sources = [(left_ref, 0, 3), (right_ref, 0, 5)]
-    for ref, base in ((inner_ref, inner), (outer_ref, outer)):
-        sources += [(ref, 0, base), (ref, rows, base + 1), (ref, 2 * rows, base + 2)]
-    slots = []
+    toward = 1 - 2 * (reg_here % 2)
+    near = []
     for at in range(1, count):
         block = listed_ref[0, at]
         step_reg = block // sectors - reg_here
         step_lon = (block % sectors - lon_here + 1 + sectors) % sectors - 1
-        slots.append((step_reg + 1) * 3 + step_lon + 1)
-    for ref, start, slot in sources:
-        place = jnp.int32(-1)
-        for at, value in enumerate(slots):
-            place = jnp.where(value == slot, at, place)
-
-        @pl.when(place >= 0)
-        def _():
-            near_ref[place] = ref[start : start + rows, :]
-
-    normed = normalise(near_ref[...].reshape((count - 1) * rows, width), gain_ref[...])
+        place = jnp.where(step_lon == 0, 2, jnp.where(step_lon < 0, 0, 1))
+        span = pl.ds(pl.multiple_of(place * rows, rows), rows)
+        other = jnp.where(step_reg == toward, inner_ref[span, :], outer_ref[span, :])
+        near.append(jnp.where(step_reg == 0, column_ref[span, :], other))
+    normed = normalise(jnp.concatenate(near, axis=0), gain_ref[...])
     keys_ref[:rows] = key_ref[...]
     keys_ref[rows:] = jnp.dot(
         normed, wqkv_ref[:, width : 2 * width], preferred_element_type=F32
     ).astype(BF16)
-    values_ref[:, :rows] = value_ref[...]
-    values_ref[:, rows:] = lax.dot_general(
-        wvt_ref[...], normed, NT, preferred_element_type=F32
-    ).astype(BF16)
-    scale = math.log2(math.e) / head**0.5
-    owner = iota((group, rows), 0) // head
+    values = lax.dot_general(wvt_ref[...], normed, NT, preferred_element_type=F32).astype(BF16)
     for part in range(parts):
         span = slice(part * group, (part + 1) * group)
-        scores = jnp.dot(keys_ref[:, span], query_ref[part], preferred_element_type=F32)
-        top = jnp.max(scores, axis=0, keepdims=True)
-        expo = jnp.exp2((scores - top) * scale)
-        total = jnp.sum(expo, axis=0, keepdims=True)
-        summed = jnp.dot(values_ref[span, :], expo.astype(BF16), preferred_element_type=F32)
-        summed = summed * (1.0 / total)
+        values_ref[part, :group, :rows] = value_ref[span]
+        values_ref[part, :group, rows:] = values[span]
+        values_ref[part, group:, :] = jnp.ones((ROWS, count * rows), BF16)
+
+    def scored(part):
+        keys = keys_ref[:, part * group : (part + 1) * group]
+        return jnp.dot(keys, query_ref[part], preferred_element_type=F32)
+
+    owner = iota((group, rows), 0) // head
+    scores = scored(0)
+    for part in range(parts):
+        now = scores
+        if part + 1 < parts:
+            scores = scored(part + 1)
+        expo = jnp.exp2(now - jnp.max(now, axis=0, keepdims=True)).astype(BF16)
+        summed = jnp.dot(values_ref[part], expo, preferred_element_type=F32)
+        summed = summed[:group] * (1.0 / summed[group : group + 1])
         merged = None
         for member in range(members):
             piece = summed[:, member * rows : (member + 1) * rows]
             merged = piece if merged is None else jnp.where(owner == member, piece, merged)
-        attended_ref[:, span] = merged.T.astype(BF16)
+        attended_ref[:, part * group : (part + 1) * group] = merged.T.astype(BF16)
     state = (
-        x_ref[...].astype(F32)
+        column_ref[2 * rows : 3 * rows, :].astype(F32)
         + jnp.dot(attended_ref[...], wout_ref[...], preferred_element_type=F32)
     ).astype(BF16)
     state_ref[...] = state
@@ -185,23 +189,12 @@
         yield jnp.where(node == where[:1], 1.0, 0.0).astype(BF16)
 
 
-def band_sum(band, latent, weights_ref, hot, acc):
+def band_shares(latent, weights_ref):
     blocks, outputs, channels = weights_ref.shape
     shares = lax.dot_general(
         weights_ref[...].reshape(blocks * outputs, channels), latent, NT, preferred_element_type=F32
     ).astype(BF16)
-    start = 0
-    for line, (_, out_rows) in enumerate(BANDS[band]):
-        for off in range(TAPS):
-            size = len(out_rows) * outputs
-            part = jnp.dot(
-                shares[start : start + size], hot(line, off), preferred_element_type=F32
-            )
-            start += size
-            for at, out_row in enumerate(out_rows):
-                piece = part[at * outputs : (at + 1) * outputs]
-                acc[out_row] = piece if acc[out_row] is None else acc[out_row] + piece
-    return acc
+    return [shares[at * outputs : (at + 1) * outputs] for at in range(blocks)]
 
 
 def lines_of(line_ref, start, cols):
@@ -212,43 +205,49 @@
 def own_kernel(begin, line_ref, inner_ref, outer_ref, latent_ref, weights_ref, out_ref, hot_ref):
     cols = out_ref.shape[2]
     rows = latent_ref.shape[0] - 2 * SIDE
-    own = lines_of(line_ref, 0, cols)
+    own = lines_of(line_ref, begin, cols)
     table = [list(hot_rows(own[line], rows, cols, line)) for line in range(2)]
-    acc = band_sum(
-        1, latent_ref[...], weights_ref, lambda line, off: table[line][off], [None, None]
-    )
+    acc = [None, None]
+    for (out_row, tap, off), share in zip(
+        band_blocks(1), band_shares(latent_ref[...], weights_ref)
+    ):
+        line = out_row + tap - REACH
+        piece = jnp.dot(share, table[line][off], preferred_element_type=F32)
+        acc[out_row] = piece if acc[out_row] is None else acc[out_row] + piece
     for row in range(2):
         out_ref[row] = acc[row]
     odd = lax.axis_index("reg") % 2 == 1
     inner, outer = lines_of(inner_ref, begin, cols), lines_of(outer_ref, begin, cols)
+    nodes = rows + 2 * SIDE
     for band, (yes, no) in enumerate(((inner, outer), (outer, inner))):
         for line in range(2):
             values = jnp.where(odd, yes[line], no[line])
             for off, hot in enumerate(hot_rows(values, rows, cols, line)):
-                hot_ref[(band * 2 + line) * TAPS + off] = hot
-
-
-def fields_kernel(inner_ref, outer_ref, above_ref, below_ref, own_ref, hot_ref, out_ref, up_ref, down_ref):
-    odd = lax.axis_index("reg") % 2
-
-    @pl.when(odd == 1)
-    def _():
-        up_ref[...] = inner_ref[...]
-        down_ref[...] = outer_ref[...]
-
-    @pl.when(odd == 0)
-    def _():
-        up_ref[...] = outer_ref[...]
-        down_ref[...] = inner_ref[...]
-
-    acc = [own_ref[0], own_ref[1]]
-    acc = band_sum(0, up_ref[...], above_ref, lambda line, off: hot_ref[line * TAPS + off], acc)
-    acc = band_sum(
-        2, down_ref[...], below_ref, lambda line, off: hot_ref[(2 + line) * TAPS + off], acc
-    )
-    out_ch = out_ref.shape[0]
+                at = (band * 2 + line) * TAPS + off
+                hot_ref[at, :nodes] = hot
+                hot_ref[at, nodes:] = jnp.zeros((hot_ref.shape[1] - nodes, cols), BF16)
+
+
+def fields_kernel(inner_ref, outer_ref, above_ref, below_ref, own_ref, hot_ref, out_ref, first_ref, second_ref):
+    odd = lax.axis_index("reg") % 2 == 1
+    inner, outer = inner_ref[...], outer_ref[...]
+    lanes = hot_ref.shape[1]
+    blank = jnp.zeros((lanes - inner.shape[0], inner.shape[1]), BF16)
+    shares_refs = (first_ref, second_ref)
+    for band, latent, weights_ref in (
+        (0, jnp.where(odd, inner, outer), above_ref),
+        (2, jnp.where(odd, outer, inner), below_ref),
+    ):
+        shares = band_shares(jnp.concatenate([latent, blank], axis=0), weights_ref)
+        for (out_row, tap, off), share in zip(band_blocks(band), shares):
+            line = out_row + tap - REACH
+            at = (line + REACH if band == 0 else line) * TAPS + off - out_row * TAPS
+            shares_refs[out_row][:, at * lanes : (at + 1) * lanes] = share
+    out_ch, _, cols = out_ref.shape
     for row in range(2):
-        out_ref[:, row, :] = acc[row][:out_ch].astype(BF16)
+        hot = hot_ref[row * TAPS : (row + 3) * TAPS].reshape(3 * TAPS * lanes, cols)
+        total = own_ref[row] + jnp.dot(shares_refs[row][...], hot, preferred_element_type=F32)
+        out_ref[:, row, :] = total[:out_ch].astype(BF16)
 
 
 def whole(memory=pltpu.VMEM):
@@ -289,23 +288,18 @@
 
     left = shifted(x, "lon", 1, True)
     right = shifted(x, "lon", -1, True)
-    line = lax.rem(assignment, rows).astype(BF16).reshape(1, lat_rows * lon_cols)
-    line = jnp.pad(line, ((0, ROWS - 1), (0, 0)))
-    column = jnp.concatenate([left, x, right, line], axis=0)
-    outer = exchanged(column, 1)
-    inner = exchanged(column, 0)
-
     outputs = -(-out_ch // ROWS) * ROWS
     taps = psi.transpose(1, 2, 3, 0).reshape(lat_rows * TAPS * TAPS, basis)
     head = width // HEADS
     members = LANES // head
     parts = HEADS // members
     sizes = [len(band_blocks(band)) for band in range(3)]
-    query, key, value, wvt, above, middle, below = pl.pallas_call(
+    own, query, key, value, wvt, above, middle, below = pl.pallas_call(
         prepare_kernel,
-        in_specs=[whole()] * 5,
-        out_specs=[whole()] * 7,
+        in_specs=[whole()] * 6,
+        out_specs=[whole()] * 8,
         out_shape=[
+            struct(rows + ROWS, width),
             struct(parts, LANES, members * rows),
             struct(rows, width),
             struct(width, rows),
@@ -316,24 +310,26 @@
         compiler_params=params(32),
         cost_estimate=cost(3e9, 1.2e7),
         name="prepare",
-    )(x, gain, w_qkv, taps, w_dec.transpose(0, 2, 1))
+    )(x, gain, w_qkv, assignment, taps, w_dec.transpose(0, 2, 1))
+    column = jnp.concatenate([left, right, own], axis=0)
+    outer = exchanged(column, 1)
+    inner = exchanged(column, 0)
 
     state, latent, west, east = pl.pallas_call(
         functools.partial(attend_kernel, sectors),
-        in_specs=[whole(pltpu.SMEM)] * 2 + [whole()] * 13,
+        in_specs=[whole(pltpu.SMEM)] * 2 + [whole()] * 11,
         out_specs=[whole()] * 4,
-        out_shape=[struct(rows, width), struct(rows, channels), struct(16, channels), struct(16, channels)],
+        out_shape=[struct(rows, width), struct(rows, channels)] + [struct(ROWS, channels)] * 2,
         scratch_shapes=[
-            pltpu.VMEM((count - 1, rows, width), BF16),
             pltpu.VMEM((count * rows, width), BF16),
-            pltpu.VMEM((width, count * rows), BF16),
+            pltpu.VMEM((parts, LANES + ROWS, count * rows), BF16),
             pltpu.VMEM((rows, width), BF16),
         ],
         compiler_params=params(32),
         cost_estimate=cost(4e9, 6e6),
         name="attend",
     )(
-        neighbours, assignment, x, left, right, inner, outer,
+        neighbours, assignment, column, inner, outer,
         gain, w_qkv, query, key, value, wvt, w_out, w_latent,
     )
 
@@ -343,25 +339,25 @@
     far = exchanged(extended, 1)
     near = exchanged(extended, 0)
 
-    nodes_ext = rows + 2 * SIDE
+    lanes = -(-(rows + 2 * SIDE) // 256) * 256
     partial, hots = pl.pallas_call(
         functools.partial(own_kernel, 3 * rows),
         in_specs=[whole()] * 5,
         out_specs=[whole()] * 2,
         out_shape=[
             struct(lat_rows, outputs, lon_cols, dtype=F32),
-            struct(4 * TAPS, nodes_ext, lon_cols),
+            struct(4 * TAPS, lanes, lon_cols),
         ],
         compiler_params=params(32),
         cost_estimate=cost(1e9, 2.5e6),
         name="own_band",
-    )(line, inner, outer, extended, middle)
+    )(column, inner, outer, extended, middle)
     fields = pl.pallas_call(
         fields_kernel,
         in_specs=[whole()] * 6,
         out_specs=whole(),
         out_shape=struct(out_ch, lat_rows, lon_cols),
-        scratch_shapes=[pltpu.VMEM((nodes_ext, channels), BF16)] * 2,
+        scratch_shapes=[pltpu.VMEM((outputs, 3 * TAPS * lanes), BF16)] * 2,
         compiler_params=params(32),
         cost_estimate=cost(2e9, 4e6),
         name="fields",

time: 42.1 us -> 40.4 us (0.960)
  other arithmetic: 1.63 us -> 0.01 us
  Pallas kernels: 10.8 us -> 10.1 us
  local copies, waits for them, and re-layouts: 4.92 us -> 5.62 us
    ppermute x4, waiting for transfers between devices: 7.27 us -> 1.63 us  [shifted(): return lax.ppermute(array, axis, pairs)]
    ppermute x4, waiting for transfers between devices: 1.58 us -> 6.99 us  [exchanged(): return lax.ppermute(array, 'reg', pairs + [(j, i) for i, j in pairs])]
    concatenate x1 -> x0, other arithmetic: 0.93 us -> none  [shards(): column = jnp.concatenate([left, x, right, line], axis=0)]
    unnamed x17 -> x22, local copies, waits for them, and re-layouts: 4.15 us -> 4.85 us
    unnamed x1 -> x0, other arithmetic: 0.69 us -> none
    pallas_call x1, Pallas kernels: 5.11 us -> 4.54 us  [shards(): pl.pallas_call(functools.partial(attend_kernel, sectors), in_specs=[whole...]
  transfers between devices with their start and end apart: 8 -> 8, of which waited for: 5 -> 4; matrix products, arithmetic and copies ran while one was open for 3% -> 2% of each run, Pallas kernels for 8% -> 8%
where the time goes in v3:
time: 40.4 us; the launch traced here: 40.1 us
  starting transfers between devices  14.9 us (37%)
  Pallas kernels  10.1 us (25%)
  waiting for transfers between devices  8.62 us (21%)
  local copies, waits for them, and re-layouts  5.62 us (14%)
  between operations  0.78 us (2%)
    ppermute x4, starting transfers between devices, exchanged(): return lax.ppermute(array, 'reg', pairs + [(j, i) for i, j in pairs])  9.27 us
    ppermute x4, waiting for transfers between devices, exchanged(): return lax.ppermute(array, 'reg', pairs + [(j, i) for i, j in pairs])  6.99 us
    ppermute x4, starting transfers between devices, shifted(): return lax.ppermute(array, axis, pairs)  5.68 us
    unnamed x22, local copies, waits for them, and re-layouts  4.85 us
    pallas_call x1, Pallas kernels, shards(): pl.pallas_call(functools.partial(attend_kernel, sectors), in_specs=[whole...  4.54 us
    pallas_call x1, Pallas kernels, shards(): pl.pallas_call(fields_kernel, in_specs=[whole()] * 6, out_specs=whole(),...  2.27 us
    pallas_call x1, Pallas kernels, shards(): pl.pallas_call(prepare_kernel, in_specs=[whole()] * 6, out_specs=[whole()...  2.03 us
    ppermute x4, waiting for transfers between devices, shifted(): return lax.ppermute(array, axis, pairs)  1.63 us
  transfers between devices with their start and end apart: 8, of which 4 were waited for; matrix products, arithmetic and copies ran while one was open for 2% of the time, Pallas kernels for 8%

profile of v3, /device:TPU:1, one launch (start us, length us, event | category | flops | bytes accessed | tf_op | source)
XLA Modules:
  0.0 40.1 jit_solution(11619871309284682190)
XLA Ops:
  0.6 3.0 %collective-permute-start.1 = (bf16[128,512]{1,0:T(8,128)(2,1)}, bf16[128,512]{1,0:T(8,128)(2,1)S(1)}, u32[]{:S(2)}, u32[]{:S(2)}) collective-permute-start(bf16[128,512]{1,0:T(8,128)(2,1)} %bitcast.7), channel_id=1, source_target_pairs={{0,3},{1,0},{2,1},{3,2},{4,7},{5,4},{6,5},{7,6},{8,11},{9,8},{10,9... | collective-permute-start | bytes 393224 | tf_op jit(solution)/shard_map/ppermute | solution.py:282
  3.7 0.0 collective-permute-start
  3.7 0.7 %copy.12 = f32[2,5,5,9]{3,2,1,0:T(8,128)S(1)} copy(f32[2,5,5,9]{3,0,2,1:T(2,128)} %bitcast.12) | data formatting | bytes 3600 | tf_op jit(solution)/shard_map/transpose | solution.py:292
  4.4 0.0 copy-start
  4.4 1.4 %copy-done = bf16[512,1536]{1,0:T(8,128)(2,1)S(1)} copy-done((bf16[512,1536]{1,0:T(8,128)(2,1)S(1)}, bf16[512,1536]{1,0:T(8,128)(2,1)}, u32[]{:S(2)}) %copy-start) | copy-done | bytes 1572888
  5.8 1.1 %copy-done.2 = bf16[9,512,84]{1,2,0:T(8,128)(2,1)S(1)} copy-done((bf16[9,512,84]{1,2,0:T(8,128)(2,1)S(1)}, bf16[9,512,84]{1,2,0:T(8,128)(2,1)}, u32[]{:S(2)}) %copy-start.2) | copy-done | bytes 774168
  7.0 0.9 %copy-done.5 = bf16[1,128,512]{2,1,0:T(8,128)(2,1)S(1)} copy-done((bf16[1,128,512]{2,1,0:T(8,128)(2,1)S(1)}, bf16[1,128,512]{2,1,0:T(8,128)(2,1)}, u32[]{:S(2)}) %copy-start.5) | copy-done | bytes 131096
  7.9 0.7 %copy-done.6 = s32[2,256]{1,0:T(2,128)S(1)} copy-done((s32[2,256]{1,0:T(2,128)S(1)}, s32[2,256]{1,0:T(2,128)}, u32[]{:S(2)}) %copy-start.6) | copy-done | bytes 2072
  8.6 0.7 %copy-done.8 = f32[512]{0:T(512)S(1)} copy-done((f32[512]{0:T(512)S(1)}, f32[512]{0:T(512)}, u32[]{:S(2)}) %copy-start.8) | copy-done | bytes 2072
  9.3 0.0 copy-start.9
  9.3 2.0 %prepare.1 = (bf16[144,512]{1,0:T(8,128)(2,1)S(1)}, bf16[4,128,512]{2,1,0:T(8,128)(2,1)S(1)}, bf16[128,512]{1,0:T(8,128)(2,1)S(1)}, bf16[512,128]{1,0:T(8,128)(2...) custom-call(bf16[128,512]{1,0:T(8,128)(2,1)S(1)} %bitcast.9, ...), custom_call_target="tpu_custom_call" | custom-call | flops 3000000000 | bytes 12000000 | tf_op jit(solution)/shard_map/prepare/pallas_call | solution.py:297
  11.4 4.0 %collective-permute-start.3 = (bf16[400,512]{1,0:T(8,128)(2,1)S(1)}, bf16[400,512]{1,0:T(8,128)(2,1)S(1)}, u32[]{:S(2)}, u32[]{:S(2)}) collective-permute-start(bf16[400,512]{1,0:T(8,128)(2,1)S(1)} %constant_dynamic-update-slice_fusion.column_ref.line_ref), channel_id=1, source_target_pairs={{4,8},{12,16},{20,24},{8,4},{16,12},{24,20},{5,9},{13,17},{21,25},... | collective-permute-start | bytes 1228808 | tf_op jit(solution)/shard_map/ppermute | solution.py:287
  15.5 0.1 collective-permute-start.2
  15.5 5.5 %collective-permute-done.3.outer_ref = bf16[400,512]{1,0:T(8,128)(2,1)S(1)} collective-permute-done((bf16[400,512]{1,0:T(8,128)(2,1)S(1)}, bf16[400,512]{1,0:T(8,128)(2,1)S(1)}, u32[]{:S(2)}, u32[]{:S(2)}) %collective-permute-start.3) | collective-permute-done | bytes 409632 | tf_op jit(solution)/shard_map/ppermute | solution.py:287
  21.1 4.5 %attend.1 = (bf16[128,512]{1,0:T(8,128)(2,1)}, bf16[128,512]{1,0:T(8,128)(2,1)S(1)}, bf16[16,512]{1,0:T(8,128)(2,1)S(1)}, bf16[16,512]{1,0:T(8,128)(2,1)S(1)}) custom-call(s32[1,5]{1,0:T(1,128)S(1)} %copy-done.9, s32[2,256]{1,0:T(2,128)S(1)} %copy-done.7, bf16[400,512]{1,0:T(8,128)(2,1)S(1)} %constant_dynamic-update-slice_fusion.column_ref.line_ref, ...), custom_call_target="tpu_custom_call" | custom-call | flops 4000000000 | bytes 6000000 | tf_op jit(solution)/shard_map/attend/pallas_call | solution.py:318
  25.7 1.7 %collective-permute-start.4 = (bf16[16,512]{1,0:T(8,128)(2,1)S(1)}, bf16[16,512]{1,0:T(8,128)(2,1)S(1)}, u32[]{:S(2)}, u32[]{:S(2)}) collective-permute-start(bf16[16,512]{1,0:T(8,128)(2,1)S(1)} %get-tuple-element.23), channel_id=1, source_target_pairs={{0,1},{1,2},{2,3},{3,0},{4,5},{5,6},{6,7},{7,4},{8,9},{9,10},{10,1... | collective-permute-start | bytes 49160 | tf_op jit(solution)/shard_map/ppermute | solution.py:282
  27.3 1.0 %collective-permute-start.5 = (bf16[16,512]{1,0:T(8,128)(2,1)S(1)}, bf16[16,512]{1,0:T(8,128)(2,1)S(1)}, u32[]{:S(2)}, u32[]{:S(2)}) collective-permute-start(bf16[16,512]{1,0:T(8,128)(2,1)S(1)} %get-tuple-element.24), channel_id=1, source_target_pairs={{0,3},{1,0},{2,1},{3,2},{4,7},{5,4},{6,5},{7,6},{8,11},{9,8},{10,9... | collective-permute-start | bytes 49160 | tf_op jit(solution)/shard_map/ppermute | solution.py:282
  28.3 1.1 %collective-permute-done.4 = bf16[16,512]{1,0:T(8,128)(2,1)S(1)} collective-permute-done((bf16[16,512]{1,0:T(8,128)(2,1)S(1)}, bf16[16,512]{1,0:T(8,128)(2,1)S(1)}, u32[]{:S(2)}, u32[]{:S(2)}) %collective-permute-start.4) | collective-permute-done | bytes 16416 | tf_op jit(solution)/shard_map/ppermute | solution.py:282
  29.4 0.5 %collective-permute-done.5 = bf16[16,512]{1,0:T(8,128)(2,1)S(1)} collective-permute-done((bf16[16,512]{1,0:T(8,128)(2,1)S(1)}, bf16[16,512]{1,0:T(8,128)(2,1)S(1)}, u32[]{:S(2)}, u32[]{:S(2)}) %collective-permute-start.5) | collective-permute-done | bytes 16416 | tf_op jit(solution)/shard_map/ppermute | solution.py:282
  29.9 5.1 %collective-permute-start.7 = (bf16[144,512]{1,0:T(8,128)(2,1)S(1)}, bf16[144,512]{1,0:T(8,128)(2,1)S(1)}, u32[]{:S(2)}, u32[]{:S(2)}) collective-permute-start(bf16[144,512]{1,0:T(8,128)(2,1)S(1)} %pad_maximum_fusion.latent_ref), channel_id=1, source_target_pairs={{4,8},{12,16},{20,24},{8,4},{16,12},{24,20},{5,9},{13,17},{21,25},... | collective-permute-start | bytes 442376 | tf_op jit(solution)/shard_map/ppermute | solution.py:287
  35.0 0.1 collective-permute-start.6
  35.1 1.3 %own_band.1 = (f32[2,96,256]{2,1,0:T(8,128)S(1)}, bf16[20,256,256]{2,1,0:T(8,128)(2,1)S(1)}) custom-call(bf16[400,512]{1,0:T(8,128)(2,1)S(1)} %constant_dynamic-update-slice_fusion.column_ref.line_ref, bf16[400,512]{1,0:T(8,128)(2,1)S(1)} %collective-permute-done.2.inner_ref, bf16[400,512]{1,0:T(8,128)(2,1)S(1)} %collective-permute-done.3.outer_ref, ...), custom_call_target="tpu_custom_call" | custom-call | flops 1000000000 | bytes 2500000 | tf_op jit(solution)/shard_map/own_band/pallas_call | solution.py:343
  36.4 1.4 %collective-permute-done.7.outer_ref = bf16[144,512]{1,0:T(8,128)(2,1)S(1)} collective-permute-done((bf16[144,512]{1,0:T(8,128)(2,1)S(1)}, bf16[144,512]{1,0:T(8,128)(2,1)S(1)}, u32[]{:S(2)}, u32[]{:S(2)}) %collective-permute-start.7) | collective-permute-done | bytes 147488 | tf_op jit(solution)/shard_map/ppermute | solution.py:287
  37.8 2.3 %fields.1 = bf16[84,2,256]{2,1,0:T(2,128)(2,1)} custom-call(bf16[144,512]{1,0:T(8,128)(2,1)S(1)} %collective-permute-done.6.inner_ref, bf16[144,512]{1,0:T(8,128)(2,1)S(1)} %collective-permute-done.7.outer_ref, bf16[15,96,512]{2,1,0:T(8,128)(2,1)S(1)} %get-tuple-element.25.above_ref, bf16[15,96,512]{2,1,0:T(8,128)(2,1)S(1)} %get-tuple-element.26.below_ref, ...), custom_call_target="tpu_custom_call" | custom-call | flops 2000000000 | bytes 4000000 | tf_op jit(solution)/shard_map/fields/pallas_call | solution.py:355
  (24 shorter events, 0.1 us)
Async XLA Ops:
  0.6 10.7 %collective-permute-start.1 = (bf16[128,512]{1,0:T(8,128)(2,1)}, bf16[128,512]{1,0:T(8,128)(2,1)S(1)}, u32[]{:S(2)}, u32[]{:S(2)}) collective-permute-start(bf16[128,512]{1,0:T(8,128)(2,1)} %bitcast.7), channel_id=1, source_target_pairs={{0,3},{1,0},{2,1},{3,2},{4,7},{5,4},{6,5},{7,6},{8,11},{9,8},{10,9... | collective-permute-start | bytes 393224 | tf_op jit(solution)/shard_map/ppermute | solution.py:282
  3.7 7.6 %collective-permute-start = (bf16[128,512]{1,0:T(8,128)(2,1)}, bf16[128,512]{1,0:T(8,128)(2,1)S(1)}, u32[]{:S(2)}, u32[]{:S(2)}) collective-permute-start(bf16[128,512]{1,0:T(8,128)(2,1)} %bitcast.8), channel_id=1, source_target_pairs={{0,1},{1,2},{2,3},{3,0},{4,5},{5,6},{6,7},{7,4},{8,9},{9,10},{10,1... | collective-permute-start | bytes 393224 | tf_op jit(solution)/shard_map/ppermute | solution.py:282
  4.4 1.4 %copy-start = (bf16[512,1536]{1,0:T(8,128)(2,1)S(1)}, bf16[512,1536]{1,0:T(8,128)(2,1)}, u32[]{:S(2)}) copy-start(bf16[512,1536]{1,0:T(8,128)(2,1)} %wqkv_ref.3) | copy-start | bytes 4718596
  5.8 1.1 %copy-start.2 = (bf16[9,512,84]{1,2,0:T(8,128)(2,1)S(1)}, bf16[9,512,84]{1,2,0:T(8,128)(2,1)}, u32[]{:S(2)}) copy-start(bf16[9,512,84]{1,2,0:T(8,128)(2,1)} %param.17) | copy-start | bytes 2322436
  7.0 0.9 %copy-start.5 = (bf16[1,128,512]{2,1,0:T(8,128)(2,1)S(1)}, bf16[1,128,512]{2,1,0:T(8,128)(2,1)}, u32[]{:S(2)}) copy-start(bf16[1,128,512]{2,1,0:T(8,128)(2,1)} %param.9) | copy-start | bytes 393220
  7.9 0.7 %copy-start.6 = (s32[2,256]{1,0:T(2,128)S(1)}, s32[2,256]{1,0:T(2,128)}, u32[]{:S(2)}) copy-start(s32[2,256]{1,0:T(2,128)} %assign_ref.3) | copy-start | bytes 6148
  8.6 0.7 %copy-start.8 = (f32[512]{0:T(512)S(1)}, f32[512]{0:T(512)}, u32[]{:S(2)}) copy-start(f32[512]{0:T(512)} %param.10) | copy-start | bytes 6148
  9.3 11.8 %copy-start.1 = (bf16[512,1536]{1,0:T(8,128)(2,1)S(1)}, bf16[512,1536]{1,0:T(8,128)(2,1)}, u32[]{:S(2)}) copy-start(bf16[512,1536]{1,0:T(8,128)(2,1)} %wqkv_ref.3) | copy-start | bytes 4718596
  9.3 11.8 %copy-start.3 = (bf16[512,512]{1,0:T(8,128)(2,1)S(1)}, bf16[512,512]{1,0:T(8,128)(2,1)}, u32[]{:S(2)}) copy-start(bf16[512,512]{1,0:T(8,128)(2,1)} %wout_ref.1) | copy-start | bytes 1572868
  9.3 11.8 %copy-start.4 = (bf16[512,512]{1,0:T(8,128)(2,1)S(1)}, bf16[512,512]{1,0:T(8,128)(2,1)}, u32[]{:S(2)}) copy-start(bf16[512,512]{1,0:T(8,128)(2,1)} %wlat_ref.1) | copy-start | bytes 1572868
  9.3 11.8 %copy-start.7 = (s32[2,256]{1,0:T(2,128)S(1)}, s32[2,256]{1,0:T(2,128)}, u32[]{:S(2)}) copy-start(s32[2,256]{1,0:T(2,128)} %assign_ref.3) | copy-start | bytes 6148
  9.3 11.8 %copy-start.9 = (s32[1,5]{1,0:T(1,128)S(1)}, s32[1,5]{1,0:T(1,128)}, u32[]{:S(2)}) copy-start(s32[1,5]{1,0:T(1,128)} %listed_ref.1) | copy-start | bytes 64
  11.4 9.7 %collective-permute-start.3 = (bf16[400,512]{1,0:T(8,128)(2,1)S(1)}, bf16[400,512]{1,0:T(8,128)(2,1)S(1)}, u32[]{:S(2)}, u32[]{:S(2)}) collective-permute-start(bf16[400,512]{1,0:T(8,128)(2,1)S(1)} %constant_dynamic-update-slice_fusion.column_ref.line_ref), channel_id=1, source_target_pairs={{4,8},{12,16},{20,24},{8,4},{16,12},{24,20},{5,9},{13,17},{21,25},... | collective-permute-start | bytes 1228808 | tf_op jit(solution)/shard_map/ppermute | solution.py:287
  15.5 5.6 %collective-permute-start.2 = (bf16[400,512]{1,0:T(8,128)(2,1)S(1)}, bf16[400,512]{1,0:T(8,128)(2,1)S(1)}, u32[]{:S(2)}, u32[]{:S(2)}) collective-permute-start(bf16[400,512]{1,0:T(8,128)(2,1)S(1)} %constant_dynamic-update-slice_fusion.column_ref.line_ref), channel_id=1, source_target_pairs={{0,4},{8,12},{16,20},{24,28},{4,0},{12,8},{20,16},{28,24},{1,5},{9... | collective-permute-start | bytes 1228808 | tf_op jit(solution)/shard_map/ppermute | solution.py:287
  25.7 3.8 %collective-permute-start.4 = (bf16[16,512]{1,0:T(8,128)(2,1)S(1)}, bf16[16,512]{1,0:T(8,128)(2,1)S(1)}, u32[]{:S(2)}, u32[]{:S(2)}) collective-permute-start(bf16[16,512]{1,0:T(8,128)(2,1)S(1)} %get-tuple-element.23), channel_id=1, source_target_pairs={{0,1},{1,2},{2,3},{3,0},{4,5},{5,6},{6,7},{7,4},{8,9},{9,10},{10,1... | collective-permute-start | bytes 49160 | tf_op jit(solution)/shard_map/ppermute | solution.py:282
  27.3 2.6 %collective-permute-start.5 = (bf16[16,512]{1,0:T(8,128)(2,1)S(1)}, bf16[16,512]{1,0:T(8,128)(2,1)S(1)}, u32[]{:S(2)}, u32[]{:S(2)}) collective-permute-start(bf16[16,512]{1,0:T(8,128)(2,1)S(1)} %get-tuple-element.24), channel_id=1, source_target_pairs={{0,3},{1,0},{2,1},{3,2},{4,7},{5,4},{6,5},{7,6},{8,11},{9,8},{10,9... | collective-permute-start | bytes 49160 | tf_op jit(solution)/shard_map/ppermute | solution.py:282
  29.9 7.9 %collective-permute-start.7 = (bf16[144,512]{1,0:T(8,128)(2,1)S(1)}, bf16[144,512]{1,0:T(8,128)(2,1)S(1)}, u32[]{:S(2)}, u32[]{:S(2)}) collective-permute-start(bf16[144,512]{1,0:T(8,128)(2,1)S(1)} %pad_maximum_fusion.latent_ref), channel_id=1, source_target_pairs={{4,8},{12,16},{20,24},{8,4},{16,12},{24,20},{5,9},{13,17},{21,25},... | collective-permute-start | bytes 442376 | tf_op jit(solution)/shard_map/ppermute | solution.py:287
  35.0 2.8 %collective-permute-start.6 = (bf16[144,512]{1,0:T(8,128)(2,1)S(1)}, bf16[144,512]{1,0:T(8,128)(2,1)S(1)}, u32[]{:S(2)}, u32[]{:S(2)}) collective-permute-start(bf16[144,512]{1,0:T(8,128)(2,1)S(1)} %pad_maximum_fusion.latent_ref), channel_id=1, source_target_pairs={{0,4},{8,12},{16,20},{24,28},{4,0},{12,8},{20,16},{28,24},{1,5},{9... | collective-permute-start | bytes 442376 | tf_op jit(solution)/shard_map/ppermute | solution.py:287

commit v4 on v3

v4 whole, which is shorter than its diff:
```python
import functools
import math

import jax
import jax.numpy as jnp
from jax import lax
from jax.experimental import pallas as pl
from jax.experimental.pallas import tpu as pltpu
from jax.sharding import PartitionSpec as P

HEADS = 16
REACH = 2
TAPS = 2 * REACH + 1
SIDE = 8
ROWS = 16
LANES = 128
EARLY = 2
F32 = jnp.float32
BF16 = jnp.bfloat16
NT = (((1,), (1,)), ((), ()))

ABOVE = ((-2, (0,)), (-1, (0, 1)))
OWN = ((0, (0, 1)), (1, (0, 1)))
BELOW = ((3, (1,)), (2, (0, 1)))


def blocks_of(band):
    return [
        (out_row, src - out_row + REACH, off)
        for src, out_rows in band
        for off in range(TAPS)
        for out_row in out_rows
    ]


def iota(shape, dim):
    return lax.broadcasted_iota(jnp.int32, shape, dim)


def normalise(rows, gain):
    values = rows.astype(F32)
    center = values - jnp.mean(values, axis=-1, keepdims=True)
    spread = jnp.mean(center * center, axis=-1, keepdims=True)
    return (center * lax.rsqrt(spread + 1e-05) * gain).astype(BF16)


def prepare_kernel(
    x_hbm, gain_hbm, wqkv_hbm, assign_hbm, psi_hbm, dec_hbm,
    own_ref, query_ref, key_ref, value_ref, wk_ref, wvt_ref, middle_ref, edges_ref,
    x_ref, gain_ref, wqkv_ref, assign_ref, psi_ref, dec_ref, psi_rows_ref, taps_ref, sems,
):
    copies = [
        pltpu.make_async_copy(source, target, sems.at[at])
        for at, (source, target) in enumerate(
            (
                (assign_hbm, assign_ref),
                (x_hbm, x_ref),
                (gain_hbm, gain_ref),
                (psi_hbm, psi_ref),
                (dec_hbm, dec_ref),
                (wqkv_hbm, wqkv_ref),
            )
        )
    ]
    for copy in copies:
        copy.start()
    rows, width = x_ref.shape
    group, members = query_ref.shape[1], query_ref.shape[2] // rows
    head = group // members
    copies[0].wait()
    local = lax.rem(assign_ref[...], rows).astype(F32)
    line = jnp.concatenate([local[:1], local[1:2]], axis=1)
    line = jnp.broadcast_to(line, (ROWS, line.shape[1]))
    own_ref[rows:] = jnp.where(iota(line.shape, 0) == 0, line, 0.0).astype(BF16)
    copies[1].wait()
    own_ref[:rows] = x_ref[...]
    copies[2].wait()
    normed = normalise(x_ref[...], gain_ref[...])

    copies[3].wait()
    basis, out_ch, channels = dec_ref.shape
    depth = basis * ROWS
    for tap in range(TAPS):
        for off in range(TAPS):
            at = (tap * TAPS + off) * 2
            psi_rows_ref[at : at + 2, :] = psi_ref[tap, off]
    spread = (iota((basis, depth), 1) // ROWS == iota((basis, depth), 0)).astype(F32)
    expanded = jnp.dot(psi_rows_ref[...], spread, preferred_element_type=F32)
    pick = iota((ROWS, depth), 1) % ROWS == iota((ROWS, depth), 0)
    for at, (out_row, tap, off) in enumerate(blocks_of(OWN) + blocks_of(ABOVE) + blocks_of(BELOW)):
        source = (tap * TAPS + off) * 2 + out_row
        taps = jnp.broadcast_to(expanded[source : source + 1], (ROWS, depth))
        taps_ref[at * ROWS : (at + 1) * ROWS, :] = jnp.where(pick, taps, 0.0).astype(BF16)
    copies[4].wait()
    inside = middle_ref.shape[0]
    outside = edges_ref.shape[1]
    for first in range(0, out_ch, ROWS):
        size = min(ROWS, out_ch - first)
        pieces = []
        for base in range(basis):
            pieces.append(dec_ref[base, first : first + size, :])
            if size < ROWS:
                pieces.append(jnp.zeros((ROWS - size, channels), BF16))
        mixing = jnp.concatenate(pieces, axis=0)
        mixed = jnp.dot(taps_ref[...], mixing, preferred_element_type=F32).astype(BF16)
        mixed = mixed.reshape(taps_ref.shape[0] // ROWS, ROWS, channels)
        middle_ref[:, first : first + ROWS, :] = mixed[:inside]
        edges_ref[0, :, first : first + ROWS, :] = mixed[inside : inside + outside]
        edges_ref[1, :, first : first + ROWS, :] = mixed[inside + outside :]

    copies[5].wait()
    query = jnp.dot(normed, wqkv_ref[:, :width], preferred_element_type=F32)
    query_t = (query * (math.log2(math.e) / head**0.5)).T.astype(BF16)
    mask = (iota((group, members * rows), 0) // head) == (iota((group, members * rows), 1) // rows)
    for part in range(width // group):
        piece = query_t[part * group : (part + 1) * group]
        wide = jnp.concatenate([piece] * members, axis=1)
        query_ref[part] = jnp.where(mask, wide, jnp.zeros_like(wide))
    wk = wqkv_ref[:, width : 2 * width]
    wk_ref[...] = wk
    key_ref[...] = jnp.dot(normed, wk, preferred_element_type=F32).astype(BF16)
    wvt = wqkv_ref[:, 2 * width :].astype(F32).T.astype(BF16)
    wvt_ref[...] = wvt
    value_ref[...] = lax.dot_general(wvt, normed, NT, preferred_element_type=F32).astype(BF16)


def listed_blocks(sectors, listed_ref):
    reg_here, lon_here = lax.axis_index("reg"), lax.axis_index("lon")
    toward = 1 - 2 * (reg_here % 2)
    found = []
    for at in range(1, listed_ref.shape[1]):
        block = listed_ref[0, at]
        step_reg = (block // sectors - reg_here) * toward
        step_lon = (block % sectors - lon_here + 1 + sectors) % sectors - 1
        place = jnp.where(step_lon == 0, 2, jnp.where(step_lon < 0, 0, 1))
        late = ((step_reg < 0) & (step_lon != 0)).astype(jnp.int32)
        found.append(late * 16 + (step_reg + 1) * 4 + place)
    for low in range(len(found)):
        for high in range(low + 1, len(found)):
            less, more = jnp.minimum(found[low], found[high]), jnp.maximum(found[low], found[high])
            found[low], found[high] = less, more
    return [(code % 16 // 4 - 1, code % 4) for code in found]


def chosen(blocks, rows, both_ref, inner_ref, center_ref, corners_ref):
    near = []
    for step, place in blocks:
        side = pl.ds(pl.multiple_of(jnp.minimum(place, 1) * rows, rows), rows)
        span = pl.ds(pl.multiple_of(place * rows, rows), rows)
        outer = center_ref[...]
        if corners_ref is not None:
            outer = jnp.where(place == 2, outer, corners_ref[side, :])
        other = jnp.where(step > 0, inner_ref[span, :], outer)
        near.append(jnp.where(step == 0, both_ref[side, :], other))
    return jnp.concatenate(near, axis=0)


def project(nodes, gain, wk_ref, wvt_ref):
    normed = normalise(nodes, gain)
    keys = jnp.dot(normed, wk_ref[...], preferred_element_type=F32).astype(BF16)
    values = lax.dot_general(wvt_ref[...], normed, NT, preferred_element_type=F32).astype(BF16)
    return keys, values


def early_kernel(
    sectors,
    listed_ref, both_ref, inner_ref, center_ref,
    gain_ref, wk_ref, wvt_ref, query_ref, key_ref, value_ref,
    top_ref, sum_ref, keys_ref, values_ref,
):
    rows = key_ref.shape[0]
    parts, group, _ = query_ref.shape
    blocks = listed_blocks(sectors, listed_ref)[:EARLY]
    nodes = chosen(blocks, rows, both_ref, inner_ref, center_ref, None)
    keys, values = project(nodes, gain_ref[...], wk_ref, wvt_ref)
    keys_ref[:rows] = key_ref[...]
    keys_ref[rows:] = keys
    for part in range(parts):
        span = slice(part * group, (part + 1) * group)
        values_ref[part, :group, :rows] = value_ref[span]
        values_ref[part, :group, rows:] = values[span]
        values_ref[part, group:, :] = jnp.ones((ROWS, keys_ref.shape[0]), BF16)

    def scored(part):
        span = slice(part * group, (part + 1) * group)
        return jnp.dot(keys_ref[:, span], query_ref[part], preferred_element_type=F32)

    scores = scored(0)
    for part in range(parts):
        now = scores
        if part + 1 < parts:
            scores = scored(part + 1)
        top = jnp.max(now, axis=0, keepdims=True)
        expo = jnp.exp2(now - top).astype(BF16)
        top_ref[part] = jnp.broadcast_to(top, top_ref.shape[1:])
        sum_ref[part] = jnp.dot(values_ref[part], expo, preferred_element_type=F32)


def late_kernel(
    sectors,
    listed_ref, assign_ref, both_ref, inner_ref, center_ref, corners_ref,
    own_ref, gain_ref, wk_ref, wvt_ref, query_ref, top_ref, sum_ref, wout_ref, wlat_ref,
    state_ref, latent_ref, west_ref, east_ref,
    attended_ref,
):
    rows, width = state_ref.shape
    parts, group, lanes = query_ref.shape
    members = lanes // rows
    head = group // members
    blocks = listed_blocks(sectors, listed_ref)[EARLY:]
    nodes = chosen(blocks, rows, both_ref, inner_ref, center_ref, corners_ref)
    keys, values = project(nodes, gain_ref[...], wk_ref, wvt_ref)
    ones = jnp.ones((ROWS, len(blocks) * rows), BF16)
    owner = iota((group, rows), 0) // head

    def scored(part):
        span = slice(part * group, (part + 1) * group)
        return jnp.dot(keys[:, span], query_ref[part], preferred_element_type=F32)

    scores = scored(0)
    for part in range(parts):
        now = scores
        if part + 1 < parts:
            scores = scored(part + 1)
        before = top_ref[part, :1]
        top = jnp.maximum(before, jnp.max(now, axis=0, keepdims=True))
        expo = jnp.exp2(now - top).astype(BF16)
        weights = jnp.concatenate([values[part * group : (part + 1) * group], ones], axis=0)
        summed = jnp.dot(weights, expo, preferred_element_type=F32)
        summed = summed + sum_ref[part] * jnp.exp2(before - top)
        summed = summed[:group] * (1.0 / summed[group : group + 1])
        merged = None
        for member in range(members):
            piece = summed[:, member * rows : (member + 1) * rows]
            merged = piece if merged is None else jnp.where(owner == member, piece, merged)
        attended_ref[:, part * group : (part + 1) * group] = merged.T.astype(BF16)
    state = (
        own_ref[:rows].astype(F32)
        + jnp.dot(attended_ref[...], wout_ref[...], preferred_element_type=F32)
    ).astype(BF16)
    state_ref[...] = state
    value = jnp.dot(state, wlat_ref[...], preferred_element_type=F32)
    latent = (value / (1.0 + jnp.exp(-value))).astype(BF16)
    latent_ref[...] = latent
    lat_rows, lon_cols = assign_ref.shape
    for ref, first in ((west_ref, 0), (east_ref, lon_cols - REACH)):
        cells = ref.shape[0]
        line, node = iota((cells, rows), 0), iota((cells, rows), 1)
        hit = jnp.zeros((cells, rows), F32)
        for row in range(lat_rows):
            for col in range(REACH):
                local = assign_ref[row, first + col] % rows
                hit = jnp.where((line == row * REACH + col) & (node == local), 1.0, hit)
        ref[...] = jnp.dot(hit.astype(BF16), latent, preferred_element_type=F32).astype(BF16)


def hot_rows(values, rows, cols, line):
    column = iota((8, cols), 1)
    node = iota((rows + 2 * SIDE, cols), 0).astype(F32)
    for off in range(TAPS):
        step = off - REACH
        where = jnp.broadcast_to(values, (8, cols))
        if step:
            where = pltpu.roll(where, (-step) % cols, 1)
        reach = column + step
        before = (rows + REACH * line + reach + REACH).astype(F32)
        after = (rows + SIDE + REACH * line + reach - cols).astype(F32)
        where = jnp.where(reach < 0, before, jnp.where(reach >= cols, after, where))
        yield jnp.where(node == where[:1], 1.0, 0.0).astype(BF16)


def shares_of(latent, weights):
    blocks, outputs, channels = weights.shape
    shares = lax.dot_general(
        weights.reshape(blocks * outputs, channels), latent, NT, preferred_element_type=F32
    ).astype(BF16)
    return [shares[at * outputs : (at + 1) * outputs] for at in range(blocks)]


def lines_of(line_ref, start, cols):
    values = line_ref[start : start + ROWS, :].astype(F32)
    return values[:1, :cols], values[:1, cols:]


def own_kernel(
    begin, own_ref, inner_ref, corners_ref, latent_ref, weights_ref, out_ref, hot_ref
):
    cols = out_ref.shape[2]
    rows = latent_ref.shape[0] - 2 * SIDE
    own = lines_of(own_ref, begin[0], cols)
    table = [list(hot_rows(own[line], rows, cols, line)) for line in range(2)]
    acc = [None, None]
    for (out_row, tap, off), share in zip(
        blocks_of(OWN), shares_of(latent_ref[...], weights_ref[...])
    ):
        line = out_row + tap - REACH
        piece = jnp.dot(share, table[line][off], preferred_element_type=F32)
        acc[out_row] = piece if acc[out_row] is None else acc[out_row] + piece
    for row in range(2):
        out_ref[row] = acc[row]
    odd = lax.axis_index("reg") % 2 == 1
    inner, outer = lines_of(inner_ref, begin[1], cols), lines_of(corners_ref, begin[2], cols)
    nodes = rows + 2 * SIDE
    for band, (yes, no) in enumerate(((inner, outer), (outer, inner))):
        for at, line in enumerate((0, 1) if band == 0 else (1, 0)):
            values = jnp.where(odd, yes[line], no[line])
            for off, hot in enumerate(hot_rows(values, rows, cols, line)):
                hot_ref[band, at, off, :nodes] = hot
                hot_ref[band, at, off, nodes:] = jnp.zeros((hot_ref.shape[3] - nodes, cols), BF16)


def band_kernel(from_inner, latent_ref, weights_ref, hot_ref, partial_ref, out_ref, one_ref, two_ref):
    odd = lax.axis_index("reg") % 2
    band = 1 - odd if from_inner else odd
    latent = latent_ref[...]
    lanes, cols = hot_ref.shape[3:]
    outputs = weights_ref.shape[2]
    blank = jnp.zeros((lanes - latent.shape[0], latent.shape[1]), BF16)
    shares = shares_of(jnp.concatenate([latent, blank], axis=0), weights_ref[band])
    for off in range(TAPS):
        span = slice(off * lanes, (off + 1) * lanes)
        one_ref[:, span] = shares[off]
        for row in range(2):
            two_ref[row * outputs : (row + 1) * outputs, span] = shares[TAPS + 2 * off + row]
    depth = TAPS * lanes
    one = jnp.dot(one_ref[...], hot_ref[band, 0].reshape(depth, cols), preferred_element_type=F32)
    two = jnp.dot(two_ref[...], hot_ref[band, 1].reshape(depth, cols), preferred_element_type=F32)
    for row in range(2):
        total = partial_ref[row] + two[row * outputs : (row + 1) * outputs]
        total = total + jnp.where(band == row, one, 0.0)
        if from_inner:
            out_ref[row] = total
        else:
            out_ref[:, row, :] = total[: out_ref.shape[0]].astype(BF16)


def whole(memory=pltpu.VMEM):
    return pl.BlockSpec(memory_space=memory)


def struct(*shape, dtype=BF16):
    return jax.ShapeDtypeStruct(shape, dtype)


def params(limit):
    return pltpu.CompilerParams(vmem_limit_bytes=limit << 20)


def cost(flops, moved):
    return pl.CostEstimate(flops=int(flops), bytes_accessed=int(moved), transcendentals=0)


def shards(nodes, norm_gain, w_qkv, w_out, w_latent, neighbours, assignment, psi, w_dec):
    _, rows, width = nodes.shape
    channels = w_latent.shape[1]
    lat_rows, lon_cols = assignment.shape
    basis, _, out_ch = w_dec.shape
    sectors = lax.axis_size("lon")
    count = neighbours.shape[1]
    x = nodes.reshape(rows, width)
    gain = norm_gain.reshape(1, width)

    def shifted(array, step):
        return lax.ppermute(array, "lon", [(i, (i + step) % sectors) for i in range(sectors)])

    def exchanged(array, first):
        size = lax.axis_size("reg")
        pairs = [(i, i + 1) for i in range(first, size - 1, 2)]
        return lax.ppermute(array, "reg", pairs + [(j, i) for i, j in pairs])

    left = shifted(x, 1)
    right = shifted(x, -1)
    center = exchanged(x, 1)

    outputs = -(-out_ch // ROWS) * ROWS
    head = width // HEADS
    members = LANES // head
    parts = HEADS // members
    inside, outside = len(blocks_of(OWN)), len(blocks_of(ABOVE))
    taps = psi.transpose(2, 3, 1, 0)
    mixing = w_dec.transpose(0, 2, 1)
    own, query, key, value, wk, wvt, middle, edges = pl.pallas_call(
        prepare_kernel,
        in_specs=[whole(pltpu.HBM)] * 6,
        out_specs=[whole()] * 8,
        out_shape=[
            struct(rows + ROWS, width),
            struct(parts, LANES, members * rows),
            struct(rows, width),
            struct(width, rows),
            struct(width, width),
            struct(width, width),
            struct(inside, outputs, channels),
            struct(2, outside, outputs, channels),
        ],
        scratch_shapes=[
            pltpu.VMEM((rows, width), BF16),
            pltpu.VMEM((1, width), F32),
            pltpu.VMEM(w_qkv.shape, BF16),
            pltpu.VMEM(assignment.shape, jnp.int32),
            pltpu.VMEM(taps.shape, F32),
            pltpu.VMEM(mixing.shape, BF16),
            pltpu.VMEM((2 * TAPS * TAPS, basis), F32),
            pltpu.VMEM(((inside + 2 * outside) * ROWS, basis * ROWS), BF16),
            pltpu.SemaphoreType.DMA((6,)),
        ],
        compiler_params=params(32),
        cost_estimate=cost(3e9, 1.2e7),
        name="prepare",
    )(x, gain, w_qkv, assignment, taps, mixing)
    both = jnp.concatenate([left, right, own[rows:]], axis=0)
    corners = exchanged(both, 1)
    inner = exchanged(jnp.concatenate([left, right, own], axis=0), 0)

    top, summed = pl.pallas_call(
        functools.partial(early_kernel, sectors),
        in_specs=[whole(pltpu.SMEM)] + [whole()] * 9,
        out_specs=[whole()] * 2,
        out_shape=[
            struct(parts, 8, members * rows, dtype=F32),
            struct(parts, LANES + ROWS, members * rows, dtype=F32),
        ],
        scratch_shapes=[
            pltpu.VMEM(((1 + EARLY) * rows, width), BF16),
            pltpu.VMEM((parts, LANES + ROWS, (1 + EARLY) * rows), BF16),
        ],
        compiler_params=params(32),
        cost_estimate=cost(3e9, 6e6),
        name="early",
    )(neighbours, both, inner, center, gain, wk, wvt, query, key, value)
    state, latent, west, east = pl.pallas_call(
        functools.partial(late_kernel, sectors),
        in_specs=[whole(pltpu.SMEM)] * 2 + [whole()] * 13,
        out_specs=[whole()] * 4,
        out_shape=[struct(rows, width), struct(rows, channels)] + [struct(ROWS, channels)] * 2,
        scratch_shapes=[pltpu.VMEM((rows, width), BF16)],
        compiler_params=params(32),
        cost_estimate=cost(3e9, 6e6),
        name="late",
    )(
        neighbours, assignment, both, inner, center, corners,
        own, gain, wk, wvt, query, top, summed, w_out, w_latent,
    )

    from_left = shifted(east, 1)
    from_right = shifted(west, -1)
    extended = jnp.concatenate([latent, from_left[:SIDE], from_right[:SIDE]], axis=0)
    far = exchanged(extended, 1)
    near = exchanged(extended, 0)

    lanes = -(-(rows + 2 * SIDE) // 256) * 256
    partial, hots = pl.pallas_call(
        functools.partial(own_kernel, (rows, 3 * rows, 2 * rows)),
        in_specs=[whole()] * 5,
        out_specs=[whole()] * 2,
        out_shape=[
            struct(lat_rows, outputs, lon_cols, dtype=F32),
            struct(2, 2, TAPS, lanes, lon_cols),
        ],
        compiler_params=params(32),
        cost_estimate=cost(1e9, 2.5e6),
        name="own_band",
    )(own, inner, corners, extended, middle)
    band_scratch = [
        pltpu.VMEM((outputs, TAPS * lanes), BF16),
        pltpu.VMEM((2 * outputs, TAPS * lanes), BF16),
    ]
    partial = pl.pallas_call(
        functools.partial(band_kernel, True),
        in_specs=[whole()] * 4,
        out_specs=whole(),
        out_shape=struct(lat_rows, outputs, lon_cols, dtype=F32),
        scratch_shapes=band_scratch,
        compiler_params=params(32),
        cost_estimate=cost(1e9, 2.5e6),
        name="inner_band",
    )(near, edges, hots, partial)
    fields = pl.pallas_call(
        functools.partial(band_kernel, False),
        in_specs=[whole()] * 4,
        out_specs=whole(),
        out_shape=struct(out_ch, lat_rows, lon_cols),
        scratch_shapes=band_scratch,
        compiler_params=params(32),
        cost_estimate=cost(1e9, 2.5e6),
        name="outer_band",
    )(far, edges, hots, partial)
    return (state.reshape(1, rows, width), fields.reshape(1, out_ch, lat_rows, lon_cols))


def solution(mesh):
    in_specs = (
        P(None, ("reg", "lon"), None),
        P(),
        P(),
        P(),
        P(),
        P(("reg", "lon"), None),
        P("reg", "lon"),
        P(None, "reg", None, None),
        P(),
    )
    out_specs = (P(None, ("reg", "lon"), None), P(None, None, "reg", "lon"))
    return jax.shard_map(shards, mesh=mesh, in_specs=in_specs, out_specs=out_specs, check_vma=False)
```

time: 40.4 us -> 40.6 us (level)
  waiting for transfers between devices: 8.62 us -> 5.29 us
  Pallas kernels: 10.1 us -> 12.2 us
  starting transfers between devices: 14.9 us -> 16.3 us
    ppermute x4 -> x5, waiting for transfers between devices: 6.99 us -> 3.96 us  [exchanged(): return lax.ppermute(array, 'reg', pairs + [(j, i) for i, j in pairs])]
    pallas_call x4 -> x6, Pallas kernels: 10.1 us -> 12.2 us  [the longest x1 3.31 us: shards(): pl.pallas_call(functools.partial(late_kernel, sectors), in_specs=[whole(p...]
    ppermute x4 -> x5, starting transfers between devices: 9.27 us -> 10.6 us  [exchanged(): return lax.ppermute(array, 'reg', pairs + [(j, i) for i, j in pairs])]
    transpose x1 -> x0, local copies, waits for them, and re-layouts: 0.75 us -> none  [shards(): taps = psi.transpose(1, 2, 3, 0).reshape(lat_rows * TAPS * TAPS, basis)]
    unnamed x22, local copies, waits for them, and re-layouts: 4.85 us -> 5.58 us
  transfers between devices with their start and end apart: 8 -> 9, of which waited for: 4 -> 5; matrix products, arithmetic and copies ran while one was open for 2% -> 0% of each run, Pallas kernels for 8% -> 18%
where the time goes in v4:
time: 40.6 us; the launch traced here: 40.3 us
  starting transfers between devices  16.3 us (40%)
  Pallas kernels  12.2 us (30%)
  local copies, waits for them, and re-layouts  5.59 us (14%)
  waiting for transfers between devices  5.29 us (13%)
  between operations  0.79 us (2%)
    ppermute x5, starting transfers between devices, exchanged(): return lax.ppermute(array, 'reg', pairs + [(j, i) for i, j in pairs])  10.6 us
    ppermute x4, starting transfers between devices, shifted(): lax.ppermute(array, 'lon', [(i, (i + step) % sectors) for i in range(sect...  5.71 us
    unnamed x22, local copies, waits for them, and re-layouts  5.58 us
    ppermute x5, waiting for transfers between devices, exchanged(): return lax.ppermute(array, 'reg', pairs + [(j, i) for i, j in pairs])  3.96 us
    pallas_call x1, Pallas kernels, shards(): pl.pallas_call(functools.partial(late_kernel, sectors), in_specs=[whole(p...  3.31 us
    pallas_call x1, Pallas kernels, shards(): pl.pallas_call(prepare_kernel, in_specs=[whole(pltpu.HBM)] * 6, out_specs...  2.83 us
    pallas_call x1, Pallas kernels, shards(): pl.pallas_call(functools.partial(early_kernel, sectors), in_specs=[whole(...  2.27 us
    pallas_call x1, Pallas kernels, shards(): pl.pallas_call(functools.partial(band_kernel, False), in_specs=[whole()]...  1.61 us
  transfers between devices with their start and end apart: 9, of which 5 were waited for; matrix products, arithmetic and copies ran while one was open for 0% of the time, Pallas kernels for 18%

profile of v4, /device:TPU:1, one launch (start us, length us, event | category | flops | bytes accessed | tf_op | source)
XLA Modules:
  0.0 40.3 jit_solution(4844403739527908103)
XLA Ops:
  0.6 3.0 %collective-permute-start.1 = (bf16[128,512]{1,0:T(8,128)(2,1)}, bf16[128,512]{1,0:T(8,128)(2,1)S(1)}, u32[]{:S(2)}, u32[]{:S(2)}) collective-permute-start(bf16[128,512]{1,0:T(8,128)(2,1)} %bitcast.7), channel_id=1, source_target_pairs={{0,3},{1,0},{2,1},{3,2},{4,7},{5,4},{6,5},{7,6},{8,11},{9,8},{10,9... | collective-permute-start | bytes 393224 | tf_op jit(solution)/shard_map/ppermute | solution.py:364
  3.7 1.4 %copy-done = bf16[512,1536]{1,0:T(8,128)(2,1)S(1)} copy-done((bf16[512,1536]{1,0:T(8,128)(2,1)S(1)}, bf16[512,1536]{1,0:T(8,128)(2,1)}, u32[]{:S(2)}) %copy-start) | copy-done | bytes 1572888
  5.1 1.1 %copy-done.1 = bf16[9,512,84]{1,2,0:T(8,128)(2,1)S(1)} copy-done((bf16[9,512,84]{1,2,0:T(8,128)(2,1)S(1)}, bf16[9,512,84]{1,2,0:T(8,128)(2,1)}, u32[]{:S(2)}) %copy-start.1) | copy-done | bytes 774168
  6.2 0.9 %copy-done.4 = bf16[1,128,512]{2,1,0:T(8,128)(2,1)S(1)} copy-done((bf16[1,128,512]{2,1,0:T(8,128)(2,1)S(1)}, bf16[1,128,512]{2,1,0:T(8,128)(2,1)}, u32[]{:S(2)}) %copy-start.4) | copy-done | bytes 131096
  7.1 0.7 %copy-done.5 = f32[9,2,5,5]{0,1,3,2:T(2,128)S(1)} copy-done((f32[9,2,5,5]{0,1,3,2:T(2,128)S(1)}, f32[9,2,5,5]{0,1,3,2:T(2,128)}, u32[]{:S(2)}) %copy-start.5) | copy-done | bytes 1824
  7.9 0.7 %copy-done.6 = s32[2,256]{1,0:T(2,128)S(1)} copy-done((s32[2,256]{1,0:T(2,128)S(1)}, s32[2,256]{1,0:T(2,128)}, u32[]{:S(2)}) %copy-start.6) | copy-done | bytes 2072
  8.6 0.7 %copy-done.8 = f32[512]{0:T(512)S(1)} copy-done((f32[512]{0:T(512)S(1)}, f32[512]{0:T(512)}, u32[]{:S(2)}) %copy-start.8) | copy-done | bytes 2072
  9.2 2.8 %prepare.1 = (bf16[144,512]{1,0:T(8,128)(2,1)S(1)}, bf16[4,128,512]{2,1,0:T(8,128)(2,1)S(1)}, bf16[128,512]{1,0:T(8,128)(2,1)S(1)}, bf16[512,128]{1,0:T(8,128)(2...) custom-call(bf16[128,512]{1,0:T(8,128)(2,1)S(1)} %bitcast.9, ...), custom_call_target="tpu_custom_call" | custom-call | flops 3000000000 | bytes 12000000 | tf_op jit(solution)/shard_map/prepare/pallas_call | solution.py:382
  12.1 1.0 %collective-permute-start.2 = (bf16[400,512]{1,0:T(8,128)(2,1)S(1)}, bf16[400,512]{1,0:T(8,128)(2,1)S(1)}, u32[]{:S(2)}, u32[]{:S(2)}) collective-permute-start(bf16[400,512]{1,0:T(8,128)(2,1)S(1)} %pad_maximum_fusion), channel_id=1, source_target_pairs={{0,4},{8,12},{16,20},{24,28},{4,0},{12,8},{20,16},{28,24},{1,5},{9... | collective-permute-start | bytes 1228808 | tf_op jit(solution)/shard_map/ppermute | solution.py:369
  13.2 3.1 %collective-permute-start.3 = (bf16[128,512]{1,0:T(8,128)(2,1)S(1)}, bf16[128,512]{1,0:T(8,128)(2,1)S(1)}, u32[]{:S(2)}, u32[]{:S(2)}) collective-permute-start(bf16[128,512]{1,0:T(8,128)(2,1)S(1)} %bitcast.10), channel_id=1, source_target_pairs={{4,8},{12,16},{20,24},{8,4},{16,12},{24,20},{5,9},{13,17},{21,25},... | collective-permute-start | bytes 393224 | tf_op jit(solution)/shard_map/ppermute | solution.py:369
  16.3 2.4 %collective-permute-start.4 = (bf16[272,512]{1,0:T(8,128)(2,1)S(1)}, bf16[272,512]{1,0:T(8,128)(2,1)S(1)}, u32[]{:S(2)}, u32[]{:S(2)}) collective-permute-start(bf16[272,512]{1,0:T(8,128)(2,1)S(1)} %pad_maximum_fusion.1.both_ref), channel_id=1, source_target_pairs={{4,8},{12,16},{20,24},{8,4},{16,12},{24,20},{5,9},{13,17},{21,25},... | collective-permute-start | bytes 835592 | tf_op jit(solution)/shard_map/ppermute | solution.py:369
  18.8 0.7 %collective-permute-done.3.center_ref = bf16[128,512]{1,0:T(8,128)(2,1)S(1)} collective-permute-done((bf16[128,512]{1,0:T(8,128)(2,1)S(1)}, bf16[128,512]{1,0:T(8,128)(2,1)S(1)}, u32[]{:S(2)}, u32[]{:S(2)}) %collective-permute-start.3) | collective-permute-done | bytes 131104 | tf_op jit(solution)/shard_map/ppermute | solution.py:369
  19.5 2.3 %early.1 = (f32[4,8,512]{2,1,0:T(8,128)S(1)}, f32[4,144,512]{2,1,0:T(8,128)S(1)}) custom-call(s32[1,5]{1,0:T(1,128)S(1)} %copy-done.10, bf16[272,512]{1,0:T(8,128)(2,1)S(1)} %pad_maximum_fusion.1.both_ref, bf16[400,512]{1,0:T(8,128)(2,1)S(1)} %collective-permute-done.2.inner_ref, bf16[128,512]{1,0:T(8,128)(2,1)S(1)} %collective-permute-done.3.center_ref, ...), custom_call_target="tpu_custom_call" | custom-call | flops 3000000000 | bytes 6000000 | tf_op jit(solution)/shard_map/early/pallas_call | solution.py:415
  21.8 2.7 %collective-permute-done.4.corners_ref = bf16[272,512]{1,0:T(8,128)(2,1)S(1)} collective-permute-done((bf16[272,512]{1,0:T(8,128)(2,1)S(1)}, bf16[272,512]{1,0:T(8,128)(2,1)S(1)}, u32[]{:S(2)}, u32[]{:S(2)}) %collective-permute-start.4) | collective-permute-done | bytes 278560 | tf_op jit(solution)/shard_map/ppermute | solution.py:369
  24.5 3.3 %late.1 = (bf16[128,512]{1,0:T(8,128)(2,1)}, bf16[128,512]{1,0:T(8,128)(2,1)S(1)}, bf16[16,512]{1,0:T(8,128)(2,1)S(1)}, bf16[16,512]{1,0:T(8,128)(2,1)S(1)}) custom-call(s32[1,5]{1,0:T(1,128)S(1)} %copy-done.10, s32[2,256]{1,0:T(2,128)S(1)} %copy-done.7, bf16[272,512]{1,0:T(8,128)(2,1)S(1)} %pad_maximum_fusion.1.both_ref, ...), custom_call_target="tpu_custom_call" | custom-call | flops 3000000000 | bytes 6000000 | tf_op jit(solution)/shard_map/late/pallas_call | solution.py:431
  27.8 1.4 %collective-permute-start.5 = (bf16[16,512]{1,0:T(8,128)(2,1)S(1)}, bf16[16,512]{1,0:T(8,128)(2,1)S(1)}, u32[]{:S(2)}, u32[]{:S(2)}) collective-permute-start(bf16[16,512]{1,0:T(8,128)(2,1)S(1)} %get-tuple-element.28), channel_id=1, source_target_pairs={{0,1},{1,2},{2,3},{3,0},{4,5},{5,6},{6,7},{7,4},{8,9},{9,10},{10,1... | collective-permute-start | bytes 49160 | tf_op jit(solution)/shard_map/ppermute | solution.py:364
  29.2 1.3 %collective-permute-start.6 = (bf16[16,512]{1,0:T(8,128)(2,1)S(1)}, bf16[16,512]{1,0:T(8,128)(2,1)S(1)}, u32[]{:S(2)}, u32[]{:S(2)}) collective-permute-start(bf16[16,512]{1,0:T(8,128)(2,1)S(1)} %get-tuple-element.29), channel_id=1, source_target_pairs={{0,3},{1,0},{2,1},{3,2},{4,7},{5,4},{6,5},{7,6},{8,11},{9,8},{10,9... | collective-permute-start | bytes 49160 | tf_op jit(solution)/shard_map/ppermute | solution.py:364
  30.5 1.1 %collective-permute-done.5 = bf16[16,512]{1,0:T(8,128)(2,1)S(1)} collective-permute-done((bf16[16,512]{1,0:T(8,128)(2,1)S(1)}, bf16[16,512]{1,0:T(8,128)(2,1)S(1)}, u32[]{:S(2)}, u32[]{:S(2)}) %collective-permute-start.5) | collective-permute-done | bytes 16416 | tf_op jit(solution)/shard_map/ppermute | solution.py:364
  31.6 0.2 collective-permute-done.6
  31.9 4.0 %collective-permute-start.7 = (bf16[144,512]{1,0:T(8,128)(2,1)S(1)}, bf16[144,512]{1,0:T(8,128)(2,1)S(1)}, u32[]{:S(2)}, u32[]{:S(2)}) collective-permute-start(bf16[144,512]{1,0:T(8,128)(2,1)S(1)} %pad_maximum_fusion.2.latent_ref), channel_id=1, source_target_pairs={{4,8},{12,16},{20,24},{8,4},{16,12},{24,20},{5,9},{13,17},{21,25},... | collective-permute-start | bytes 442376 | tf_op jit(solution)/shard_map/ppermute | solution.py:369
  35.8 1.3 %own_band.1 = (f32[2,96,256]{2,1,0:T(8,128)S(1)}, bf16[2,2,5,256,256]{4,3,2,1,0:T(8,128)(2,1)S(1)}) custom-call(bf16[144,512]{1,0:T(8,128)(2,1)S(1)} %get-tuple-element.18.own_ref, bf16[400,512]{1,0:T(8,128)(2,1)S(1)} %collective-permute-done.2.inner_ref, bf16[272,512]{1,0:T(8,128)(2,1)S(1)} %collective-permute-done.4.corners_ref, ...), custom_call_target="tpu_custom_call" | custom-call | flops 1000000000 | bytes 2500000 | tf_op jit(solution)/shard_map/own_band/pallas_call | solution.py:452
  37.1 0.9 %inner_band.1.partial_ref = f32[2,96,256]{2,1,0:T(8,128)S(1)} custom-call(bf16[144,512]{1,0:T(8,128)(2,1)S(1)} %collective-permute-done.8.latent_ref, bf16[2,15,96,512]{3,2,1,0:T(8,128)(2,1)S(1)} %get-tuple-element.30.weights_ref, bf16[2,2,5,256,256]{4,3,2,1,0:T(8,128)(2,1)S(1)} %get-tuple-element.32.hot_ref, f32[2,96,256]{2,1,0:T(8,128)S(1)} %get-tuple-element.33.partial_ref), custom_call_target="tpu_custom_call" | custom-call | flops 1000000000 | bytes 2500000 | tf_op jit(solution)/shard_map/inner_band/pallas_call | solution.py:468
  38.1 0.6 %collective-permute-done.7.latent_ref = bf16[144,512]{1,0:T(8,128)(2,1)S(1)} collective-permute-done((bf16[144,512]{1,0:T(8,128)(2,1)S(1)}, bf16[144,512]{1,0:T(8,128)(2,1)S(1)}, u32[]{:S(2)}, u32[]{:S(2)}) %collective-permute-start.7) | collective-permute-done | bytes 147488 | tf_op jit(solution)/shard_map/ppermute | solution.py:369
  38.7 1.6 %outer_band.1 = bf16[84,2,256]{2,1,0:T(2,128)(2,1)} custom-call(bf16[144,512]{1,0:T(8,128)(2,1)S(1)} %collective-permute-done.7.latent_ref, bf16[2,15,96,512]{3,2,1,0:T(8,128)(2,1)S(1)} %get-tuple-element.30.weights_ref, bf16[2,2,5,256,256]{4,3,2,1,0:T(8,128)(2,1)S(1)} %get-tuple-element.32.hot_ref, f32[2,96,256]{2,1,0:T(8,128)S(1)} %inner_band.1.partial_ref), custom_call_target="tpu_custom_call" | custom-call | flops 1000000000 | bytes 2500000 | tf_op jit(solution)/shard_map/outer_band/pallas_call | solution.py:478
  (28 shorter events, 0.2 us)
Async XLA Ops:
  0.6 11.5 %collective-permute-start.1 = (bf16[128,512]{1,0:T(8,128)(2,1)}, bf16[128,512]{1,0:T(8,128)(2,1)S(1)}, u32[]{:S(2)}, u32[]{:S(2)}) collective-permute-start(bf16[128,512]{1,0:T(8,128)(2,1)} %bitcast.7), channel_id=1, source_target_pairs={{0,3},{1,0},{2,1},{3,2},{4,7},{5,4},{6,5},{7,6},{8,11},{9,8},{10,9... | collective-permute-start | bytes 393224 | tf_op jit(solution)/shard_map/ppermute | solution.py:364
  3.7 8.4 %collective-permute-start = (bf16[128,512]{1,0:T(8,128)(2,1)}, bf16[128,512]{1,0:T(8,128)(2,1)S(1)}, u32[]{:S(2)}, u32[]{:S(2)}) collective-permute-start(bf16[128,512]{1,0:T(8,128)(2,1)} %bitcast.8), channel_id=1, source_target_pairs={{0,1},{1,2},{2,3},{3,0},{4,5},{5,6},{6,7},{7,4},{8,9},{9,10},{10,1... | collective-permute-start | bytes 393224 | tf_op jit(solution)/shard_map/ppermute | solution.py:364
  3.7 1.4 %copy-start = (bf16[512,1536]{1,0:T(8,128)(2,1)S(1)}, bf16[512,1536]{1,0:T(8,128)(2,1)}, u32[]{:S(2)}) copy-start(bf16[512,1536]{1,0:T(8,128)(2,1)} %wqkv_hbm.1) | copy-start | bytes 4718596
  5.1 1.1 %copy-start.1 = (bf16[9,512,84]{1,2,0:T(8,128)(2,1)S(1)}, bf16[9,512,84]{1,2,0:T(8,128)(2,1)}, u32[]{:S(2)}) copy-start(bf16[9,512,84]{1,2,0:T(8,128)(2,1)} %param.17) | copy-start | bytes 2322436
  6.2 0.9 %copy-start.4 = (bf16[1,128,512]{2,1,0:T(8,128)(2,1)S(1)}, bf16[1,128,512]{2,1,0:T(8,128)(2,1)}, u32[]{:S(2)}) copy-start(bf16[1,128,512]{2,1,0:T(8,128)(2,1)} %param.9) | copy-start | bytes 393220
  7.1 0.7 %copy-start.5 = (f32[9,2,5,5]{0,1,3,2:T(2,128)S(1)}, f32[9,2,5,5]{0,1,3,2:T(2,128)}, u32[]{:S(2)}) copy-start(f32[9,2,5,5]{0,1,3,2:T(2,128)} %param.16) | copy-start | bytes 5404
  7.9 0.7 %copy-start.6 = (s32[2,256]{1,0:T(2,128)S(1)}, s32[2,256]{1,0:T(2,128)}, u32[]{:S(2)}) copy-start(s32[2,256]{1,0:T(2,128)} %assign_ref.1) | copy-start | bytes 6148
  8.6 0.7 %copy-start.8 = (f32[512]{0:T(512)S(1)}, f32[512]{0:T(512)}, u32[]{:S(2)}) copy-start(f32[512]{0:T(512)} %param.10) | copy-start | bytes 6148
  9.2 10.2 %copy-start.9 = (f32[512]{0:T(512)S(1)}, f32[512]{0:T(512)}, u32[]{:S(2)}) copy-start(f32[512]{0:T(512)} %param.10) | copy-start | bytes 6148
  9.2 10.2 %copy-start.10 = (s32[1,5]{1,0:T(1,128)S(1)}, s32[1,5]{1,0:T(1,128)}, u32[]{:S(2)}) copy-start(s32[1,5]{1,0:T(1,128)} %listed_ref.3) | copy-start | bytes 64
  12.1 7.3 %collective-permute-start.2 = (bf16[400,512]{1,0:T(8,128)(2,1)S(1)}, bf16[400,512]{1,0:T(8,128)(2,1)S(1)}, u32[]{:S(2)}, u32[]{:S(2)}) collective-permute-start(bf16[400,512]{1,0:T(8,128)(2,1)S(1)} %pad_maximum_fusion), channel_id=1, source_target_pairs={{0,4},{8,12},{16,20},{24,28},{4,0},{12,8},{20,16},{28,24},{1,5},{9... | collective-permute-start | bytes 1228808 | tf_op jit(solution)/shard_map/ppermute | solution.py:369
  13.2 6.3 %collective-permute-start.3 = (bf16[128,512]{1,0:T(8,128)(2,1)S(1)}, bf16[128,512]{1,0:T(8,128)(2,1)S(1)}, u32[]{:S(2)}, u32[]{:S(2)}) collective-permute-start(bf16[128,512]{1,0:T(8,128)(2,1)S(1)} %bitcast.10), channel_id=1, source_target_pairs={{4,8},{12,16},{20,24},{8,4},{16,12},{24,20},{5,9},{13,17},{21,25},... | collective-permute-start | bytes 393224 | tf_op jit(solution)/shard_map/ppermute | solution.py:369
  16.3 8.2 %collective-permute-start.4 = (bf16[272,512]{1,0:T(8,128)(2,1)S(1)}, bf16[272,512]{1,0:T(8,128)(2,1)S(1)}, u32[]{:S(2)}, u32[]{:S(2)}) collective-permute-start(bf16[272,512]{1,0:T(8,128)(2,1)S(1)} %pad_maximum_fusion.1.both_ref), channel_id=1, source_target_pairs={{4,8},{12,16},{20,24},{8,4},{16,12},{24,20},{5,9},{13,17},{21,25},... | collective-permute-start | bytes 835592 | tf_op jit(solution)/shard_map/ppermute | solution.py:369
  19.4 5.0 %copy-start.2 = (bf16[512,512]{1,0:T(8,128)(2,1)S(1)}, bf16[512,512]{1,0:T(8,128)(2,1)}, u32[]{:S(2)}) copy-start(bf16[512,512]{1,0:T(8,128)(2,1)} %wout_ref.1) | copy-start | bytes 1572868
  19.5 5.0 %copy-start.3 = (bf16[512,512]{1,0:T(8,128)(2,1)S(1)}, bf16[512,512]{1,0:T(8,128)(2,1)}, u32[]{:S(2)}) copy-start(bf16[512,512]{1,0:T(8,128)(2,1)} %wlat_ref.1) | copy-start | bytes 1572868
  19.5 5.0 %copy-start.7 = (s32[2,256]{1,0:T(2,128)S(1)}, s32[2,256]{1,0:T(2,128)}, u32[]{:S(2)}) copy-start(s32[2,256]{1,0:T(2,128)} %assign_ref.1) | copy-start | bytes 6148
  27.8 3.8 %collective-permute-start.5 = (bf16[16,512]{1,0:T(8,128)(2,1)S(1)}, bf16[16,512]{1,0:T(8,128)(2,1)S(1)}, u32[]{:S(2)}, u32[]{:S(2)}) collective-permute-start(bf16[16,512]{1,0:T(8,128)(2,1)S(1)} %get-tuple-element.28), channel_id=1, source_target_pairs={{0,1},{1,2},{2,3},{3,0},{4,5},{5,6},{6,7},{7,4},{8,9},{9,10},{10,1... | collective-permute-start | bytes 49160 | tf_op jit(solution)/shard_map/ppermute | solution.py:364
  29.2 2.6 %collective-permute-start.6 = (bf16[16,512]{1,0:T(8,128)(2,1)S(1)}, bf16[16,512]{1,0:T(8,128)(2,1)S(1)}, u32[]{:S(2)}, u32[]{:S(2)}) collective-permute-start(bf16[16,512]{1,0:T(8,128)(2,1)S(1)} %get-tuple-element.29), channel_id=1, source_target_pairs={{0,3},{1,0},{2,1},{3,2},{4,7},{5,4},{6,5},{7,6},{8,11},{9,8},{10,9... | collective-permute-start | bytes 49160 | tf_op jit(solution)/shard_map/ppermute | solution.py:364
  31.8 5.3 %collective-permute-start.8 = (bf16[144,512]{1,0:T(8,128)(2,1)S(1)}, bf16[144,512]{1,0:T(8,128)(2,1)S(1)}, u32[]{:S(2)}, u32[]{:S(2)}) collective-permute-start(bf16[144,512]{1,0:T(8,128)(2,1)S(1)} %pad_maximum_fusion.2.latent_ref), channel_id=1, source_target_pairs={{0,4},{8,12},{16,20},{24,28},{4,0},{12,8},{20,16},{28,24},{1,5},{9... | collective-permute-start | bytes 442376 | tf_op jit(solution)/shard_map/ppermute | solution.py:369
  31.9 6.8 %collective-permute-start.7 = (bf16[144,512]{1,0:T(8,128)(2,1)S(1)}, bf16[144,512]{1,0:T(8,128)(2,1)S(1)}, u32[]{:S(2)}, u32[]{:S(2)}) collective-permute-start(bf16[144,512]{1,0:T(8,128)(2,1)S(1)} %pad_maximum_fusion.2.latent_ref), channel_id=1, source_target_pairs={{4,8},{12,16},{20,24},{8,4},{16,12},{24,20},{5,9},{13,17},{21,25},... | collective-permute-start | bytes 442376 | tf_op jit(solution)/shard_map/ppermute | solution.py:369

commit v5 on v4

--- a/solution.py
+++ b/solution.py
@@ -407,11 +407,14 @@
         compiler_params=params(32),
         cost_estimate=cost(3e9, 1.2e7),
         name="prepare",
-    )(x, gain, w_qkv, assignment, taps, mixing)
+    )(*[pltpu.with_memory_space_constraint(a, pltpu.HBM) for a in (x, gain, w_qkv, assignment, taps, mixing)])
+    left, right, center = lax.optimization_barrier((left, right, center))
     both = jnp.concatenate([left, right, own[rows:]], axis=0)
     corners = exchanged(both, 1)
     inner = exchanged(jnp.concatenate([left, right, own], axis=0), 0)
 
+    listed = pltpu.with_memory_space_constraint(neighbours, pltpu.SMEM)
+    cells = pltpu.with_memory_space_constraint(assignment, pltpu.SMEM)
     top, summed = pl.pallas_call(
         functools.partial(early_kernel, sectors),
         in_specs=[whole(pltpu.SMEM)] + [whole()] * 9,
@@ -427,7 +430,7 @@
         compiler_params=params(32),
         cost_estimate=cost(3e9, 6e6),
         name="early",
-    )(neighbours, both, inner, center, gain, wk, wvt, query, key, value)
+    )(listed, both, inner, center, gain, wk, wvt, query, key, value)
     state, latent, west, east = pl.pallas_call(
         functools.partial(late_kernel, sectors),
         in_specs=[whole(pltpu.SMEM)] * 2 + [whole()] * 13,
@@ -438,7 +441,7 @@
         cost_estimate=cost(3e9, 6e6),
         name="late",
     )(
-        neighbours, assignment, both, inner, center, corners,
+        listed, cells, both, inner, center, corners,
         own, gain, wk, wvt, query, top, summed, w_out, w_latent,
     )
 

time: 40.6 us -> 38.6 us (0.951)
  local copies, waits for them, and re-layouts: 5.59 us -> 0.03 us
  starting transfers between devices: 16.3 us -> 18.7 us
  waiting for transfers between devices: 5.29 us -> 6.11 us
  Pallas kernels: 12.2 us -> 12.8 us
    unnamed x22 -> x10, local copies, waits for them, and re-layouts: 5.58 us -> 0.03 us
    ppermute x5, starting transfers between devices: 10.6 us -> 14.1 us  [exchanged(): return lax.ppermute(array, 'reg', pairs + [(j, i) for i, j in pairs])]
    ppermute x4, waiting for transfers between devices: 1.33 us -> 3.63 us  [shifted(): lax.ppermute(array, 'lon', [(i, (i + step) % sectors) for i in range(sect...]
    ppermute x5, waiting for transfers between devices: 3.96 us -> 2.48 us  [exchanged(): return lax.ppermute(array, 'reg', pairs + [(j, i) for i, j in pairs])]
    ppermute x4, starting transfers between devices: 5.71 us -> 4.59 us  [shifted(): lax.ppermute(array, 'lon', [(i, (i + step) % sectors) for i in range(sect...]
    pallas_call x1, Pallas kernels: 2.83 us -> 3.4 us  [shards(): pl.pallas_call(prepare_kernel, in_specs=[whole(pltpu.HBM)] * 6, out_specs...]
  transfers between devices with their start and end apart: 9 -> 9, of which waited for: 5 -> 5; matrix products, arithmetic and copies ran while one was open for 0% -> 0% of each run, Pallas kernels for 18% -> 20%
where the time goes in v5:
time: 38.6 us; the launch traced here: 38.4 us
  starting transfers between devices  18.7 us (48%)
  Pallas kernels  12.8 us (33%)
  waiting for transfers between devices  6.11 us (16%)
  between operations  0.81 us (2%)
    ppermute x5, starting transfers between devices, exchanged(): return lax.ppermute(array, 'reg', pairs + [(j, i) for i, j in pairs])  14.1 us
    ppermute x4, starting transfers between devices, shifted(): lax.ppermute(array, 'lon', [(i, (i + step) % sectors) for i in range(sect...  4.59 us
    ppermute x4, waiting for transfers between devices, shifted(): lax.ppermute(array, 'lon', [(i, (i + step) % sectors) for i in range(sect...  3.63 us
    pallas_call x1, Pallas kernels, shards(): pl.pallas_call(prepare_kernel, in_specs=[whole(pltpu.HBM)] * 6, out_specs...  3.4 us
    pallas_call x1, Pallas kernels, shards(): pl.pallas_call(functools.partial(late_kernel, sectors), in_specs=[whole(p...  3.3 us
    ppermute x5, waiting for transfers between devices, exchanged(): return lax.ppermute(array, 'reg', pairs + [(j, i) for i, j in pairs])  2.48 us
    pallas_call x1, Pallas kernels, shards(): pl.pallas_call(functools.partial(early_kernel, sectors), in_specs=[whole(...  2.26 us
    pallas_call x1, Pallas kernels, shards(): pl.pallas_call(functools.partial(band_kernel, False), in_specs=[whole()]...  1.61 us
  transfers between devices with their start and end apart: 9, of which 5 were waited for; matrix products, arithmetic and copies ran while one was open for 0% of the time, Pallas kernels for 20%

profile of v5, /device:TPU:1, one launch (start us, length us, event | category | flops | bytes accessed | tf_op | source)
XLA Modules:
  0.0 38.4 jit_solution(7255279257725809135)
XLA Ops:
  0.6 4.6 %collective-permute-start.2 = (bf16[128,512]{1,0:T(8,128)(2,1)}, bf16[128,512]{1,0:T(8,128)(2,1)S(1)}, u32[]{:S(2)}, u32[]{:S(2)}) collective-permute-start(bf16[128,512]{1,0:T(8,128)(2,1)} %bitcast.11), channel_id=1, source_target_pairs={{4,8},{12,16},{20,24},{8,4},{16,12},{24,20},{5,9},{13,17},{21,25},... | collective-permute-start | bytes 393224 | tf_op jit(solution)/shard_map/ppermute | solution.py:369
  5.2 2.2 %collective-permute-start.1 = (bf16[128,512]{1,0:T(8,128)(2,1)}, bf16[128,512]{1,0:T(8,128)(2,1)S(1)}, u32[]{:S(2)}, u32[]{:S(2)}) collective-permute-start(bf16[128,512]{1,0:T(8,128)(2,1)} %bitcast.12), channel_id=1, source_target_pairs={{0,3},{1,0},{2,1},{3,2},{4,7},{5,4},{6,5},{7,6},{8,11},{9,8},{10,9... | collective-permute-start | bytes 393224 | tf_op jit(solution)/shard_map/ppermute | solution.py:364
  7.5 0.0 collective-permute-start
  7.5 3.4 %prepare.1 = (bf16[144,512]{1,0:T(8,128)(2,1)S(1)}, bf16[4,128,512]{2,1,0:T(8,128)(2,1)S(1)}, bf16[128,512]{1,0:T(8,128)(2,1)S(1)}, bf16[512,128]{1,0:T(8,128)(2...) custom-call(bf16[128,512]{1,0:T(8,128)(2,1)} %bitcast.14, ...), custom_call_target="tpu_custom_call" | custom-call | flops 3000000000 | bytes 12000000 | tf_op jit(solution)/shard_map/prepare/pallas_call | solution.py:382
  10.9 0.0 collective-permute-done.2.center_ref
  10.9 2.2 %collective-permute-done = bf16[128,512]{1,0:T(8,128)(2,1)S(1)} collective-permute-done((bf16[128,512]{1,0:T(8,128)(2,1)}, bf16[128,512]{1,0:T(8,128)(2,1)S(1)}, u32[]{:S(2)}, u32[]{:S(2)}) %collective-permute-start) | collective-permute-done | bytes 131104 | tf_op jit(solution)/shard_map/ppermute | solution.py:364
  13.1 0.1 collective-permute-start.3
  13.2 4.3 %collective-permute-start.4 = (bf16[272,512]{1,0:T(8,128)(2,1)S(1)}, bf16[272,512]{1,0:T(8,128)(2,1)S(1)}, u32[]{:S(2)}, u32[]{:S(2)}) collective-permute-start(bf16[272,512]{1,0:T(8,128)(2,1)S(1)} %pad_maximum_fusion.1.both_ref), channel_id=1, source_target_pairs={{4,8},{12,16},{20,24},{8,4},{16,12},{24,20},{5,9},{13,17},{21,25},... | collective-permute-start | bytes 835592 | tf_op jit(solution)/shard_map/ppermute | solution.py:369
  17.5 0.0 copy-start
  17.5 0.0 copy-start.1
  17.6 0.0 copy-start.2
  17.6 2.3 %early.1 = (f32[4,8,512]{2,1,0:T(8,128)S(1)}, f32[4,144,512]{2,1,0:T(8,128)S(1)}) custom-call(s32[1,5]{1,0:T(1,128)S(1)} %copy-done.4, bf16[272,512]{1,0:T(8,128)(2,1)S(1)} %pad_maximum_fusion.1.both_ref, bf16[400,512]{1,0:T(8,128)(2,1)S(1)} %collective-permute-done.3.inner_ref, bf16[128,512]{1,0:T(8,128)(2,1)S(1)} %collective-permute-done.2.center_ref, ...), custom_call_target="tpu_custom_call" | custom-call | flops 3000000000 | bytes 6000000 | tf_op jit(solution)/shard_map/early/pallas_call | solution.py:418
  19.8 1.9 %collective-permute-done.4.corners_ref = bf16[272,512]{1,0:T(8,128)(2,1)S(1)} collective-permute-done((bf16[272,512]{1,0:T(8,128)(2,1)S(1)}, bf16[272,512]{1,0:T(8,128)(2,1)S(1)}, u32[]{:S(2)}, u32[]{:S(2)}) %collective-permute-start.4) | collective-permute-done | bytes 278560 | tf_op jit(solution)/shard_map/ppermute | solution.py:369
  21.7 3.3 %late.1 = (bf16[128,512]{1,0:T(8,128)(2,1)}, bf16[128,512]{1,0:T(8,128)(2,1)S(1)}, bf16[16,512]{1,0:T(8,128)(2,1)S(1)}, bf16[16,512]{1,0:T(8,128)(2,1)S(1)}) custom-call(s32[1,5]{1,0:T(1,128)S(1)} %copy-done.4, s32[2,256]{1,0:T(2,128)S(1)} %copy-done.2, bf16[272,512]{1,0:T(8,128)(2,1)S(1)} %pad_maximum_fusion.1.both_ref, ...), custom_call_target="tpu_custom_call" | custom-call | flops 3000000000 | bytes 6000000 | tf_op jit(solution)/shard_map/late/pallas_call | solution.py:434
  25.0 1.2 %collective-permute-start.5 = (bf16[16,512]{1,0:T(8,128)(2,1)S(1)}, bf16[16,512]{1,0:T(8,128)(2,1)S(1)}, u32[]{:S(2)}, u32[]{:S(2)}) collective-permute-start(bf16[16,512]{1,0:T(8,128)(2,1)S(1)} %get-tuple-element.34), channel_id=1, source_target_pairs={{0,1},{1,2},{2,3},{3,0},{4,5},{5,6},{6,7},{7,4},{8,9},{9,10},{10,1... | collective-permute-start | bytes 49160 | tf_op jit(solution)/shard_map/ppermute | solution.py:364
  26.3 1.1 %collective-permute-start.6 = (bf16[16,512]{1,0:T(8,128)(2,1)S(1)}, bf16[16,512]{1,0:T(8,128)(2,1)S(1)}, u32[]{:S(2)}, u32[]{:S(2)}) collective-permute-start(bf16[16,512]{1,0:T(8,128)(2,1)S(1)} %get-tuple-element.35), channel_id=1, source_target_pairs={{0,3},{1,0},{2,1},{3,2},{4,7},{5,4},{6,5},{7,6},{8,11},{9,8},{10,9... | collective-permute-start | bytes 49160 | tf_op jit(solution)/shard_map/ppermute | solution.py:364
  27.4 1.1 %collective-permute-done.5 = bf16[16,512]{1,0:T(8,128)(2,1)S(1)} collective-permute-done((bf16[16,512]{1,0:T(8,128)(2,1)S(1)}, bf16[16,512]{1,0:T(8,128)(2,1)S(1)}, u32[]{:S(2)}, u32[]{:S(2)}) %collective-permute-start.5) | collective-permute-done | bytes 16416 | tf_op jit(solution)/shard_map/ppermute | solution.py:364
  28.5 0.3 collective-permute-done.6
  28.9 0.1 collective-permute-start.8
  28.9 5.1 %collective-permute-start.7 = (bf16[144,512]{1,0:T(8,128)(2,1)S(1)}, bf16[144,512]{1,0:T(8,128)(2,1)S(1)}, u32[]{:S(2)}, u32[]{:S(2)}) collective-permute-start(bf16[144,512]{1,0:T(8,128)(2,1)S(1)} %pad_maximum_fusion.2.latent_ref), channel_id=1, source_target_pairs={{4,8},{12,16},{20,24},{8,4},{16,12},{24,20},{5,9},{13,17},{21,25},... | collective-permute-start | bytes 442376 | tf_op jit(solution)/shard_map/ppermute | solution.py:369
  34.0 1.3 %own_band.1 = (f32[2,96,256]{2,1,0:T(8,128)S(1)}, bf16[2,2,5,256,256]{4,3,2,1,0:T(8,128)(2,1)S(1)}) custom-call(bf16[144,512]{1,0:T(8,128)(2,1)S(1)} %get-tuple-element.23.own_ref, bf16[400,512]{1,0:T(8,128)(2,1)S(1)} %collective-permute-done.3.inner_ref, bf16[272,512]{1,0:T(8,128)(2,1)S(1)} %collective-permute-done.4.corners_ref, ...), custom_call_target="tpu_custom_call" | custom-call | flops 1000000000 | bytes 2500000 | tf_op jit(solution)/shard_map/own_band/pallas_call | solution.py:455
  35.3 0.9 %inner_band.1.partial_ref = f32[2,96,256]{2,1,0:T(8,128)S(1)} custom-call(bf16[144,512]{1,0:T(8,128)(2,1)S(1)} %collective-permute-done.8.latent_ref, bf16[2,15,96,512]{3,2,1,0:T(8,128)(2,1)S(1)} %get-tuple-element.36.weights_ref, bf16[2,2,5,256,256]{4,3,2,1,0:T(8,128)(2,1)S(1)} %get-tuple-element.38.hot_ref, f32[2,96,256]{2,1,0:T(8,128)S(1)} %get-tuple-element.39.partial_ref), custom_call_target="tpu_custom_call" | custom-call | flops 1000000000 | bytes 2500000 | tf_op jit(solution)/shard_map/inner_band/pallas_call | solution.py:471
  36.2 0.6 %collective-permute-done.7.latent_ref = bf16[144,512]{1,0:T(8,128)(2,1)S(1)} collective-permute-done((bf16[144,512]{1,0:T(8,128)(2,1)S(1)}, bf16[144,512]{1,0:T(8,128)(2,1)S(1)}, u32[]{:S(2)}, u32[]{:S(2)}) %collective-permute-start.7) | collective-permute-done | bytes 147488 | tf_op jit(solution)/shard_map/ppermute | solution.py:369
  36.8 1.6 %outer_band.1 = bf16[84,2,256]{2,1,0:T(2,128)(2,1)} custom-call(bf16[144,512]{1,0:T(8,128)(2,1)S(1)} %collective-permute-done.7.latent_ref, bf16[2,15,96,512]{3,2,1,0:T(8,128)(2,1)S(1)} %get-tuple-element.36.weights_ref, bf16[2,2,5,256,256]{4,3,2,1,0:T(8,128)(2,1)S(1)} %get-tuple-element.38.hot_ref, f32[2,96,256]{2,1,0:T(8,128)S(1)} %inner_band.1.partial_ref), custom_call_target="tpu_custom_call" | custom-call | flops 1000000000 | bytes 2500000 | tf_op jit(solution)/shard_map/outer_band/pallas_call | solution.py:481
  (16 shorter events, 0.1 us)
Async XLA Ops:
  0.6 10.2 %collective-permute-start.2 = (bf16[128,512]{1,0:T(8,128)(2,1)}, bf16[128,512]{1,0:T(8,128)(2,1)S(1)}, u32[]{:S(2)}, u32[]{:S(2)}) collective-permute-start(bf16[128,512]{1,0:T(8,128)(2,1)} %bitcast.11), channel_id=1, source_target_pairs={{4,8},{12,16},{20,24},{8,4},{16,12},{24,20},{5,9},{13,17},{21,25},... | collective-permute-start | bytes 393224 | tf_op jit(solution)/shard_map/ppermute | solution.py:369
  5.2 5.6 %collective-permute-start.1 = (bf16[128,512]{1,0:T(8,128)(2,1)}, bf16[128,512]{1,0:T(8,128)(2,1)S(1)}, u32[]{:S(2)}, u32[]{:S(2)}) collective-permute-start(bf16[128,512]{1,0:T(8,128)(2,1)} %bitcast.12), channel_id=1, source_target_pairs={{0,3},{1,0},{2,1},{3,2},{4,7},{5,4},{6,5},{7,6},{8,11},{9,8},{10,9... | collective-permute-start | bytes 393224 | tf_op jit(solution)/shard_map/ppermute | solution.py:364
  7.5 5.6 %collective-permute-start = (bf16[128,512]{1,0:T(8,128)(2,1)}, bf16[128,512]{1,0:T(8,128)(2,1)S(1)}, u32[]{:S(2)}, u32[]{:S(2)}) collective-permute-start(bf16[128,512]{1,0:T(8,128)(2,1)} %bitcast.13), channel_id=1, source_target_pairs={{0,1},{1,2},{2,3},{3,0},{4,5},{5,6},{6,7},{7,4},{8,9},{9,10},{10,1... | collective-permute-start | bytes 393224 | tf_op jit(solution)/shard_map/ppermute | solution.py:364
  7.5 10.1 %copy-start.3 = (f32[512]{0:T(512)S(1)}, f32[512]{0:T(512)}, u32[]{:S(2)}) copy-start(f32[512]{0:T(512)} %param.10) | copy-start | bytes 6148
  7.5 10.1 %copy-start.4 = (s32[1,5]{1,0:T(1,128)S(1)}, s32[1,5]{1,0:T(1,128)}, u32[]{:S(2)}) copy-start(s32[1,5]{1,0:T(1,128)} %listed_ref.3) | copy-start | bytes 64
  13.1 4.4 %collective-permute-start.3 = (bf16[400,512]{1,0:T(8,128)(2,1)S(1)}, bf16[400,512]{1,0:T(8,128)(2,1)S(1)}, u32[]{:S(2)}, u32[]{:S(2)}) collective-permute-start(bf16[400,512]{1,0:T(8,128)(2,1)S(1)} %pad_maximum_fusion), channel_id=1, source_target_pairs={{0,4},{8,12},{16,20},{24,28},{4,0},{12,8},{20,16},{28,24},{1,5},{9... | collective-permute-start | bytes 1228808 | tf_op jit(solution)/shard_map/ppermute | solution.py:369
  13.2 8.5 %collective-permute-start.4 = (bf16[272,512]{1,0:T(8,128)(2,1)S(1)}, bf16[272,512]{1,0:T(8,128)(2,1)S(1)}, u32[]{:S(2)}, u32[]{:S(2)}) collective-permute-start(bf16[272,512]{1,0:T(8,128)(2,1)S(1)} %pad_maximum_fusion.1.both_ref), channel_id=1, source_target_pairs={{4,8},{12,16},{20,24},{8,4},{16,12},{24,20},{5,9},{13,17},{21,25},... | collective-permute-start | bytes 835592 | tf_op jit(solution)/shard_map/ppermute | solution.py:369
  17.5 4.2 %copy-start = (bf16[512,512]{1,0:T(8,128)(2,1)S(1)}, bf16[512,512]{1,0:T(8,128)(2,1)}, u32[]{:S(2)}) copy-start(bf16[512,512]{1,0:T(8,128)(2,1)} %wout_ref.1) | copy-start | bytes 1572868
  17.5 4.2 %copy-start.1 = (bf16[512,512]{1,0:T(8,128)(2,1)S(1)}, bf16[512,512]{1,0:T(8,128)(2,1)}, u32[]{:S(2)}) copy-start(bf16[512,512]{1,0:T(8,128)(2,1)} %wlat_ref.1) | copy-start | bytes 1572868
  17.6 4.2 %copy-start.2 = (s32[2,256]{1,0:T(2,128)S(1)}, s32[2,256]{1,0:T(2,128)}, u32[]{:S(2)}) copy-start(s32[2,256]{1,0:T(2,128)} %assign_ref.1) | copy-start | bytes 6148
  25.0 3.5 %collective-permute-start.5 = (bf16[16,512]{1,0:T(8,128)(2,1)S(1)}, bf16[16,512]{1,0:T(8,128)(2,1)S(1)}, u32[]{:S(2)}, u32[]{:S(2)}) collective-permute-start(bf16[16,512]{1,0:T(8,128)(2,1)S(1)} %get-tuple-element.34), channel_id=1, source_target_pairs={{0,1},{1,2},{2,3},{3,0},{4,5},{5,6},{6,7},{7,4},{8,9},{9,10},{10,1... | collective-permute-start | bytes 49160 | tf_op jit(solution)/shard_map/ppermute | solution.py:364
  26.3 2.6 %collective-permute-start.6 = (bf16[16,512]{1,0:T(8,128)(2,1)S(1)}, bf16[16,512]{1,0:T(8,128)(2,1)S(1)}, u32[]{:S(2)}, u32[]{:S(2)}) collective-permute-start(bf16[16,512]{1,0:T(8,128)(2,1)S(1)} %get-tuple-element.35), channel_id=1, source_target_pairs={{0,3},{1,0},{2,1},{3,2},{4,7},{5,4},{6,5},{7,6},{8,11},{9,8},{10,9... | collective-permute-start | bytes 49160 | tf_op jit(solution)/shard_map/ppermute | solution.py:364
  28.9 6.4 %collective-permute-start.8 = (bf16[144,512]{1,0:T(8,128)(2,1)S(1)}, bf16[144,512]{1,0:T(8,128)(2,1)S(1)}, u32[]{:S(2)}, u32[]{:S(2)}) collective-permute-start(bf16[144,512]{1,0:T(8,128)(2,1)S(1)} %pad_maximum_fusion.2.latent_ref), channel_id=1, source_target_pairs={{0,4},{8,12},{16,20},{24,28},{4,0},{12,8},{20,16},{28,24},{1,5},{9... | collective-permute-start | bytes 442376 | tf_op jit(solution)/shard_map/ppermute | solution.py:369
  28.9 7.9 %collective-permute-start.7 = (bf16[144,512]{1,0:T(8,128)(2,1)S(1)}, bf16[144,512]{1,0:T(8,128)(2,1)S(1)}, u32[]{:S(2)}, u32[]{:S(2)}) collective-permute-start(bf16[144,512]{1,0:T(8,128)(2,1)S(1)} %pad_maximum_fusion.2.latent_ref), channel_id=1, source_target_pairs={{4,8},{12,16},{20,24},{8,4},{16,12},{24,20},{5,9},{13,17},{21,25},... | collective-permute-start | bytes 442376 | tf_op jit(solution)/shard_map/ppermute | solution.py:369

commit v6 on v4

--- a/solution.py
+++ b/solution.py
@@ -15,6 +15,7 @@
 ROWS = 16
 LANES = 128
 EARLY = 2
+CANDIDATES = 8
 F32 = jnp.float32
 BF16 = jnp.bfloat16
 NT = (((1,), (1,)), ((), ()))
@@ -44,40 +45,14 @@
     return (center * lax.rsqrt(spread + 1e-05) * gain).astype(BF16)
 
 
-def prepare_kernel(
-    x_hbm, gain_hbm, wqkv_hbm, assign_hbm, psi_hbm, dec_hbm,
-    own_ref, query_ref, key_ref, value_ref, wk_ref, wvt_ref, middle_ref, edges_ref,
-    x_ref, gain_ref, wqkv_ref, assign_ref, psi_ref, dec_ref, psi_rows_ref, taps_ref, sems,
-):
+def mix_kernel(psi_hbm, dec_hbm, middle_ref, edges_ref, psi_ref, dec_ref, psi_rows_ref, taps_ref, sems):
     copies = [
-        pltpu.make_async_copy(source, target, sems.at[at])
-        for at, (source, target) in enumerate(
-            (
-                (assign_hbm, assign_ref),
-                (x_hbm, x_ref),
-                (gain_hbm, gain_ref),
-                (psi_hbm, psi_ref),
-                (dec_hbm, dec_ref),
-                (wqkv_hbm, wqkv_ref),
-            )
-        )
+        pltpu.make_async_copy(psi_hbm, psi_ref, sems.at[0]),
+        pltpu.make_async_copy(dec_hbm, dec_ref, sems.at[1]),
     ]
     for copy in copies:
         copy.start()
-    rows, width = x_ref.shape
-    group, members = query_ref.shape[1], query_ref.shape[2] // rows
-    head = group // members
     copies[0].wait()
-    local = lax.rem(assign_ref[...], rows).astype(F32)
-    line = jnp.concatenate([local[:1], local[1:2]], axis=1)
-    line = jnp.broadcast_to(line, (ROWS, line.shape[1]))
-    own_ref[rows:] = jnp.where(iota(line.shape, 0) == 0, line, 0.0).astype(BF16)
-    copies[1].wait()
-    own_ref[:rows] = x_ref[...]
-    copies[2].wait()
-    normed = normalise(x_ref[...], gain_ref[...])
-
-    copies[3].wait()
     basis, out_ch, channels = dec_ref.shape
     depth = basis * ROWS
     for tap in range(TAPS):
@@ -91,7 +66,7 @@
         source = (tap * TAPS + off) * 2 + out_row
         taps = jnp.broadcast_to(expanded[source : source + 1], (ROWS, depth))
         taps_ref[at * ROWS : (at + 1) * ROWS, :] = jnp.where(pick, taps, 0.0).astype(BF16)
-    copies[4].wait()
+    copies[1].wait()
     inside = middle_ref.shape[0]
     outside = edges_ref.shape[1]
     for first in range(0, out_ch, ROWS):
@@ -108,7 +83,73 @@
         edges_ref[0, :, first : first + ROWS, :] = mixed[inside : inside + outside]
         edges_ref[1, :, first : first + ROWS, :] = mixed[inside + outside :]
 
-    copies[5].wait()
+
+def listed_blocks(sectors, listed_ref):
+    reg_here, lon_here = lax.axis_index("reg"), lax.axis_index("lon")
+    toward = 1 - 2 * (reg_here % 2)
+    found = []
+    for at in range(1, listed_ref.shape[1]):
+        block = listed_ref[0, at]
+        step_reg = (block // sectors - reg_here) * toward
+        step_lon = (block % sectors - lon_here + 1 + sectors) % sectors - 1
+        place = jnp.where(step_lon == 0, 2, jnp.where(step_lon < 0, 0, 1))
+        outer = jnp.where(step_lon == 0, 5, 6 + place)
+        found.append(jnp.where(step_reg == 0, place, jnp.where(step_reg > 0, 2 + place, outer)))
+    for low in range(len(found)):
+        for high in range(low + 1, len(found)):
+            less, more = jnp.minimum(found[low], found[high]), jnp.maximum(found[low], found[high])
+            found[low], found[high] = less, more
+    return found
+
+
+def prepare_kernel(
+    sectors,
+    x_hbm, gain_hbm, wqkv_hbm, assign_hbm, listed_hbm,
+    own_ref, query_ref, key_ref, value_ref, wk_ref, wvt_ref, choice_ref, cells_ref,
+    x_ref, gain_ref, wqkv_ref, assign_ref, cell_ref, listed_ref, sems,
+):
+    copies = [
+        pltpu.make_async_copy(source, target, sems.at[at])
+        for at, (source, target) in enumerate(
+            (
+                (x_hbm, x_ref),
+                (gain_hbm, gain_ref),
+                (wqkv_hbm, wqkv_ref),
+                (assign_hbm, assign_ref),
+                (assign_hbm, cell_ref),
+                (listed_hbm, listed_ref),
+            )
+        )
+    ]
+    for copy in copies:
+        copy.start()
+    rows, width = x_ref.shape
+    group, members = query_ref.shape[1], query_ref.shape[2] // rows
+    head = group // members
+    for copy in copies[3:]:
+        copy.wait()
+    local = lax.rem(assign_ref[...], rows).astype(F32)
+    line = jnp.concatenate([local[:1], local[1:2]], axis=1)
+    line = jnp.broadcast_to(line, (ROWS, line.shape[1]))
+    own_ref[rows:] = jnp.where(iota(line.shape, 0) == 0, line, 0.0).astype(BF16)
+    for at, number in enumerate(listed_blocks(sectors, listed_ref)):
+        for candidate in range(CANDIDATES):
+            same = jnp.full((ROWS, LANES), jnp.where(number == candidate, 1.0, 0.0), F32)
+            choice_ref[at, candidate] = same.astype(BF16)
+    lat_rows, lon_cols = cell_ref.shape
+    place, node = iota((ROWS, rows), 0), iota((ROWS, rows), 1)
+    for side, first in enumerate((0, lon_cols - REACH)):
+        hit = jnp.zeros((ROWS, rows), F32)
+        for row in range(lat_rows):
+            for col in range(REACH):
+                cell = cell_ref[row, first + col] % rows
+                hit = jnp.where((place == row * REACH + col) & (node == cell), 1.0, hit)
+        cells_ref[side * ROWS : (side + 1) * ROWS] = hit.astype(BF16)
+    copies[0].wait()
+    own_ref[:rows] = x_ref[...]
+    copies[1].wait()
+    normed = normalise(x_ref[...], gain_ref[...])
+    copies[2].wait()
     query = jnp.dot(normed, wqkv_ref[:, :width], preferred_element_type=F32)
     query_t = (query * (math.log2(math.e) / head**0.5)).T.astype(BF16)
     mask = (iota((group, members * rows), 0) // head) == (iota((group, members * rows), 1) // rows)
@@ -124,34 +165,21 @@
     value_ref[...] = lax.dot_general(wvt, normed, NT, preferred_element_type=F32).astype(BF16)
 
 
-def listed_blocks(sectors, listed_ref):
-    reg_here, lon_here = lax.axis_index("reg"), lax.axis_index("lon")
-    toward = 1 - 2 * (reg_here % 2)
-    found = []
-    for at in range(1, listed_ref.shape[1]):
-        block = listed_ref[0, at]
-        step_reg = (block // sectors - reg_here) * toward
-        step_lon = (block % sectors - lon_here + 1 + sectors) % sectors - 1
-        place = jnp.where(step_lon == 0, 2, jnp.where(step_lon < 0, 0, 1))
-        late = ((step_reg < 0) & (step_lon != 0)).astype(jnp.int32)
-        found.append(late * 16 + (step_reg + 1) * 4 + place)
-    for low in range(len(found)):
-        for high in range(low + 1, len(found)):
-            less, more = jnp.minimum(found[low], found[high]), jnp.maximum(found[low], found[high])
-            found[low], found[high] = less, more
-    return [(code % 16 // 4 - 1, code % 4) for code in found]
-
-
-def chosen(blocks, rows, both_ref, inner_ref, center_ref, corners_ref):
+def chosen(entries, rows, choice_ref, both_ref, inner_ref, center_ref, corners_ref):
+    candidates = [both_ref[:rows], both_ref[rows : 2 * rows]]
+    candidates += [inner_ref[at * rows : (at + 1) * rows] for at in range(3)]
+    candidates.append(center_ref[...])
+    if corners_ref is not None:
+        candidates += [corners_ref[:rows], corners_ref[rows : 2 * rows]]
+    tall, wide = rows // ROWS, center_ref.shape[1] // LANES
     near = []
-    for step, place in blocks:
-        side = pl.ds(pl.multiple_of(jnp.minimum(place, 1) * rows, rows), rows)
-        span = pl.ds(pl.multiple_of(place * rows, rows), rows)
-        outer = center_ref[...]
-        if corners_ref is not None:
-            outer = jnp.where(place == 2, outer, corners_ref[side, :])
-        other = jnp.where(step > 0, inner_ref[span, :], outer)
-        near.append(jnp.where(step == 0, both_ref[side, :], other))
+    for entry in entries:
+        total = None
+        for at, candidate in enumerate(candidates):
+            weight = jnp.concatenate([choice_ref[entry, at]] * wide, axis=1)
+            part = candidate * jnp.concatenate([weight] * tall, axis=0)
+            total = part if total is None else total + part
+        near.append(total)
     return jnp.concatenate(near, axis=0)
 
 
@@ -163,15 +191,13 @@
 
 
 def early_kernel(
-    sectors,
-    listed_ref, both_ref, inner_ref, center_ref,
+    choice_ref, both_ref, inner_ref, center_ref,
     gain_ref, wk_ref, wvt_ref, query_ref, key_ref, value_ref,
     top_ref, sum_ref, keys_ref, values_ref,
 ):
     rows = key_ref.shape[0]
     parts, group, _ = query_ref.shape
-    blocks = listed_blocks(sectors, listed_ref)[:EARLY]
-    nodes = chosen(blocks, rows, both_ref, inner_ref, center_ref, None)
+    nodes = chosen(range(EARLY), rows, choice_ref, both_ref, inner_ref, center_ref, None)
     keys, values = project(nodes, gain_ref[...], wk_ref, wvt_ref)
     keys_ref[:rows] = key_ref[...]
     keys_ref[rows:] = keys
@@ -197,8 +223,7 @@
 
 
 def late_kernel(
-    sectors,
-    listed_ref, assign_ref, both_ref, inner_ref, center_ref, corners_ref,
+    choice_ref, cells_ref, both_ref, inner_ref, center_ref, corners_ref,
     own_ref, gain_ref, wk_ref, wvt_ref, query_ref, top_ref, sum_ref, wout_ref, wlat_ref,
     state_ref, latent_ref, west_ref, east_ref,
     attended_ref,
@@ -207,10 +232,10 @@
     parts, group, lanes = query_ref.shape
     members = lanes // rows
     head = group // members
-    blocks = listed_blocks(sectors, listed_ref)[EARLY:]
-    nodes = chosen(blocks, rows, both_ref, inner_ref, center_ref, corners_ref)
+    entries = range(EARLY, choice_ref.shape[0])
+    nodes = chosen(entries, rows, choice_ref, both_ref, inner_ref, center_ref, corners_ref)
     keys, values = project(nodes, gain_ref[...], wk_ref, wvt_ref)
-    ones = jnp.ones((ROWS, len(blocks) * rows), BF16)
+    ones = jnp.ones((ROWS, nodes.shape[0]), BF16)
     owner = iota((group, rows), 0) // head
 
     def scored(part):
@@ -242,16 +267,9 @@
     value = jnp.dot(state, wlat_ref[...], preferred_element_type=F32)
     latent = (value / (1.0 + jnp.exp(-value))).astype(BF16)
     latent_ref[...] = latent
-    lat_rows, lon_cols = assign_ref.shape
-    for ref, first in ((west_ref, 0), (east_ref, lon_cols - REACH)):
-        cells = ref.shape[0]
-        line, node = iota((cells, rows), 0), iota((cells, rows), 1)
-        hit = jnp.zeros((cells, rows), F32)
-        for row in range(lat_rows):
-            for col in range(REACH):
-                local = assign_ref[row, first + col] % rows
-                hit = jnp.where((line == row * REACH + col) & (node == local), 1.0, hit)
-        ref[...] = jnp.dot(hit.astype(BF16), latent, preferred_element_type=F32).astype(BF16)
+    cells = jnp.dot(cells_ref[...], latent, preferred_element_type=F32).astype(BF16)
+    west_ref[...] = cells[:ROWS]
+    east_ref[...] = cells[ROWS:]
 
 
 def hot_rows(values, rows, cols, line):
@@ -283,8 +301,10 @@
 
 
 def own_kernel(
-    begin, own_ref, inner_ref, corners_ref, latent_ref, weights_ref, out_ref, hot_ref
+    begin, state_ref, own_ref, inner_ref, corners_ref, latent_ref, weights_ref,
+    out_ref, hot_ref, kept_ref,
 ):
+    kept_ref[...] = state_ref[...]
     cols = out_ref.shape[2]
     rows = latent_ref.shape[0] - 2 * SIDE
     own = lines_of(own_ref, begin[0], cols)
@@ -368,9 +388,12 @@
         pairs = [(i, i + 1) for i in range(first, size - 1, 2)]
         return lax.ppermute(array, "reg", pairs + [(j, i) for i, j in pairs])
 
+    def in_hbm(*arrays):
+        return [pltpu.with_memory_space_constraint(array, pltpu.HBM) for array in arrays]
+
+    center = exchanged(x, 1)
     left = shifted(x, 1)
     right = shifted(x, -1)
-    center = exchanged(x, 1)
 
     outputs = -(-out_ch // ROWS) * ROWS
     head = width // HEADS
@@ -379,9 +402,9 @@
     inside, outside = len(blocks_of(OWN)), len(blocks_of(ABOVE))
     taps = psi.transpose(2, 3, 1, 0)
     mixing = w_dec.transpose(0, 2, 1)
-    own, query, key, value, wk, wvt, middle, edges = pl.pallas_call(
-        prepare_kernel,
-        in_specs=[whole(pltpu.HBM)] * 6,
+    own, query, key, value, wk, wvt, choice, cells = pl.pallas_call(
+        functools.partial(prepare_kernel, sectors),
+        in_specs=[whole(pltpu.HBM)] * 5,
         out_specs=[whole()] * 8,
         out_shape=[
             struct(rows + ROWS, width),
@@ -390,31 +413,31 @@
             struct(width, rows),
             struct(width, width),
             struct(width, width),
-            struct(inside, outputs, channels),
-            struct(2, outside, outputs, channels),
+            struct(count - 1, CANDIDATES, ROWS, LANES),
+            struct(2 * ROWS, rows),
         ],
         scratch_shapes=[
             pltpu.VMEM((rows, width), BF16),
             pltpu.VMEM((1, width), F32),
             pltpu.VMEM(w_qkv.shape, BF16),
             pltpu.VMEM(assignment.shape, jnp.int32),
-            pltpu.VMEM(taps.shape, F32),
-            pltpu.VMEM(mixing.shape, BF16),
-            pltpu.VMEM((2 * TAPS * TAPS, basis), F32),
-            pltpu.VMEM(((inside + 2 * outside) * ROWS, basis * ROWS), BF16),
+            pltpu.SMEM(assignment.shape, jnp.int32),
+            pltpu.SMEM(neighbours.shape, jnp.int32),
             pltpu.SemaphoreType.DMA((6,)),
         ],
         compiler_params=params(32),
-        cost_estimate=cost(3e9, 1.2e7),
+        cost_estimate=cost(2e9, 5e6),
         name="prepare",
-    )(x, gain, w_qkv, assignment, taps, mixing)
+    )(*in_hbm(x, gain, w_qkv, assignment, neighbours))
+    center, left = lax.optimization_barrier((center, left))
+    center, right = lax.optimization_barrier((center, right))
     both = jnp.concatenate([left, right, own[rows:]], axis=0)
     corners = exchanged(both, 1)
     inner = exchanged(jnp.concatenate([left, right, own], axis=0), 0)
 
     top, summed = pl.pallas_call(
-        functools.partial(early_kernel, sectors),
-        in_specs=[whole(pltpu.SMEM)] + [whole()] * 9,
+        early_kernel,
+        in_specs=[whole()] * 10,
         out_specs=[whole()] * 2,
         out_shape=[
             struct(parts, 8, members * rows, dtype=F32),
@@ -427,18 +450,37 @@
         compiler_params=params(32),
         cost_estimate=cost(3e9, 6e6),
         name="early",
-    )(neighbours, both, inner, center, gain, wk, wvt, query, key, value)
+    )(choice, both, inner, center, gain, wk, wvt, query, key, value)
+    taps, mixing, top = lax.optimization_barrier((taps, mixing, top))
+    middle, edges = pl.pallas_call(
+        mix_kernel,
+        in_specs=[whole(pltpu.HBM)] * 2,
+        out_specs=[whole()] * 2,
+        out_shape=[struct(inside, outputs, channels), struct(2, outside, outputs, channels)],
+        scratch_shapes=[
+            pltpu.VMEM(taps.shape, F32),
+            pltpu.VMEM(mixing.shape, BF16),
+            pltpu.VMEM((2 * TAPS * TAPS, basis), F32),
+            pltpu.VMEM(((inside + 2 * outside) * ROWS, basis * ROWS), BF16),
+            pltpu.SemaphoreType.DMA((2,)),
+        ],
+        compiler_params=params(32),
+        cost_estimate=cost(2e9, 5e6),
+        name="mix",
+    )(*in_hbm(taps, mixing))
+    top, middle = lax.optimization_barrier((top, middle))
     state, latent, west, east = pl.pallas_call(
-        functools.partial(late_kernel, sectors),
-        in_specs=[whole(pltpu.SMEM)] * 2 + [whole()] * 13,
+        late_kernel,
+        in_specs=[whole()] * 15,
         out_specs=[whole()] * 4,
-        out_shape=[struct(rows, width), struct(rows, channels)] + [struct(ROWS, channels)] * 2,
+        out_shape=[pltpu.VMEM((rows, width), BF16), struct(rows, channels)]
+        + [struct(ROWS, channels)] * 2,
         scratch_shapes=[pltpu.VMEM((rows, width), BF16)],
         compiler_params=params(32),
         cost_estimate=cost(3e9, 6e6),
         name="late",
     )(
-        neighbours, assignment, both, inner, center, corners,
+        choice, cells, both, inner, center, corners,
         own, gain, wk, wvt, query, top, summed, w_out, w_latent,
     )
 
@@ -449,18 +491,19 @@
     near = exchanged(extended, 0)
 
     lanes = -(-(rows + 2 * SIDE) // 256) * 256
-    partial, hots = pl.pallas_call(
+    partial, hots, state = pl.pallas_call(
         functools.partial(own_kernel, (rows, 3 * rows, 2 * rows)),
-        in_specs=[whole()] * 5,
-        out_specs=[whole()] * 2,
+        in_specs=[whole()] * 6,
+        out_specs=[whole()] * 3,
         out_shape=[
             struct(lat_rows, outputs, lon_cols, dtype=F32),
             struct(2, 2, TAPS, lanes, lon_cols),
+            struct(rows, width),
         ],
         compiler_params=params(32),
         cost_estimate=cost(1e9, 2.5e6),
         name="own_band",
-    )(own, inner, corners, extended, middle)
+    )(state, own, inner, corners, extended, middle)
     band_scratch = [
         pltpu.VMEM((outputs, TAPS * lanes), BF16),
         pltpu.VMEM((2 * outputs, TAPS * lanes), BF16),

time: 40.6 us -> 35 us (0.86)
  local copies, waits for them, and re-layouts: 5.59 us -> 0.02 us
  waiting for transfers between devices: 5.29 us -> 2.77 us
  starting transfers between devices: 16.3 us -> 18.1 us
  Pallas kernels: 12.2 us -> 13.1 us
    unnamed x22 -> x6, local copies, waits for them, and re-layouts: 5.58 us -> 0.02 us
    ppermute x5, waiting for transfers between devices: 3.96 us -> 1.02 us  [exchanged(): return lax.ppermute(array, 'reg', pairs + [(j, i) for i, j in pairs])]
    ppermute x5, starting transfers between devices: 10.6 us -> 12.7 us  [exchanged(): return lax.ppermute(array, 'reg', pairs + [(j, i) for i, j in pairs])]
    pallas_call x1, Pallas kernels: 1.28 us -> 1.8 us  [shards(): pl.pallas_call(functools.partial(own_kernel, (rows, 3 * rows, 2 * rows)),...]
    ppermute x4, waiting for transfers between devices: 1.33 us -> 1.74 us  [shifted(): lax.ppermute(array, 'lon', [(i, (i + step) % sectors) for i in range(sect...]
    pallas_call x3 -> x4, Pallas kernels: 8.41 us -> 8.77 us  [the longest x1 2.69 us: shards(): pl.pallas_call(mix_kernel, in_specs=[whole(pltpu.HBM)] * 2, out_specs=[wh...]
  transfers between devices with their start and end apart: 9 -> 9, of which waited for: 5 -> 6; matrix products, arithmetic and copies ran while one was open for 0% -> 0% of each run, Pallas kernels for 18% -> 27%
where the time goes in v6:
time: 35 us; the launch traced here: 34.8 us
  starting transfers between devices  18.1 us (52%)
  Pallas kernels  13.1 us (37%)
  waiting for transfers between devices  2.77 us (8%)
  between operations  0.75 us (2%)
    ppermute x5, starting transfers between devices, exchanged(): return lax.ppermute(array, 'reg', pairs + [(j, i) for i, j in pairs])  12.7 us
    ppermute x4, starting transfers between devices, shifted(): lax.ppermute(array, 'lon', [(i, (i + step) % sectors) for i in range(sect...  5.42 us
    pallas_call x1, Pallas kernels, shards(): pl.pallas_call(mix_kernel, in_specs=[whole(pltpu.HBM)] * 2, out_specs=[wh...  2.69 us
    pallas_call x1, Pallas kernels, shards(): pl.pallas_call(functools.partial(prepare_kernel, sectors), in_specs=[whol...  2.2 us
    pallas_call x1, Pallas kernels, shards(): pl.pallas_call(late_kernel, in_specs=[whole()] * 15, out_specs=[whole()]...  2.2 us
    pallas_call x1, Pallas kernels, shards(): pl.pallas_call(functools.partial(own_kernel, (rows, 3 * rows, 2 * rows)),...  1.8 us
    ppermute x4, waiting for transfers between devices, shifted(): lax.ppermute(array, 'lon', [(i, (i + step) % sectors) for i in range(sect...  1.74 us
    pallas_call x1, Pallas kernels, shards(): pl.pallas_call(early_kernel, in_specs=[whole()] * 10, out_specs=[whole()]...  1.68 us
  transfers between devices with their start and end apart: 9, of which 6 were waited for; matrix products, arithmetic and copies ran while one was open for 0% of the time, Pallas kernels for 27%

profile of v6, /device:TPU:1, one launch (start us, length us, event | category | flops | bytes accessed | tf_op | source)
XLA Modules:
  0.0 34.8 jit_solution(56629965936298958)
XLA Ops:
  0.6 3.0 %collective-permute-start.2 = (bf16[128,512]{1,0:T(8,128)(2,1)}, bf16[128,512]{1,0:T(8,128)(2,1)S(1)}, u32[]{:S(2)}, u32[]{:S(2)}) collective-permute-start(bf16[128,512]{1,0:T(8,128)(2,1)} %bitcast.11), channel_id=1, source_target_pairs={{0,3},{1,0},{2,1},{3,2},{4,7},{5,4},{6,5},{7,6},{8,11},{9,8},{10,9... | collective-permute-start | bytes 393224 | tf_op jit(solution)/shard_map/ppermute | solution.py:384
  3.7 4.0 %collective-permute-start = (bf16[128,512]{1,0:T(8,128)(2,1)}, bf16[128,512]{1,0:T(8,128)(2,1)S(1)}, u32[]{:S(2)}, u32[]{:S(2)}) collective-permute-start(bf16[128,512]{1,0:T(8,128)(2,1)} %bitcast.13), channel_id=1, source_target_pairs={{4,8},{12,16},{20,24},{8,4},{16,12},{24,20},{5,9},{13,17},{21,25},... | collective-permute-start | bytes 393224 | tf_op jit(solution)/shard_map/ppermute | solution.py:389
  7.7 2.2 %prepare.1 = (bf16[144,512]{1,0:T(8,128)(2,1)S(1)}, bf16[4,128,512]{2,1,0:T(8,128)(2,1)S(1)}, bf16[128,512]{1,0:T(8,128)(2,1)S(1)}, bf16[512,128]{1,0:T(8,128)(2...) custom-call(bf16[128,512]{1,0:T(8,128)(2,1)} %bitcast.14, ...), custom_call_target="tpu_custom_call" | custom-call | flops 2000000000 | bytes 5000000 | tf_op jit(solution)/shard_map/prepare/pallas_call | solution.py:405
  9.9 0.3 collective-permute-done.1
  10.2 0.6 %collective-permute-done.center_ref = bf16[128,512]{1,0:T(8,128)(2,1)S(1)} collective-permute-done((bf16[128,512]{1,0:T(8,128)(2,1)}, bf16[128,512]{1,0:T(8,128)(2,1)S(1)}, u32[]{:S(2)}, u32[]{:S(2)}) %collective-permute-start) | collective-permute-done | bytes 131104 | tf_op jit(solution)/shard_map/ppermute | solution.py:389
  10.9 0.0 collective-permute-done.2
  10.9 0.6 %collective-permute-start.3 = (bf16[400,512]{1,0:T(8,128)(2,1)S(1)}, bf16[400,512]{1,0:T(8,128)(2,1)S(1)}, u32[]{:S(2)}, u32[]{:S(2)}) collective-permute-start(bf16[400,512]{1,0:T(8,128)(2,1)S(1)} %pad_maximum_fusion), channel_id=1, source_target_pairs={{0,4},{8,12},{16,20},{24,28},{4,0},{12,8},{20,16},{28,24},{1,5},{9... | collective-permute-start | bytes 1228808 | tf_op jit(solution)/shard_map/ppermute | solution.py:389
  11.5 3.1 %collective-permute-start.4 = (bf16[272,512]{1,0:T(8,128)(2,1)S(1)}, bf16[272,512]{1,0:T(8,128)(2,1)S(1)}, u32[]{:S(2)}, u32[]{:S(2)}) collective-permute-start(bf16[272,512]{1,0:T(8,128)(2,1)S(1)} %pad_maximum_fusion.1.both_ref), channel_id=1, source_target_pairs={{4,8},{12,16},{20,24},{8,4},{16,12},{24,20},{5,9},{13,17},{21,25},... | collective-permute-start | bytes 835592 | tf_op jit(solution)/shard_map/ppermute | solution.py:389
  14.7 1.7 %early.1 = (f32[4,8,512]{2,1,0:T(8,128)S(1)}, f32[4,144,512]{2,1,0:T(8,128)S(1)}) custom-call(bf16[4,8,16,128]{3,2,1,0:T(8,128)(2,1)S(1)} %get-tuple-element.30.choice_ref, bf16[272,512]{1,0:T(8,128)(2,1)S(1)} %pad_maximum_fusion.1.both_ref, bf16[400,512]{1,0:T(8,128)(2,1)S(1)} %collective-permute-done.3.inner_ref, ...), custom_call_target="tpu_custom_call" | custom-call | flops 3000000000 | bytes 6000000 | tf_op jit(solution)/shard_map/early/pallas_call | solution.py:438
  16.4 0.0 copy-start
  16.4 0.0 copy-start.1
  16.4 2.7 %mix.1 = (bf16[20,96,512]{2,1,0:T(8,128)(2,1)S(1)}, bf16[2,15,96,512]{3,2,1,0:T(8,128)(2,1)S(1)}) custom-call(f32[5,5,2,9]{3,2,1,0:T(2,128)} %bitcast.15, bf16[9,84,512]{2,1,0:T(8,128)(2,1)} %bitcast.10), custom_call_target="tpu_custom_call" | custom-call | flops 2000000000 | bytes 5000000 | tf_op jit(solution)/shard_map/mix/pallas_call | solution.py:455
  19.1 0.3 collective-permute-done.4.corners_ref
  19.4 2.2 %late.1 = (bf16[128,512]{1,0:T(8,128)(2,1)S(1)}, bf16[128,512]{1,0:T(8,128)(2,1)S(1)}, bf16[16,512]{1,0:T(8,128)(2,1)S(1)}, bf16[16,512]{1,0:T(8,128)(2,1)S(1)}) custom-call(bf16[4,8,16,128]{3,2,1,0:T(8,128)(2,1)S(1)} %get-tuple-element.30.choice_ref, bf16[32,128]{1,0:T(8,128)(2,1)S(1)} %get-tuple-element.31.cells_ref, ...), custom_call_target="tpu_custom_call" | custom-call | flops 3000000000 | bytes 6000000 | tf_op jit(solution)/shard_map/late/pallas_call | solution.py:472
  21.6 1.2 %collective-permute-start.5 = (bf16[16,512]{1,0:T(8,128)(2,1)S(1)}, bf16[16,512]{1,0:T(8,128)(2,1)S(1)}, u32[]{:S(2)}, u32[]{:S(2)}) collective-permute-start(bf16[16,512]{1,0:T(8,128)(2,1)S(1)} %get-tuple-element.51), channel_id=1, source_target_pairs={{0,1},{1,2},{2,3},{3,0},{4,5},{5,6},{6,7},{7,4},{8,9},{9,10},{10,1... | collective-permute-start | bytes 49160 | tf_op jit(solution)/shard_map/ppermute | solution.py:384
  22.8 1.1 %collective-permute-start.6 = (bf16[16,512]{1,0:T(8,128)(2,1)S(1)}, bf16[16,512]{1,0:T(8,128)(2,1)S(1)}, u32[]{:S(2)}, u32[]{:S(2)}) collective-permute-start(bf16[16,512]{1,0:T(8,128)(2,1)S(1)} %get-tuple-element.52), channel_id=1, source_target_pairs={{0,3},{1,0},{2,1},{3,2},{4,7},{5,4},{6,5},{7,6},{8,11},{9,8},{10,9... | collective-permute-start | bytes 49160 | tf_op jit(solution)/shard_map/ppermute | solution.py:384
  24.0 1.2 %collective-permute-done.5 = bf16[16,512]{1,0:T(8,128)(2,1)S(1)} collective-permute-done((bf16[16,512]{1,0:T(8,128)(2,1)S(1)}, bf16[16,512]{1,0:T(8,128)(2,1)S(1)}, u32[]{:S(2)}, u32[]{:S(2)}) %collective-permute-start.5) | collective-permute-done | bytes 16416 | tf_op jit(solution)/shard_map/ppermute | solution.py:384
  25.2 0.3 collective-permute-done.6
  25.4 0.1 collective-permute-start.8
  25.5 4.8 %collective-permute-start.7 = (bf16[144,512]{1,0:T(8,128)(2,1)S(1)}, bf16[144,512]{1,0:T(8,128)(2,1)S(1)}, u32[]{:S(2)}, u32[]{:S(2)}) collective-permute-start(bf16[144,512]{1,0:T(8,128)(2,1)S(1)} %pad_maximum_fusion.2.latent_ref), channel_id=1, source_target_pairs={{4,8},{12,16},{20,24},{8,4},{16,12},{24,20},{5,9},{13,17},{21,25},... | collective-permute-start | bytes 442376 | tf_op jit(solution)/shard_map/ppermute | solution.py:389
  30.4 1.8 %own_band.1 = (f32[2,96,256]{2,1,0:T(8,128)S(1)}, bf16[2,2,5,256,256]{4,3,2,1,0:T(8,128)(2,1)S(1)}, bf16[128,512]{1,0:T(8,128)(2,1)}) custom-call(bf16[128,512]{1,0:T(8,128)(2,1)S(1)} %get-tuple-element.49.state_ref, bf16[144,512]{1,0:T(8,128)(2,1)S(1)} %get-tuple-element.35.own_ref, bf16[400,512]{1,0:T(8,128)(2,1)S(1)} %collective-permute-done.3.inner_ref, ...), custom_call_target="tpu_custom_call" | custom-call | flops 1000000000 | bytes 2500000 | tf_op jit(solution)/shard_map/own_band/pallas_call | solution.py:494
  32.2 0.9 %inner_band.1.partial_ref = f32[2,96,256]{2,1,0:T(8,128)S(1)} custom-call(bf16[144,512]{1,0:T(8,128)(2,1)S(1)} %collective-permute-done.8.latent_ref, bf16[2,15,96,512]{3,2,1,0:T(8,128)(2,1)S(1)} %get-tuple-element.55.weights_ref, bf16[2,2,5,256,256]{4,3,2,1,0:T(8,128)(2,1)S(1)} %get-tuple-element.56.hot_ref, f32[2,96,256]{2,1,0:T(8,128)S(1)} %get-tuple-element.57.partial_ref), custom_call_target="tpu_custom_call" | custom-call | flops 1000000000 | bytes 2500000 | tf_op jit(solution)/shard_map/inner_band/pallas_call | solution.py:511
  33.1 0.1 collective-permute-done.7.latent_ref
  33.2 1.6 %outer_band.1 = bf16[84,2,256]{2,1,0:T(2,128)(2,1)} custom-call(bf16[144,512]{1,0:T(8,128)(2,1)S(1)} %collective-permute-done.7.latent_ref, bf16[2,15,96,512]{3,2,1,0:T(8,128)(2,1)S(1)} %get-tuple-element.55.weights_ref, bf16[2,2,5,256,256]{4,3,2,1,0:T(8,128)(2,1)S(1)} %get-tuple-element.56.hot_ref, f32[2,96,256]{2,1,0:T(8,128)S(1)} %inner_band.1.partial_ref), custom_call_target="tpu_custom_call" | custom-call | flops 1000000000 | bytes 2500000 | tf_op jit(solution)/shard_map/outer_band/pallas_call | solution.py:521
  (13 shorter events, 0.1 us)
Async XLA Ops:
  0.6 10.2 %collective-permute-start.2 = (bf16[128,512]{1,0:T(8,128)(2,1)}, bf16[128,512]{1,0:T(8,128)(2,1)S(1)}, u32[]{:S(2)}, u32[]{:S(2)}) collective-permute-start(bf16[128,512]{1,0:T(8,128)(2,1)} %bitcast.11), channel_id=1, source_target_pairs={{0,3},{1,0},{2,1},{3,2},{4,7},{5,4},{6,5},{7,6},{8,11},{9,8},{10,9... | collective-permute-start | bytes 393224 | tf_op jit(solution)/shard_map/ppermute | solution.py:384
  3.7 6.6 %collective-permute-start.1 = (bf16[128,512]{1,0:T(8,128)(2,1)}, bf16[128,512]{1,0:T(8,128)(2,1)S(1)}, u32[]{:S(2)}, u32[]{:S(2)}) collective-permute-start(bf16[128,512]{1,0:T(8,128)(2,1)} %bitcast.12), channel_id=1, source_target_pairs={{0,1},{1,2},{2,3},{3,0},{4,5},{5,6},{6,7},{7,4},{8,9},{9,10},{10,1... | collective-permute-start | bytes 393224 | tf_op jit(solution)/shard_map/ppermute | solution.py:384
  3.7 7.2 %collective-permute-start = (bf16[128,512]{1,0:T(8,128)(2,1)}, bf16[128,512]{1,0:T(8,128)(2,1)S(1)}, u32[]{:S(2)}, u32[]{:S(2)}) collective-permute-start(bf16[128,512]{1,0:T(8,128)(2,1)} %bitcast.13), channel_id=1, source_target_pairs={{4,8},{12,16},{20,24},{8,4},{16,12},{24,20},{5,9},{13,17},{21,25},... | collective-permute-start | bytes 393224 | tf_op jit(solution)/shard_map/ppermute | solution.py:389
  7.7 6.9 %copy-start.2 = (f32[512]{0:T(512)S(1)}, f32[512]{0:T(512)}, u32[]{:S(2)}) copy-start(f32[512]{0:T(512)} %param.10) | copy-start | bytes 6148
  10.9 3.8 %collective-permute-start.3 = (bf16[400,512]{1,0:T(8,128)(2,1)S(1)}, bf16[400,512]{1,0:T(8,128)(2,1)S(1)}, u32[]{:S(2)}, u32[]{:S(2)}) collective-permute-start(bf16[400,512]{1,0:T(8,128)(2,1)S(1)} %pad_maximum_fusion), channel_id=1, source_target_pairs={{0,4},{8,12},{16,20},{24,28},{4,0},{12,8},{20,16},{28,24},{1,5},{9... | collective-permute-start | bytes 1228808 | tf_op jit(solution)/shard_map/ppermute | solution.py:389
  11.5 7.9 %collective-permute-start.4 = (bf16[272,512]{1,0:T(8,128)(2,1)S(1)}, bf16[272,512]{1,0:T(8,128)(2,1)S(1)}, u32[]{:S(2)}, u32[]{:S(2)}) collective-permute-start(bf16[272,512]{1,0:T(8,128)(2,1)S(1)} %pad_maximum_fusion.1.both_ref), channel_id=1, source_target_pairs={{4,8},{12,16},{20,24},{8,4},{16,12},{24,20},{5,9},{13,17},{21,25},... | collective-permute-start | bytes 835592 | tf_op jit(solution)/shard_map/ppermute | solution.py:389
  16.4 3.0 %copy-start = (bf16[512,512]{1,0:T(8,128)(2,1)S(1)}, bf16[512,512]{1,0:T(8,128)(2,1)}, u32[]{:S(2)}) copy-start(bf16[512,512]{1,0:T(8,128)(2,1)} %wout_ref.1) | copy-start | bytes 1572868
  16.4 3.0 %copy-start.1 = (bf16[512,512]{1,0:T(8,128)(2,1)S(1)}, bf16[512,512]{1,0:T(8,128)(2,1)}, u32[]{:S(2)}) copy-start(bf16[512,512]{1,0:T(8,128)(2,1)} %wlat_ref.1) | copy-start | bytes 1572868
  21.6 3.6 %collective-permute-start.5 = (bf16[16,512]{1,0:T(8,128)(2,1)S(1)}, bf16[16,512]{1,0:T(8,128)(2,1)S(1)}, u32[]{:S(2)}, u32[]{:S(2)}) collective-permute-start(bf16[16,512]{1,0:T(8,128)(2,1)S(1)} %get-tuple-element.51), channel_id=1, source_target_pairs={{0,1},{1,2},{2,3},{3,0},{4,5},{5,6},{6,7},{7,4},{8,9},{9,10},{10,1... | collective-permute-start | bytes 49160 | tf_op jit(solution)/shard_map/ppermute | solution.py:384
  22.8 2.6 %collective-permute-start.6 = (bf16[16,512]{1,0:T(8,128)(2,1)S(1)}, bf16[16,512]{1,0:T(8,128)(2,1)S(1)}, u32[]{:S(2)}, u32[]{:S(2)}) collective-permute-start(bf16[16,512]{1,0:T(8,128)(2,1)S(1)} %get-tuple-element.52), channel_id=1, source_target_pairs={{0,3},{1,0},{2,1},{3,2},{4,7},{5,4},{6,5},{7,6},{8,11},{9,8},{10,9... | collective-permute-start | bytes 49160 | tf_op jit(solution)/shard_map/ppermute | solution.py:384
  25.4 6.7 %collective-permute-start.8 = (bf16[144,512]{1,0:T(8,128)(2,1)S(1)}, bf16[144,512]{1,0:T(8,128)(2,1)S(1)}, u32[]{:S(2)}, u32[]{:S(2)}) collective-permute-start(bf16[144,512]{1,0:T(8,128)(2,1)S(1)} %pad_maximum_fusion.2.latent_ref), channel_id=1, source_target_pairs={{0,4},{8,12},{16,20},{24,28},{4,0},{12,8},{20,16},{28,24},{1,5},{9... | collective-permute-start | bytes 442376 | tf_op jit(solution)/shard_map/ppermute | solution.py:389
  25.5 7.7 %collective-permute-start.7 = (bf16[144,512]{1,0:T(8,128)(2,1)S(1)}, bf16[144,512]{1,0:T(8,128)(2,1)S(1)}, u32[]{:S(2)}, u32[]{:S(2)}) collective-permute-start(bf16[144,512]{1,0:T(8,128)(2,1)S(1)} %pad_maximum_fusion.2.latent_ref), channel_id=1, source_target_pairs={{4,8},{12,16},{20,24},{8,4},{16,12},{24,20},{5,9},{13,17},{21,25},... | collective-permute-start | bytes 442376 | tf_op jit(solution)/shard_map/ppermute | solution.py:389

commit v7 on v6

--- a/solution.py
+++ b/solution.py
@@ -45,14 +45,7 @@
     return (center * lax.rsqrt(spread + 1e-05) * gain).astype(BF16)
 
 
-def mix_kernel(psi_hbm, dec_hbm, middle_ref, edges_ref, psi_ref, dec_ref, psi_rows_ref, taps_ref, sems):
-    copies = [
-        pltpu.make_async_copy(psi_hbm, psi_ref, sems.at[0]),
-        pltpu.make_async_copy(dec_hbm, dec_ref, sems.at[1]),
-    ]
-    for copy in copies:
-        copy.start()
-    copies[0].wait()
+def mix_kernel(blocks, psi_ref, dec_ref, mixed_ref, psi_rows_ref, taps_ref):
     basis, out_ch, channels = dec_ref.shape
     depth = basis * ROWS
     for tap in range(TAPS):
@@ -62,13 +55,10 @@
     spread = (iota((basis, depth), 1) // ROWS == iota((basis, depth), 0)).astype(F32)
     expanded = jnp.dot(psi_rows_ref[...], spread, preferred_element_type=F32)
     pick = iota((ROWS, depth), 1) % ROWS == iota((ROWS, depth), 0)
-    for at, (out_row, tap, off) in enumerate(blocks_of(OWN) + blocks_of(ABOVE) + blocks_of(BELOW)):
+    for at, (out_row, tap, off) in enumerate(blocks):
         source = (tap * TAPS + off) * 2 + out_row
         taps = jnp.broadcast_to(expanded[source : source + 1], (ROWS, depth))
         taps_ref[at * ROWS : (at + 1) * ROWS, :] = jnp.where(pick, taps, 0.0).astype(BF16)
-    copies[1].wait()
-    inside = middle_ref.shape[0]
-    outside = edges_ref.shape[1]
     for first in range(0, out_ch, ROWS):
         size = min(ROWS, out_ch - first)
         pieces = []
@@ -78,10 +68,7 @@
                 pieces.append(jnp.zeros((ROWS - size, channels), BF16))
         mixing = jnp.concatenate(pieces, axis=0)
         mixed = jnp.dot(taps_ref[...], mixing, preferred_element_type=F32).astype(BF16)
-        mixed = mixed.reshape(taps_ref.shape[0] // ROWS, ROWS, channels)
-        middle_ref[:, first : first + ROWS, :] = mixed[:inside]
-        edges_ref[0, :, first : first + ROWS, :] = mixed[inside : inside + outside]
-        edges_ref[1, :, first : first + ROWS, :] = mixed[inside + outside :]
+        mixed_ref[:, first : first + ROWS, :] = mixed.reshape(len(blocks), ROWS, channels)
 
 
 def listed_blocks(sectors, listed_ref):
@@ -93,7 +80,7 @@
         step_reg = (block // sectors - reg_here) * toward
         step_lon = (block % sectors - lon_here + 1 + sectors) % sectors - 1
         place = jnp.where(step_lon == 0, 2, jnp.where(step_lon < 0, 0, 1))
-        outer = jnp.where(step_lon == 0, 5, 6 + place)
+        outer = jnp.where(step_lon == 0, 5, 7 - place)
         found.append(jnp.where(step_reg == 0, place, jnp.where(step_reg > 0, 2 + place, outer)))
     for low in range(len(found)):
         for high in range(low + 1, len(found)):
@@ -102,20 +89,34 @@
     return found
 
 
+def gather_kernel(x_hbm, assign_hbm, own_ref, assign_ref, sems):
+    rows = own_ref.shape[0] - ROWS
+    copies = [
+        pltpu.make_async_copy(assign_hbm, assign_ref, sems.at[0]),
+        pltpu.make_async_copy(x_hbm, own_ref.at[pl.ds(0, rows)], sems.at[1]),
+    ]
+    for copy in copies:
+        copy.start()
+    copies[0].wait()
+    local = lax.rem(assign_ref[...], rows).astype(F32)
+    line = jnp.concatenate([local[:1], local[1:2]], axis=1)
+    line = jnp.broadcast_to(line, (ROWS, line.shape[1]))
+    own_ref[rows:] = jnp.where(iota(line.shape, 0) == 0, line, 0.0).astype(BF16)
+    copies[1].wait()
+
+
 def prepare_kernel(
     sectors,
-    x_hbm, gain_hbm, wqkv_hbm, assign_hbm, listed_hbm,
-    own_ref, query_ref, key_ref, value_ref, wk_ref, wvt_ref, choice_ref, cells_ref,
-    x_ref, gain_ref, wqkv_ref, assign_ref, cell_ref, listed_ref, sems,
+    own_ref, gain_hbm, wqkv_hbm, assign_hbm, listed_hbm,
+    query_ref, key_ref, value_ref, wk_ref, wvt_ref, choice_ref, cells_ref,
+    gain_ref, wqkv_ref, cell_ref, listed_ref, sems,
 ):
     copies = [
         pltpu.make_async_copy(source, target, sems.at[at])
         for at, (source, target) in enumerate(
             (
-                (x_hbm, x_ref),
                 (gain_hbm, gain_ref),
                 (wqkv_hbm, wqkv_ref),
-                (assign_hbm, assign_ref),
                 (assign_hbm, cell_ref),
                 (listed_hbm, listed_ref),
             )
@@ -123,15 +124,11 @@
     ]
     for copy in copies:
         copy.start()
-    rows, width = x_ref.shape
+    rows, width = key_ref.shape
     group, members = query_ref.shape[1], query_ref.shape[2] // rows
     head = group // members
-    for copy in copies[3:]:
+    for copy in copies[2:]:
         copy.wait()
-    local = lax.rem(assign_ref[...], rows).astype(F32)
-    line = jnp.concatenate([local[:1], local[1:2]], axis=1)
-    line = jnp.broadcast_to(line, (ROWS, line.shape[1]))
-    own_ref[rows:] = jnp.where(iota(line.shape, 0) == 0, line, 0.0).astype(BF16)
     for at, number in enumerate(listed_blocks(sectors, listed_ref)):
         for candidate in range(CANDIDATES):
             same = jnp.full((ROWS, LANES), jnp.where(number == candidate, 1.0, 0.0), F32)
@@ -146,10 +143,8 @@
                 hit = jnp.where((place == row * REACH + col) & (node == cell), 1.0, hit)
         cells_ref[side * ROWS : (side + 1) * ROWS] = hit.astype(BF16)
     copies[0].wait()
-    own_ref[:rows] = x_ref[...]
+    normed = normalise(own_ref[:rows], gain_ref[...])
     copies[1].wait()
-    normed = normalise(x_ref[...], gain_ref[...])
-    copies[2].wait()
     query = jnp.dot(normed, wqkv_ref[:, :width], preferred_element_type=F32)
     query_t = (query * (math.log2(math.e) / head**0.5)).T.astype(BF16)
     mask = (iota((group, members * rows), 0) // head) == (iota((group, members * rows), 1) // rows)
@@ -165,13 +160,13 @@
     value_ref[...] = lax.dot_general(wvt, normed, NT, preferred_element_type=F32).astype(BF16)
 
 
-def chosen(entries, rows, choice_ref, both_ref, inner_ref, center_ref, corners_ref):
-    candidates = [both_ref[:rows], both_ref[rows : 2 * rows]]
-    candidates += [inner_ref[at * rows : (at + 1) * rows] for at in range(3)]
-    candidates.append(center_ref[...])
-    if corners_ref is not None:
-        candidates += [corners_ref[:rows], corners_ref[rows : 2 * rows]]
-    tall, wide = rows // ROWS, center_ref.shape[1] // LANES
+def chosen(entries, rows, choice_ref, west_ref, east_ref, beside_ref, inner_ref, outer_ref, corner_ref):
+    candidates = [west_ref[...], east_ref[...]]
+    candidates += [beside_ref[...], inner_ref[:rows], inner_ref[rows : 2 * rows]]
+    candidates.append(outer_ref[rows : 2 * rows])
+    if corner_ref is not None:
+        candidates += [outer_ref[:rows], corner_ref[...]]
+    tall, wide = rows // ROWS, west_ref.shape[1] // LANES
     near = []
     for entry in entries:
         total = None
@@ -191,13 +186,13 @@
 
 
 def early_kernel(
-    choice_ref, both_ref, inner_ref, center_ref,
+    choice_ref, west_ref, east_ref, beside_ref, inner_ref, outer_ref,
     gain_ref, wk_ref, wvt_ref, query_ref, key_ref, value_ref,
     top_ref, sum_ref, keys_ref, values_ref,
 ):
     rows = key_ref.shape[0]
     parts, group, _ = query_ref.shape
-    nodes = chosen(range(EARLY), rows, choice_ref, both_ref, inner_ref, center_ref, None)
+    nodes = chosen(range(EARLY), rows, choice_ref, west_ref, east_ref, beside_ref, inner_ref, outer_ref, None)
     keys, values = project(nodes, gain_ref[...], wk_ref, wvt_ref)
     keys_ref[:rows] = key_ref[...]
     keys_ref[rows:] = keys
@@ -223,9 +218,9 @@
 
 
 def late_kernel(
-    choice_ref, cells_ref, both_ref, inner_ref, center_ref, corners_ref,
+    choice_ref, cells_ref, west_ref, east_ref, beside_ref, inner_ref, outer_ref, corner_ref,
     own_ref, gain_ref, wk_ref, wvt_ref, query_ref, top_ref, sum_ref, wout_ref, wlat_ref,
-    state_ref, latent_ref, west_ref, east_ref,
+    state_ref, latent_ref, first_ref, last_ref,
     attended_ref,
 ):
     rows, width = state_ref.shape
@@ -233,7 +228,9 @@
     members = lanes // rows
     head = group // members
     entries = range(EARLY, choice_ref.shape[0])
-    nodes = chosen(entries, rows, choice_ref, both_ref, inner_ref, center_ref, corners_ref)
+    nodes = chosen(
+        entries, rows, choice_ref, west_ref, east_ref, beside_ref, inner_ref, outer_ref, corner_ref
+    )
     keys, values = project(nodes, gain_ref[...], wk_ref, wvt_ref)
     ones = jnp.ones((ROWS, nodes.shape[0]), BF16)
     owner = iota((group, rows), 0) // head
@@ -268,8 +265,8 @@
     latent = (value / (1.0 + jnp.exp(-value))).astype(BF16)
     latent_ref[...] = latent
     cells = jnp.dot(cells_ref[...], latent, preferred_element_type=F32).astype(BF16)
-    west_ref[...] = cells[:ROWS]
-    east_ref[...] = cells[ROWS:]
+    first_ref[...] = cells[:ROWS]
+    last_ref[...] = cells[ROWS:]
 
 
 def hot_rows(values, rows, cols, line):
@@ -301,7 +298,7 @@
 
 
 def own_kernel(
-    begin, state_ref, own_ref, inner_ref, corners_ref, latent_ref, weights_ref,
+    begin, state_ref, own_ref, inner_ref, outer_ref, latent_ref, weights_ref,
     out_ref, hot_ref, kept_ref,
 ):
     kept_ref[...] = state_ref[...]
@@ -319,7 +316,7 @@
     for row in range(2):
         out_ref[row] = acc[row]
     odd = lax.axis_index("reg") % 2 == 1
-    inner, outer = lines_of(inner_ref, begin[1], cols), lines_of(corners_ref, begin[2], cols)
+    inner, outer = lines_of(inner_ref, begin[1], cols), lines_of(outer_ref, begin[2], cols)
     nodes = rows + 2 * SIDE
     for band, (yes, no) in enumerate(((inner, outer), (outer, inner))):
         for at, line in enumerate((0, 1) if band == 0 else (1, 0)):
@@ -334,9 +331,11 @@
     band = 1 - odd if from_inner else odd
     latent = latent_ref[...]
     lanes, cols = hot_ref.shape[3:]
-    outputs = weights_ref.shape[2]
+    outputs = weights_ref.shape[1]
     blank = jnp.zeros((lanes - latent.shape[0], latent.shape[1]), BF16)
-    shares = shares_of(jnp.concatenate([latent, blank], axis=0), weights_ref[band])
+    blocks = len(blocks_of(ABOVE))
+    weights = weights_ref[pl.ds(band * blocks, blocks)]
+    shares = shares_of(jnp.concatenate([latent, blank], axis=0), weights)
     for off in range(TAPS):
         span = slice(off * lanes, (off + 1) * lanes)
         one_ref[:, span] = shares[off]
@@ -391,23 +390,50 @@
     def in_hbm(*arrays):
         return [pltpu.with_memory_space_constraint(array, pltpu.HBM) for array in arrays]
 
-    center = exchanged(x, 1)
-    left = shifted(x, 1)
-    right = shifted(x, -1)
+    west = shifted(x, 1)
+    east = shifted(x, -1)
 
     outputs = -(-out_ch // ROWS) * ROWS
     head = width // HEADS
     members = LANES // head
     parts = HEADS // members
-    inside, outside = len(blocks_of(OWN)), len(blocks_of(ABOVE))
-    taps = psi.transpose(2, 3, 1, 0)
-    mixing = w_dec.transpose(0, 2, 1)
-    own, query, key, value, wk, wvt, choice, cells = pl.pallas_call(
+    def mixed(blocks, name, after):
+        taps = psi.transpose(2, 3, 1, 0)
+        mixing = w_dec.transpose(0, 2, 1)
+        taps, mixing, after = lax.optimization_barrier((taps, mixing, after))
+        weights = pl.pallas_call(
+            functools.partial(mix_kernel, blocks),
+            in_specs=[whole()] * 2,
+            out_specs=whole(),
+            out_shape=struct(len(blocks), outputs, channels),
+            scratch_shapes=[
+                pltpu.VMEM((2 * TAPS * TAPS, basis), F32),
+                pltpu.VMEM((len(blocks) * ROWS, basis * ROWS), BF16),
+            ],
+            compiler_params=params(32),
+            cost_estimate=cost(1e9, 3e6),
+            name=name,
+        )(taps, mixing)
+        return weights, after
+
+    own = pl.pallas_call(
+        gather_kernel,
+        in_specs=[whole(pltpu.HBM)] * 2,
+        out_specs=whole(),
+        out_shape=struct(rows + ROWS, width),
+        scratch_shapes=[
+            pltpu.VMEM(assignment.shape, jnp.int32),
+            pltpu.SemaphoreType.DMA((2,)),
+        ],
+        compiler_params=params(32),
+        cost_estimate=cost(1e8, 1e6),
+        name="gather",
+    )(*in_hbm(x, assignment))
+    query, key, value, wk, wvt, choice, cells = pl.pallas_call(
         functools.partial(prepare_kernel, sectors),
-        in_specs=[whole(pltpu.HBM)] * 5,
-        out_specs=[whole()] * 8,
+        in_specs=[whole()] + [whole(pltpu.HBM)] * 4,
+        out_specs=[whole()] * 7,
         out_shape=[
-            struct(rows + ROWS, width),
             struct(parts, LANES, members * rows),
             struct(rows, width),
             struct(width, rows),
@@ -417,27 +443,29 @@
             struct(2 * ROWS, rows),
         ],
         scratch_shapes=[
-            pltpu.VMEM((rows, width), BF16),
             pltpu.VMEM((1, width), F32),
             pltpu.VMEM(w_qkv.shape, BF16),
-            pltpu.VMEM(assignment.shape, jnp.int32),
             pltpu.SMEM(assignment.shape, jnp.int32),
             pltpu.SMEM(neighbours.shape, jnp.int32),
-            pltpu.SemaphoreType.DMA((6,)),
+            pltpu.SemaphoreType.DMA((4,)),
         ],
         compiler_params=params(32),
         cost_estimate=cost(2e9, 5e6),
         name="prepare",
-    )(*in_hbm(x, gain, w_qkv, assignment, neighbours))
-    center, left = lax.optimization_barrier((center, left))
-    center, right = lax.optimization_barrier((center, right))
-    both = jnp.concatenate([left, right, own[rows:]], axis=0)
-    corners = exchanged(both, 1)
-    inner = exchanged(jnp.concatenate([left, right, own], axis=0), 0)
+    )(own, *in_hbm(gain, w_qkv, assignment, neighbours))
+    east, query = lax.optimization_barrier((east, query))
+    message = jnp.concatenate([east, own], axis=0)
+    outer = exchanged(message, 1)
+    inner = exchanged(message, 0)
+    corner = exchanged(west, 1)
+    beside = exchanged(west, 0)
+    edges, beside = mixed(blocks_of(ABOVE) + blocks_of(BELOW), "mix_edges", beside)
+    beside, edges = lax.optimization_barrier((beside, edges))
+
 
     top, summed = pl.pallas_call(
         early_kernel,
-        in_specs=[whole()] * 10,
+        in_specs=[whole()] * 12,
         out_specs=[whole()] * 2,
         out_shape=[
             struct(parts, 8, members * rows, dtype=F32),
@@ -450,28 +478,10 @@
         compiler_params=params(32),
         cost_estimate=cost(3e9, 6e6),
         name="early",
-    )(choice, both, inner, center, gain, wk, wvt, query, key, value)
-    taps, mixing, top = lax.optimization_barrier((taps, mixing, top))
-    middle, edges = pl.pallas_call(
-        mix_kernel,
-        in_specs=[whole(pltpu.HBM)] * 2,
-        out_specs=[whole()] * 2,
-        out_shape=[struct(inside, outputs, channels), struct(2, outside, outputs, channels)],
-        scratch_shapes=[
-            pltpu.VMEM(taps.shape, F32),
-            pltpu.VMEM(mixing.shape, BF16),
-            pltpu.VMEM((2 * TAPS * TAPS, basis), F32),
-            pltpu.VMEM(((inside + 2 * outside) * ROWS, basis * ROWS), BF16),
-            pltpu.SemaphoreType.DMA((2,)),
-        ],
-        compiler_params=params(32),
-        cost_estimate=cost(2e9, 5e6),
-        name="mix",
-    )(*in_hbm(taps, mixing))
-    top, middle = lax.optimization_barrier((top, middle))
-    state, latent, west, east = pl.pallas_call(
+    )(choice, west, east, beside, inner, outer, gain, wk, wvt, query, key, value)
+    state, latent, first, last = pl.pallas_call(
         late_kernel,
-        in_specs=[whole()] * 15,
+        in_specs=[whole()] * 17,
         out_specs=[whole()] * 4,
         out_shape=[pltpu.VMEM((rows, width), BF16), struct(rows, channels)]
         + [struct(ROWS, channels)] * 2,
@@ -480,19 +490,21 @@
         cost_estimate=cost(3e9, 6e6),
         name="late",
     )(
-        choice, cells, both, inner, center, corners,
+        choice, cells, west, east, beside, inner, outer, corner,
         own, gain, wk, wvt, query, top, summed, w_out, w_latent,
     )
 
-    from_left = shifted(east, 1)
-    from_right = shifted(west, -1)
+    from_left = shifted(last, 1)
+    from_right = shifted(first, -1)
+    middle, latent = mixed(blocks_of(OWN), "mix_own", latent)
+    from_left, middle = lax.optimization_barrier((from_left, middle))
     extended = jnp.concatenate([latent, from_left[:SIDE], from_right[:SIDE]], axis=0)
     far = exchanged(extended, 1)
     near = exchanged(extended, 0)
 
     lanes = -(-(rows + 2 * SIDE) // 256) * 256
     partial, hots, state = pl.pallas_call(
-        functools.partial(own_kernel, (rows, 3 * rows, 2 * rows)),
+        functools.partial(own_kernel, (rows, 2 * rows, 2 * rows)),
         in_specs=[whole()] * 6,
         out_specs=[whole()] * 3,
         out_shape=[
@@ -503,7 +515,7 @@
         compiler_params=params(32),
         cost_estimate=cost(1e9, 2.5e6),
         name="own_band",
-    )(state, own, inner, corners, extended, middle)
+    )(state, own, inner, outer, extended, middle)
     band_scratch = [
         pltpu.VMEM((outputs, TAPS * lanes), BF16),
         pltpu.VMEM((2 * outputs, TAPS * lanes), BF16),

time: 35 us -> 35.1 us (level)
  waiting for transfers between devices: 2.77 us -> 1.15 us
  starting transfers between devices: 18.1 us -> 19.6 us
    ppermute x4, waiting for transfers between devices: 1.74 us -> 0.79 us  [shifted(): lax.ppermute(array, 'lon', [(i, (i + step) % sectors) for i in range(sect...]
    ppermute x5 -> x6, starting transfers between devices: 12.7 us -> 13.5 us  [exchanged(): return lax.ppermute(array, 'reg', pairs + [(j, i) for i, j in pairs])]
    ppermute x4, starting transfers between devices: 5.42 us -> 6.12 us  [shifted(): lax.ppermute(array, 'lon', [(i, (i + step) % sectors) for i in range(sect...]
    ppermute x5 -> x6, waiting for transfers between devices: 1.02 us -> 0.36 us  [exchanged(): return lax.ppermute(array, 'reg', pairs + [(j, i) for i, j in pairs])]
    pallas_call x4 -> x6, Pallas kernels: 8.37 us -> 8.52 us  [the longest x1 2.22 us: shards(): pl.pallas_call(late_kernel, in_specs=[whole()] * 17, out_specs=[whole()]...]
  transfers between devices with their start and end apart: 9 -> 10, of which waited for: 6 -> 4; matrix products, arithmetic and copies ran while one was open for 0% -> 0% of each run, Pallas kernels for 27% -> 27%
where the time goes in v7:
time: 35.1 us; the launch traced here: 34.8 us
  starting transfers between devices  19.6 us (56%)
  Pallas kernels  13.1 us (37%)
  waiting for transfers between devices  1.15 us (3%)
  between operations  0.84 us (2%)
    ppermute x6, starting transfers between devices, exchanged(): return lax.ppermute(array, 'reg', pairs + [(j, i) for i, j in pairs])  13.5 us
    ppermute x4, starting transfers between devices, shifted(): lax.ppermute(array, 'lon', [(i, (i + step) % sectors) for i in range(sect...  6.12 us
    pallas_call x1, Pallas kernels, shards(): pl.pallas_call(late_kernel, in_specs=[whole()] * 17, out_specs=[whole()]...  2.22 us
    pallas_call x1, Pallas kernels, shards(): pl.pallas_call(functools.partial(prepare_kernel, sectors), in_specs=[whol...  2.09 us
    pallas_call x2, Pallas kernels, mixed(): pl.pallas_call(functools.partial(mix_kernel, blocks), in_specs=[whole()]...  1.82 us
    pallas_call x1, Pallas kernels, shards(): pl.pallas_call(functools.partial(own_kernel, (rows, 2 * rows, 2 * rows)),...  1.8 us
    pallas_call x1, Pallas kernels, shards(): pl.pallas_call(early_kernel, in_specs=[whole()] * 12, out_specs=[whole()]...  1.69 us
    pallas_call x1, Pallas kernels, shards(): pl.pallas_call(functools.partial(band_kernel, False), in_specs=[whole()]...  1.61 us
  transfers between devices with their start and end apart: 10, of which 4 were waited for; matrix products, arithmetic and copies ran while one was open for 0% of the time, Pallas kernels for 27%

profile of v7, /device:TPU:1, one launch (start us, length us, event | category | flops | bytes accessed | tf_op | source)
XLA Modules:
  0.0 34.8 jit_solution(16351539883935002968)
XLA Ops:
  0.6 3.0 %collective-permute-start.1 = (bf16[128,512]{1,0:T(8,128)(2,1)}, bf16[128,512]{1,0:T(8,128)(2,1)S(1)}, u32[]{:S(2)}, u32[]{:S(2)}) collective-permute-start(bf16[128,512]{1,0:T(8,128)(2,1)} %bitcast.14), channel_id=1, source_target_pairs={{0,3},{1,0},{2,1},{3,2},{4,7},{5,4},{6,5},{7,6},{8,11},{9,8},{10,9... | collective-permute-start | bytes 393224 | tf_op jit(solution)/shard_map/ppermute | solution.py:383
  3.7 1.0 %gather.1.own_ref = bf16[144,512]{1,0:T(8,128)(2,1)S(1)} custom-call(bf16[128,512]{1,0:T(8,128)(2,1)} %bitcast.16, s32[2,256]{1,0:T(2,128)} %assign_hbm.3), custom_call_target="tpu_custom_call" | custom-call | flops 100000000 | bytes 1000000 | tf_op jit(solution)/shard_map/gather/pallas_call | solution.py:419
  4.7 0.0 copy-start.1
  4.7 2.1 %prepare.1 = (bf16[4,128,512]{2,1,0:T(8,128)(2,1)S(1)}, bf16[128,512]{1,0:T(8,128)(2,1)S(1)}, bf16[512,128]{1,0:T(8,128)(2,1)S(1)}, bf16[512,512]{1,0:T(8,128)(2...) custom-call(bf16[144,512]{1,0:T(8,128)(2,1)S(1)} %gather.1.own_ref, ...), custom_call_target="tpu_custom_call" | custom-call | flops 2000000000 | bytes 5000000 | tf_op jit(solution)/shard_map/prepare/pallas_call | solution.py:432
  6.8 5.1 %collective-permute-start.4 = (bf16[272,512]{1,0:T(8,128)(2,1)S(1)}, bf16[272,512]{1,0:T(8,128)(2,1)S(1)}, u32[]{:S(2)}, u32[]{:S(2)}) collective-permute-start(bf16[272,512]{1,0:T(8,128)(2,1)S(1)} %pad_maximum_fusion), channel_id=1, source_target_pairs={{4,8},{12,16},{20,24},{8,4},{16,12},{24,20},{5,9},{13,17},{21,25},... | collective-permute-start | bytes 835592 | tf_op jit(solution)/shard_map/ppermute | solution.py:388
  12.0 0.1 collective-permute-start.3
  12.1 0.5 %collective-permute-start.2 = (bf16[128,512]{1,0:T(8,128)(2,1)S(1)}, bf16[128,512]{1,0:T(8,128)(2,1)S(1)}, u32[]{:S(2)}, u32[]{:S(2)}) collective-permute-start(bf16[128,512]{1,0:T(8,128)(2,1)S(1)} %collective-permute-done.west_ref), channel_id=1, source_target_pairs={{0,4},{8,12},{16,20},{24,28},{4,0},{12,8},{20,16},{28,24},{1,5},{9... | collective-permute-start | bytes 393224 | tf_op jit(solution)/shard_map/ppermute | solution.py:388
  12.6 3.2 %collective-permute-start.5 = (bf16[128,512]{1,0:T(8,128)(2,1)S(1)}, bf16[128,512]{1,0:T(8,128)(2,1)S(1)}, u32[]{:S(2)}, u32[]{:S(2)}) collective-permute-start(bf16[128,512]{1,0:T(8,128)(2,1)S(1)} %collective-permute-done.west_ref), channel_id=1, source_target_pairs={{4,8},{12,16},{20,24},{8,4},{16,12},{24,20},{5,9},{13,17},{21,25},... | collective-permute-start | bytes 393224 | tf_op jit(solution)/shard_map/ppermute | solution.py:388
  15.8 1.0 %mix_edges.1.weights_ref = bf16[30,96,512]{2,1,0:T(8,128)(2,1)S(1)} custom-call(f32[5,5,2,9]{3,2,1,0:T(2,128)S(1)} %bitcast.8, bf16[9,84,512]{2,1,0:T(8,128)(2,1)S(1)} %bitcast.6), custom_call_target="tpu_custom_call" | custom-call | flops 1000000000 | bytes 3000000 | tf_op jit(solution)/shard_map/mix_edges/pallas_call | solution.py:404
  16.8 0.0 copy-start.2
  16.9 1.7 %early.1 = (f32[4,8,512]{2,1,0:T(8,128)S(1)}, f32[4,144,512]{2,1,0:T(8,128)S(1)}) custom-call(bf16[4,8,16,128]{3,2,1,0:T(8,128)(2,1)S(1)} %get-tuple-element.30.choice_ref, bf16[128,512]{1,0:T(8,128)(2,1)S(1)} %collective-permute-done.west_ref, bf16[128,512]{1,0:T(8,128)(2,1)S(1)} %collective-permute-done.1.east_ref, ...), custom_call_target="tpu_custom_call" | custom-call | flops 3000000000 | bytes 6000000 | tf_op jit(solution)/shard_map/early/pallas_call | solution.py:466
  18.6 0.3 collective-permute-done.5.corner_ref
  18.8 2.2 %late.1 = (bf16[128,512]{1,0:T(8,128)(2,1)S(1)}, bf16[128,512]{1,0:T(8,128)(2,1)S(1)}, bf16[16,512]{1,0:T(8,128)(2,1)S(1)}, bf16[16,512]{1,0:T(8,128)(2,1)S(1)}) custom-call(bf16[4,8,16,128]{3,2,1,0:T(8,128)(2,1)S(1)} %get-tuple-element.30.choice_ref, bf16[32,128]{1,0:T(8,128)(2,1)S(1)} %get-tuple-element.31.cells_ref, ...), custom_call_target="tpu_custom_call" | custom-call | flops 3000000000 | bytes 6000000 | tf_op jit(solution)/shard_map/late/pallas_call | solution.py:482
  21.1 2.0 %collective-permute-start.6 = (bf16[16,512]{1,0:T(8,128)(2,1)S(1)}, bf16[16,512]{1,0:T(8,128)(2,1)S(1)}, u32[]{:S(2)}, u32[]{:S(2)}) collective-permute-start(bf16[16,512]{1,0:T(8,128)(2,1)S(1)} %get-tuple-element.48), channel_id=1, source_target_pairs={{0,1},{1,2},{2,3},{3,0},{4,5},{5,6},{6,7},{7,4},{8,9},{9,10},{10,1... | collective-permute-start | bytes 49160 | tf_op jit(solution)/shard_map/ppermute | solution.py:383
  23.1 1.0 %collective-permute-start.7 = (bf16[16,512]{1,0:T(8,128)(2,1)S(1)}, bf16[16,512]{1,0:T(8,128)(2,1)S(1)}, u32[]{:S(2)}, u32[]{:S(2)}) collective-permute-start(bf16[16,512]{1,0:T(8,128)(2,1)S(1)} %get-tuple-element.52), channel_id=1, source_target_pairs={{0,3},{1,0},{2,1},{3,2},{4,7},{5,4},{6,5},{7,6},{8,11},{9,8},{10,9... | collective-permute-start | bytes 49160 | tf_op jit(solution)/shard_map/ppermute | solution.py:383
  24.1 0.8 %mix_own.1.weights_ref = bf16[20,96,512]{2,1,0:T(8,128)(2,1)S(1)} custom-call(f32[5,5,2,9]{3,2,1,0:T(2,128)S(1)} %bitcast.9, bf16[9,84,512]{2,1,0:T(8,128)(2,1)S(1)} %bitcast.7), custom_call_target="tpu_custom_call" | custom-call | flops 1000000000 | bytes 3000000 | tf_op jit(solution)/shard_map/mix_own/pallas_call | solution.py:404
  24.9 0.3 collective-permute-done.6
  25.2 0.5 %collective-permute-done.7 = bf16[16,512]{1,0:T(8,128)(2,1)S(1)} collective-permute-done((bf16[16,512]{1,0:T(8,128)(2,1)S(1)}, bf16[16,512]{1,0:T(8,128)(2,1)S(1)}, u32[]{:S(2)}, u32[]{:S(2)}) %collective-permute-start.7) | collective-permute-done | bytes 16416 | tf_op jit(solution)/shard_map/ppermute | solution.py:383
  25.7 0.1 collective-permute-start.9
  25.8 4.6 %collective-permute-start.8 = (bf16[144,512]{1,0:T(8,128)(2,1)S(1)}, bf16[144,512]{1,0:T(8,128)(2,1)S(1)}, u32[]{:S(2)}, u32[]{:S(2)}) collective-permute-start(bf16[144,512]{1,0:T(8,128)(2,1)S(1)} %pad_maximum_fusion.1.latent_ref), channel_id=1, source_target_pairs={{4,8},{12,16},{20,24},{8,4},{16,12},{24,20},{5,9},{13,17},{21,25},... | collective-permute-start | bytes 442376 | tf_op jit(solution)/shard_map/ppermute | solution.py:388
  30.4 1.8 %own_band.1 = (f32[2,96,256]{2,1,0:T(8,128)S(1)}, bf16[2,2,5,256,256]{4,3,2,1,0:T(8,128)(2,1)S(1)}, bf16[128,512]{1,0:T(8,128)(2,1)}) custom-call(bf16[128,512]{1,0:T(8,128)(2,1)S(1)} %get-tuple-element.45.state_ref, bf16[144,512]{1,0:T(8,128)(2,1)S(1)} %gather.1.own_ref, bf16[272,512]{1,0:T(8,128)(2,1)S(1)} %collective-permute-done.3.inner_ref, ...), custom_call_target="tpu_custom_call" | custom-call | flops 1000000000 | bytes 2500000 | tf_op jit(solution)/shard_map/own_band/pallas_call | solution.py:506
  32.2 0.9 %inner_band.1.partial_ref = f32[2,96,256]{2,1,0:T(8,128)S(1)} custom-call(bf16[144,512]{1,0:T(8,128)(2,1)S(1)} %collective-permute-done.9.latent_ref, bf16[30,96,512]{2,1,0:T(8,128)(2,1)S(1)} %mix_edges.1.weights_ref, bf16[2,2,5,256,256]{4,3,2,1,0:T(8,128)(2,1)S(1)} %get-tuple-element.56.hot_ref, f32[2,96,256]{2,1,0:T(8,128)S(1)} %get-tuple-element.57.partial_ref), custom_call_target="tpu_custom_call" | custom-call | flops 1000000000 | bytes 2500000 | tf_op jit(solution)/shard_map/inner_band/pallas_call | solution.py:523
  33.2 0.1 collective-permute-done.8.latent_ref
  33.2 1.6 %outer_band.1 = bf16[84,2,256]{2,1,0:T(2,128)(2,1)} custom-call(bf16[144,512]{1,0:T(8,128)(2,1)S(1)} %collective-permute-done.8.latent_ref, bf16[30,96,512]{2,1,0:T(8,128)(2,1)S(1)} %mix_edges.1.weights_ref, bf16[2,2,5,256,256]{4,3,2,1,0:T(8,128)(2,1)S(1)} %get-tuple-element.56.hot_ref, f32[2,96,256]{2,1,0:T(8,128)S(1)} %inner_band.1.partial_ref), custom_call_target="tpu_custom_call" | custom-call | flops 1000000000 | bytes 2500000 | tf_op jit(solution)/shard_map/outer_band/pallas_call | solution.py:533
  (19 shorter events, 0.1 us)
Async XLA Ops:
  0.6 6.2 %collective-permute-start.1 = (bf16[128,512]{1,0:T(8,128)(2,1)}, bf16[128,512]{1,0:T(8,128)(2,1)S(1)}, u32[]{:S(2)}, u32[]{:S(2)}) collective-permute-start(bf16[128,512]{1,0:T(8,128)(2,1)} %bitcast.14), channel_id=1, source_target_pairs={{0,3},{1,0},{2,1},{3,2},{4,7},{5,4},{6,5},{7,6},{8,11},{9,8},{10,9... | collective-permute-start | bytes 393224 | tf_op jit(solution)/shard_map/ppermute | solution.py:383
  3.7 8.4 %collective-permute-start = (bf16[128,512]{1,0:T(8,128)(2,1)}, bf16[128,512]{1,0:T(8,128)(2,1)S(1)}, u32[]{:S(2)}, u32[]{:S(2)}) collective-permute-start(bf16[128,512]{1,0:T(8,128)(2,1)} %bitcast.15), channel_id=1, source_target_pairs={{0,1},{1,2},{2,3},{3,0},{4,5},{5,6},{6,7},{7,4},{8,9},{9,10},{10,1... | collective-permute-start | bytes 393224 | tf_op jit(solution)/shard_map/ppermute | solution.py:383
  4.7 11.1 %copy-start = (bf16[9,512,84]{1,2,0:T(8,128)(2,1)S(1)}, bf16[9,512,84]{1,2,0:T(8,128)(2,1)}, u32[]{:S(2)}) copy-start(bf16[9,512,84]{1,2,0:T(8,128)(2,1)} %param.17) | copy-start | bytes 2322436
  4.7 11.1 %copy-start.1 = (f32[9,2,5,5]{0,1,3,2:T(2,128)S(1)}, f32[9,2,5,5]{0,1,3,2:T(2,128)}, u32[]{:S(2)}) copy-start(f32[9,2,5,5]{0,1,3,2:T(2,128)} %param.16) | copy-start | bytes 5404
  6.8 10.0 %copy-start.4 = (f32[512]{0:T(512)S(1)}, f32[512]{0:T(512)}, u32[]{:S(2)}) copy-start(f32[512]{0:T(512)} %param.10) | copy-start | bytes 6148
  6.8 10.0 %collective-permute-start.4 = (bf16[272,512]{1,0:T(8,128)(2,1)S(1)}, bf16[272,512]{1,0:T(8,128)(2,1)S(1)}, u32[]{:S(2)}, u32[]{:S(2)}) collective-permute-start(bf16[272,512]{1,0:T(8,128)(2,1)S(1)} %pad_maximum_fusion), channel_id=1, source_target_pairs={{4,8},{12,16},{20,24},{8,4},{16,12},{24,20},{5,9},{13,17},{21,25},... | collective-permute-start | bytes 835592 | tf_op jit(solution)/shard_map/ppermute | solution.py:388
  12.0 4.8 %collective-permute-start.3 = (bf16[272,512]{1,0:T(8,128)(2,1)S(1)}, bf16[272,512]{1,0:T(8,128)(2,1)S(1)}, u32[]{:S(2)}, u32[]{:S(2)}) collective-permute-start(bf16[272,512]{1,0:T(8,128)(2,1)S(1)} %pad_maximum_fusion), channel_id=1, source_target_pairs={{0,4},{8,12},{16,20},{24,28},{4,0},{12,8},{20,16},{28,24},{1,5},{9... | collective-permute-start | bytes 835592 | tf_op jit(solution)/shard_map/ppermute | solution.py:388
  12.1 3.7 %collective-permute-start.2 = (bf16[128,512]{1,0:T(8,128)(2,1)S(1)}, bf16[128,512]{1,0:T(8,128)(2,1)S(1)}, u32[]{:S(2)}, u32[]{:S(2)}) collective-permute-start(bf16[128,512]{1,0:T(8,128)(2,1)S(1)} %collective-permute-done.west_ref), channel_id=1, source_target_pairs={{0,4},{8,12},{16,20},{24,28},{4,0},{12,8},{20,16},{28,24},{1,5},{9... | collective-permute-start | bytes 393224 | tf_op jit(solution)/shard_map/ppermute | solution.py:388
  12.6 6.3 %collective-permute-start.5 = (bf16[128,512]{1,0:T(8,128)(2,1)S(1)}, bf16[128,512]{1,0:T(8,128)(2,1)S(1)}, u32[]{:S(2)}, u32[]{:S(2)}) collective-permute-start(bf16[128,512]{1,0:T(8,128)(2,1)S(1)} %collective-permute-done.west_ref), channel_id=1, source_target_pairs={{4,8},{12,16},{20,24},{8,4},{16,12},{24,20},{5,9},{13,17},{21,25},... | collective-permute-start | bytes 393224 | tf_op jit(solution)/shard_map/ppermute | solution.py:388
  16.8 2.0 %copy-start.2 = (bf16[512,512]{1,0:T(8,128)(2,1)S(1)}, bf16[512,512]{1,0:T(8,128)(2,1)}, u32[]{:S(2)}) copy-start(bf16[512,512]{1,0:T(8,128)(2,1)} %wout_ref.1) | copy-start | bytes 1572868
  16.9 2.0 %copy-start.3 = (bf16[512,512]{1,0:T(8,128)(2,1)S(1)}, bf16[512,512]{1,0:T(8,128)(2,1)}, u32[]{:S(2)}) copy-start(bf16[512,512]{1,0:T(8,128)(2,1)} %wlat_ref.1) | copy-start | bytes 1572868
  21.1 4.2 %collective-permute-start.6 = (bf16[16,512]{1,0:T(8,128)(2,1)S(1)}, bf16[16,512]{1,0:T(8,128)(2,1)S(1)}, u32[]{:S(2)}, u32[]{:S(2)}) collective-permute-start(bf16[16,512]{1,0:T(8,128)(2,1)S(1)} %get-tuple-element.48), channel_id=1, source_target_pairs={{0,1},{1,2},{2,3},{3,0},{4,5},{5,6},{6,7},{7,4},{8,9},{9,10},{10,1... | collective-permute-start | bytes 49160 | tf_op jit(solution)/shard_map/ppermute | solution.py:383
  23.1 2.6 %collective-permute-start.7 = (bf16[16,512]{1,0:T(8,128)(2,1)S(1)}, bf16[16,512]{1,0:T(8,128)(2,1)S(1)}, u32[]{:S(2)}, u32[]{:S(2)}) collective-permute-start(bf16[16,512]{1,0:T(8,128)(2,1)S(1)} %get-tuple-element.52), channel_id=1, source_target_pairs={{0,3},{1,0},{2,1},{3,2},{4,7},{5,4},{6,5},{7,6},{8,11},{9,8},{10,9... | collective-permute-start | bytes 49160 | tf_op jit(solution)/shard_map/ppermute | solution.py:383
  25.7 6.5 %collective-permute-start.9 = (bf16[144,512]{1,0:T(8,128)(2,1)S(1)}, bf16[144,512]{1,0:T(8,128)(2,1)S(1)}, u32[]{:S(2)}, u32[]{:S(2)}) collective-permute-start(bf16[144,512]{1,0:T(8,128)(2,1)S(1)} %pad_maximum_fusion.1.latent_ref), channel_id=1, source_target_pairs={{0,4},{8,12},{16,20},{24,28},{4,0},{12,8},{20,16},{28,24},{1,5},{9... | collective-permute-start | bytes 442376 | tf_op jit(solution)/shard_map/ppermute | solution.py:388
  25.8 7.4 %collective-permute-start.8 = (bf16[144,512]{1,0:T(8,128)(2,1)S(1)}, bf16[144,512]{1,0:T(8,128)(2,1)S(1)}, u32[]{:S(2)}, u32[]{:S(2)}) collective-permute-start(bf16[144,512]{1,0:T(8,128)(2,1)S(1)} %pad_maximum_fusion.1.latent_ref), channel_id=1, source_target_pairs={{4,8},{12,16},{20,24},{8,4},{16,12},{24,20},{5,9},{13,17},{21,25},... | collective-permute-start | bytes 442376 | tf_op jit(solution)/shard_map/ppermute | solution.py:388

commit v8 on v7

--- a/solution.py
+++ b/solution.py
@@ -15,7 +15,7 @@
 ROWS = 16
 LANES = 128
 EARLY = 2
-CANDIDATES = 8
+CANDIDATES = 5
 F32 = jnp.float32
 BF16 = jnp.bfloat16
 NT = (((1,), (1,)), ((), ()))
@@ -80,7 +80,7 @@
         step_reg = (block // sectors - reg_here) * toward
         step_lon = (block % sectors - lon_here + 1 + sectors) % sectors - 1
         place = jnp.where(step_lon == 0, 2, jnp.where(step_lon < 0, 0, 1))
-        outer = jnp.where(step_lon == 0, 5, 7 - place)
+        outer = jnp.where(step_lon == 0, 5, 6 + place)
         found.append(jnp.where(step_reg == 0, place, jnp.where(step_reg > 0, 2 + place, outer)))
     for low in range(len(found)):
         for high in range(low + 1, len(found)):
@@ -89,34 +89,21 @@
     return found
 
 
-def gather_kernel(x_hbm, assign_hbm, own_ref, assign_ref, sems):
-    rows = own_ref.shape[0] - ROWS
-    copies = [
-        pltpu.make_async_copy(assign_hbm, assign_ref, sems.at[0]),
-        pltpu.make_async_copy(x_hbm, own_ref.at[pl.ds(0, rows)], sems.at[1]),
-    ]
-    for copy in copies:
-        copy.start()
-    copies[0].wait()
-    local = lax.rem(assign_ref[...], rows).astype(F32)
-    line = jnp.concatenate([local[:1], local[1:2]], axis=1)
-    line = jnp.broadcast_to(line, (ROWS, line.shape[1]))
-    own_ref[rows:] = jnp.where(iota(line.shape, 0) == 0, line, 0.0).astype(BF16)
-    copies[1].wait()
-
-
 def prepare_kernel(
     sectors,
-    own_ref, gain_hbm, wqkv_hbm, assign_hbm, listed_hbm,
-    query_ref, key_ref, value_ref, wk_ref, wvt_ref, choice_ref, cells_ref,
-    gain_ref, wqkv_ref, cell_ref, listed_ref, sems,
+    x_hbm, gain_hbm, wqkv_hbm, assign_hbm, listed_hbm,
+    own_ref, query_ref, key_ref, value_ref, wk_ref, wvt_ref, choice_ref, cells_ref,
+    gain_ref, wqkv_ref, assign_ref, cell_ref, listed_ref, sems,
 ):
+    rows, width = key_ref.shape
     copies = [
         pltpu.make_async_copy(source, target, sems.at[at])
         for at, (source, target) in enumerate(
             (
+                (x_hbm, own_ref.at[pl.ds(0, rows)]),
                 (gain_hbm, gain_ref),
                 (wqkv_hbm, wqkv_ref),
+                (assign_hbm, assign_ref),
                 (assign_hbm, cell_ref),
                 (listed_hbm, listed_ref),
             )
@@ -124,14 +111,17 @@
     ]
     for copy in copies:
         copy.start()
-    rows, width = key_ref.shape
     group, members = query_ref.shape[1], query_ref.shape[2] // rows
     head = group // members
-    for copy in copies[2:]:
+    for copy in copies[3:]:
         copy.wait()
+    local = lax.rem(assign_ref[...], rows).astype(F32)
+    line = jnp.concatenate([local[:1], local[1:2]], axis=1)
+    line = jnp.broadcast_to(line, (ROWS, line.shape[1]))
+    own_ref[rows:] = jnp.where(iota(line.shape, 0) == 0, line, 0.0).astype(BF16)
     for at, number in enumerate(listed_blocks(sectors, listed_ref)):
         for candidate in range(CANDIDATES):
-            same = jnp.full((ROWS, LANES), jnp.where(number == candidate, 1.0, 0.0), F32)
+            same = jnp.full((ROWS, LANES), jnp.where(number == at + candidate, 1.0, 0.0), F32)
             choice_ref[at, candidate] = same.astype(BF16)
     lat_rows, lon_cols = cell_ref.shape
     place, node = iota((ROWS, rows), 0), iota((ROWS, rows), 1)
@@ -143,8 +133,9 @@
                 hit = jnp.where((place == row * REACH + col) & (node == cell), 1.0, hit)
         cells_ref[side * ROWS : (side + 1) * ROWS] = hit.astype(BF16)
     copies[0].wait()
+    copies[1].wait()
     normed = normalise(own_ref[:rows], gain_ref[...])
-    copies[1].wait()
+    copies[2].wait()
     query = jnp.dot(normed, wqkv_ref[:, :width], preferred_element_type=F32)
     query_t = (query * (math.log2(math.e) / head**0.5)).T.astype(BF16)
     mask = (iota((group, members * rows), 0) // head) == (iota((group, members * rows), 1) // rows)
@@ -160,19 +151,14 @@
     value_ref[...] = lax.dot_general(wvt, normed, NT, preferred_element_type=F32).astype(BF16)
 
 
-def chosen(entries, rows, choice_ref, west_ref, east_ref, beside_ref, inner_ref, outer_ref, corner_ref):
-    candidates = [west_ref[...], east_ref[...]]
-    candidates += [beside_ref[...], inner_ref[:rows], inner_ref[rows : 2 * rows]]
-    candidates.append(outer_ref[rows : 2 * rows])
-    if corner_ref is not None:
-        candidates += [outer_ref[:rows], corner_ref[...]]
-    tall, wide = rows // ROWS, west_ref.shape[1] // LANES
+def chosen(entries, rows, choice_ref, candidates):
+    tall, wide = rows // ROWS, candidates[-1].shape[1] // LANES
     near = []
     for entry in entries:
         total = None
-        for at, candidate in enumerate(candidates):
+        for at in range(CANDIDATES):
             weight = jnp.concatenate([choice_ref[entry, at]] * wide, axis=1)
-            part = candidate * jnp.concatenate([weight] * tall, axis=0)
+            part = candidates[entry + at] * jnp.concatenate([weight] * tall, axis=0)
             total = part if total is None else total + part
         near.append(total)
     return jnp.concatenate(near, axis=0)
@@ -186,13 +172,16 @@
 
 
 def early_kernel(
-    choice_ref, west_ref, east_ref, beside_ref, inner_ref, outer_ref,
+    choice_ref, west_ref, east_ref, inner_ref, center_ref,
     gain_ref, wk_ref, wvt_ref, query_ref, key_ref, value_ref,
     top_ref, sum_ref, keys_ref, values_ref,
 ):
     rows = key_ref.shape[0]
     parts, group, _ = query_ref.shape
-    nodes = chosen(range(EARLY), rows, choice_ref, west_ref, east_ref, beside_ref, inner_ref, outer_ref, None)
+    candidates = [west_ref[...], east_ref[...]]
+    candidates += [inner_ref[at * rows : (at + 1) * rows] for at in range(3)]
+    candidates.append(center_ref[...])
+    nodes = chosen(range(EARLY), rows, choice_ref, candidates)
     keys, values = project(nodes, gain_ref[...], wk_ref, wvt_ref)
     keys_ref[:rows] = key_ref[...]
     keys_ref[rows:] = keys
@@ -218,7 +207,7 @@
 
 
 def late_kernel(
-    choice_ref, cells_ref, west_ref, east_ref, beside_ref, inner_ref, outer_ref, corner_ref,
+    choice_ref, cells_ref, inner_ref, center_ref, outer_ref,
     own_ref, gain_ref, wk_ref, wvt_ref, query_ref, top_ref, sum_ref, wout_ref, wlat_ref,
     state_ref, latent_ref, first_ref, last_ref,
     attended_ref,
@@ -227,10 +216,9 @@
     parts, group, lanes = query_ref.shape
     members = lanes // rows
     head = group // members
-    entries = range(EARLY, choice_ref.shape[0])
-    nodes = chosen(
-        entries, rows, choice_ref, west_ref, east_ref, beside_ref, inner_ref, outer_ref, corner_ref
-    )
+    candidates = [None, None] + [inner_ref[at * rows : (at + 1) * rows] for at in range(3)]
+    candidates += [center_ref[...], outer_ref[:rows], outer_ref[rows : 2 * rows]]
+    nodes = chosen(range(EARLY, choice_ref.shape[0]), rows, choice_ref, candidates)
     keys, values = project(nodes, gain_ref[...], wk_ref, wvt_ref)
     ones = jnp.ones((ROWS, nodes.shape[0]), BF16)
     owner = iota((group, rows), 0) // head
@@ -390,6 +378,7 @@
     def in_hbm(*arrays):
         return [pltpu.with_memory_space_constraint(array, pltpu.HBM) for array in arrays]
 
+    center = exchanged(x, 1)
     west = shifted(x, 1)
     east = shifted(x, -1)
 
@@ -416,24 +405,12 @@
         )(taps, mixing)
         return weights, after
 
-    own = pl.pallas_call(
-        gather_kernel,
-        in_specs=[whole(pltpu.HBM)] * 2,
-        out_specs=whole(),
-        out_shape=struct(rows + ROWS, width),
-        scratch_shapes=[
-            pltpu.VMEM(assignment.shape, jnp.int32),
-            pltpu.SemaphoreType.DMA((2,)),
-        ],
-        compiler_params=params(32),
-        cost_estimate=cost(1e8, 1e6),
-        name="gather",
-    )(*in_hbm(x, assignment))
-    query, key, value, wk, wvt, choice, cells = pl.pallas_call(
+    own, query, key, value, wk, wvt, choice, cells = pl.pallas_call(
         functools.partial(prepare_kernel, sectors),
-        in_specs=[whole()] + [whole(pltpu.HBM)] * 4,
-        out_specs=[whole()] * 7,
+        in_specs=[whole(pltpu.HBM)] * 5,
+        out_specs=[whole()] * 8,
         out_shape=[
+            struct(rows + ROWS, width),
             struct(parts, LANES, members * rows),
             struct(rows, width),
             struct(width, rows),
@@ -445,27 +422,22 @@
         scratch_shapes=[
             pltpu.VMEM((1, width), F32),
             pltpu.VMEM(w_qkv.shape, BF16),
+            pltpu.VMEM(assignment.shape, jnp.int32),
             pltpu.SMEM(assignment.shape, jnp.int32),
             pltpu.SMEM(neighbours.shape, jnp.int32),
-            pltpu.SemaphoreType.DMA((4,)),
+            pltpu.SemaphoreType.DMA((6,)),
         ],
         compiler_params=params(32),
         cost_estimate=cost(2e9, 5e6),
         name="prepare",
-    )(own, *in_hbm(gain, w_qkv, assignment, neighbours))
-    east, query = lax.optimization_barrier((east, query))
-    message = jnp.concatenate([east, own], axis=0)
-    outer = exchanged(message, 1)
-    inner = exchanged(message, 0)
-    corner = exchanged(west, 1)
-    beside = exchanged(west, 0)
-    edges, beside = mixed(blocks_of(ABOVE) + blocks_of(BELOW), "mix_edges", beside)
-    beside, edges = lax.optimization_barrier((beside, edges))
-
-
+    )(*in_hbm(x, gain, w_qkv, assignment, neighbours))
+    center, west = lax.optimization_barrier((center, west))
+    center, east = lax.optimization_barrier((center, east))
+    outer = exchanged(jnp.concatenate([west, east, own[rows:]], axis=0), 1)
+    inner = exchanged(jnp.concatenate([west, east, own], axis=0), 0)
     top, summed = pl.pallas_call(
         early_kernel,
-        in_specs=[whole()] * 12,
+        in_specs=[whole()] * 11,
         out_specs=[whole()] * 2,
         out_shape=[
             struct(parts, 8, members * rows, dtype=F32),
@@ -478,10 +450,12 @@
         compiler_params=params(32),
         cost_estimate=cost(3e9, 6e6),
         name="early",
-    )(choice, west, east, beside, inner, outer, gain, wk, wvt, query, key, value)
+    )(choice, west, east, inner, center, gain, wk, wvt, query, key, value)
+    edges, top = mixed(blocks_of(ABOVE) + blocks_of(BELOW), "mix_edges", top)
+    top, edges = lax.optimization_barrier((top, edges))
     state, latent, first, last = pl.pallas_call(
         late_kernel,
-        in_specs=[whole()] * 17,
+        in_specs=[whole()] * 14,
         out_specs=[whole()] * 4,
         out_shape=[pltpu.VMEM((rows, width), BF16), struct(rows, channels)]
         + [struct(ROWS, channels)] * 2,
@@ -490,7 +464,7 @@
         cost_estimate=cost(3e9, 6e6),
         name="late",
     )(
-        choice, cells, west, east, beside, inner, outer, corner,
+        choice, cells, inner, center, outer,
         own, gain, wk, wvt, query, top, summed, w_out, w_latent,
     )
 
@@ -504,7 +478,7 @@
 
     lanes = -(-(rows + 2 * SIDE) // 256) * 256
     partial, hots, state = pl.pallas_call(
-        functools.partial(own_kernel, (rows, 2 * rows, 2 * rows)),
+        functools.partial(own_kernel, (rows, 3 * rows, 2 * rows)),
         in_specs=[whole()] * 6,
         out_specs=[whole()] * 3,
         out_shape=[

time: 35.1 us -> 34.9 us (level)
  waiting for transfers between devices: 1.15 us -> 3.58 us
  starting transfers between devices: 19.6 us -> 18.1 us
  Pallas kernels: 13.1 us -> 12.2 us
    ppermute x6 -> x5, waiting for transfers between devices: 0.36 us -> 2.63 us  [exchanged(): return lax.ppermute(array, 'reg', pairs + [(j, i) for i, j in pairs])]
    pallas_call x4 -> x3, Pallas kernels: 6.7 us -> 5.62 us  [the longest x1 2.14 us: shards(): pl.pallas_call(late_kernel, in_specs=[whole()] * 14, out_specs=[whole()]...]
    ppermute x6 -> x5, starting transfers between devices: 13.5 us -> 12.7 us  [exchanged(): return lax.ppermute(array, 'reg', pairs + [(j, i) for i, j in pairs])]
    ppermute x4, starting transfers between devices: 6.12 us -> 5.42 us  [shifted(): lax.ppermute(array, 'lon', [(i, (i + step) % sectors) for i in range(sect...]
  transfers between devices with their start and end apart: 10 -> 9, of which waited for: 4 -> 6; matrix products, arithmetic and copies ran while one was open for 0% -> 0% of each run, Pallas kernels for 27% -> 24%
where the time goes in v8:
time: 34.9 us; the launch traced here: 34.7 us
  starting transfers between devices  18.1 us (52%)
  Pallas kernels  12.2 us (35%)
  waiting for transfers between devices  3.58 us (10%)
  between operations  0.79 us (2%)
    ppermute x5, starting transfers between devices, exchanged(): return lax.ppermute(array, 'reg', pairs + [(j, i) for i, j in pairs])  12.7 us
    ppermute x4, starting transfers between devices, shifted(): lax.ppermute(array, 'lon', [(i, (i + step) % sectors) for i in range(sect...  5.42 us
    ppermute x5, waiting for transfers between devices, exchanged(): return lax.ppermute(array, 'reg', pairs + [(j, i) for i, j in pairs])  2.63 us
    pallas_call x1, Pallas kernels, shards(): pl.pallas_call(functools.partial(prepare_kernel, sectors), in_specs=[whol...  2.19 us
    pallas_call x1, Pallas kernels, shards(): pl.pallas_call(late_kernel, in_specs=[whole()] * 14, out_specs=[whole()]...  2.14 us
    pallas_call x2, Pallas kernels, mixed(): pl.pallas_call(functools.partial(mix_kernel, blocks), in_specs=[whole()]...  1.83 us
    pallas_call x1, Pallas kernels, shards(): pl.pallas_call(functools.partial(own_kernel, (rows, 3 * rows, 2 * rows)),...  1.8 us
    pallas_call x1, Pallas kernels, shards(): pl.pallas_call(early_kernel, in_specs=[whole()] * 11, out_specs=[whole()]...  1.67 us
  transfers between devices with their start and end apart: 9, of which 6 were waited for; matrix products, arithmetic and copies ran while one was open for 0% of the time, Pallas kernels for 24%

profile of v8, /device:TPU:1, one launch (start us, length us, event | category | flops | bytes accessed | tf_op | source)
XLA Modules:
  0.0 34.7 jit_solution(204170959714563533)
XLA Ops:
  0.6 3.0 %collective-permute-start.2 = (bf16[128,512]{1,0:T(8,128)(2,1)}, bf16[128,512]{1,0:T(8,128)(2,1)S(1)}, u32[]{:S(2)}, u32[]{:S(2)}) collective-permute-start(bf16[128,512]{1,0:T(8,128)(2,1)} %bitcast.14), channel_id=1, source_target_pairs={{0,3},{1,0},{2,1},{3,2},{4,7},{5,4},{6,5},{7,6},{8,11},{9,8},{10,9... | collective-permute-start | bytes 393224 | tf_op jit(solution)/shard_map/ppermute | solution.py:371
  3.7 4.0 %collective-permute-start = (bf16[128,512]{1,0:T(8,128)(2,1)}, bf16[128,512]{1,0:T(8,128)(2,1)S(1)}, u32[]{:S(2)}, u32[]{:S(2)}) collective-permute-start(bf16[128,512]{1,0:T(8,128)(2,1)} %bitcast.16), channel_id=1, source_target_pairs={{4,8},{12,16},{20,24},{8,4},{16,12},{24,20},{5,9},{13,17},{21,25},... | collective-permute-start | bytes 393224 | tf_op jit(solution)/shard_map/ppermute | solution.py:376
  7.7 2.2 %prepare.1 = (bf16[144,512]{1,0:T(8,128)(2,1)S(1)}, bf16[4,128,512]{2,1,0:T(8,128)(2,1)S(1)}, bf16[128,512]{1,0:T(8,128)(2,1)S(1)}, bf16[512,128]{1,0:T(8,128)(2...) custom-call(bf16[128,512]{1,0:T(8,128)(2,1)} %bitcast.17, ...), custom_call_target="tpu_custom_call" | custom-call | flops 2000000000 | bytes 5000000 | tf_op jit(solution)/shard_map/prepare/pallas_call | solution.py:408
  9.9 0.3 collective-permute-done.1.west_ref
  10.2 0.6 %collective-permute-done.center_ref = bf16[128,512]{1,0:T(8,128)(2,1)S(1)} collective-permute-done((bf16[128,512]{1,0:T(8,128)(2,1)}, bf16[128,512]{1,0:T(8,128)(2,1)S(1)}, u32[]{:S(2)}, u32[]{:S(2)}) %collective-permute-start) | collective-permute-done | bytes 131104 | tf_op jit(solution)/shard_map/ppermute | solution.py:376
  10.9 0.6 %collective-permute-start.3 = (bf16[400,512]{1,0:T(8,128)(2,1)S(1)}, bf16[400,512]{1,0:T(8,128)(2,1)S(1)}, u32[]{:S(2)}, u32[]{:S(2)}) collective-permute-start(bf16[400,512]{1,0:T(8,128)(2,1)S(1)} %pad_maximum_fusion), channel_id=1, source_target_pairs={{0,4},{8,12},{16,20},{24,28},{4,0},{12,8},{20,16},{28,24},{1,5},{9... | collective-permute-start | bytes 1228808 | tf_op jit(solution)/shard_map/ppermute | solution.py:376
  11.5 3.1 %collective-permute-start.4 = (bf16[272,512]{1,0:T(8,128)(2,1)S(1)}, bf16[272,512]{1,0:T(8,128)(2,1)S(1)}, u32[]{:S(2)}, u32[]{:S(2)}) collective-permute-start(bf16[272,512]{1,0:T(8,128)(2,1)S(1)} %pad_maximum_fusion.1), channel_id=1, source_target_pairs={{4,8},{12,16},{20,24},{8,4},{16,12},{24,20},{5,9},{13,17},{21,25},... | collective-permute-start | bytes 835592 | tf_op jit(solution)/shard_map/ppermute | solution.py:376
  14.7 0.0 copy-start
  14.7 0.0 copy-start.1
  14.7 1.7 %early.1 = (f32[4,8,512]{2,1,0:T(8,128)S(1)}, f32[4,144,512]{2,1,0:T(8,128)S(1)}) custom-call(bf16[4,5,16,128]{3,2,1,0:T(8,128)(2,1)S(1)} %get-tuple-element.33.choice_ref, bf16[128,512]{1,0:T(8,128)(2,1)S(1)} %collective-permute-done.1.west_ref, bf16[128,512]{1,0:T(8,128)(2,1)S(1)} %collective-permute-done.2.east_ref, ...), custom_call_target="tpu_custom_call" | custom-call | flops 3000000000 | bytes 6000000 | tf_op jit(solution)/shard_map/early/pallas_call | solution.py:438
  16.4 1.0 %mix_edges.1.weights_ref = bf16[30,96,512]{2,1,0:T(8,128)(2,1)S(1)} custom-call(f32[5,5,2,9]{3,2,1,0:T(2,128)S(1)} %bitcast.8, bf16[9,84,512]{2,1,0:T(8,128)(2,1)S(1)} %bitcast.6), custom_call_target="tpu_custom_call" | custom-call | flops 1000000000 | bytes 3000000 | tf_op jit(solution)/shard_map/mix_edges/pallas_call | solution.py:393
  17.5 1.9 %collective-permute-done.4.outer_ref = bf16[272,512]{1,0:T(8,128)(2,1)S(1)} collective-permute-done((bf16[272,512]{1,0:T(8,128)(2,1)S(1)}, bf16[272,512]{1,0:T(8,128)(2,1)S(1)}, u32[]{:S(2)}, u32[]{:S(2)}) %collective-permute-start.4) | collective-permute-done | bytes 278560 | tf_op jit(solution)/shard_map/ppermute | solution.py:376
  19.4 2.1 %late.1 = (bf16[128,512]{1,0:T(8,128)(2,1)S(1)}, bf16[128,512]{1,0:T(8,128)(2,1)S(1)}, bf16[16,512]{1,0:T(8,128)(2,1)S(1)}, bf16[16,512]{1,0:T(8,128)(2,1)S(1)}) custom-call(bf16[4,5,16,128]{3,2,1,0:T(8,128)(2,1)S(1)} %get-tuple-element.33.choice_ref, bf16[32,128]{1,0:T(8,128)(2,1)S(1)} %get-tuple-element.34.cells_ref, ...), custom_call_target="tpu_custom_call" | custom-call | flops 3000000000 | bytes 6000000 | tf_op jit(solution)/shard_map/late/pallas_call | solution.py:456
  21.5 1.2 %collective-permute-start.5 = (bf16[16,512]{1,0:T(8,128)(2,1)S(1)}, bf16[16,512]{1,0:T(8,128)(2,1)S(1)}, u32[]{:S(2)}, u32[]{:S(2)}) collective-permute-start(bf16[16,512]{1,0:T(8,128)(2,1)S(1)} %get-tuple-element.54), channel_id=1, source_target_pairs={{0,1},{1,2},{2,3},{3,0},{4,5},{5,6},{6,7},{7,4},{8,9},{9,10},{10,1... | collective-permute-start | bytes 49160 | tf_op jit(solution)/shard_map/ppermute | solution.py:371
  22.8 1.2 %collective-permute-start.6 = (bf16[16,512]{1,0:T(8,128)(2,1)S(1)}, bf16[16,512]{1,0:T(8,128)(2,1)S(1)}, u32[]{:S(2)}, u32[]{:S(2)}) collective-permute-start(bf16[16,512]{1,0:T(8,128)(2,1)S(1)} %get-tuple-element.58), channel_id=1, source_target_pairs={{0,3},{1,0},{2,1},{3,2},{4,7},{5,4},{6,5},{7,6},{8,11},{9,8},{10,9... | collective-permute-start | bytes 49160 | tf_op jit(solution)/shard_map/ppermute | solution.py:371
  23.9 0.8 %mix_own.1.weights_ref = bf16[20,96,512]{2,1,0:T(8,128)(2,1)S(1)} custom-call(f32[5,5,2,9]{3,2,1,0:T(2,128)S(1)} %bitcast.9, bf16[9,84,512]{2,1,0:T(8,128)(2,1)S(1)} %bitcast.7), custom_call_target="tpu_custom_call" | custom-call | flops 1000000000 | bytes 3000000 | tf_op jit(solution)/shard_map/mix_own/pallas_call | solution.py:393
  24.7 0.3 collective-permute-done.5
  25.0 0.3 collective-permute-done.6
  25.4 0.1 collective-permute-start.8
  25.5 4.9 %collective-permute-start.7 = (bf16[144,512]{1,0:T(8,128)(2,1)S(1)}, bf16[144,512]{1,0:T(8,128)(2,1)S(1)}, u32[]{:S(2)}, u32[]{:S(2)}) collective-permute-start(bf16[144,512]{1,0:T(8,128)(2,1)S(1)} %pad_maximum_fusion.2.latent_ref), channel_id=1, source_target_pairs={{4,8},{12,16},{20,24},{8,4},{16,12},{24,20},{5,9},{13,17},{21,25},... | collective-permute-start | bytes 442376 | tf_op jit(solution)/shard_map/ppermute | solution.py:376
  30.3 1.8 %own_band.1 = (f32[2,96,256]{2,1,0:T(8,128)S(1)}, bf16[2,2,5,256,256]{4,3,2,1,0:T(8,128)(2,1)S(1)}, bf16[128,512]{1,0:T(8,128)(2,1)}) custom-call(bf16[128,512]{1,0:T(8,128)(2,1)S(1)} %get-tuple-element.51.state_ref, bf16[144,512]{1,0:T(8,128)(2,1)S(1)} %get-tuple-element.38.own_ref, bf16[400,512]{1,0:T(8,128)(2,1)S(1)} %collective-permute-done.3.inner_ref, ...), custom_call_target="tpu_custom_call" | custom-call | flops 1000000000 | bytes 2500000 | tf_op jit(solution)/shard_map/own_band/pallas_call | solution.py:480
  32.1 0.9 %inner_band.1.partial_ref = f32[2,96,256]{2,1,0:T(8,128)S(1)} custom-call(bf16[144,512]{1,0:T(8,128)(2,1)S(1)} %collective-permute-done.8.latent_ref, bf16[30,96,512]{2,1,0:T(8,128)(2,1)S(1)} %mix_edges.1.weights_ref, bf16[2,2,5,256,256]{4,3,2,1,0:T(8,128)(2,1)S(1)} %get-tuple-element.62.hot_ref, f32[2,96,256]{2,1,0:T(8,128)S(1)} %get-tuple-element.63.partial_ref), custom_call_target="tpu_custom_call" | custom-call | flops 1000000000 | bytes 2500000 | tf_op jit(solution)/shard_map/inner_band/pallas_call | solution.py:497
  33.1 0.1 collective-permute-done.7.latent_ref
  33.1 1.6 %outer_band.1 = bf16[84,2,256]{2,1,0:T(2,128)(2,1)} custom-call(bf16[144,512]{1,0:T(8,128)(2,1)S(1)} %collective-permute-done.7.latent_ref, bf16[30,96,512]{2,1,0:T(8,128)(2,1)S(1)} %mix_edges.1.weights_ref, bf16[2,2,5,256,256]{4,3,2,1,0:T(8,128)(2,1)S(1)} %get-tuple-element.62.hot_ref, f32[2,96,256]{2,1,0:T(8,128)S(1)} %inner_band.1.partial_ref), custom_call_target="tpu_custom_call" | custom-call | flops 1000000000 | bytes 2500000 | tf_op jit(solution)/shard_map/outer_band/pallas_call | solution.py:507
  (18 shorter events, 0.1 us)
Async XLA Ops:
  0.6 10.2 %collective-permute-start.2 = (bf16[128,512]{1,0:T(8,128)(2,1)}, bf16[128,512]{1,0:T(8,128)(2,1)S(1)}, u32[]{:S(2)}, u32[]{:S(2)}) collective-permute-start(bf16[128,512]{1,0:T(8,128)(2,1)} %bitcast.14), channel_id=1, source_target_pairs={{0,3},{1,0},{2,1},{3,2},{4,7},{5,4},{6,5},{7,6},{8,11},{9,8},{10,9... | collective-permute-start | bytes 393224 | tf_op jit(solution)/shard_map/ppermute | solution.py:371
  3.7 6.6 %collective-permute-start.1 = (bf16[128,512]{1,0:T(8,128)(2,1)}, bf16[128,512]{1,0:T(8,128)(2,1)S(1)}, u32[]{:S(2)}, u32[]{:S(2)}) collective-permute-start(bf16[128,512]{1,0:T(8,128)(2,1)} %bitcast.15), channel_id=1, source_target_pairs={{0,1},{1,2},{2,3},{3,0},{4,5},{5,6},{6,7},{7,4},{8,9},{9,10},{10,1... | collective-permute-start | bytes 393224 | tf_op jit(solution)/shard_map/ppermute | solution.py:371
  3.7 7.2 %collective-permute-start = (bf16[128,512]{1,0:T(8,128)(2,1)}, bf16[128,512]{1,0:T(8,128)(2,1)S(1)}, u32[]{:S(2)}, u32[]{:S(2)}) collective-permute-start(bf16[128,512]{1,0:T(8,128)(2,1)} %bitcast.16), channel_id=1, source_target_pairs={{4,8},{12,16},{20,24},{8,4},{16,12},{24,20},{5,9},{13,17},{21,25},... | collective-permute-start | bytes 393224 | tf_op jit(solution)/shard_map/ppermute | solution.py:376
  7.7 6.9 %copy-start.4 = (f32[512]{0:T(512)S(1)}, f32[512]{0:T(512)}, u32[]{:S(2)}) copy-start(f32[512]{0:T(512)} %param.10) | copy-start | bytes 6148
  10.9 3.8 %collective-permute-start.3 = (bf16[400,512]{1,0:T(8,128)(2,1)S(1)}, bf16[400,512]{1,0:T(8,128)(2,1)S(1)}, u32[]{:S(2)}, u32[]{:S(2)}) collective-permute-start(bf16[400,512]{1,0:T(8,128)(2,1)S(1)} %pad_maximum_fusion), channel_id=1, source_target_pairs={{0,4},{8,12},{16,20},{24,28},{4,0},{12,8},{20,16},{28,24},{1,5},{9... | collective-permute-start | bytes 1228808 | tf_op jit(solution)/shard_map/ppermute | solution.py:376
  11.5 7.9 %collective-permute-start.4 = (bf16[272,512]{1,0:T(8,128)(2,1)S(1)}, bf16[272,512]{1,0:T(8,128)(2,1)S(1)}, u32[]{:S(2)}, u32[]{:S(2)}) collective-permute-start(bf16[272,512]{1,0:T(8,128)(2,1)S(1)} %pad_maximum_fusion.1), channel_id=1, source_target_pairs={{4,8},{12,16},{20,24},{8,4},{16,12},{24,20},{5,9},{13,17},{21,25},... | collective-permute-start | bytes 835592 | tf_op jit(solution)/shard_map/ppermute | solution.py:376
  14.7 1.7 %copy-start = (bf16[9,512,84]{1,2,0:T(8,128)(2,1)S(1)}, bf16[9,512,84]{1,2,0:T(8,128)(2,1)}, u32[]{:S(2)}) copy-start(bf16[9,512,84]{1,2,0:T(8,128)(2,1)} %param.17) | copy-start | bytes 2322436
  14.7 1.7 %copy-start.1 = (f32[9,2,5,5]{0,1,3,2:T(2,128)S(1)}, f32[9,2,5,5]{0,1,3,2:T(2,128)}, u32[]{:S(2)}) copy-start(f32[9,2,5,5]{0,1,3,2:T(2,128)} %param.16) | copy-start | bytes 5404
  16.4 3.0 %copy-start.2 = (bf16[512,512]{1,0:T(8,128)(2,1)S(1)}, bf16[512,512]{1,0:T(8,128)(2,1)}, u32[]{:S(2)}) copy-start(bf16[512,512]{1,0:T(8,128)(2,1)} %wout_ref.1) | copy-start | bytes 1572868
  16.4 3.0 %copy-start.3 = (bf16[512,512]{1,0:T(8,128)(2,1)S(1)}, bf16[512,512]{1,0:T(8,128)(2,1)}, u32[]{:S(2)}) copy-start(bf16[512,512]{1,0:T(8,128)(2,1)} %wlat_ref.1) | copy-start | bytes 1572868
  21.5 3.5 %collective-permute-start.5 = (bf16[16,512]{1,0:T(8,128)(2,1)S(1)}, bf16[16,512]{1,0:T(8,128)(2,1)S(1)}, u32[]{:S(2)}, u32[]{:S(2)}) collective-permute-start(bf16[16,512]{1,0:T(8,128)(2,1)S(1)} %get-tuple-element.54), channel_id=1, source_target_pairs={{0,1},{1,2},{2,3},{3,0},{4,5},{5,6},{6,7},{7,4},{8,9},{9,10},{10,1... | collective-permute-start | bytes 49160 | tf_op jit(solution)/shard_map/ppermute | solution.py:371
  22.8 2.6 %collective-permute-start.6 = (bf16[16,512]{1,0:T(8,128)(2,1)S(1)}, bf16[16,512]{1,0:T(8,128)(2,1)S(1)}, u32[]{:S(2)}, u32[]{:S(2)}) collective-permute-start(bf16[16,512]{1,0:T(8,128)(2,1)S(1)} %get-tuple-element.58), channel_id=1, source_target_pairs={{0,3},{1,0},{2,1},{3,2},{4,7},{5,4},{6,5},{7,6},{8,11},{9,8},{10,9... | collective-permute-start | bytes 49160 | tf_op jit(solution)/shard_map/ppermute | solution.py:371
  25.4 6.8 %collective-permute-start.8 = (bf16[144,512]{1,0:T(8,128)(2,1)S(1)}, bf16[144,512]{1,0:T(8,128)(2,1)S(1)}, u32[]{:S(2)}, u32[]{:S(2)}) collective-permute-start(bf16[144,512]{1,0:T(8,128)(2,1)S(1)} %pad_maximum_fusion.2.latent_ref), channel_id=1, source_target_pairs={{0,4},{8,12},{16,20},{24,28},{4,0},{12,8},{20,16},{28,24},{1,5},{9... | collective-permute-start | bytes 442376 | tf_op jit(solution)/shard_map/ppermute | solution.py:376
  25.5 7.7 %collective-permute-start.7 = (bf16[144,512]{1,0:T(8,128)(2,1)S(1)}, bf16[144,512]{1,0:T(8,128)(2,1)S(1)}, u32[]{:S(2)}, u32[]{:S(2)}) collective-permute-start(bf16[144,512]{1,0:T(8,128)(2,1)S(1)} %pad_maximum_fusion.2.latent_ref), channel_id=1, source_target_pairs={{4,8},{12,16},{20,24},{8,4},{16,12},{24,20},{5,9},{13,17},{21,25},... | collective-permute-start | bytes 442376 | tf_op jit(solution)/shard_map/ppermute | solution.py:376

commit v9 on v8

--- a/solution.py
+++ b/solution.py
@@ -222,6 +222,7 @@
     keys, values = project(nodes, gain_ref[...], wk_ref, wvt_ref)
     ones = jnp.ones((ROWS, nodes.shape[0]), BF16)
     owner = iota((group, rows), 0) // head
+    state = own_ref[:rows].astype(F32)
 
     def scored(part):
         span = slice(part * group, (part + 1) * group)
@@ -244,10 +245,12 @@
             piece = summed[:, member * rows : (member + 1) * rows]
             merged = piece if merged is None else jnp.where(owner == member, piece, merged)
         attended_ref[:, part * group : (part + 1) * group] = merged.T.astype(BF16)
-    state = (
-        own_ref[:rows].astype(F32)
-        + jnp.dot(attended_ref[...], wout_ref[...], preferred_element_type=F32)
-    ).astype(BF16)
+        if part % 2:
+            span = slice((part - 1) * group, (part + 1) * group)
+            state = state + jnp.dot(
+                attended_ref[:, span], wout_ref[span, :], preferred_element_type=F32
+            )
+    state = state.astype(BF16)
     state_ref[...] = state
     value = jnp.dot(state, wlat_ref[...], preferred_element_type=F32)
     latent = (value / (1.0 + jnp.exp(-value))).astype(BF16)
@@ -332,13 +335,19 @@
     depth = TAPS * lanes
     one = jnp.dot(one_ref[...], hot_ref[band, 0].reshape(depth, cols), preferred_element_type=F32)
     two = jnp.dot(two_ref[...], hot_ref[band, 1].reshape(depth, cols), preferred_element_type=F32)
+    totals = []
     for row in range(2):
         total = partial_ref[row] + two[row * outputs : (row + 1) * outputs]
-        total = total + jnp.where(band == row, one, 0.0)
-        if from_inner:
-            out_ref[row] = total
-        else:
-            out_ref[:, row, :] = total[: out_ref.shape[0]].astype(BF16)
+        totals.append(total + jnp.where(band == row, one, 0.0))
+    if from_inner:
+        out_ref[0], out_ref[1] = totals
+    else:
+        out_ch = out_ref.shape[0]
+        rounded = jnp.concatenate(totals, axis=0).astype(BF16)
+        place, source = iota((2 * out_ch, 2 * outputs), 0), iota((2 * out_ch, 2 * outputs), 1)
+        order = (source == place % 2 * outputs + place // 2).astype(F32).astype(BF16)
+        paired = jnp.dot(order, rounded, preferred_element_type=F32).astype(BF16)
+        out_ref[...] = paired.reshape(out_ref.shape)
 
 
 def whole(memory=pltpu.VMEM):

time: 34.9 us -> 35.3 us (1.011)
  Pallas kernels: 12.2 us -> 12.6 us
where the time goes in v9:
time: 35.3 us; the launch traced here: 35.1 us
  starting transfers between devices  18.1 us (51%)
  Pallas kernels  12.6 us (36%)
  waiting for transfers between devices  3.58 us (10%)
  between operations  0.79 us (2%)
    ppermute x5, starting transfers between devices, exchanged(): return lax.ppermute(array, 'reg', pairs + [(j, i) for i, j in pairs])  12.7 us
    ppermute x4, starting transfers between devices, shifted(): lax.ppermute(array, 'lon', [(i, (i + step) % sectors) for i in range(sect...  5.42 us
    ppermute x5, waiting for transfers between devices, exchanged(): return lax.ppermute(array, 'reg', pairs + [(j, i) for i, j in pairs])  2.63 us
    pallas_call x1, Pallas kernels, shards(): pl.pallas_call(late_kernel, in_specs=[whole()] * 14, out_specs=[whole()]...  2.4 us
    pallas_call x1, Pallas kernels, shards(): pl.pallas_call(functools.partial(prepare_kernel, sectors), in_specs=[whol...  2.19 us
    pallas_call x2, Pallas kernels, mixed(): pl.pallas_call(functools.partial(mix_kernel, blocks), in_specs=[whole()]...  1.83 us
    pallas_call x1, Pallas kernels, shards(): pl.pallas_call(functools.partial(own_kernel, (rows, 3 * rows, 2 * rows)),...  1.8 us
    pallas_call x1, Pallas kernels, shards(): pl.pallas_call(functools.partial(band_kernel, False), in_specs=[whole()]...  1.75 us
  transfers between devices with their start and end apart: 9, of which 6 were waited for; matrix products, arithmetic and copies ran while one was open for 0% of the time, Pallas kernels for 24%

profile of v9, /device:TPU:1, one launch (start us, length us, event | category | flops | bytes accessed | tf_op | source)
XLA Modules:
  0.0 35.1 jit_solution(9745759531910559714)
XLA Ops:
  0.6 3.0 %collective-permute-start.2 = (bf16[128,512]{1,0:T(8,128)(2,1)}, bf16[128,512]{1,0:T(8,128)(2,1)S(1)}, u32[]{:S(2)}, u32[]{:S(2)}) collective-permute-start(bf16[128,512]{1,0:T(8,128)(2,1)} %bitcast.14), channel_id=1, source_target_pairs={{0,3},{1,0},{2,1},{3,2},{4,7},{5,4},{6,5},{7,6},{8,11},{9,8},{10,9... | collective-permute-start | bytes 393224 | tf_op jit(solution)/shard_map/ppermute | solution.py:380
  3.7 4.0 %collective-permute-start = (bf16[128,512]{1,0:T(8,128)(2,1)}, bf16[128,512]{1,0:T(8,128)(2,1)S(1)}, u32[]{:S(2)}, u32[]{:S(2)}) collective-permute-start(bf16[128,512]{1,0:T(8,128)(2,1)} %bitcast.16), channel_id=1, source_target_pairs={{4,8},{12,16},{20,24},{8,4},{16,12},{24,20},{5,9},{13,17},{21,25},... | collective-permute-start | bytes 393224 | tf_op jit(solution)/shard_map/ppermute | solution.py:385
  7.7 2.2 %prepare.1 = (bf16[144,512]{1,0:T(8,128)(2,1)S(1)}, bf16[4,128,512]{2,1,0:T(8,128)(2,1)S(1)}, bf16[128,512]{1,0:T(8,128)(2,1)S(1)}, bf16[512,128]{1,0:T(8,128)(2...) custom-call(bf16[128,512]{1,0:T(8,128)(2,1)} %bitcast.17, ...), custom_call_target="tpu_custom_call" | custom-call | flops 2000000000 | bytes 5000000 | tf_op jit(solution)/shard_map/prepare/pallas_call | solution.py:417
  9.9 0.3 collective-permute-done.1.west_ref
  10.2 0.6 %collective-permute-done.center_ref = bf16[128,512]{1,0:T(8,128)(2,1)S(1)} collective-permute-done((bf16[128,512]{1,0:T(8,128)(2,1)}, bf16[128,512]{1,0:T(8,128)(2,1)S(1)}, u32[]{:S(2)}, u32[]{:S(2)}) %collective-permute-start) | collective-permute-done | bytes 131104 | tf_op jit(solution)/shard_map/ppermute | solution.py:385
  10.9 0.6 %collective-permute-start.3 = (bf16[400,512]{1,0:T(8,128)(2,1)S(1)}, bf16[400,512]{1,0:T(8,128)(2,1)S(1)}, u32[]{:S(2)}, u32[]{:S(2)}) collective-permute-start(bf16[400,512]{1,0:T(8,128)(2,1)S(1)} %pad_maximum_fusion), channel_id=1, source_target_pairs={{0,4},{8,12},{16,20},{24,28},{4,0},{12,8},{20,16},{28,24},{1,5},{9... | collective-permute-start | bytes 1228808 | tf_op jit(solution)/shard_map/ppermute | solution.py:385
  11.5 3.1 %collective-permute-start.4 = (bf16[272,512]{1,0:T(8,128)(2,1)S(1)}, bf16[272,512]{1,0:T(8,128)(2,1)S(1)}, u32[]{:S(2)}, u32[]{:S(2)}) collective-permute-start(bf16[272,512]{1,0:T(8,128)(2,1)S(1)} %pad_maximum_fusion.1), channel_id=1, source_target_pairs={{4,8},{12,16},{20,24},{8,4},{16,12},{24,20},{5,9},{13,17},{21,25},... | collective-permute-start | bytes 835592 | tf_op jit(solution)/shard_map/ppermute | solution.py:385
  14.7 0.0 copy-start
  14.7 0.0 copy-start.1
  14.7 1.7 %early.1 = (f32[4,8,512]{2,1,0:T(8,128)S(1)}, f32[4,144,512]{2,1,0:T(8,128)S(1)}) custom-call(bf16[4,5,16,128]{3,2,1,0:T(8,128)(2,1)S(1)} %get-tuple-element.33.choice_ref, bf16[128,512]{1,0:T(8,128)(2,1)S(1)} %collective-permute-done.1.west_ref, bf16[128,512]{1,0:T(8,128)(2,1)S(1)} %collective-permute-done.2.east_ref, ...), custom_call_target="tpu_custom_call" | custom-call | flops 3000000000 | bytes 6000000 | tf_op jit(solution)/shard_map/early/pallas_call | solution.py:447
  16.4 1.0 %mix_edges.1.weights_ref = bf16[30,96,512]{2,1,0:T(8,128)(2,1)S(1)} custom-call(f32[5,5,2,9]{3,2,1,0:T(2,128)S(1)} %bitcast.8, bf16[9,84,512]{2,1,0:T(8,128)(2,1)S(1)} %bitcast.6), custom_call_target="tpu_custom_call" | custom-call | flops 1000000000 | bytes 3000000 | tf_op jit(solution)/shard_map/mix_edges/pallas_call | solution.py:402
  17.5 1.9 %collective-permute-done.4.outer_ref = bf16[272,512]{1,0:T(8,128)(2,1)S(1)} collective-permute-done((bf16[272,512]{1,0:T(8,128)(2,1)S(1)}, bf16[272,512]{1,0:T(8,128)(2,1)S(1)}, u32[]{:S(2)}, u32[]{:S(2)}) %collective-permute-start.4) | collective-permute-done | bytes 278560 | tf_op jit(solution)/shard_map/ppermute | solution.py:385
  19.4 2.4 %late.1 = (bf16[128,512]{1,0:T(8,128)(2,1)S(1)}, bf16[128,512]{1,0:T(8,128)(2,1)S(1)}, bf16[16,512]{1,0:T(8,128)(2,1)S(1)}, bf16[16,512]{1,0:T(8,128)(2,1)S(1)}) custom-call(bf16[4,5,16,128]{3,2,1,0:T(8,128)(2,1)S(1)} %get-tuple-element.33.choice_ref, bf16[32,128]{1,0:T(8,128)(2,1)S(1)} %get-tuple-element.34.cells_ref, ...), custom_call_target="tpu_custom_call" | custom-call | flops 3000000000 | bytes 6000000 | tf_op jit(solution)/shard_map/late/pallas_call | solution.py:465
  21.8 1.2 %collective-permute-start.5 = (bf16[16,512]{1,0:T(8,128)(2,1)S(1)}, bf16[16,512]{1,0:T(8,128)(2,1)S(1)}, u32[]{:S(2)}, u32[]{:S(2)}) collective-permute-start(bf16[16,512]{1,0:T(8,128)(2,1)S(1)} %get-tuple-element.54), channel_id=1, source_target_pairs={{0,1},{1,2},{2,3},{3,0},{4,5},{5,6},{6,7},{7,4},{8,9},{9,10},{10,1... | collective-permute-start | bytes 49160 | tf_op jit(solution)/shard_map/ppermute | solution.py:380
  23.0 1.2 %collective-permute-start.6 = (bf16[16,512]{1,0:T(8,128)(2,1)S(1)}, bf16[16,512]{1,0:T(8,128)(2,1)S(1)}, u32[]{:S(2)}, u32[]{:S(2)}) collective-permute-start(bf16[16,512]{1,0:T(8,128)(2,1)S(1)} %get-tuple-element.58), channel_id=1, source_target_pairs={{0,3},{1,0},{2,1},{3,2},{4,7},{5,4},{6,5},{7,6},{8,11},{9,8},{10,9... | collective-permute-start | bytes 49160 | tf_op jit(solution)/shard_map/ppermute | solution.py:380
  24.2 0.8 %mix_own.1.weights_ref = bf16[20,96,512]{2,1,0:T(8,128)(2,1)S(1)} custom-call(f32[5,5,2,9]{3,2,1,0:T(2,128)S(1)} %bitcast.9, bf16[9,84,512]{2,1,0:T(8,128)(2,1)S(1)} %bitcast.7), custom_call_target="tpu_custom_call" | custom-call | flops 1000000000 | bytes 3000000 | tf_op jit(solution)/shard_map/mix_own/pallas_call | solution.py:402
  25.0 0.3 collective-permute-done.5
  25.3 0.3 collective-permute-done.6
  25.6 0.1 collective-permute-start.8
  25.7 4.9 %collective-permute-start.7 = (bf16[144,512]{1,0:T(8,128)(2,1)S(1)}, bf16[144,512]{1,0:T(8,128)(2,1)S(1)}, u32[]{:S(2)}, u32[]{:S(2)}) collective-permute-start(bf16[144,512]{1,0:T(8,128)(2,1)S(1)} %pad_maximum_fusion.2.latent_ref), channel_id=1, source_target_pairs={{4,8},{12,16},{20,24},{8,4},{16,12},{24,20},{5,9},{13,17},{21,25},... | collective-permute-start | bytes 442376 | tf_op jit(solution)/shard_map/ppermute | solution.py:385
  30.6 1.8 %own_band.1 = (f32[2,96,256]{2,1,0:T(8,128)S(1)}, bf16[2,2,5,256,256]{4,3,2,1,0:T(8,128)(2,1)S(1)}, bf16[128,512]{1,0:T(8,128)(2,1)}) custom-call(bf16[128,512]{1,0:T(8,128)(2,1)S(1)} %get-tuple-element.51.state_ref, bf16[144,512]{1,0:T(8,128)(2,1)S(1)} %get-tuple-element.38.own_ref, bf16[400,512]{1,0:T(8,128)(2,1)S(1)} %collective-permute-done.3.inner_ref, ...), custom_call_target="tpu_custom_call" | custom-call | flops 1000000000 | bytes 2500000 | tf_op jit(solution)/shard_map/own_band/pallas_call | solution.py:489
  32.4 0.9 %inner_band.1.partial_ref = f32[2,96,256]{2,1,0:T(8,128)S(1)} custom-call(bf16[144,512]{1,0:T(8,128)(2,1)S(1)} %collective-permute-done.8.latent_ref, bf16[30,96,512]{2,1,0:T(8,128)(2,1)S(1)} %mix_edges.1.weights_ref, bf16[2,2,5,256,256]{4,3,2,1,0:T(8,128)(2,1)S(1)} %get-tuple-element.62.hot_ref, f32[2,96,256]{2,1,0:T(8,128)S(1)} %get-tuple-element.63.partial_ref), custom_call_target="tpu_custom_call" | custom-call | flops 1000000000 | bytes 2500000 | tf_op jit(solution)/shard_map/inner_band/pallas_call | solution.py:506
  33.3 0.1 collective-permute-done.7.latent_ref
  33.4 1.7 %outer_band.1 = bf16[84,2,256]{2,1,0:T(2,128)(2,1)} custom-call(bf16[144,512]{1,0:T(8,128)(2,1)S(1)} %collective-permute-done.7.latent_ref, bf16[30,96,512]{2,1,0:T(8,128)(2,1)S(1)} %mix_edges.1.weights_ref, bf16[2,2,5,256,256]{4,3,2,1,0:T(8,128)(2,1)S(1)} %get-tuple-element.62.hot_ref, f32[2,96,256]{2,1,0:T(8,128)S(1)} %inner_band.1.partial_ref), custom_call_target="tpu_custom_call" | custom-call | flops 1000000000 | bytes 2500000 | tf_op jit(solution)/shard_map/outer_band/pallas_call | solution.py:516
  (18 shorter events, 0.1 us)
Async XLA Ops:
  0.6 10.2 %collective-permute-start.2 = (bf16[128,512]{1,0:T(8,128)(2,1)}, bf16[128,512]{1,0:T(8,128)(2,1)S(1)}, u32[]{:S(2)}, u32[]{:S(2)}) collective-permute-start(bf16[128,512]{1,0:T(8,128)(2,1)} %bitcast.14), channel_id=1, source_target_pairs={{0,3},{1,0},{2,1},{3,2},{4,7},{5,4},{6,5},{7,6},{8,11},{9,8},{10,9... | collective-permute-start | bytes 393224 | tf_op jit(solution)/shard_map/ppermute | solution.py:380
  3.7 6.6 %collective-permute-start.1 = (bf16[128,512]{1,0:T(8,128)(2,1)}, bf16[128,512]{1,0:T(8,128)(2,1)S(1)}, u32[]{:S(2)}, u32[]{:S(2)}) collective-permute-start(bf16[128,512]{1,0:T(8,128)(2,1)} %bitcast.15), channel_id=1, source_target_pairs={{0,1},{1,2},{2,3},{3,0},{4,5},{5,6},{6,7},{7,4},{8,9},{9,10},{10,1... | collective-permute-start | bytes 393224 | tf_op jit(solution)/shard_map/ppermute | solution.py:380
  3.7 7.2 %collective-permute-start = (bf16[128,512]{1,0:T(8,128)(2,1)}, bf16[128,512]{1,0:T(8,128)(2,1)S(1)}, u32[]{:S(2)}, u32[]{:S(2)}) collective-permute-start(bf16[128,512]{1,0:T(8,128)(2,1)} %bitcast.16), channel_id=1, source_target_pairs={{4,8},{12,16},{20,24},{8,4},{16,12},{24,20},{5,9},{13,17},{21,25},... | collective-permute-start | bytes 393224 | tf_op jit(solution)/shard_map/ppermute | solution.py:385
  7.7 6.9 %copy-start.4 = (f32[512]{0:T(512)S(1)}, f32[512]{0:T(512)}, u32[]{:S(2)}) copy-start(f32[512]{0:T(512)} %param.10) | copy-start | bytes 6148
  10.9 3.8 %collective-permute-start.3 = (bf16[400,512]{1,0:T(8,128)(2,1)S(1)}, bf16[400,512]{1,0:T(8,128)(2,1)S(1)}, u32[]{:S(2)}, u32[]{:S(2)}) collective-permute-start(bf16[400,512]{1,0:T(8,128)(2,1)S(1)} %pad_maximum_fusion), channel_id=1, source_target_pairs={{0,4},{8,12},{16,20},{24,28},{4,0},{12,8},{20,16},{28,24},{1,5},{9... | collective-permute-start | bytes 1228808 | tf_op jit(solution)/shard_map/ppermute | solution.py:385
  11.5 7.9 %collective-permute-start.4 = (bf16[272,512]{1,0:T(8,128)(2,1)S(1)}, bf16[272,512]{1,0:T(8,128)(2,1)S(1)}, u32[]{:S(2)}, u32[]{:S(2)}) collective-permute-start(bf16[272,512]{1,0:T(8,128)(2,1)S(1)} %pad_maximum_fusion.1), channel_id=1, source_target_pairs={{4,8},{12,16},{20,24},{8,4},{16,12},{24,20},{5,9},{13,17},{21,25},... | collective-permute-start | bytes 835592 | tf_op jit(solution)/shard_map/ppermute | solution.py:385
  14.7 1.7 %copy-start = (bf16[9,512,84]{1,2,0:T(8,128)(2,1)S(1)}, bf16[9,512,84]{1,2,0:T(8,128)(2,1)}, u32[]{:S(2)}) copy-start(bf16[9,512,84]{1,2,0:T(8,128)(2,1)} %param.17) | copy-start | bytes 2322436
  14.7 1.7 %copy-start.1 = (f32[9,2,5,5]{0,1,3,2:T(2,128)S(1)}, f32[9,2,5,5]{0,1,3,2:T(2,128)}, u32[]{:S(2)}) copy-start(f32[9,2,5,5]{0,1,3,2:T(2,128)} %param.16) | copy-start | bytes 5404
  16.4 3.0 %copy-start.2 = (bf16[512,512]{1,0:T(8,128)(2,1)S(1)}, bf16[512,512]{1,0:T(8,128)(2,1)}, u32[]{:S(2)}) copy-start(bf16[512,512]{1,0:T(8,128)(2,1)} %wout_ref.1) | copy-start | bytes 1572868
  16.4 3.0 %copy-start.3 = (bf16[512,512]{1,0:T(8,128)(2,1)S(1)}, bf16[512,512]{1,0:T(8,128)(2,1)}, u32[]{:S(2)}) copy-start(bf16[512,512]{1,0:T(8,128)(2,1)} %wlat_ref.1) | copy-start | bytes 1572868
  21.8 3.5 %collective-permute-start.5 = (bf16[16,512]{1,0:T(8,128)(2,1)S(1)}, bf16[16,512]{1,0:T(8,128)(2,1)S(1)}, u32[]{:S(2)}, u32[]{:S(2)}) collective-permute-start(bf16[16,512]{1,0:T(8,128)(2,1)S(1)} %get-tuple-element.54), channel_id=1, source_target_pairs={{0,1},{1,2},{2,3},{3,0},{4,5},{5,6},{6,7},{7,4},{8,9},{9,10},{10,1... | collective-permute-start | bytes 49160 | tf_op jit(solution)/shard_map/ppermute | solution.py:380
  23.0 2.6 %collective-permute-start.6 = (bf16[16,512]{1,0:T(8,128)(2,1)S(1)}, bf16[16,512]{1,0:T(8,128)(2,1)S(1)}, u32[]{:S(2)}, u32[]{:S(2)}) collective-permute-start(bf16[16,512]{1,0:T(8,128)(2,1)S(1)} %get-tuple-element.58), channel_id=1, source_target_pairs={{0,3},{1,0},{2,1},{3,2},{4,7},{5,4},{6,5},{7,6},{8,11},{9,8},{10,9... | collective-permute-start | bytes 49160 | tf_op jit(solution)/shard_map/ppermute | solution.py:380
  25.6 6.8 %collective-permute-start.8 = (bf16[144,512]{1,0:T(8,128)(2,1)S(1)}, bf16[144,512]{1,0:T(8,128)(2,1)S(1)}, u32[]{:S(2)}, u32[]{:S(2)}) collective-permute-start(bf16[144,512]{1,0:T(8,128)(2,1)S(1)} %pad_maximum_fusion.2.latent_ref), channel_id=1, source_target_pairs={{0,4},{8,12},{16,20},{24,28},{4,0},{12,8},{20,16},{28,24},{1,5},{9... | collective-permute-start | bytes 442376 | tf_op jit(solution)/shard_map/ppermute | solution.py:385
  25.7 7.7 %collective-permute-start.7 = (bf16[144,512]{1,0:T(8,128)(2,1)S(1)}, bf16[144,512]{1,0:T(8,128)(2,1)S(1)}, u32[]{:S(2)}, u32[]{:S(2)}) collective-permute-start(bf16[144,512]{1,0:T(8,128)(2,1)S(1)} %pad_maximum_fusion.2.latent_ref), channel_id=1, source_target_pairs={{4,8},{12,16},{20,24},{8,4},{16,12},{24,20},{5,9},{13,17},{21,25},... | collective-permute-start | bytes 442376 | tf_op jit(solution)/shard_map/ppermute | solution.py:385

commit v10 on v7

--- a/solution.py
+++ b/solution.py
@@ -15,7 +15,7 @@
 ROWS = 16
 LANES = 128
 EARLY = 2
-CANDIDATES = 8
+CANDIDATES = 5
 F32 = jnp.float32
 BF16 = jnp.bfloat16
 NT = (((1,), (1,)), ((), ()))
@@ -79,9 +79,10 @@
         block = listed_ref[0, at]
         step_reg = (block // sectors - reg_here) * toward
         step_lon = (block % sectors - lon_here + 1 + sectors) % sectors - 1
-        place = jnp.where(step_lon == 0, 2, jnp.where(step_lon < 0, 0, 1))
-        outer = jnp.where(step_lon == 0, 5, 7 - place)
-        found.append(jnp.where(step_reg == 0, place, jnp.where(step_reg > 0, 2 + place, outer)))
+        side = jnp.where(step_lon == 0, 0, jnp.where(step_lon > 0, 1, 4))
+        ahead = jnp.where(step_lon < 0, 0, 1)
+        behind = jnp.where(step_lon < 0, 7, 4 + side)
+        found.append(jnp.where(step_reg == 0, ahead, jnp.where(step_reg > 0, 2 + side, behind)))
     for low in range(len(found)):
         for high in range(low + 1, len(found)):
             less, more = jnp.minimum(found[low], found[high]), jnp.maximum(found[low], found[high])
@@ -131,7 +132,7 @@
         copy.wait()
     for at, number in enumerate(listed_blocks(sectors, listed_ref)):
         for candidate in range(CANDIDATES):
-            same = jnp.full((ROWS, LANES), jnp.where(number == candidate, 1.0, 0.0), F32)
+            same = jnp.full((ROWS, LANES), jnp.where(number == at + candidate, 1.0, 0.0), F32)
             choice_ref[at, candidate] = same.astype(BF16)
     lat_rows, lon_cols = cell_ref.shape
     place, node = iota((ROWS, rows), 0), iota((ROWS, rows), 1)
@@ -160,19 +161,14 @@
     value_ref[...] = lax.dot_general(wvt, normed, NT, preferred_element_type=F32).astype(BF16)
 
 
-def chosen(entries, rows, choice_ref, west_ref, east_ref, beside_ref, inner_ref, outer_ref, corner_ref):
-    candidates = [west_ref[...], east_ref[...]]
-    candidates += [beside_ref[...], inner_ref[:rows], inner_ref[rows : 2 * rows]]
-    candidates.append(outer_ref[rows : 2 * rows])
-    if corner_ref is not None:
-        candidates += [outer_ref[:rows], corner_ref[...]]
-    tall, wide = rows // ROWS, west_ref.shape[1] // LANES
+def chosen(entries, rows, choice_ref, candidates):
+    tall, wide = rows // ROWS, candidates[-1].shape[1] // LANES
     near = []
     for entry in entries:
         total = None
-        for at, candidate in enumerate(candidates):
+        for at in range(CANDIDATES):
             weight = jnp.concatenate([choice_ref[entry, at]] * wide, axis=1)
-            part = candidate * jnp.concatenate([weight] * tall, axis=0)
+            part = candidates[entry + at] * jnp.concatenate([weight] * tall, axis=0)
             total = part if total is None else total + part
         near.append(total)
     return jnp.concatenate(near, axis=0)
@@ -186,13 +182,15 @@
 
 
 def early_kernel(
-    choice_ref, west_ref, east_ref, beside_ref, inner_ref, outer_ref,
+    choice_ref, west_ref, east_ref, inner_ref, outer_ref,
     gain_ref, wk_ref, wvt_ref, query_ref, key_ref, value_ref,
     top_ref, sum_ref, keys_ref, values_ref,
 ):
     rows = key_ref.shape[0]
     parts, group, _ = query_ref.shape
-    nodes = chosen(range(EARLY), rows, choice_ref, west_ref, east_ref, beside_ref, inner_ref, outer_ref, None)
+    candidates = [west_ref[...], east_ref[...]]
+    candidates += [ref[rows : 2 * rows] if center else ref[:rows] for ref in (inner_ref, outer_ref) for center in (1, 0)]
+    nodes = chosen(range(EARLY), rows, choice_ref, candidates)
     keys, values = project(nodes, gain_ref[...], wk_ref, wvt_ref)
     keys_ref[:rows] = key_ref[...]
     keys_ref[rows:] = keys
@@ -218,7 +216,7 @@
 
 
 def late_kernel(
-    choice_ref, cells_ref, west_ref, east_ref, beside_ref, inner_ref, outer_ref, corner_ref,
+    choice_ref, cells_ref, inner_ref, outer_ref, beside_ref, corner_ref,
     own_ref, gain_ref, wk_ref, wvt_ref, query_ref, top_ref, sum_ref, wout_ref, wlat_ref,
     state_ref, latent_ref, first_ref, last_ref,
     attended_ref,
@@ -227,10 +225,10 @@
     parts, group, lanes = query_ref.shape
     members = lanes // rows
     head = group // members
-    entries = range(EARLY, choice_ref.shape[0])
-    nodes = chosen(
-        entries, rows, choice_ref, west_ref, east_ref, beside_ref, inner_ref, outer_ref, corner_ref
-    )
+    candidates = [None, None]
+    candidates += [ref[rows : 2 * rows] if center else ref[:rows] for ref in (inner_ref, outer_ref) for center in (1, 0)]
+    candidates += [beside_ref[...], corner_ref[...]]
+    nodes = chosen(range(EARLY, choice_ref.shape[0]), rows, choice_ref, candidates)
     keys, values = project(nodes, gain_ref[...], wk_ref, wvt_ref)
     ones = jnp.ones((ROWS, nodes.shape[0]), BF16)
     owner = iota((group, rows), 0) // head
@@ -411,7 +409,7 @@
                 pltpu.VMEM((len(blocks) * ROWS, basis * ROWS), BF16),
             ],
             compiler_params=params(32),
-            cost_estimate=cost(1e9, 3e6),
+            cost_estimate=cost(1e3, 1e3),
             name=name,
         )(taps, mixing)
         return weights, after
@@ -426,7 +424,7 @@
             pltpu.SemaphoreType.DMA((2,)),
         ],
         compiler_params=params(32),
-        cost_estimate=cost(1e8, 1e6),
+        cost_estimate=cost(1e3, 1e3),
         name="gather",
     )(*in_hbm(x, assignment))
     query, key, value, wk, wvt, choice, cells = pl.pallas_call(
@@ -453,19 +451,20 @@
         cost_estimate=cost(2e9, 5e6),
         name="prepare",
     )(own, *in_hbm(gain, w_qkv, assignment, neighbours))
-    east, query = lax.optimization_barrier((east, query))
     message = jnp.concatenate([east, own], axis=0)
+    message_a = message
+    west_a = west
+    inner = exchanged(message_a, 0)
     outer = exchanged(message, 1)
-    inner = exchanged(message, 0)
+    west, message = lax.optimization_barrier((west, message))
     corner = exchanged(west, 1)
-    beside = exchanged(west, 0)
-    edges, beside = mixed(blocks_of(ABOVE) + blocks_of(BELOW), "mix_edges", beside)
-    beside, edges = lax.optimization_barrier((beside, edges))
-
+    beside = exchanged(west_a, 0)
+    edges, inner = mixed(blocks_of(ABOVE) + blocks_of(BELOW), "mix_edges", inner)
+    inner, edges = lax.optimization_barrier((inner, edges))
 
     top, summed = pl.pallas_call(
         early_kernel,
-        in_specs=[whole()] * 12,
+        in_specs=[whole()] * 11,
         out_specs=[whole()] * 2,
         out_shape=[
             struct(parts, 8, members * rows, dtype=F32),
@@ -476,12 +475,12 @@
             pltpu.VMEM((parts, LANES + ROWS, (1 + EARLY) * rows), BF16),
         ],
         compiler_params=params(32),
-        cost_estimate=cost(3e9, 6e6),
+        cost_estimate=cost(1e3, 1e3),
         name="early",
-    )(choice, west, east, beside, inner, outer, gain, wk, wvt, query, key, value)
+    )(choice, west, east, inner, outer, gain, wk, wvt, query, key, value)
     state, latent, first, last = pl.pallas_call(
         late_kernel,
-        in_specs=[whole()] * 17,
+        in_specs=[whole()] * 15,
         out_specs=[whole()] * 4,
         out_shape=[pltpu.VMEM((rows, width), BF16), struct(rows, channels)]
         + [struct(ROWS, channels)] * 2,
@@ -490,7 +489,7 @@
         cost_estimate=cost(3e9, 6e6),
         name="late",
     )(
-        choice, cells, west, east, beside, inner, outer, corner,
+        choice, cells, inner, outer, beside, corner,
         own, gain, wk, wvt, query, top, summed, w_out, w_latent,
     )
 

time: 35.1 us -> 36.6 us (1.043)
  waiting for transfers between devices: 1.15 us -> 3.19 us
    ppermute x4, waiting for transfers between devices: 0.79 us -> 2.56 us  [shifted(): lax.ppermute(array, 'lon', [(i, (i + step) % sectors) for i in range(sect...]
    ppermute x6, starting transfers between devices: 13.5 us -> 13.2 us  [exchanged(): return lax.ppermute(array, 'reg', pairs + [(j, i) for i, j in pairs])]
  transfers between devices with their start and end apart: 10 -> 10, of which waited for: 4 -> 4; matrix products, arithmetic and copies ran while one was open for 0% -> 0% of each run, Pallas kernels for 27% -> 26%
where the time goes in v10:
time: 36.6 us; the launch traced here: 36.4 us
  starting transfers between devices  19.3 us (53%)
  Pallas kernels  13.1 us (36%)
  waiting for transfers between devices  3.19 us (9%)
  between operations  0.84 us (2%)
    ppermute x6, starting transfers between devices, exchanged(): return lax.ppermute(array, 'reg', pairs + [(j, i) for i, j in pairs])  13.2 us
    ppermute x4, starting transfers between devices, shifted(): lax.ppermute(array, 'lon', [(i, (i + step) % sectors) for i in range(sect...  6.1 us
    ppermute x4, waiting for transfers between devices, shifted(): lax.ppermute(array, 'lon', [(i, (i + step) % sectors) for i in range(sect...  2.56 us
    pallas_call x1, Pallas kernels, shards(): pl.pallas_call(late_kernel, in_specs=[whole()] * 15, out_specs=[whole()]...  2.15 us
    pallas_call x1, Pallas kernels, shards(): pl.pallas_call(functools.partial(prepare_kernel, sectors), in_specs=[whol...  2.09 us
    pallas_call x2, Pallas kernels, mixed(): pl.pallas_call(functools.partial(mix_kernel, blocks), in_specs=[whole()]...  1.82 us
    pallas_call x1, Pallas kernels, shards(): pl.pallas_call(functools.partial(own_kernel, (rows, 2 * rows, 2 * rows)),...  1.8 us
    pallas_call x1, Pallas kernels, shards(): pl.pallas_call(early_kernel, in_specs=[whole()] * 11, out_specs=[whole()]...  1.66 us
  transfers between devices with their start and end apart: 10, of which 4 were waited for; matrix products, arithmetic and copies ran while one was open for 0% of the time, Pallas kernels for 26%

profile of v10, /device:TPU:1, one launch (start us, length us, event | category | flops | bytes accessed | tf_op | source)
XLA Modules:
  0.0 36.4 jit_solution(15839662695481159620)
XLA Ops:
  0.6 3.0 %collective-permute-start = (bf16[128,512]{1,0:T(8,128)(2,1)}, bf16[128,512]{1,0:T(8,128)(2,1)S(1)}, u32[]{:S(2)}, u32[]{:S(2)}) collective-permute-start(bf16[128,512]{1,0:T(8,128)(2,1)} %bitcast.13), channel_id=1, source_target_pairs={{0,3},{1,0},{2,1},{3,2},{4,7},{5,4},{6,5},{7,6},{8,11},{9,8},{10,9... | collective-permute-start | bytes 393224 | tf_op jit(solution)/shard_map/ppermute | solution.py:381
  3.7 1.0 %gather.1.own_ref = bf16[144,512]{1,0:T(8,128)(2,1)S(1)} custom-call(bf16[128,512]{1,0:T(8,128)(2,1)} %bitcast.15, s32[2,256]{1,0:T(2,128)} %assign_hbm.3), custom_call_target="tpu_custom_call" | custom-call | flops 1000 | bytes 1000 | tf_op jit(solution)/shard_map/gather/pallas_call | solution.py:417
  4.7 1.5 %collective-permute-done.east_ref = bf16[128,512]{1,0:T(8,128)(2,1)S(1)} collective-permute-done((bf16[128,512]{1,0:T(8,128)(2,1)}, bf16[128,512]{1,0:T(8,128)(2,1)S(1)}, u32[]{:S(2)}, u32[]{:S(2)}) %collective-permute-start) | collective-permute-done | bytes 131104 | tf_op jit(solution)/shard_map/ppermute | solution.py:381
  6.2 2.8 %collective-permute-start.1 = (bf16[272,512]{1,0:T(8,128)(2,1)S(1)}, bf16[272,512]{1,0:T(8,128)(2,1)S(1)}, u32[]{:S(2)}, u32[]{:S(2)}) collective-permute-start(bf16[272,512]{1,0:T(8,128)(2,1)S(1)} %pad_maximum_fusion), channel_id=1, source_target_pairs={{0,4},{8,12},{16,20},{24,28},{4,0},{12,8},{20,16},{28,24},{1,5},{9... | collective-permute-start | bytes 835592 | tf_op jit(solution)/shard_map/ppermute | solution.py:386
  8.9 3.1 %collective-permute-start.2 = (bf16[272,512]{1,0:T(8,128)(2,1)S(1)}, bf16[272,512]{1,0:T(8,128)(2,1)S(1)}, u32[]{:S(2)}, u32[]{:S(2)}) collective-permute-start(bf16[272,512]{1,0:T(8,128)(2,1)S(1)} %pad_maximum_fusion), channel_id=1, source_target_pairs={{4,8},{12,16},{20,24},{8,4},{16,12},{24,20},{5,9},{13,17},{21,25},... | collective-permute-start | bytes 835592 | tf_op jit(solution)/shard_map/ppermute | solution.py:386
  12.1 2.4 %collective-permute-start.5 = (bf16[128,512]{1,0:T(8,128)(2,1)S(1)}, bf16[128,512]{1,0:T(8,128)(2,1)S(1)}, u32[]{:S(2)}, u32[]{:S(2)}) collective-permute-start(bf16[128,512]{1,0:T(8,128)(2,1)S(1)} %collective-permute-done.3.west_ref), channel_id=1, source_target_pairs={{4,8},{12,16},{20,24},{8,4},{16,12},{24,20},{5,9},{13,17},{21,25},... | collective-permute-start | bytes 393224 | tf_op jit(solution)/shard_map/ppermute | solution.py:386
  14.5 0.1 collective-permute-start.4
  14.6 2.1 %prepare.1 = (bf16[4,128,512]{2,1,0:T(8,128)(2,1)S(1)}, bf16[128,512]{1,0:T(8,128)(2,1)S(1)}, bf16[512,128]{1,0:T(8,128)(2,1)S(1)}, bf16[512,512]{1,0:T(8,128)(2...) custom-call(bf16[144,512]{1,0:T(8,128)(2,1)S(1)} %gather.1.own_ref, ...), custom_call_target="tpu_custom_call" | custom-call | flops 2000000000 | bytes 5000000 | tf_op jit(solution)/shard_map/prepare/pallas_call | solution.py:430
  16.7 0.0 copy-start.2
  16.8 1.0 %mix_edges.1.weights_ref = bf16[30,96,512]{2,1,0:T(8,128)(2,1)S(1)} custom-call(f32[5,5,2,9]{3,2,1,0:T(2,128)S(1)} %bitcast.8, bf16[9,84,512]{2,1,0:T(8,128)(2,1)S(1)} %bitcast.6), custom_call_target="tpu_custom_call" | custom-call | flops 1000 | bytes 1000 | tf_op jit(solution)/shard_map/mix_edges/pallas_call | solution.py:402
  17.8 0.0 copy-start.4
  17.9 1.7 %early.1 = (f32[4,8,512]{2,1,0:T(8,128)S(1)}, f32[4,144,512]{2,1,0:T(8,128)S(1)}) custom-call(bf16[4,5,16,128]{3,2,1,0:T(8,128)(2,1)S(1)} %get-tuple-element.29.choice_ref, bf16[128,512]{1,0:T(8,128)(2,1)S(1)} %collective-permute-done.3.west_ref, bf16[128,512]{1,0:T(8,128)(2,1)S(1)} %collective-permute-done.east_ref, ...), custom_call_target="tpu_custom_call" | custom-call | flops 1000 | bytes 1000 | tf_op jit(solution)/shard_map/early/pallas_call | solution.py:465
  19.6 2.1 %late.1 = (bf16[128,512]{1,0:T(8,128)(2,1)S(1)}, bf16[128,512]{1,0:T(8,128)(2,1)S(1)}, bf16[16,512]{1,0:T(8,128)(2,1)S(1)}, bf16[16,512]{1,0:T(8,128)(2,1)S(1)}) custom-call(bf16[4,5,16,128]{3,2,1,0:T(8,128)(2,1)S(1)} %get-tuple-element.29.choice_ref, bf16[32,128]{1,0:T(8,128)(2,1)S(1)} %get-tuple-element.30.cells_ref, ...), custom_call_target="tpu_custom_call" | custom-call | flops 3000000000 | bytes 6000000 | tf_op jit(solution)/shard_map/late/pallas_call | solution.py:481
  21.7 2.0 %collective-permute-start.6 = (bf16[16,512]{1,0:T(8,128)(2,1)S(1)}, bf16[16,512]{1,0:T(8,128)(2,1)S(1)}, u32[]{:S(2)}, u32[]{:S(2)}) collective-permute-start(bf16[16,512]{1,0:T(8,128)(2,1)S(1)} %get-tuple-element.46), channel_id=1, source_target_pairs={{0,1},{1,2},{2,3},{3,0},{4,5},{5,6},{6,7},{7,4},{8,9},{9,10},{10,1... | collective-permute-start | bytes 49160 | tf_op jit(solution)/shard_map/ppermute | solution.py:381
  23.7 1.0 %collective-permute-start.7 = (bf16[16,512]{1,0:T(8,128)(2,1)S(1)}, bf16[16,512]{1,0:T(8,128)(2,1)S(1)}, u32[]{:S(2)}, u32[]{:S(2)}) collective-permute-start(bf16[16,512]{1,0:T(8,128)(2,1)S(1)} %get-tuple-element.50), channel_id=1, source_target_pairs={{0,3},{1,0},{2,1},{3,2},{4,7},{5,4},{6,5},{7,6},{8,11},{9,8},{10,9... | collective-permute-start | bytes 49160 | tf_op jit(solution)/shard_map/ppermute | solution.py:381
  24.8 0.8 %mix_own.1.weights_ref = bf16[20,96,512]{2,1,0:T(8,128)(2,1)S(1)} custom-call(f32[5,5,2,9]{3,2,1,0:T(2,128)S(1)} %bitcast.9, bf16[9,84,512]{2,1,0:T(8,128)(2,1)S(1)} %bitcast.7), custom_call_target="tpu_custom_call" | custom-call | flops 1000 | bytes 1000 | tf_op jit(solution)/shard_map/mix_own/pallas_call | solution.py:402
  25.6 0.3 collective-permute-done.6
  25.8 0.8 %collective-permute-done.7 = bf16[16,512]{1,0:T(8,128)(2,1)S(1)} collective-permute-done((bf16[16,512]{1,0:T(8,128)(2,1)S(1)}, bf16[16,512]{1,0:T(8,128)(2,1)S(1)}, u32[]{:S(2)}, u32[]{:S(2)}) %collective-permute-start.7) | collective-permute-done | bytes 16416 | tf_op jit(solution)/shard_map/ppermute | solution.py:381
  26.6 1.7 %collective-permute-start.9 = (bf16[144,512]{1,0:T(8,128)(2,1)S(1)}, bf16[144,512]{1,0:T(8,128)(2,1)S(1)}, u32[]{:S(2)}, u32[]{:S(2)}) collective-permute-start(bf16[144,512]{1,0:T(8,128)(2,1)S(1)} %pad_maximum_fusion.1.latent_ref), channel_id=1, source_target_pairs={{0,4},{8,12},{16,20},{24,28},{4,0},{12,8},{20,16},{28,24},{1,5},{9... | collective-permute-start | bytes 442376 | tf_op jit(solution)/shard_map/ppermute | solution.py:386
  28.3 3.1 %collective-permute-start.8 = (bf16[144,512]{1,0:T(8,128)(2,1)S(1)}, bf16[144,512]{1,0:T(8,128)(2,1)S(1)}, u32[]{:S(2)}, u32[]{:S(2)}) collective-permute-start(bf16[144,512]{1,0:T(8,128)(2,1)S(1)} %pad_maximum_fusion.1.latent_ref), channel_id=1, source_target_pairs={{4,8},{12,16},{20,24},{8,4},{16,12},{24,20},{5,9},{13,17},{21,25},... | collective-permute-start | bytes 442376 | tf_op jit(solution)/shard_map/ppermute | solution.py:386
  31.4 1.8 %own_band.1 = (f32[2,96,256]{2,1,0:T(8,128)S(1)}, bf16[2,2,5,256,256]{4,3,2,1,0:T(8,128)(2,1)S(1)}, bf16[128,512]{1,0:T(8,128)(2,1)}) custom-call(bf16[128,512]{1,0:T(8,128)(2,1)S(1)} %get-tuple-element.43.state_ref, bf16[144,512]{1,0:T(8,128)(2,1)S(1)} %gather.1.own_ref, bf16[272,512]{1,0:T(8,128)(2,1)S(1)} %collective-permute-done.1.inner_ref, ...), custom_call_target="tpu_custom_call" | custom-call | flops 1000000000 | bytes 2500000 | tf_op jit(solution)/shard_map/own_band/pallas_call | solution.py:505
  33.2 0.9 %inner_band.1.partial_ref = f32[2,96,256]{2,1,0:T(8,128)S(1)} custom-call(bf16[144,512]{1,0:T(8,128)(2,1)S(1)} %collective-permute-done.9.latent_ref, bf16[30,96,512]{2,1,0:T(8,128)(2,1)S(1)} %mix_edges.1.weights_ref, bf16[2,2,5,256,256]{4,3,2,1,0:T(8,128)(2,1)S(1)} %get-tuple-element.54.hot_ref, f32[2,96,256]{2,1,0:T(8,128)S(1)} %get-tuple-element.55.partial_ref), custom_call_target="tpu_custom_call" | custom-call | flops 1000000000 | bytes 2500000 | tf_op jit(solution)/shard_map/inner_band/pallas_call | solution.py:522
  34.2 0.6 %collective-permute-done.8.latent_ref = bf16[144,512]{1,0:T(8,128)(2,1)S(1)} collective-permute-done((bf16[144,512]{1,0:T(8,128)(2,1)S(1)}, bf16[144,512]{1,0:T(8,128)(2,1)S(1)}, u32[]{:S(2)}, u32[]{:S(2)}) %collective-permute-start.8) | collective-permute-done | bytes 147488 | tf_op jit(solution)/shard_map/ppermute | solution.py:386
  34.8 1.6 %outer_band.1 = bf16[84,2,256]{2,1,0:T(2,128)(2,1)} custom-call(bf16[144,512]{1,0:T(8,128)(2,1)S(1)} %collective-permute-done.8.latent_ref, bf16[30,96,512]{2,1,0:T(8,128)(2,1)S(1)} %mix_edges.1.weights_ref, bf16[2,2,5,256,256]{4,3,2,1,0:T(8,128)(2,1)S(1)} %get-tuple-element.54.hot_ref, f32[2,96,256]{2,1,0:T(8,128)S(1)} %inner_band.1.partial_ref), custom_call_target="tpu_custom_call" | custom-call | flops 1000000000 | bytes 2500000 | tf_op jit(solution)/shard_map/outer_band/pallas_call | solution.py:532
  (19 shorter events, 0.1 us)
Async XLA Ops:
  0.6 5.5 %collective-permute-start = (bf16[128,512]{1,0:T(8,128)(2,1)}, bf16[128,512]{1,0:T(8,128)(2,1)S(1)}, u32[]{:S(2)}, u32[]{:S(2)}) collective-permute-start(bf16[128,512]{1,0:T(8,128)(2,1)} %bitcast.13), channel_id=1, source_target_pairs={{0,3},{1,0},{2,1},{3,2},{4,7},{5,4},{6,5},{7,6},{8,11},{9,8},{10,9... | collective-permute-start | bytes 393224 | tf_op jit(solution)/shard_map/ppermute | solution.py:381
  3.7 8.4 %collective-permute-start.3 = (bf16[128,512]{1,0:T(8,128)(2,1)}, bf16[128,512]{1,0:T(8,128)(2,1)S(1)}, u32[]{:S(2)}, u32[]{:S(2)}) collective-permute-start(bf16[128,512]{1,0:T(8,128)(2,1)} %bitcast.14), channel_id=1, source_target_pairs={{0,1},{1,2},{2,3},{3,0},{4,5},{5,6},{6,7},{7,4},{8,9},{9,10},{10,1... | collective-permute-start | bytes 393224 | tf_op jit(solution)/shard_map/ppermute | solution.py:381
  6.2 10.6 %collective-permute-start.1 = (bf16[272,512]{1,0:T(8,128)(2,1)S(1)}, bf16[272,512]{1,0:T(8,128)(2,1)S(1)}, u32[]{:S(2)}, u32[]{:S(2)}) collective-permute-start(bf16[272,512]{1,0:T(8,128)(2,1)S(1)} %pad_maximum_fusion), channel_id=1, source_target_pairs={{0,4},{8,12},{16,20},{24,28},{4,0},{12,8},{20,16},{28,24},{1,5},{9... | collective-permute-start | bytes 835592 | tf_op jit(solution)/shard_map/ppermute | solution.py:386
  8.9 8.9 %collective-permute-start.2 = (bf16[272,512]{1,0:T(8,128)(2,1)S(1)}, bf16[272,512]{1,0:T(8,128)(2,1)S(1)}, u32[]{:S(2)}, u32[]{:S(2)}) collective-permute-start(bf16[272,512]{1,0:T(8,128)(2,1)S(1)} %pad_maximum_fusion), channel_id=1, source_target_pairs={{4,8},{12,16},{20,24},{8,4},{16,12},{24,20},{5,9},{13,17},{21,25},... | collective-permute-start | bytes 835592 | tf_op jit(solution)/shard_map/ppermute | solution.py:386
  12.1 7.5 %collective-permute-start.5 = (bf16[128,512]{1,0:T(8,128)(2,1)S(1)}, bf16[128,512]{1,0:T(8,128)(2,1)S(1)}, u32[]{:S(2)}, u32[]{:S(2)}) collective-permute-start(bf16[128,512]{1,0:T(8,128)(2,1)S(1)} %collective-permute-done.3.west_ref), channel_id=1, source_target_pairs={{4,8},{12,16},{20,24},{8,4},{16,12},{24,20},{5,9},{13,17},{21,25},... | collective-permute-start | bytes 393224 | tf_op jit(solution)/shard_map/ppermute | solution.py:386
  14.5 5.0 %collective-permute-start.4 = (bf16[128,512]{1,0:T(8,128)(2,1)S(1)}, bf16[128,512]{1,0:T(8,128)(2,1)S(1)}, u32[]{:S(2)}, u32[]{:S(2)}) collective-permute-start(bf16[128,512]{1,0:T(8,128)(2,1)S(1)} %collective-permute-done.3.west_ref), channel_id=1, source_target_pairs={{0,4},{8,12},{16,20},{24,28},{4,0},{12,8},{20,16},{28,24},{1,5},{9... | collective-permute-start | bytes 393224 | tf_op jit(solution)/shard_map/ppermute | solution.py:386
  14.6 2.1 %copy-start = (bf16[9,512,84]{1,2,0:T(8,128)(2,1)S(1)}, bf16[9,512,84]{1,2,0:T(8,128)(2,1)}, u32[]{:S(2)}) copy-start(bf16[9,512,84]{1,2,0:T(8,128)(2,1)} %param.17) | copy-start | bytes 2322436
  14.6 2.1 %copy-start.1 = (f32[9,2,5,5]{0,1,3,2:T(2,128)S(1)}, f32[9,2,5,5]{0,1,3,2:T(2,128)}, u32[]{:S(2)}) copy-start(f32[9,2,5,5]{0,1,3,2:T(2,128)} %param.16) | copy-start | bytes 5404
  16.7 1.1 %copy-start.2 = (f32[512]{0:T(512)S(1)}, f32[512]{0:T(512)}, u32[]{:S(2)}) copy-start(f32[512]{0:T(512)} %param.10) | copy-start | bytes 6148
  17.8 1.7 %copy-start.3 = (bf16[512,512]{1,0:T(8,128)(2,1)S(1)}, bf16[512,512]{1,0:T(8,128)(2,1)}, u32[]{:S(2)}) copy-start(bf16[512,512]{1,0:T(8,128)(2,1)} %wout_ref.1) | copy-start | bytes 1572868
  17.8 1.7 %copy-start.4 = (bf16[512,512]{1,0:T(8,128)(2,1)S(1)}, bf16[512,512]{1,0:T(8,128)(2,1)}, u32[]{:S(2)}) copy-start(bf16[512,512]{1,0:T(8,128)(2,1)} %wlat_ref.1) | copy-start | bytes 1572868
  21.7 4.1 %collective-permute-start.6 = (bf16[16,512]{1,0:T(8,128)(2,1)S(1)}, bf16[16,512]{1,0:T(8,128)(2,1)S(1)}, u32[]{:S(2)}, u32[]{:S(2)}) collective-permute-start(bf16[16,512]{1,0:T(8,128)(2,1)S(1)} %get-tuple-element.46), channel_id=1, source_target_pairs={{0,1},{1,2},{2,3},{3,0},{4,5},{5,6},{6,7},{7,4},{8,9},{9,10},{10,1... | collective-permute-start | bytes 49160 | tf_op jit(solution)/shard_map/ppermute | solution.py:381
  23.7 2.9 %collective-permute-start.7 = (bf16[16,512]{1,0:T(8,128)(2,1)S(1)}, bf16[16,512]{1,0:T(8,128)(2,1)S(1)}, u32[]{:S(2)}, u32[]{:S(2)}) collective-permute-start(bf16[16,512]{1,0:T(8,128)(2,1)S(1)} %get-tuple-element.50), channel_id=1, source_target_pairs={{0,3},{1,0},{2,1},{3,2},{4,7},{5,4},{6,5},{7,6},{8,11},{9,8},{10,9... | collective-permute-start | bytes 49160 | tf_op jit(solution)/shard_map/ppermute | solution.py:381
  26.6 6.6 %collective-permute-start.9 = (bf16[144,512]{1,0:T(8,128)(2,1)S(1)}, bf16[144,512]{1,0:T(8,128)(2,1)S(1)}, u32[]{:S(2)}, u32[]{:S(2)}) collective-permute-start(bf16[144,512]{1,0:T(8,128)(2,1)S(1)} %pad_maximum_fusion.1.latent_ref), channel_id=1, source_target_pairs={{0,4},{8,12},{16,20},{24,28},{4,0},{12,8},{20,16},{28,24},{1,5},{9... | collective-permute-start | bytes 442376 | tf_op jit(solution)/shard_map/ppermute | solution.py:386
  28.3 6.5 %collective-permute-start.8 = (bf16[144,512]{1,0:T(8,128)(2,1)S(1)}, bf16[144,512]{1,0:T(8,128)(2,1)S(1)}, u32[]{:S(2)}, u32[]{:S(2)}) collective-permute-start(bf16[144,512]{1,0:T(8,128)(2,1)S(1)} %pad_maximum_fusion.1.latent_ref), channel_id=1, source_target_pairs={{4,8},{12,16},{20,24},{8,4},{16,12},{24,20},{5,9},{13,17},{21,25},... | collective-permute-start | bytes 442376 | tf_op jit(solution)/shard_map/ppermute | solution.py:386

commit v11 on v10

--- a/solution.py
+++ b/solution.py
@@ -409,7 +409,7 @@
                 pltpu.VMEM((len(blocks) * ROWS, basis * ROWS), BF16),
             ],
             compiler_params=params(32),
-            cost_estimate=cost(1e3, 1e3),
+            cost_estimate=cost(2e9, 6e6),
             name=name,
         )(taps, mixing)
         return weights, after
@@ -448,20 +448,20 @@
             pltpu.SemaphoreType.DMA((4,)),
         ],
         compiler_params=params(32),
-        cost_estimate=cost(2e9, 5e6),
+        cost_estimate=cost(5e8, 1e6),
         name="prepare",
     )(own, *in_hbm(gain, w_qkv, assignment, neighbours))
+    own, query = lax.optimization_barrier((own, query))
     message = jnp.concatenate([east, own], axis=0)
     message_a = message
     west_a = west
     inner = exchanged(message_a, 0)
     outer = exchanged(message, 1)
-    west, message = lax.optimization_barrier((west, message))
     corner = exchanged(west, 1)
     beside = exchanged(west_a, 0)
-    edges, inner = mixed(blocks_of(ABOVE) + blocks_of(BELOW), "mix_edges", inner)
+
+    edges, west_m = mixed(blocks_of(ABOVE) + blocks_of(BELOW), "mix_edges", west)
     inner, edges = lax.optimization_barrier((inner, edges))
-
     top, summed = pl.pallas_call(
         early_kernel,
         in_specs=[whole()] * 11,
@@ -475,7 +475,7 @@
             pltpu.VMEM((parts, LANES + ROWS, (1 + EARLY) * rows), BF16),
         ],
         compiler_params=params(32),
-        cost_estimate=cost(1e3, 1e3),
+        cost_estimate=cost(3e9, 6e6),
         name="early",
     )(choice, west, east, inner, outer, gain, wk, wvt, query, key, value)
     state, latent, first, last = pl.pallas_call(

time: 36.6 us -> 34.6 us (0.945)
  starting transfers between devices: 19.3 us -> 18.2 us
  waiting for transfers between devices: 3.19 us -> 2.3 us
    ppermute x4, waiting for transfers between devices: 2.56 us -> 1.11 us  [shifted(): lax.ppermute(array, 'lon', [(i, (i + step) % sectors) for i in range(sect...]
    ppermute x6, starting transfers between devices: 13.2 us -> 12.1 us  [exchanged(): return lax.ppermute(array, 'reg', pairs + [(j, i) for i, j in pairs])]
    ppermute x6, waiting for transfers between devices: 0.63 us -> 1.19 us  [exchanged(): return lax.ppermute(array, 'reg', pairs + [(j, i) for i, j in pairs])]
  transfers between devices with their start and end apart: 10 -> 10, of which waited for: 4 -> 4; matrix products, arithmetic and copies ran while one was open for 0% -> 0% of each run, Pallas kernels for 26% -> 27%
where the time goes in v11:
time: 34.6 us; the launch traced here: 34.4 us
  starting transfers between devices  18.2 us (53%)
  Pallas kernels  13 us (38%)
  waiting for transfers between devices  2.3 us (7%)
  between operations  0.83 us (2%)
    ppermute x6, starting transfers between devices, exchanged(): return lax.ppermute(array, 'reg', pairs + [(j, i) for i, j in pairs])  12.1 us
    ppermute x4, starting transfers between devices, shifted(): lax.ppermute(array, 'lon', [(i, (i + step) % sectors) for i in range(sect...  6.1 us
    pallas_call x1, Pallas kernels, shards(): pl.pallas_call(late_kernel, in_specs=[whole()] * 15, out_specs=[whole()]...  2.14 us
    pallas_call x1, Pallas kernels, shards(): pl.pallas_call(functools.partial(prepare_kernel, sectors), in_specs=[whol...  2.01 us
    pallas_call x2, Pallas kernels, mixed(): pl.pallas_call(functools.partial(mix_kernel, blocks), in_specs=[whole()]...  1.82 us
    pallas_call x1, Pallas kernels, shards(): pl.pallas_call(functools.partial(own_kernel, (rows, 2 * rows, 2 * rows)),...  1.8 us
    pallas_call x1, Pallas kernels, shards(): pl.pallas_call(early_kernel, in_specs=[whole()] * 11, out_specs=[whole()]...  1.66 us
    pallas_call x1, Pallas kernels, shards(): pl.pallas_call(functools.partial(band_kernel, False), in_specs=[whole()]...  1.61 us
  transfers between devices with their start and end apart: 10, of which 4 were waited for; matrix products, arithmetic and copies ran while one was open for 0% of the time, Pallas kernels for 27%

profile of v11, /device:TPU:1, one launch (start us, length us, event | category | flops | bytes accessed | tf_op | source)
XLA Modules:
  0.0 34.4 jit_solution(818186336790692527)
XLA Ops:
  0.6 3.0 %collective-permute-start = (bf16[128,512]{1,0:T(8,128)(2,1)}, bf16[128,512]{1,0:T(8,128)(2,1)S(1)}, u32[]{:S(2)}, u32[]{:S(2)}) collective-permute-start(bf16[128,512]{1,0:T(8,128)(2,1)} %bitcast.13), channel_id=1, source_target_pairs={{0,3},{1,0},{2,1},{3,2},{4,7},{5,4},{6,5},{7,6},{8,11},{9,8},{10,9... | collective-permute-start | bytes 393224 | tf_op jit(solution)/shard_map/ppermute | solution.py:381
  3.7 1.0 %gather.1.own_ref = bf16[144,512]{1,0:T(8,128)(2,1)S(1)} custom-call(bf16[128,512]{1,0:T(8,128)(2,1)} %bitcast.15, s32[2,256]{1,0:T(2,128)} %assign_hbm.3), custom_call_target="tpu_custom_call" | custom-call | flops 1000 | bytes 1000 | tf_op jit(solution)/shard_map/gather/pallas_call | solution.py:417
  4.7 2.0 %prepare.1 = (bf16[4,128,512]{2,1,0:T(8,128)(2,1)S(1)}, bf16[128,512]{1,0:T(8,128)(2,1)S(1)}, bf16[512,128]{1,0:T(8,128)(2,1)S(1)}, bf16[512,512]{1,0:T(8,128)(2...) custom-call(bf16[144,512]{1,0:T(8,128)(2,1)S(1)} %gather.1.own_ref, ...), custom_call_target="tpu_custom_call" | custom-call | flops 500000000 | bytes 1000000 | tf_op jit(solution)/shard_map/prepare/pallas_call | solution.py:430
  6.7 0.0 collective-permute-done.east_ref
  6.8 2.2 %collective-permute-start.1 = (bf16[272,512]{1,0:T(8,128)(2,1)S(1)}, bf16[272,512]{1,0:T(8,128)(2,1)S(1)}, u32[]{:S(2)}, u32[]{:S(2)}) collective-permute-start(bf16[272,512]{1,0:T(8,128)(2,1)S(1)} %constant_dynamic-update-slice_fusion), channel_id=1, source_target_pairs={{0,4},{8,12},{16,20},{24,28},{4,0},{12,8},{20,16},{28,24},{1,5},{9... | collective-permute-start | bytes 835592 | tf_op jit(solution)/shard_map/ppermute | solution.py:386
  9.0 3.1 %collective-permute-start.3 = (bf16[272,512]{1,0:T(8,128)(2,1)S(1)}, bf16[272,512]{1,0:T(8,128)(2,1)S(1)}, u32[]{:S(2)}, u32[]{:S(2)}) collective-permute-start(bf16[272,512]{1,0:T(8,128)(2,1)S(1)} %constant_dynamic-update-slice_fusion), channel_id=1, source_target_pairs={{4,8},{12,16},{20,24},{8,4},{16,12},{24,20},{5,9},{13,17},{21,25},... | collective-permute-start | bytes 835592 | tf_op jit(solution)/shard_map/ppermute | solution.py:386
  12.1 0.0 copy-start.4
  12.1 2.4 %collective-permute-start.5 = (bf16[128,512]{1,0:T(8,128)(2,1)S(1)}, bf16[128,512]{1,0:T(8,128)(2,1)S(1)}, u32[]{:S(2)}, u32[]{:S(2)}) collective-permute-start(bf16[128,512]{1,0:T(8,128)(2,1)S(1)} %collective-permute-done.2.west_ref), channel_id=1, source_target_pairs={{4,8},{12,16},{20,24},{8,4},{16,12},{24,20},{5,9},{13,17},{21,25},... | collective-permute-start | bytes 393224 | tf_op jit(solution)/shard_map/ppermute | solution.py:386
  14.6 0.1 collective-permute-start.4
  14.7 1.0 %mix_edges.1.weights_ref = bf16[30,96,512]{2,1,0:T(8,128)(2,1)S(1)} custom-call(f32[5,5,2,9]{3,2,1,0:T(2,128)S(1)} %bitcast.8, bf16[9,84,512]{2,1,0:T(8,128)(2,1)S(1)} %bitcast.6), custom_call_target="tpu_custom_call" | custom-call | flops 2000000000 | bytes 6000000 | tf_op jit(solution)/shard_map/mix_edges/pallas_call | solution.py:402
  15.7 1.1 %collective-permute-done.3.outer_ref = bf16[272,512]{1,0:T(8,128)(2,1)S(1)} collective-permute-done((bf16[272,512]{1,0:T(8,128)(2,1)S(1)}, bf16[272,512]{1,0:T(8,128)(2,1)S(1)}, u32[]{:S(2)}, u32[]{:S(2)}) %collective-permute-start.3) | collective-permute-done | bytes 278560 | tf_op jit(solution)/shard_map/ppermute | solution.py:386
  16.8 1.7 %early.1 = (f32[4,8,512]{2,1,0:T(8,128)S(1)}, f32[4,144,512]{2,1,0:T(8,128)S(1)}) custom-call(bf16[4,5,16,128]{3,2,1,0:T(8,128)(2,1)S(1)} %get-tuple-element.29.choice_ref, bf16[128,512]{1,0:T(8,128)(2,1)S(1)} %collective-permute-done.2.west_ref, bf16[128,512]{1,0:T(8,128)(2,1)S(1)} %collective-permute-done.east_ref, ...), custom_call_target="tpu_custom_call" | custom-call | flops 3000000000 | bytes 6000000 | tf_op jit(solution)/shard_map/early/pallas_call | solution.py:465
  18.5 2.1 %late.1 = (bf16[128,512]{1,0:T(8,128)(2,1)S(1)}, bf16[128,512]{1,0:T(8,128)(2,1)S(1)}, bf16[16,512]{1,0:T(8,128)(2,1)S(1)}, bf16[16,512]{1,0:T(8,128)(2,1)S(1)}) custom-call(bf16[4,5,16,128]{3,2,1,0:T(8,128)(2,1)S(1)} %get-tuple-element.29.choice_ref, bf16[32,128]{1,0:T(8,128)(2,1)S(1)} %get-tuple-element.30.cells_ref, ...), custom_call_target="tpu_custom_call" | custom-call | flops 3000000000 | bytes 6000000 | tf_op jit(solution)/shard_map/late/pallas_call | solution.py:481
  20.7 2.0 %collective-permute-start.6 = (bf16[16,512]{1,0:T(8,128)(2,1)S(1)}, bf16[16,512]{1,0:T(8,128)(2,1)S(1)}, u32[]{:S(2)}, u32[]{:S(2)}) collective-permute-start(bf16[16,512]{1,0:T(8,128)(2,1)S(1)} %get-tuple-element.46), channel_id=1, source_target_pairs={{0,1},{1,2},{2,3},{3,0},{4,5},{5,6},{6,7},{7,4},{8,9},{9,10},{10,1... | collective-permute-start | bytes 49160 | tf_op jit(solution)/shard_map/ppermute | solution.py:381
  22.7 1.0 %collective-permute-start.7 = (bf16[16,512]{1,0:T(8,128)(2,1)S(1)}, bf16[16,512]{1,0:T(8,128)(2,1)S(1)}, u32[]{:S(2)}, u32[]{:S(2)}) collective-permute-start(bf16[16,512]{1,0:T(8,128)(2,1)S(1)} %get-tuple-element.50), channel_id=1, source_target_pairs={{0,3},{1,0},{2,1},{3,2},{4,7},{5,4},{6,5},{7,6},{8,11},{9,8},{10,9... | collective-permute-start | bytes 49160 | tf_op jit(solution)/shard_map/ppermute | solution.py:381
  23.7 0.8 %mix_own.1.weights_ref = bf16[20,96,512]{2,1,0:T(8,128)(2,1)S(1)} custom-call(f32[5,5,2,9]{3,2,1,0:T(2,128)S(1)} %bitcast.9, bf16[9,84,512]{2,1,0:T(8,128)(2,1)S(1)} %bitcast.7), custom_call_target="tpu_custom_call" | custom-call | flops 2000000000 | bytes 6000000 | tf_op jit(solution)/shard_map/mix_own/pallas_call | solution.py:402
  24.5 0.3 collective-permute-done.6
  24.8 0.8 %collective-permute-done.7 = bf16[16,512]{1,0:T(8,128)(2,1)S(1)} collective-permute-done((bf16[16,512]{1,0:T(8,128)(2,1)S(1)}, bf16[16,512]{1,0:T(8,128)(2,1)S(1)}, u32[]{:S(2)}, u32[]{:S(2)}) %collective-permute-start.7) | collective-permute-done | bytes 16416 | tf_op jit(solution)/shard_map/ppermute | solution.py:381
  25.7 0.6 %collective-permute-start.9 = (bf16[144,512]{1,0:T(8,128)(2,1)S(1)}, bf16[144,512]{1,0:T(8,128)(2,1)S(1)}, u32[]{:S(2)}, u32[]{:S(2)}) collective-permute-start(bf16[144,512]{1,0:T(8,128)(2,1)S(1)} %pad_maximum_fusion.latent_ref), channel_id=1, source_target_pairs={{0,4},{8,12},{16,20},{24,28},{4,0},{12,8},{20,16},{28,24},{1,5},{9... | collective-permute-start | bytes 442376 | tf_op jit(solution)/shard_map/ppermute | solution.py:386
  26.3 3.7 %collective-permute-start.8 = (bf16[144,512]{1,0:T(8,128)(2,1)S(1)}, bf16[144,512]{1,0:T(8,128)(2,1)S(1)}, u32[]{:S(2)}, u32[]{:S(2)}) collective-permute-start(bf16[144,512]{1,0:T(8,128)(2,1)S(1)} %pad_maximum_fusion.latent_ref), channel_id=1, source_target_pairs={{4,8},{12,16},{20,24},{8,4},{16,12},{24,20},{5,9},{13,17},{21,25},... | collective-permute-start | bytes 442376 | tf_op jit(solution)/shard_map/ppermute | solution.py:386
  30.0 1.8 %own_band.1 = (f32[2,96,256]{2,1,0:T(8,128)S(1)}, bf16[2,2,5,256,256]{4,3,2,1,0:T(8,128)(2,1)S(1)}, bf16[128,512]{1,0:T(8,128)(2,1)}) custom-call(bf16[128,512]{1,0:T(8,128)(2,1)S(1)} %get-tuple-element.43.state_ref, bf16[144,512]{1,0:T(8,128)(2,1)S(1)} %gather.1.own_ref, bf16[272,512]{1,0:T(8,128)(2,1)S(1)} %collective-permute-done.1.inner_ref, ...), custom_call_target="tpu_custom_call" | custom-call | flops 1000000000 | bytes 2500000 | tf_op jit(solution)/shard_map/own_band/pallas_call | solution.py:505
  31.8 0.9 %inner_band.1.partial_ref = f32[2,96,256]{2,1,0:T(8,128)S(1)} custom-call(bf16[144,512]{1,0:T(8,128)(2,1)S(1)} %collective-permute-done.9.latent_ref, bf16[30,96,512]{2,1,0:T(8,128)(2,1)S(1)} %mix_edges.1.weights_ref, bf16[2,2,5,256,256]{4,3,2,1,0:T(8,128)(2,1)S(1)} %get-tuple-element.54.hot_ref, f32[2,96,256]{2,1,0:T(8,128)S(1)} %get-tuple-element.55.partial_ref), custom_call_target="tpu_custom_call" | custom-call | flops 1000000000 | bytes 2500000 | tf_op jit(solution)/shard_map/inner_band/pallas_call | solution.py:522
  32.7 0.1 collective-permute-done.8.latent_ref
  32.8 1.6 %outer_band.1 = bf16[84,2,256]{2,1,0:T(2,128)(2,1)} custom-call(bf16[144,512]{1,0:T(8,128)(2,1)S(1)} %collective-permute-done.8.latent_ref, bf16[30,96,512]{2,1,0:T(8,128)(2,1)S(1)} %mix_edges.1.weights_ref, bf16[2,2,5,256,256]{4,3,2,1,0:T(8,128)(2,1)S(1)} %get-tuple-element.54.hot_ref, f32[2,96,256]{2,1,0:T(8,128)S(1)} %inner_band.1.partial_ref), custom_call_target="tpu_custom_call" | custom-call | flops 1000000000 | bytes 2500000 | tf_op jit(solution)/shard_map/outer_band/pallas_call | solution.py:532
  (20 shorter events, 0.1 us)
Async XLA Ops:
  0.6 14.0 %copy-start = (bf16[9,512,84]{1,2,0:T(8,128)(2,1)S(1)}, bf16[9,512,84]{1,2,0:T(8,128)(2,1)}, u32[]{:S(2)}) copy-start(bf16[9,512,84]{1,2,0:T(8,128)(2,1)} %param.17) | copy-start | bytes 2322436
  0.6 14.0 %copy-start.3 = (f32[9,2,5,5]{0,1,3,2:T(2,128)S(1)}, f32[9,2,5,5]{0,1,3,2:T(2,128)}, u32[]{:S(2)}) copy-start(f32[9,2,5,5]{0,1,3,2:T(2,128)} %param.16) | copy-start | bytes 5404
  0.6 6.1 %collective-permute-start = (bf16[128,512]{1,0:T(8,128)(2,1)}, bf16[128,512]{1,0:T(8,128)(2,1)S(1)}, u32[]{:S(2)}, u32[]{:S(2)}) collective-permute-start(bf16[128,512]{1,0:T(8,128)(2,1)} %bitcast.13), channel_id=1, source_target_pairs={{0,3},{1,0},{2,1},{3,2},{4,7},{5,4},{6,5},{7,6},{8,11},{9,8},{10,9... | collective-permute-start | bytes 393224 | tf_op jit(solution)/shard_map/ppermute | solution.py:381
  3.7 8.4 %collective-permute-start.2 = (bf16[128,512]{1,0:T(8,128)(2,1)}, bf16[128,512]{1,0:T(8,128)(2,1)S(1)}, u32[]{:S(2)}, u32[]{:S(2)}) collective-permute-start(bf16[128,512]{1,0:T(8,128)(2,1)} %bitcast.14), channel_id=1, source_target_pairs={{0,1},{1,2},{2,3},{3,0},{4,5},{5,6},{6,7},{7,4},{8,9},{9,10},{10,1... | collective-permute-start | bytes 393224 | tf_op jit(solution)/shard_map/ppermute | solution.py:381
  6.8 8.9 %collective-permute-start.1 = (bf16[272,512]{1,0:T(8,128)(2,1)S(1)}, bf16[272,512]{1,0:T(8,128)(2,1)S(1)}, u32[]{:S(2)}, u32[]{:S(2)}) collective-permute-start(bf16[272,512]{1,0:T(8,128)(2,1)S(1)} %constant_dynamic-update-slice_fusion), channel_id=1, source_target_pairs={{0,4},{8,12},{16,20},{24,28},{4,0},{12,8},{20,16},{28,24},{1,5},{9... | collective-permute-start | bytes 835592 | tf_op jit(solution)/shard_map/ppermute | solution.py:386
  9.0 7.9 %collective-permute-start.3 = (bf16[272,512]{1,0:T(8,128)(2,1)S(1)}, bf16[272,512]{1,0:T(8,128)(2,1)S(1)}, u32[]{:S(2)}, u32[]{:S(2)}) collective-permute-start(bf16[272,512]{1,0:T(8,128)(2,1)S(1)} %constant_dynamic-update-slice_fusion), channel_id=1, source_target_pairs={{4,8},{12,16},{20,24},{8,4},{16,12},{24,20},{5,9},{13,17},{21,25},... | collective-permute-start | bytes 835592 | tf_op jit(solution)/shard_map/ppermute | solution.py:386
  12.1 4.7 %copy-start.4 = (f32[512]{0:T(512)S(1)}, f32[512]{0:T(512)}, u32[]{:S(2)}) copy-start(f32[512]{0:T(512)} %param.10) | copy-start | bytes 6148
  12.1 6.4 %collective-permute-start.5 = (bf16[128,512]{1,0:T(8,128)(2,1)S(1)}, bf16[128,512]{1,0:T(8,128)(2,1)S(1)}, u32[]{:S(2)}, u32[]{:S(2)}) collective-permute-start(bf16[128,512]{1,0:T(8,128)(2,1)S(1)} %collective-permute-done.2.west_ref), channel_id=1, source_target_pairs={{4,8},{12,16},{20,24},{8,4},{16,12},{24,20},{5,9},{13,17},{21,25},... | collective-permute-start | bytes 393224 | tf_op jit(solution)/shard_map/ppermute | solution.py:386
  14.6 4.0 %collective-permute-start.4 = (bf16[128,512]{1,0:T(8,128)(2,1)S(1)}, bf16[128,512]{1,0:T(8,128)(2,1)S(1)}, u32[]{:S(2)}, u32[]{:S(2)}) collective-permute-start(bf16[128,512]{1,0:T(8,128)(2,1)S(1)} %collective-permute-done.2.west_ref), channel_id=1, source_target_pairs={{0,4},{8,12},{16,20},{24,28},{4,0},{12,8},{20,16},{28,24},{1,5},{9... | collective-permute-start | bytes 393224 | tf_op jit(solution)/shard_map/ppermute | solution.py:386
  16.8 1.7 %copy-start.1 = (bf16[512,512]{1,0:T(8,128)(2,1)S(1)}, bf16[512,512]{1,0:T(8,128)(2,1)}, u32[]{:S(2)}) copy-start(bf16[512,512]{1,0:T(8,128)(2,1)} %wout_ref.1) | copy-start | bytes 1572868
  16.8 1.7 %copy-start.2 = (bf16[512,512]{1,0:T(8,128)(2,1)S(1)}, bf16[512,512]{1,0:T(8,128)(2,1)}, u32[]{:S(2)}) copy-start(bf16[512,512]{1,0:T(8,128)(2,1)} %wlat_ref.1) | copy-start | bytes 1572868
  20.7 4.1 %collective-permute-start.6 = (bf16[16,512]{1,0:T(8,128)(2,1)S(1)}, bf16[16,512]{1,0:T(8,128)(2,1)S(1)}, u32[]{:S(2)}, u32[]{:S(2)}) collective-permute-start(bf16[16,512]{1,0:T(8,128)(2,1)S(1)} %get-tuple-element.46), channel_id=1, source_target_pairs={{0,1},{1,2},{2,3},{3,0},{4,5},{5,6},{6,7},{7,4},{8,9},{9,10},{10,1... | collective-permute-start | bytes 49160 | tf_op jit(solution)/shard_map/ppermute | solution.py:381
  22.7 2.9 %collective-permute-start.7 = (bf16[16,512]{1,0:T(8,128)(2,1)S(1)}, bf16[16,512]{1,0:T(8,128)(2,1)S(1)}, u32[]{:S(2)}, u32[]{:S(2)}) collective-permute-start(bf16[16,512]{1,0:T(8,128)(2,1)S(1)} %get-tuple-element.50), channel_id=1, source_target_pairs={{0,3},{1,0},{2,1},{3,2},{4,7},{5,4},{6,5},{7,6},{8,11},{9,8},{10,9... | collective-permute-start | bytes 49160 | tf_op jit(solution)/shard_map/ppermute | solution.py:381
  25.7 6.1 %collective-permute-start.9 = (bf16[144,512]{1,0:T(8,128)(2,1)S(1)}, bf16[144,512]{1,0:T(8,128)(2,1)S(1)}, u32[]{:S(2)}, u32[]{:S(2)}) collective-permute-start(bf16[144,512]{1,0:T(8,128)(2,1)S(1)} %pad_maximum_fusion.latent_ref), channel_id=1, source_target_pairs={{0,4},{8,12},{16,20},{24,28},{4,0},{12,8},{20,16},{28,24},{1,5},{9... | collective-permute-start | bytes 442376 | tf_op jit(solution)/shard_map/ppermute | solution.py:386
  26.3 6.5 %collective-permute-start.8 = (bf16[144,512]{1,0:T(8,128)(2,1)S(1)}, bf16[144,512]{1,0:T(8,128)(2,1)S(1)}, u32[]{:S(2)}, u32[]{:S(2)}) collective-permute-start(bf16[144,512]{1,0:T(8,128)(2,1)S(1)} %pad_maximum_fusion.latent_ref), channel_id=1, source_target_pairs={{4,8},{12,16},{20,24},{8,4},{16,12},{24,20},{5,9},{13,17},{21,25},... | collective-permute-start | bytes 442376 | tf_op jit(solution)/shard_map/ppermute | solution.py:386

commit v12 on v11

--- a/solution.py
+++ b/solution.py
@@ -79,9 +79,10 @@
         block = listed_ref[0, at]
         step_reg = (block // sectors - reg_here) * toward
         step_lon = (block % sectors - lon_here + 1 + sectors) % sectors - 1
-        side = jnp.where(step_lon == 0, 0, jnp.where(step_lon > 0, 1, 4))
-        ahead = jnp.where(step_lon < 0, 0, 1)
-        behind = jnp.where(step_lon < 0, 7, 4 + side)
+        lean = step_lon * (1 - 2 * (lon_here % 2))
+        side = jnp.where(lean == 0, 0, jnp.where(lean > 0, 1, 4))
+        ahead = jnp.where(lean < 0, 0, 1)
+        behind = jnp.where(lean < 0, 7, 4 + side)
         found.append(jnp.where(step_reg == 0, ahead, jnp.where(step_reg > 0, 2 + side, behind)))
     for low in range(len(found)):
         for high in range(low + 1, len(found)):
@@ -136,7 +137,8 @@
             choice_ref[at, candidate] = same.astype(BF16)
     lat_rows, lon_cols = cell_ref.shape
     place, node = iota((ROWS, rows), 0), iota((ROWS, rows), 1)
-    for side, first in enumerate((0, lon_cols - REACH)):
+    odd = lax.axis_index("lon") % 2
+    for side, first in enumerate(((1 - odd) * (lon_cols - REACH), odd * (lon_cols - REACH))):
         hit = jnp.zeros((ROWS, rows), F32)
         for row in range(lat_rows):
             for col in range(REACH):
@@ -182,13 +184,13 @@
 
 
 def early_kernel(
-    choice_ref, west_ref, east_ref, inner_ref, outer_ref,
+    choice_ref, other_ref, pair_ref, inner_ref, outer_ref,
     gain_ref, wk_ref, wvt_ref, query_ref, key_ref, value_ref,
     top_ref, sum_ref, keys_ref, values_ref,
 ):
     rows = key_ref.shape[0]
     parts, group, _ = query_ref.shape
-    candidates = [west_ref[...], east_ref[...]]
+    candidates = [other_ref[...], pair_ref[...]]
     candidates += [ref[rows : 2 * rows] if center else ref[:rows] for ref in (inner_ref, outer_ref) for center in (1, 0)]
     nodes = chosen(range(EARLY), rows, choice_ref, candidates)
     keys, values = project(nodes, gain_ref[...], wk_ref, wvt_ref)
@@ -218,7 +220,7 @@
 def late_kernel(
     choice_ref, cells_ref, inner_ref, outer_ref, beside_ref, corner_ref,
     own_ref, gain_ref, wk_ref, wvt_ref, query_ref, top_ref, sum_ref, wout_ref, wlat_ref,
-    state_ref, latent_ref, first_ref, last_ref,
+    state_ref, latent_ref, to_pair_ref, to_other_ref,
     attended_ref,
 ):
     rows, width = state_ref.shape
@@ -263,11 +265,12 @@
     latent = (value / (1.0 + jnp.exp(-value))).astype(BF16)
     latent_ref[...] = latent
     cells = jnp.dot(cells_ref[...], latent, preferred_element_type=F32).astype(BF16)
-    first_ref[...] = cells[:ROWS]
-    last_ref[...] = cells[ROWS:]
+    to_pair_ref[...] = cells[:ROWS]
+    to_other_ref[...] = cells[ROWS:]
 
 
 def hot_rows(values, rows, cols, line):
+    odd = lax.axis_index("lon") % 2
     column = iota((8, cols), 1)
     node = iota((rows + 2 * SIDE, cols), 0).astype(F32)
     for off in range(TAPS):
@@ -276,8 +279,8 @@
         if step:
             where = pltpu.roll(where, (-step) % cols, 1)
         reach = column + step
-        before = (rows + REACH * line + reach + REACH).astype(F32)
-        after = (rows + SIDE + REACH * line + reach - cols).astype(F32)
+        before = (rows + (1 - odd) * SIDE + REACH * line + reach + REACH).astype(F32)
+        after = (rows + odd * SIDE + REACH * line + reach - cols).astype(F32)
         where = jnp.where(reach < 0, before, jnp.where(reach >= cols, after, where))
         yield jnp.where(node == where[:1], 1.0, 0.0).astype(BF16)
 
@@ -377,8 +380,9 @@
     x = nodes.reshape(rows, width)
     gain = norm_gain.reshape(1, width)
 
-    def shifted(array, step):
-        return lax.ppermute(array, "lon", [(i, (i + step) % sectors) for i in range(sectors)])
+    def paired(array, first):
+        pairs = [(i, (i + 1) % sectors) for i in range(first, sectors, 2)]
+        return lax.ppermute(array, "lon", pairs + [(j, i) for i, j in pairs])
 
     def exchanged(array, first):
         size = lax.axis_size("reg")
@@ -388,8 +392,8 @@
     def in_hbm(*arrays):
         return [pltpu.with_memory_space_constraint(array, pltpu.HBM) for array in arrays]
 
-    west = shifted(x, 1)
-    east = shifted(x, -1)
+    other = paired(x, 1)
+    pair = paired(x, 0)
 
     outputs = -(-out_ch // ROWS) * ROWS
     head = width // HEADS
@@ -452,15 +456,15 @@
         name="prepare",
     )(own, *in_hbm(gain, w_qkv, assignment, neighbours))
     own, query = lax.optimization_barrier((own, query))
-    message = jnp.concatenate([east, own], axis=0)
+    message = jnp.concatenate([pair, own], axis=0)
     message_a = message
-    west_a = west
+    other_a = other
     inner = exchanged(message_a, 0)
     outer = exchanged(message, 1)
-    corner = exchanged(west, 1)
-    beside = exchanged(west_a, 0)
-
-    edges, west_m = mixed(blocks_of(ABOVE) + blocks_of(BELOW), "mix_edges", west)
+    corner = exchanged(other, 1)
+    beside = exchanged(other_a, 0)
+
+    edges, other_m = mixed(blocks_of(ABOVE) + blocks_of(BELOW), "mix_edges", other)
     inner, edges = lax.optimization_barrier((inner, edges))
     top, summed = pl.pallas_call(
         early_kernel,
@@ -477,8 +481,8 @@
         compiler_params=params(32),
         cost_estimate=cost(3e9, 6e6),
         name="early",
-    )(choice, west, east, inner, outer, gain, wk, wvt, query, key, value)
-    state, latent, first, last = pl.pallas_call(
+    )(choice, other, pair, inner, outer, gain, wk, wvt, query, key, value)
+    state, latent, to_pair, to_other = pl.pallas_call(
         late_kernel,
         in_specs=[whole()] * 15,
         out_specs=[whole()] * 4,
@@ -493,11 +497,11 @@
         own, gain, wk, wvt, query, top, summed, w_out, w_latent,
     )
 
-    from_left = shifted(last, 1)
-    from_right = shifted(first, -1)
+    from_pair = paired(to_pair, 0)
+    from_other = paired(to_other, 1)
     middle, latent = mixed(blocks_of(OWN), "mix_own", latent)
-    from_left, middle = lax.optimization_barrier((from_left, middle))
-    extended = jnp.concatenate([latent, from_left[:SIDE], from_right[:SIDE]], axis=0)
+    from_pair, middle = lax.optimization_barrier((from_pair, middle))
+    extended = jnp.concatenate([latent, from_pair[:SIDE], from_other[:SIDE]], axis=0)
     far = exchanged(extended, 1)
     near = exchanged(extended, 0)
 

time: 34.6 us -> 34.7 us (level)
  starting transfers between devices: 18.2 us -> 18.7 us
    ppermute x6, waiting for transfers between devices: 1.19 us -> 0.48 us  [exchanged(): return lax.ppermute(array, 'reg', pairs + [(j, i) for i, j in pairs])]
    ppermute x4, waiting for transfers between devices: 1.11 us -> 1.48 us  [paired(): return lax.ppermute(array, 'lon', pairs + [(j, i) for i, j in pairs])]
  transfers between devices with their start and end apart: 10 -> 10, of which waited for: 4 -> 3; matrix products, arithmetic and copies ran while one was open for 0% -> 0% of each run, Pallas kernels for 27% -> 27%
where the time goes in v12:
time: 34.7 us; the launch traced here: 34.5 us
  starting transfers between devices  18.7 us (54%)
  Pallas kernels  12.9 us (37%)
  waiting for transfers between devices  1.97 us (6%)
  between operations  0.85 us (2%)
    ppermute x6, starting transfers between devices, exchanged(): return lax.ppermute(array, 'reg', pairs + [(j, i) for i, j in pairs])  12.3 us
    ppermute x4, starting transfers between devices, paired(): return lax.ppermute(array, 'lon', pairs + [(j, i) for i, j in pairs])  6.38 us
    pallas_call x1, Pallas kernels, shards(): pl.pallas_call(late_kernel, in_specs=[whole()] * 15, out_specs=[whole()]...  2.14 us
    pallas_call x1, Pallas kernels, shards(): pl.pallas_call(functools.partial(prepare_kernel, sectors), in_specs=[whol...  2.02 us
    pallas_call x2, Pallas kernels, mixed(): pl.pallas_call(functools.partial(mix_kernel, blocks), in_specs=[whole()]...  1.82 us
    pallas_call x1, Pallas kernels, shards(): pl.pallas_call(functools.partial(own_kernel, (rows, 2 * rows, 2 * rows)),...  1.8 us
    pallas_call x1, Pallas kernels, shards(): pl.pallas_call(early_kernel, in_specs=[whole()] * 11, out_specs=[whole()]...  1.65 us
    pallas_call x1, Pallas kernels, shards(): pl.pallas_call(functools.partial(band_kernel, False), in_specs=[whole()]...  1.61 us
  transfers between devices with their start and end apart: 10, of which 3 were waited for; matrix products, arithmetic and copies ran while one was open for 0% of the time, Pallas kernels for 27%

profile of v12, /device:TPU:1, one launch (start us, length us, event | category | flops | bytes accessed | tf_op | source)
XLA Modules:
  0.0 34.5 jit_solution(11551271584728447308)
XLA Ops:
  0.6 2.1 %collective-permute-start = (bf16[128,512]{1,0:T(8,128)(2,1)}, bf16[128,512]{1,0:T(8,128)(2,1)S(1)}, u32[]{:S(2)}, u32[]{:S(2)}) collective-permute-start(bf16[128,512]{1,0:T(8,128)(2,1)} %bitcast.13), channel_id=1, source_target_pairs={{0,1},{2,3},{1,0},{3,2},{4,5},{6,7},{5,4},{7,6},{8,9},{10,11},{9,8... | collective-permute-start | bytes 393224 | tf_op jit(solution)/shard_map/ppermute | solution.py:385
  2.8 1.2 %collective-permute-start.2 = (bf16[128,512]{1,0:T(8,128)(2,1)}, bf16[128,512]{1,0:T(8,128)(2,1)S(1)}, u32[]{:S(2)}, u32[]{:S(2)}) collective-permute-start(bf16[128,512]{1,0:T(8,128)(2,1)} %bitcast.14), channel_id=1, source_target_pairs={{1,2},{3,0},{2,1},{0,3},{5,6},{7,4},{6,5},{4,7},{9,10},{11,8},{10,... | collective-permute-start | bytes 393224 | tf_op jit(solution)/shard_map/ppermute | solution.py:385
  4.0 1.0 %gather.1.own_ref = bf16[144,512]{1,0:T(8,128)(2,1)S(1)} custom-call(bf16[128,512]{1,0:T(8,128)(2,1)} %bitcast.15, s32[2,256]{1,0:T(2,128)} %assign_hbm.3), custom_call_target="tpu_custom_call" | custom-call | flops 1000 | bytes 1000 | tf_op jit(solution)/shard_map/gather/pallas_call | solution.py:421
  4.9 2.0 %prepare.1 = (bf16[4,128,512]{2,1,0:T(8,128)(2,1)S(1)}, bf16[128,512]{1,0:T(8,128)(2,1)S(1)}, bf16[512,128]{1,0:T(8,128)(2,1)S(1)}, bf16[512,512]{1,0:T(8,128)(2...) custom-call(bf16[144,512]{1,0:T(8,128)(2,1)S(1)} %gather.1.own_ref, ...), custom_call_target="tpu_custom_call" | custom-call | flops 500000000 | bytes 1000000 | tf_op jit(solution)/shard_map/prepare/pallas_call | solution.py:434
  7.0 0.0 collective-permute-done.pair_ref
  7.0 1.3 %collective-permute-start.1 = (bf16[272,512]{1,0:T(8,128)(2,1)S(1)}, bf16[272,512]{1,0:T(8,128)(2,1)S(1)}, u32[]{:S(2)}, u32[]{:S(2)}) collective-permute-start(bf16[272,512]{1,0:T(8,128)(2,1)S(1)} %constant_dynamic-update-slice_fusion), channel_id=1, source_target_pairs={{0,4},{8,12},{16,20},{24,28},{4,0},{12,8},{20,16},{28,24},{1,5},{9... | collective-permute-start | bytes 835592 | tf_op jit(solution)/shard_map/ppermute | solution.py:390
  8.3 3.2 %collective-permute-start.3 = (bf16[272,512]{1,0:T(8,128)(2,1)S(1)}, bf16[272,512]{1,0:T(8,128)(2,1)S(1)}, u32[]{:S(2)}, u32[]{:S(2)}) collective-permute-start(bf16[272,512]{1,0:T(8,128)(2,1)S(1)} %constant_dynamic-update-slice_fusion), channel_id=1, source_target_pairs={{4,8},{12,16},{20,24},{8,4},{16,12},{24,20},{5,9},{13,17},{21,25},... | collective-permute-start | bytes 835592 | tf_op jit(solution)/shard_map/ppermute | solution.py:390
  11.5 0.0 copy-start.4
  11.5 3.1 %collective-permute-start.5 = (bf16[128,512]{1,0:T(8,128)(2,1)S(1)}, bf16[128,512]{1,0:T(8,128)(2,1)S(1)}, u32[]{:S(2)}, u32[]{:S(2)}) collective-permute-start(bf16[128,512]{1,0:T(8,128)(2,1)S(1)} %collective-permute-done.2.other_ref), channel_id=1, source_target_pairs={{4,8},{12,16},{20,24},{8,4},{16,12},{24,20},{5,9},{13,17},{21,25},... | collective-permute-start | bytes 393224 | tf_op jit(solution)/shard_map/ppermute | solution.py:390
  14.7 0.1 collective-permute-start.4
  14.8 1.0 %mix_edges.1.weights_ref = bf16[30,96,512]{2,1,0:T(8,128)(2,1)S(1)} custom-call(f32[5,5,2,9]{3,2,1,0:T(2,128)S(1)} %bitcast.8, bf16[9,84,512]{2,1,0:T(8,128)(2,1)S(1)} %bitcast.6), custom_call_target="tpu_custom_call" | custom-call | flops 2000000000 | bytes 6000000 | tf_op jit(solution)/shard_map/mix_edges/pallas_call | solution.py:406
  15.8 0.3 %collective-permute-done.3.outer_ref = bf16[272,512]{1,0:T(8,128)(2,1)S(1)} collective-permute-done((bf16[272,512]{1,0:T(8,128)(2,1)S(1)}, bf16[272,512]{1,0:T(8,128)(2,1)S(1)}, u32[]{:S(2)}, u32[]{:S(2)}) %collective-permute-start.3) | collective-permute-done | bytes 278560 | tf_op jit(solution)/shard_map/ppermute | solution.py:390
  16.2 1.6 %early.1 = (f32[4,8,512]{2,1,0:T(8,128)S(1)}, f32[4,144,512]{2,1,0:T(8,128)S(1)}) custom-call(bf16[4,5,16,128]{3,2,1,0:T(8,128)(2,1)S(1)} %get-tuple-element.29.choice_ref, bf16[128,512]{1,0:T(8,128)(2,1)S(1)} %collective-permute-done.2.other_ref, bf16[128,512]{1,0:T(8,128)(2,1)S(1)} %collective-permute-done.pair_ref, ...), custom_call_target="tpu_custom_call" | custom-call | flops 3000000000 | bytes 6000000 | tf_op jit(solution)/shard_map/early/pallas_call | solution.py:469
  17.9 2.1 %late.1 = (bf16[128,512]{1,0:T(8,128)(2,1)S(1)}, bf16[128,512]{1,0:T(8,128)(2,1)S(1)}, bf16[16,512]{1,0:T(8,128)(2,1)S(1)}, bf16[16,512]{1,0:T(8,128)(2,1)S(1)}) custom-call(bf16[4,5,16,128]{3,2,1,0:T(8,128)(2,1)S(1)} %get-tuple-element.29.choice_ref, bf16[32,128]{1,0:T(8,128)(2,1)S(1)} %get-tuple-element.30.cells_ref, ...), custom_call_target="tpu_custom_call" | custom-call | flops 3000000000 | bytes 6000000 | tf_op jit(solution)/shard_map/late/pallas_call | solution.py:485
  20.0 1.9 %collective-permute-start.6 = (bf16[16,512]{1,0:T(8,128)(2,1)S(1)}, bf16[16,512]{1,0:T(8,128)(2,1)S(1)}, u32[]{:S(2)}, u32[]{:S(2)}) collective-permute-start(bf16[16,512]{1,0:T(8,128)(2,1)S(1)} %get-tuple-element.46), channel_id=1, source_target_pairs={{0,1},{2,3},{1,0},{3,2},{4,5},{6,7},{5,4},{7,6},{8,9},{10,11},{9,8... | collective-permute-start | bytes 49160 | tf_op jit(solution)/shard_map/ppermute | solution.py:385
  21.9 1.2 %collective-permute-start.7 = (bf16[16,512]{1,0:T(8,128)(2,1)S(1)}, bf16[16,512]{1,0:T(8,128)(2,1)S(1)}, u32[]{:S(2)}, u32[]{:S(2)}) collective-permute-start(bf16[16,512]{1,0:T(8,128)(2,1)S(1)} %get-tuple-element.50), channel_id=1, source_target_pairs={{1,2},{3,0},{2,1},{0,3},{5,6},{7,4},{6,5},{4,7},{9,10},{11,8},{10,... | collective-permute-start | bytes 49160 | tf_op jit(solution)/shard_map/ppermute | solution.py:385
  23.1 0.8 %mix_own.1.weights_ref = bf16[20,96,512]{2,1,0:T(8,128)(2,1)S(1)} custom-call(f32[5,5,2,9]{3,2,1,0:T(2,128)S(1)} %bitcast.9, bf16[9,84,512]{2,1,0:T(8,128)(2,1)S(1)} %bitcast.7), custom_call_target="tpu_custom_call" | custom-call | flops 2000000000 | bytes 6000000 | tf_op jit(solution)/shard_map/mix_own/pallas_call | solution.py:406
  23.9 1.5 %collective-permute-done.7 = bf16[16,512]{1,0:T(8,128)(2,1)S(1)} collective-permute-done((bf16[16,512]{1,0:T(8,128)(2,1)S(1)}, bf16[16,512]{1,0:T(8,128)(2,1)S(1)}, u32[]{:S(2)}, u32[]{:S(2)}) %collective-permute-start.7) | collective-permute-done | bytes 16416 | tf_op jit(solution)/shard_map/ppermute | solution.py:385
  25.4 1.0 %collective-permute-start.9 = (bf16[144,512]{1,0:T(8,128)(2,1)S(1)}, bf16[144,512]{1,0:T(8,128)(2,1)S(1)}, u32[]{:S(2)}, u32[]{:S(2)}) collective-permute-start(bf16[144,512]{1,0:T(8,128)(2,1)S(1)} %pad_maximum_fusion.latent_ref), channel_id=1, source_target_pairs={{0,4},{8,12},{16,20},{24,28},{4,0},{12,8},{20,16},{28,24},{1,5},{9... | collective-permute-start | bytes 442376 | tf_op jit(solution)/shard_map/ppermute | solution.py:390
  26.4 3.6 %collective-permute-start.8 = (bf16[144,512]{1,0:T(8,128)(2,1)S(1)}, bf16[144,512]{1,0:T(8,128)(2,1)S(1)}, u32[]{:S(2)}, u32[]{:S(2)}) collective-permute-start(bf16[144,512]{1,0:T(8,128)(2,1)S(1)} %pad_maximum_fusion.latent_ref), channel_id=1, source_target_pairs={{4,8},{12,16},{20,24},{8,4},{16,12},{24,20},{5,9},{13,17},{21,25},... | collective-permute-start | bytes 442376 | tf_op jit(solution)/shard_map/ppermute | solution.py:390
  30.0 1.8 %own_band.1 = (f32[2,96,256]{2,1,0:T(8,128)S(1)}, bf16[2,2,5,256,256]{4,3,2,1,0:T(8,128)(2,1)S(1)}, bf16[128,512]{1,0:T(8,128)(2,1)}) custom-call(bf16[128,512]{1,0:T(8,128)(2,1)S(1)} %get-tuple-element.43.state_ref, bf16[144,512]{1,0:T(8,128)(2,1)S(1)} %gather.1.own_ref, bf16[272,512]{1,0:T(8,128)(2,1)S(1)} %collective-permute-done.1.inner_ref, ...), custom_call_target="tpu_custom_call" | custom-call | flops 1000000000 | bytes 2500000 | tf_op jit(solution)/shard_map/own_band/pallas_call | solution.py:509
  31.8 0.9 %inner_band.1.partial_ref = f32[2,96,256]{2,1,0:T(8,128)S(1)} custom-call(bf16[144,512]{1,0:T(8,128)(2,1)S(1)} %collective-permute-done.9.latent_ref, bf16[30,96,512]{2,1,0:T(8,128)(2,1)S(1)} %mix_edges.1.weights_ref, bf16[2,2,5,256,256]{4,3,2,1,0:T(8,128)(2,1)S(1)} %get-tuple-element.54.hot_ref, f32[2,96,256]{2,1,0:T(8,128)S(1)} %get-tuple-element.55.partial_ref), custom_call_target="tpu_custom_call" | custom-call | flops 1000000000 | bytes 2500000 | tf_op jit(solution)/shard_map/inner_band/pallas_call | solution.py:526
  32.7 0.1 collective-permute-done.8.latent_ref
  32.9 1.6 %outer_band.1 = bf16[84,2,256]{2,1,0:T(2,128)(2,1)} custom-call(bf16[144,512]{1,0:T(8,128)(2,1)S(1)} %collective-permute-done.8.latent_ref, bf16[30,96,512]{2,1,0:T(8,128)(2,1)S(1)} %mix_edges.1.weights_ref, bf16[2,2,5,256,256]{4,3,2,1,0:T(8,128)(2,1)S(1)} %get-tuple-element.54.hot_ref, f32[2,96,256]{2,1,0:T(8,128)S(1)} %inner_band.1.partial_ref), custom_call_target="tpu_custom_call" | custom-call | flops 1000000000 | bytes 2500000 | tf_op jit(solution)/shard_map/outer_band/pallas_call | solution.py:536
  (20 shorter events, 0.1 us)
Async XLA Ops:
  0.6 14.1 %copy-start = (bf16[9,512,84]{1,2,0:T(8,128)(2,1)S(1)}, bf16[9,512,84]{1,2,0:T(8,128)(2,1)}, u32[]{:S(2)}) copy-start(bf16[9,512,84]{1,2,0:T(8,128)(2,1)} %param.17) | copy-start | bytes 2322436
  0.6 14.1 %copy-start.3 = (f32[9,2,5,5]{0,1,3,2:T(2,128)S(1)}, f32[9,2,5,5]{0,1,3,2:T(2,128)}, u32[]{:S(2)}) copy-start(f32[9,2,5,5]{0,1,3,2:T(2,128)} %param.16) | copy-start | bytes 5404
  0.6 6.3 %collective-permute-start = (bf16[128,512]{1,0:T(8,128)(2,1)}, bf16[128,512]{1,0:T(8,128)(2,1)S(1)}, u32[]{:S(2)}, u32[]{:S(2)}) collective-permute-start(bf16[128,512]{1,0:T(8,128)(2,1)} %bitcast.13), channel_id=1, source_target_pairs={{0,1},{2,3},{1,0},{3,2},{4,5},{6,7},{5,4},{7,6},{8,9},{10,11},{9,8... | collective-permute-start | bytes 393224 | tf_op jit(solution)/shard_map/ppermute | solution.py:385
  2.8 8.8 %collective-permute-start.2 = (bf16[128,512]{1,0:T(8,128)(2,1)}, bf16[128,512]{1,0:T(8,128)(2,1)S(1)}, u32[]{:S(2)}, u32[]{:S(2)}) collective-permute-start(bf16[128,512]{1,0:T(8,128)(2,1)} %bitcast.14), channel_id=1, source_target_pairs={{1,2},{3,0},{2,1},{0,3},{5,6},{7,4},{6,5},{4,7},{9,10},{11,8},{10,... | collective-permute-start | bytes 393224 | tf_op jit(solution)/shard_map/ppermute | solution.py:385
  7.0 8.8 %collective-permute-start.1 = (bf16[272,512]{1,0:T(8,128)(2,1)S(1)}, bf16[272,512]{1,0:T(8,128)(2,1)S(1)}, u32[]{:S(2)}, u32[]{:S(2)}) collective-permute-start(bf16[272,512]{1,0:T(8,128)(2,1)S(1)} %constant_dynamic-update-slice_fusion), channel_id=1, source_target_pairs={{0,4},{8,12},{16,20},{24,28},{4,0},{12,8},{20,16},{28,24},{1,5},{9... | collective-permute-start | bytes 835592 | tf_op jit(solution)/shard_map/ppermute | solution.py:390
  8.3 7.9 %collective-permute-start.3 = (bf16[272,512]{1,0:T(8,128)(2,1)S(1)}, bf16[272,512]{1,0:T(8,128)(2,1)S(1)}, u32[]{:S(2)}, u32[]{:S(2)}) collective-permute-start(bf16[272,512]{1,0:T(8,128)(2,1)S(1)} %constant_dynamic-update-slice_fusion), channel_id=1, source_target_pairs={{4,8},{12,16},{20,24},{8,4},{16,12},{24,20},{5,9},{13,17},{21,25},... | collective-permute-start | bytes 835592 | tf_op jit(solution)/shard_map/ppermute | solution.py:390
  11.5 4.6 %copy-start.4 = (f32[512]{0:T(512)S(1)}, f32[512]{0:T(512)}, u32[]{:S(2)}) copy-start(f32[512]{0:T(512)} %param.10) | copy-start | bytes 6148
  11.5 6.3 %collective-permute-start.5 = (bf16[128,512]{1,0:T(8,128)(2,1)S(1)}, bf16[128,512]{1,0:T(8,128)(2,1)S(1)}, u32[]{:S(2)}, u32[]{:S(2)}) collective-permute-start(bf16[128,512]{1,0:T(8,128)(2,1)S(1)} %collective-permute-done.2.other_ref), channel_id=1, source_target_pairs={{4,8},{12,16},{20,24},{8,4},{16,12},{24,20},{5,9},{13,17},{21,25},... | collective-permute-start | bytes 393224 | tf_op jit(solution)/shard_map/ppermute | solution.py:390
  14.7 3.2 %collective-permute-start.4 = (bf16[128,512]{1,0:T(8,128)(2,1)S(1)}, bf16[128,512]{1,0:T(8,128)(2,1)S(1)}, u32[]{:S(2)}, u32[]{:S(2)}) collective-permute-start(bf16[128,512]{1,0:T(8,128)(2,1)S(1)} %collective-permute-done.2.other_ref), channel_id=1, source_target_pairs={{0,4},{8,12},{16,20},{24,28},{4,0},{12,8},{20,16},{28,24},{1,5},{9... | collective-permute-start | bytes 393224 | tf_op jit(solution)/shard_map/ppermute | solution.py:390
  16.2 1.7 %copy-start.1 = (bf16[512,512]{1,0:T(8,128)(2,1)S(1)}, bf16[512,512]{1,0:T(8,128)(2,1)}, u32[]{:S(2)}) copy-start(bf16[512,512]{1,0:T(8,128)(2,1)} %wout_ref.1) | copy-start | bytes 1572868
  16.2 1.7 %copy-start.2 = (bf16[512,512]{1,0:T(8,128)(2,1)S(1)}, bf16[512,512]{1,0:T(8,128)(2,1)}, u32[]{:S(2)}) copy-start(bf16[512,512]{1,0:T(8,128)(2,1)} %wlat_ref.1) | copy-start | bytes 1572868
  20.0 3.9 %collective-permute-start.6 = (bf16[16,512]{1,0:T(8,128)(2,1)S(1)}, bf16[16,512]{1,0:T(8,128)(2,1)S(1)}, u32[]{:S(2)}, u32[]{:S(2)}) collective-permute-start(bf16[16,512]{1,0:T(8,128)(2,1)S(1)} %get-tuple-element.46), channel_id=1, source_target_pairs={{0,1},{2,3},{1,0},{3,2},{4,5},{6,7},{5,4},{7,6},{8,9},{10,11},{9,8... | collective-permute-start | bytes 49160 | tf_op jit(solution)/shard_map/ppermute | solution.py:385
  21.9 3.5 %collective-permute-start.7 = (bf16[16,512]{1,0:T(8,128)(2,1)S(1)}, bf16[16,512]{1,0:T(8,128)(2,1)S(1)}, u32[]{:S(2)}, u32[]{:S(2)}) collective-permute-start(bf16[16,512]{1,0:T(8,128)(2,1)S(1)} %get-tuple-element.50), channel_id=1, source_target_pairs={{1,2},{3,0},{2,1},{0,3},{5,6},{7,4},{6,5},{4,7},{9,10},{11,8},{10,... | collective-permute-start | bytes 49160 | tf_op jit(solution)/shard_map/ppermute | solution.py:385
  25.4 6.4 %collective-permute-start.9 = (bf16[144,512]{1,0:T(8,128)(2,1)S(1)}, bf16[144,512]{1,0:T(8,128)(2,1)S(1)}, u32[]{:S(2)}, u32[]{:S(2)}) collective-permute-start(bf16[144,512]{1,0:T(8,128)(2,1)S(1)} %pad_maximum_fusion.latent_ref), channel_id=1, source_target_pairs={{0,4},{8,12},{16,20},{24,28},{4,0},{12,8},{20,16},{28,24},{1,5},{9... | collective-permute-start | bytes 442376 | tf_op jit(solution)/shard_map/ppermute | solution.py:390
  26.4 6.5 %collective-permute-start.8 = (bf16[144,512]{1,0:T(8,128)(2,1)S(1)}, bf16[144,512]{1,0:T(8,128)(2,1)S(1)}, u32[]{:S(2)}, u32[]{:S(2)}) collective-permute-start(bf16[144,512]{1,0:T(8,128)(2,1)S(1)} %pad_maximum_fusion.latent_ref), channel_id=1, source_target_pairs={{4,8},{12,16},{20,24},{8,4},{16,12},{24,20},{5,9},{13,17},{21,25},... | collective-permute-start | bytes 442376 | tf_op jit(solution)/shard_map/ppermute | solution.py:390

commit v13 on v12

--- a/solution.py
+++ b/solution.py
@@ -14,7 +14,7 @@
 SIDE = 8
 ROWS = 16
 LANES = 128
-EARLY = 2
+EARLY = 1
 CANDIDATES = 5
 F32 = jnp.float32
 BF16 = jnp.bfloat16
@@ -80,10 +80,9 @@
         step_reg = (block // sectors - reg_here) * toward
         step_lon = (block % sectors - lon_here + 1 + sectors) % sectors - 1
         lean = step_lon * (1 - 2 * (lon_here % 2))
-        side = jnp.where(lean == 0, 0, jnp.where(lean > 0, 1, 4))
+        place = jnp.where(lean == 0, 0, jnp.where(lean > 0, 1, 2))
         ahead = jnp.where(lean < 0, 0, 1)
-        behind = jnp.where(lean < 0, 7, 4 + side)
-        found.append(jnp.where(step_reg == 0, ahead, jnp.where(step_reg > 0, 2 + side, behind)))
+        found.append(jnp.where(step_reg == 0, ahead, jnp.where(step_reg > 0, 2, 5) + jnp.where(step_reg == 0, 0, place)))
     for low in range(len(found)):
         for high in range(low + 1, len(found)):
             less, more = jnp.minimum(found[low], found[high]), jnp.maximum(found[low], found[high])
@@ -183,15 +182,23 @@
     return keys, values
 
 
+def own_heads(summed, rows):
+    members = summed.shape[1] // rows
+    head = summed.shape[0] // members
+    return [
+        summed[at * head : (at + 1) * head, at * rows : (at + 1) * rows] for at in range(members)
+    ]
+
+
 def early_kernel(
-    choice_ref, other_ref, pair_ref, inner_ref, outer_ref,
+    choice_ref, other_ref, pair_ref, inner_ref, beside_ref,
     gain_ref, wk_ref, wvt_ref, query_ref, key_ref, value_ref,
     top_ref, sum_ref, keys_ref, values_ref,
 ):
     rows = key_ref.shape[0]
     parts, group, _ = query_ref.shape
     candidates = [other_ref[...], pair_ref[...]]
-    candidates += [ref[rows : 2 * rows] if center else ref[:rows] for ref in (inner_ref, outer_ref) for center in (1, 0)]
+    candidates += [inner_ref[rows : 2 * rows], inner_ref[:rows], beside_ref[...]]
     nodes = chosen(range(EARLY), rows, choice_ref, candidates)
     keys, values = project(nodes, gain_ref[...], wk_ref, wvt_ref)
     keys_ref[:rows] = key_ref[...]
@@ -213,12 +220,14 @@
             scores = scored(part + 1)
         top = jnp.max(now, axis=0, keepdims=True)
         expo = jnp.exp2(now - top).astype(BF16)
-        top_ref[part] = jnp.broadcast_to(top, top_ref.shape[1:])
-        sum_ref[part] = jnp.dot(values_ref[part], expo, preferred_element_type=F32)
+        summed = jnp.dot(values_ref[part], expo, preferred_element_type=F32)
+        top_ref[part, 0] = jnp.broadcast_to(top, top_ref.shape[2:])
+        top_ref[part, 1] = jnp.broadcast_to(summed[group : group + 1], top_ref.shape[2:])
+        sum_ref[part] = jnp.concatenate(own_heads(summed[:group], rows), axis=0)
 
 
 def late_kernel(
-    choice_ref, cells_ref, inner_ref, outer_ref, beside_ref, corner_ref,
+    choice_ref, cells_ref, pair_ref, inner_ref, beside_ref, outer_ref, corner_ref,
     own_ref, gain_ref, wk_ref, wvt_ref, query_ref, top_ref, sum_ref, wout_ref, wlat_ref,
     state_ref, latent_ref, to_pair_ref, to_other_ref,
     attended_ref,
@@ -227,13 +236,11 @@
     parts, group, lanes = query_ref.shape
     members = lanes // rows
     head = group // members
-    candidates = [None, None]
-    candidates += [ref[rows : 2 * rows] if center else ref[:rows] for ref in (inner_ref, outer_ref) for center in (1, 0)]
-    candidates += [beside_ref[...], corner_ref[...]]
+    candidates = [None, pair_ref[...], inner_ref[rows : 2 * rows], inner_ref[:rows], beside_ref[...]]
+    candidates += [outer_ref[rows : 2 * rows], outer_ref[:rows], corner_ref[...]]
     nodes = chosen(range(EARLY, choice_ref.shape[0]), rows, choice_ref, candidates)
     keys, values = project(nodes, gain_ref[...], wk_ref, wvt_ref)
     ones = jnp.ones((ROWS, nodes.shape[0]), BF16)
-    owner = iota((group, rows), 0) // head
 
     def scored(part):
         span = slice(part * group, (part + 1) * group)
@@ -244,17 +251,19 @@
         now = scores
         if part + 1 < parts:
             scores = scored(part + 1)
-        before = top_ref[part, :1]
+        before = top_ref[part, 0, :1]
         top = jnp.maximum(before, jnp.max(now, axis=0, keepdims=True))
         expo = jnp.exp2(now - top).astype(BF16)
         weights = jnp.concatenate([values[part * group : (part + 1) * group], ones], axis=0)
         summed = jnp.dot(weights, expo, preferred_element_type=F32)
-        summed = summed + sum_ref[part] * jnp.exp2(before - top)
-        summed = summed[:group] * (1.0 / summed[group : group + 1])
-        merged = None
-        for member in range(members):
-            piece = summed[:, member * rows : (member + 1) * rows]
-            merged = piece if merged is None else jnp.where(owner == member, piece, merged)
+        shrink = jnp.exp2(before - top)
+        share = 1.0 / (summed[group : group + 1] + top_ref[part, 1, :1] * shrink)
+        merged = []
+        for member, piece in enumerate(own_heads(summed[:group], rows)):
+            span = slice(member * rows, (member + 1) * rows)
+            earlier = sum_ref[part, member * head : (member + 1) * head]
+            merged.append((piece + earlier * shrink[:, span]) * share[:, span])
+        merged = jnp.concatenate(merged, axis=0)
         attended_ref[:, part * group : (part + 1) * group] = merged.T.astype(BF16)
     state = (
         own_ref[:rows].astype(F32)
@@ -471,8 +480,8 @@
         in_specs=[whole()] * 11,
         out_specs=[whole()] * 2,
         out_shape=[
-            struct(parts, 8, members * rows, dtype=F32),
-            struct(parts, LANES + ROWS, members * rows, dtype=F32),
+            struct(parts, 2, 8, members * rows, dtype=F32),
+            struct(parts, LANES, rows, dtype=F32),
         ],
         scratch_shapes=[
             pltpu.VMEM(((1 + EARLY) * rows, width), BF16),
@@ -481,10 +490,10 @@
         compiler_params=params(32),
         cost_estimate=cost(3e9, 6e6),
         name="early",
-    )(choice, other, pair, inner, outer, gain, wk, wvt, query, key, value)
+    )(choice, other, pair, inner, beside, gain, wk, wvt, query, key, value)
     state, latent, to_pair, to_other = pl.pallas_call(
         late_kernel,
-        in_specs=[whole()] * 15,
+        in_specs=[whole()] * 16,
         out_specs=[whole()] * 4,
         out_shape=[pltpu.VMEM((rows, width), BF16), struct(rows, channels)]
         + [struct(ROWS, channels)] * 2,
@@ -493,7 +502,7 @@
         cost_estimate=cost(3e9, 6e6),
         name="late",
     )(
-        choice, cells, inner, outer, beside, corner,
+        choice, cells, pair, inner, beside, outer, corner,
         own, gain, wk, wvt, query, top, summed, w_out, w_latent,
     )
 

time: 34.7 us -> 35 us (level)
  waiting for transfers between devices: 1.97 us -> 2.73 us
  starting transfers between devices: 18.7 us -> 18 us
    pallas_call x1, Pallas kernels: 2.14 us -> 2.7 us  [shards(): pl.pallas_call(late_kernel, in_specs=[whole()] * 16, out_specs=[whole()]...]
    ppermute x6, starting transfers between devices: 12.3 us -> 11.8 us  [exchanged(): return lax.ppermute(array, 'reg', pairs + [(j, i) for i, j in pairs])]
    ppermute x6, waiting for transfers between devices: 0.48 us -> 0.87 us  [exchanged(): return lax.ppermute(array, 'reg', pairs + [(j, i) for i, j in pairs])]
    ppermute x4, waiting for transfers between devices: 1.48 us -> 1.86 us  [paired(): return lax.ppermute(array, 'lon', pairs + [(j, i) for i, j in pairs])]
    pallas_call x1, Pallas kernels: 1.65 us -> 1.3 us  [shards(): pl.pallas_call(early_kernel, in_specs=[whole()] * 11, out_specs=[whole()]...]
  transfers between devices with their start and end apart: 10 -> 10, of which waited for: 3 -> 4; matrix products, arithmetic and copies ran while one was open for 0% -> 0% of each run, Pallas kernels for 27% -> 25%
where the time goes in v13:
time: 35 us; the launch traced here: 34.8 us
  starting transfers between devices  18 us (51%)
  Pallas kernels  13.1 us (37%)
  waiting for transfers between devices  2.73 us (8%)
  between operations  0.82 us (2%)
    ppermute x6, starting transfers between devices, exchanged(): return lax.ppermute(array, 'reg', pairs + [(j, i) for i, j in pairs])  11.8 us
    ppermute x4, starting transfers between devices, paired(): return lax.ppermute(array, 'lon', pairs + [(j, i) for i, j in pairs])  6.25 us
    pallas_call x1, Pallas kernels, shards(): pl.pallas_call(late_kernel, in_specs=[whole()] * 16, out_specs=[whole()]...  2.7 us
    pallas_call x1, Pallas kernels, shards(): pl.pallas_call(functools.partial(prepare_kernel, sectors), in_specs=[whol...  2.02 us
    ppermute x4, waiting for transfers between devices, paired(): return lax.ppermute(array, 'lon', pairs + [(j, i) for i, j in pairs])  1.86 us
    pallas_call x2, Pallas kernels, mixed(): pl.pallas_call(functools.partial(mix_kernel, blocks), in_specs=[whole()]...  1.82 us
    pallas_call x1, Pallas kernels, shards(): pl.pallas_call(functools.partial(own_kernel, (rows, 2 * rows, 2 * rows)),...  1.8 us
    pallas_call x1, Pallas kernels, shards(): pl.pallas_call(functools.partial(band_kernel, False), in_specs=[whole()]...  1.61 us
  transfers between devices with their start and end apart: 10, of which 4 were waited for; matrix products, arithmetic and copies ran while one was open for 0% of the time, Pallas kernels for 25%

profile of v13, /device:TPU:1, one launch (start us, length us, event | category | flops | bytes accessed | tf_op | source)
XLA Modules:
  0.0 34.8 jit_solution(10818622460274443690)
XLA Ops:
  0.6 2.1 %collective-permute-start = (bf16[128,512]{1,0:T(8,128)(2,1)}, bf16[128,512]{1,0:T(8,128)(2,1)S(1)}, u32[]{:S(2)}, u32[]{:S(2)}) collective-permute-start(bf16[128,512]{1,0:T(8,128)(2,1)} %bitcast.13), channel_id=1, source_target_pairs={{0,1},{2,3},{1,0},{3,2},{4,5},{6,7},{5,4},{7,6},{8,9},{10,11},{9,8... | collective-permute-start | bytes 393224 | tf_op jit(solution)/shard_map/ppermute | solution.py:394
  2.8 1.2 %collective-permute-start.2 = (bf16[128,512]{1,0:T(8,128)(2,1)}, bf16[128,512]{1,0:T(8,128)(2,1)S(1)}, u32[]{:S(2)}, u32[]{:S(2)}) collective-permute-start(bf16[128,512]{1,0:T(8,128)(2,1)} %bitcast.14), channel_id=1, source_target_pairs={{1,2},{3,0},{2,1},{0,3},{5,6},{7,4},{6,5},{4,7},{9,10},{11,8},{10,... | collective-permute-start | bytes 393224 | tf_op jit(solution)/shard_map/ppermute | solution.py:394
  4.0 1.0 %gather.1.own_ref = bf16[144,512]{1,0:T(8,128)(2,1)S(1)} custom-call(bf16[128,512]{1,0:T(8,128)(2,1)} %bitcast.15, s32[2,256]{1,0:T(2,128)} %assign_hbm.3), custom_call_target="tpu_custom_call" | custom-call | flops 1000 | bytes 1000 | tf_op jit(solution)/shard_map/gather/pallas_call | solution.py:430
  4.9 2.0 %prepare.1 = (bf16[4,128,512]{2,1,0:T(8,128)(2,1)S(1)}, bf16[128,512]{1,0:T(8,128)(2,1)S(1)}, bf16[512,128]{1,0:T(8,128)(2,1)S(1)}, bf16[512,512]{1,0:T(8,128)(2...) custom-call(bf16[144,512]{1,0:T(8,128)(2,1)S(1)} %gather.1.own_ref, ...), custom_call_target="tpu_custom_call" | custom-call | flops 500000000 | bytes 1000000 | tf_op jit(solution)/shard_map/prepare/pallas_call | solution.py:443
  7.0 1.3 %collective-permute-start.1 = (bf16[272,512]{1,0:T(8,128)(2,1)S(1)}, bf16[272,512]{1,0:T(8,128)(2,1)S(1)}, u32[]{:S(2)}, u32[]{:S(2)}) collective-permute-start(bf16[272,512]{1,0:T(8,128)(2,1)S(1)} %constant_dynamic-update-slice_fusion), channel_id=1, source_target_pairs={{0,4},{8,12},{16,20},{24,28},{4,0},{12,8},{20,16},{28,24},{1,5},{9... | collective-permute-start | bytes 835592 | tf_op jit(solution)/shard_map/ppermute | solution.py:399
  8.3 3.2 %collective-permute-start.4 = (bf16[272,512]{1,0:T(8,128)(2,1)S(1)}, bf16[272,512]{1,0:T(8,128)(2,1)S(1)}, u32[]{:S(2)}, u32[]{:S(2)}) collective-permute-start(bf16[272,512]{1,0:T(8,128)(2,1)S(1)} %constant_dynamic-update-slice_fusion), channel_id=1, source_target_pairs={{4,8},{12,16},{20,24},{8,4},{16,12},{24,20},{5,9},{13,17},{21,25},... | collective-permute-start | bytes 835592 | tf_op jit(solution)/shard_map/ppermute | solution.py:399
  11.5 0.0 copy-start.4
  11.5 3.1 %collective-permute-start.5 = (bf16[128,512]{1,0:T(8,128)(2,1)S(1)}, bf16[128,512]{1,0:T(8,128)(2,1)S(1)}, u32[]{:S(2)}, u32[]{:S(2)}) collective-permute-start(bf16[128,512]{1,0:T(8,128)(2,1)S(1)} %collective-permute-done.2.other_ref), channel_id=1, source_target_pairs={{4,8},{12,16},{20,24},{8,4},{16,12},{24,20},{5,9},{13,17},{21,25},... | collective-permute-start | bytes 393224 | tf_op jit(solution)/shard_map/ppermute | solution.py:399
  14.7 0.1 collective-permute-start.3
  14.8 1.0 %mix_edges.1.weights_ref = bf16[30,96,512]{2,1,0:T(8,128)(2,1)S(1)} custom-call(f32[5,5,2,9]{3,2,1,0:T(2,128)S(1)} %bitcast.8, bf16[9,84,512]{2,1,0:T(8,128)(2,1)S(1)} %bitcast.6), custom_call_target="tpu_custom_call" | custom-call | flops 2000000000 | bytes 6000000 | tf_op jit(solution)/shard_map/mix_edges/pallas_call | solution.py:415
  15.8 0.3 collective-permute-done.3.beside_ref
  16.1 1.3 %early.1 = (f32[4,2,8,512]{3,2,1,0:T(8,128)S(1)}, f32[4,128,128]{2,1,0:T(8,128)S(1)}) custom-call(bf16[4,5,16,128]{3,2,1,0:T(8,128)(2,1)S(1)} %get-tuple-element.29.choice_ref, bf16[128,512]{1,0:T(8,128)(2,1)S(1)} %collective-permute-done.2.other_ref, bf16[128,512]{1,0:T(8,128)(2,1)S(1)} %collective-permute-done.pair_ref, ...), custom_call_target="tpu_custom_call" | custom-call | flops 3000000000 | bytes 6000000 | tf_op jit(solution)/shard_map/early/pallas_call | solution.py:478
  17.4 0.4 %collective-permute-done.5.corner_ref = bf16[128,512]{1,0:T(8,128)(2,1)S(1)} collective-permute-done((bf16[128,512]{1,0:T(8,128)(2,1)S(1)}, bf16[128,512]{1,0:T(8,128)(2,1)S(1)}, u32[]{:S(2)}, u32[]{:S(2)}) %collective-permute-start.5) | collective-permute-done | bytes 131104 | tf_op jit(solution)/shard_map/ppermute | solution.py:399
  17.8 2.7 %late.1 = (bf16[128,512]{1,0:T(8,128)(2,1)S(1)}, bf16[128,512]{1,0:T(8,128)(2,1)S(1)}, bf16[16,512]{1,0:T(8,128)(2,1)S(1)}, bf16[16,512]{1,0:T(8,128)(2,1)S(1)}) custom-call(bf16[4,5,16,128]{3,2,1,0:T(8,128)(2,1)S(1)} %get-tuple-element.29.choice_ref, bf16[32,128]{1,0:T(8,128)(2,1)S(1)} %get-tuple-element.30.cells_ref, ...), custom_call_target="tpu_custom_call" | custom-call | flops 3000000000 | bytes 6000000 | tf_op jit(solution)/shard_map/late/pallas_call | solution.py:494
  20.5 1.7 %collective-permute-start.6 = (bf16[16,512]{1,0:T(8,128)(2,1)S(1)}, bf16[16,512]{1,0:T(8,128)(2,1)S(1)}, u32[]{:S(2)}, u32[]{:S(2)}) collective-permute-start(bf16[16,512]{1,0:T(8,128)(2,1)S(1)} %get-tuple-element.46), channel_id=1, source_target_pairs={{0,1},{2,3},{1,0},{3,2},{4,5},{6,7},{5,4},{7,6},{8,9},{10,11},{9,8... | collective-permute-start | bytes 49160 | tf_op jit(solution)/shard_map/ppermute | solution.py:394
  22.3 1.2 %collective-permute-start.7 = (bf16[16,512]{1,0:T(8,128)(2,1)S(1)}, bf16[16,512]{1,0:T(8,128)(2,1)S(1)}, u32[]{:S(2)}, u32[]{:S(2)}) collective-permute-start(bf16[16,512]{1,0:T(8,128)(2,1)S(1)} %get-tuple-element.50), channel_id=1, source_target_pairs={{1,2},{3,0},{2,1},{0,3},{5,6},{7,4},{6,5},{4,7},{9,10},{11,8},{10,... | collective-permute-start | bytes 49160 | tf_op jit(solution)/shard_map/ppermute | solution.py:394
  23.5 0.8 %mix_own.1.weights_ref = bf16[20,96,512]{2,1,0:T(8,128)(2,1)S(1)} custom-call(f32[5,5,2,9]{3,2,1,0:T(2,128)S(1)} %bitcast.9, bf16[9,84,512]{2,1,0:T(8,128)(2,1)S(1)} %bitcast.7), custom_call_target="tpu_custom_call" | custom-call | flops 2000000000 | bytes 6000000 | tf_op jit(solution)/shard_map/mix_own/pallas_call | solution.py:415
  24.3 1.9 %collective-permute-done.7 = bf16[16,512]{1,0:T(8,128)(2,1)S(1)} collective-permute-done((bf16[16,512]{1,0:T(8,128)(2,1)S(1)}, bf16[16,512]{1,0:T(8,128)(2,1)S(1)}, u32[]{:S(2)}, u32[]{:S(2)}) %collective-permute-start.7) | collective-permute-done | bytes 16416 | tf_op jit(solution)/shard_map/ppermute | solution.py:394
  26.1 0.6 %collective-permute-start.9 = (bf16[144,512]{1,0:T(8,128)(2,1)S(1)}, bf16[144,512]{1,0:T(8,128)(2,1)S(1)}, u32[]{:S(2)}, u32[]{:S(2)}) collective-permute-start(bf16[144,512]{1,0:T(8,128)(2,1)S(1)} %pad_maximum_fusion.latent_ref), channel_id=1, source_target_pairs={{0,4},{8,12},{16,20},{24,28},{4,0},{12,8},{20,16},{28,24},{1,5},{9... | collective-permute-start | bytes 442376 | tf_op jit(solution)/shard_map/ppermute | solution.py:399
  26.7 3.5 %collective-permute-start.8 = (bf16[144,512]{1,0:T(8,128)(2,1)S(1)}, bf16[144,512]{1,0:T(8,128)(2,1)S(1)}, u32[]{:S(2)}, u32[]{:S(2)}) collective-permute-start(bf16[144,512]{1,0:T(8,128)(2,1)S(1)} %pad_maximum_fusion.latent_ref), channel_id=1, source_target_pairs={{4,8},{12,16},{20,24},{8,4},{16,12},{24,20},{5,9},{13,17},{21,25},... | collective-permute-start | bytes 442376 | tf_op jit(solution)/shard_map/ppermute | solution.py:399
  30.3 1.8 %own_band.1 = (f32[2,96,256]{2,1,0:T(8,128)S(1)}, bf16[2,2,5,256,256]{4,3,2,1,0:T(8,128)(2,1)S(1)}, bf16[128,512]{1,0:T(8,128)(2,1)}) custom-call(bf16[128,512]{1,0:T(8,128)(2,1)S(1)} %get-tuple-element.43.state_ref, bf16[144,512]{1,0:T(8,128)(2,1)S(1)} %gather.1.own_ref, bf16[272,512]{1,0:T(8,128)(2,1)S(1)} %collective-permute-done.1.inner_ref, ...), custom_call_target="tpu_custom_call" | custom-call | flops 1000000000 | bytes 2500000 | tf_op jit(solution)/shard_map/own_band/pallas_call | solution.py:518
  32.1 0.9 %inner_band.1.partial_ref = f32[2,96,256]{2,1,0:T(8,128)S(1)} custom-call(bf16[144,512]{1,0:T(8,128)(2,1)S(1)} %collective-permute-done.9.latent_ref, bf16[30,96,512]{2,1,0:T(8,128)(2,1)S(1)} %mix_edges.1.weights_ref, bf16[2,2,5,256,256]{4,3,2,1,0:T(8,128)(2,1)S(1)} %get-tuple-element.54.hot_ref, f32[2,96,256]{2,1,0:T(8,128)S(1)} %get-tuple-element.55.partial_ref), custom_call_target="tpu_custom_call" | custom-call | flops 1000000000 | bytes 2500000 | tf_op jit(solution)/shard_map/inner_band/pallas_call | solution.py:535
  33.0 0.2 collective-permute-done.8.latent_ref
  33.1 1.6 %outer_band.1 = bf16[84,2,256]{2,1,0:T(2,128)(2,1)} custom-call(bf16[144,512]{1,0:T(8,128)(2,1)S(1)} %collective-permute-done.8.latent_ref, bf16[30,96,512]{2,1,0:T(8,128)(2,1)S(1)} %mix_edges.1.weights_ref, bf16[2,2,5,256,256]{4,3,2,1,0:T(8,128)(2,1)S(1)} %get-tuple-element.54.hot_ref, f32[2,96,256]{2,1,0:T(8,128)S(1)} %inner_band.1.partial_ref), custom_call_target="tpu_custom_call" | custom-call | flops 1000000000 | bytes 2500000 | tf_op jit(solution)/shard_map/outer_band/pallas_call | solution.py:545
  (20 shorter events, 0.1 us)
Async XLA Ops:
  0.6 14.1 %copy-start = (bf16[9,512,84]{1,2,0:T(8,128)(2,1)S(1)}, bf16[9,512,84]{1,2,0:T(8,128)(2,1)}, u32[]{:S(2)}) copy-start(bf16[9,512,84]{1,2,0:T(8,128)(2,1)} %param.17) | copy-start | bytes 2322436
  0.6 14.1 %copy-start.3 = (f32[9,2,5,5]{0,1,3,2:T(2,128)S(1)}, f32[9,2,5,5]{0,1,3,2:T(2,128)}, u32[]{:S(2)}) copy-start(f32[9,2,5,5]{0,1,3,2:T(2,128)} %param.16) | copy-start | bytes 5404
  0.6 6.3 %collective-permute-start = (bf16[128,512]{1,0:T(8,128)(2,1)}, bf16[128,512]{1,0:T(8,128)(2,1)S(1)}, u32[]{:S(2)}, u32[]{:S(2)}) collective-permute-start(bf16[128,512]{1,0:T(8,128)(2,1)} %bitcast.13), channel_id=1, source_target_pairs={{0,1},{2,3},{1,0},{3,2},{4,5},{6,7},{5,4},{7,6},{8,9},{10,11},{9,8... | collective-permute-start | bytes 393224 | tf_op jit(solution)/shard_map/ppermute | solution.py:394
  2.8 8.8 %collective-permute-start.2 = (bf16[128,512]{1,0:T(8,128)(2,1)}, bf16[128,512]{1,0:T(8,128)(2,1)S(1)}, u32[]{:S(2)}, u32[]{:S(2)}) collective-permute-start(bf16[128,512]{1,0:T(8,128)(2,1)} %bitcast.14), channel_id=1, source_target_pairs={{1,2},{3,0},{2,1},{0,3},{5,6},{7,4},{6,5},{4,7},{9,10},{11,8},{10,... | collective-permute-start | bytes 393224 | tf_op jit(solution)/shard_map/ppermute | solution.py:394
  7.0 8.8 %collective-permute-start.1 = (bf16[272,512]{1,0:T(8,128)(2,1)S(1)}, bf16[272,512]{1,0:T(8,128)(2,1)S(1)}, u32[]{:S(2)}, u32[]{:S(2)}) collective-permute-start(bf16[272,512]{1,0:T(8,128)(2,1)S(1)} %constant_dynamic-update-slice_fusion), channel_id=1, source_target_pairs={{0,4},{8,12},{16,20},{24,28},{4,0},{12,8},{20,16},{28,24},{1,5},{9... | collective-permute-start | bytes 835592 | tf_op jit(solution)/shard_map/ppermute | solution.py:399
  8.3 9.5 %collective-permute-start.4 = (bf16[272,512]{1,0:T(8,128)(2,1)S(1)}, bf16[272,512]{1,0:T(8,128)(2,1)S(1)}, u32[]{:S(2)}, u32[]{:S(2)}) collective-permute-start(bf16[272,512]{1,0:T(8,128)(2,1)S(1)} %constant_dynamic-update-slice_fusion), channel_id=1, source_target_pairs={{4,8},{12,16},{20,24},{8,4},{16,12},{24,20},{5,9},{13,17},{21,25},... | collective-permute-start | bytes 835592 | tf_op jit(solution)/shard_map/ppermute | solution.py:399
  11.5 4.5 %copy-start.4 = (f32[512]{0:T(512)S(1)}, f32[512]{0:T(512)}, u32[]{:S(2)}) copy-start(f32[512]{0:T(512)} %param.10) | copy-start | bytes 6148
  11.5 6.3 %collective-permute-start.5 = (bf16[128,512]{1,0:T(8,128)(2,1)S(1)}, bf16[128,512]{1,0:T(8,128)(2,1)S(1)}, u32[]{:S(2)}, u32[]{:S(2)}) collective-permute-start(bf16[128,512]{1,0:T(8,128)(2,1)S(1)} %collective-permute-done.2.other_ref), channel_id=1, source_target_pairs={{4,8},{12,16},{20,24},{8,4},{16,12},{24,20},{5,9},{13,17},{21,25},... | collective-permute-start | bytes 393224 | tf_op jit(solution)/shard_map/ppermute | solution.py:399
  14.7 1.4 %collective-permute-start.3 = (bf16[128,512]{1,0:T(8,128)(2,1)S(1)}, bf16[128,512]{1,0:T(8,128)(2,1)S(1)}, u32[]{:S(2)}, u32[]{:S(2)}) collective-permute-start(bf16[128,512]{1,0:T(8,128)(2,1)S(1)} %collective-permute-done.2.other_ref), channel_id=1, source_target_pairs={{0,4},{8,12},{16,20},{24,28},{4,0},{12,8},{20,16},{28,24},{1,5},{9... | collective-permute-start | bytes 393224 | tf_op jit(solution)/shard_map/ppermute | solution.py:399
  16.1 1.8 %copy-start.1 = (bf16[512,512]{1,0:T(8,128)(2,1)S(1)}, bf16[512,512]{1,0:T(8,128)(2,1)}, u32[]{:S(2)}) copy-start(bf16[512,512]{1,0:T(8,128)(2,1)} %wout_ref.1) | copy-start | bytes 1572868
  16.1 1.8 %copy-start.2 = (bf16[512,512]{1,0:T(8,128)(2,1)S(1)}, bf16[512,512]{1,0:T(8,128)(2,1)}, u32[]{:S(2)}) copy-start(bf16[512,512]{1,0:T(8,128)(2,1)} %wlat_ref.1) | copy-start | bytes 1572868
  20.5 3.7 %collective-permute-start.6 = (bf16[16,512]{1,0:T(8,128)(2,1)S(1)}, bf16[16,512]{1,0:T(8,128)(2,1)S(1)}, u32[]{:S(2)}, u32[]{:S(2)}) collective-permute-start(bf16[16,512]{1,0:T(8,128)(2,1)S(1)} %get-tuple-element.46), channel_id=1, source_target_pairs={{0,1},{2,3},{1,0},{3,2},{4,5},{6,7},{5,4},{7,6},{8,9},{10,11},{9,8... | collective-permute-start | bytes 49160 | tf_op jit(solution)/shard_map/ppermute | solution.py:394
  22.3 3.9 %collective-permute-start.7 = (bf16[16,512]{1,0:T(8,128)(2,1)S(1)}, bf16[16,512]{1,0:T(8,128)(2,1)S(1)}, u32[]{:S(2)}, u32[]{:S(2)}) collective-permute-start(bf16[16,512]{1,0:T(8,128)(2,1)S(1)} %get-tuple-element.50), channel_id=1, source_target_pairs={{1,2},{3,0},{2,1},{0,3},{5,6},{7,4},{6,5},{4,7},{9,10},{11,8},{10,... | collective-permute-start | bytes 49160 | tf_op jit(solution)/shard_map/ppermute | solution.py:394
  26.1 5.9 %collective-permute-start.9 = (bf16[144,512]{1,0:T(8,128)(2,1)S(1)}, bf16[144,512]{1,0:T(8,128)(2,1)S(1)}, u32[]{:S(2)}, u32[]{:S(2)}) collective-permute-start(bf16[144,512]{1,0:T(8,128)(2,1)S(1)} %pad_maximum_fusion.latent_ref), channel_id=1, source_target_pairs={{0,4},{8,12},{16,20},{24,28},{4,0},{12,8},{20,16},{28,24},{1,5},{9... | collective-permute-start | bytes 442376 | tf_op jit(solution)/shard_map/ppermute | solution.py:399
  26.7 6.5 %collective-permute-start.8 = (bf16[144,512]{1,0:T(8,128)(2,1)S(1)}, bf16[144,512]{1,0:T(8,128)(2,1)S(1)}, u32[]{:S(2)}, u32[]{:S(2)}) collective-permute-start(bf16[144,512]{1,0:T(8,128)(2,1)S(1)} %pad_maximum_fusion.latent_ref), channel_id=1, source_target_pairs={{4,8},{12,16},{20,24},{8,4},{16,12},{24,20},{5,9},{13,17},{21,25},... | collective-permute-start | bytes 442376 | tf_op jit(solution)/shard_map/ppermute | solution.py:399

commit v14 on v13

--- a/solution.py
+++ b/solution.py
@@ -15,6 +15,7 @@
 ROWS = 16
 LANES = 128
 EARLY = 1
+MIDDLE = 2
 CANDIDATES = 5
 F32 = jnp.float32
 BF16 = jnp.bfloat16
@@ -226,44 +227,62 @@
         sum_ref[part] = jnp.concatenate(own_heads(summed[:group], rows), axis=0)
 
 
+def updated(keys, values, query_ref, top_ref, sum_ref, part):
+    group, rows = query_ref.shape[1], sum_ref.shape[2]
+    span = slice(part * group, (part + 1) * group)
+    scores = jnp.dot(keys[:, span], query_ref[part], preferred_element_type=F32)
+    before = top_ref[part, 0, :1]
+    top = jnp.maximum(before, jnp.max(scores, axis=0, keepdims=True))
+    expo = jnp.exp2(scores - top).astype(BF16)
+    ones = jnp.ones((ROWS, keys.shape[0]), BF16)
+    weights = jnp.concatenate([values[span], ones], axis=0)
+    summed = jnp.dot(weights, expo, preferred_element_type=F32)
+    shrink = jnp.exp2(before - top)
+    total = summed[group : group + 1] + top_ref[part, 1, :1] * shrink
+    pieces = own_heads(summed[:group], rows)
+    head = group // len(pieces)
+    sums = [
+        piece + sum_ref[part, at * head : (at + 1) * head] * shrink[:, at * rows : (at + 1) * rows]
+        for at, piece in enumerate(pieces)
+    ]
+    return top, total, sums
+
+
+def middle_kernel(
+    choice_ref, pair_ref, inner_ref, beside_ref, outer_ref,
+    gain_ref, wk_ref, wvt_ref, query_ref, top_ref, sum_ref,
+    new_top_ref, new_sum_ref,
+):
+    rows = sum_ref.shape[2]
+    candidates = [None, pair_ref[...], inner_ref[rows : 2 * rows], inner_ref[:rows], beside_ref[...]]
+    candidates += [outer_ref[rows : 2 * rows], outer_ref[:rows]]
+    nodes = chosen(range(EARLY, EARLY + MIDDLE), rows, choice_ref, candidates)
+    keys, values = project(nodes, gain_ref[...], wk_ref, wvt_ref)
+    for part in range(query_ref.shape[0]):
+        top, total, sums = updated(keys, values, query_ref, top_ref, sum_ref, part)
+        new_top_ref[part, 0] = jnp.broadcast_to(top, new_top_ref.shape[2:])
+        new_top_ref[part, 1] = jnp.broadcast_to(total, new_top_ref.shape[2:])
+        new_sum_ref[part] = jnp.concatenate(sums, axis=0)
+
+
 def late_kernel(
-    choice_ref, cells_ref, pair_ref, inner_ref, beside_ref, outer_ref, corner_ref,
+    choice_ref, cells_ref, inner_ref, beside_ref, outer_ref, corner_ref,
     own_ref, gain_ref, wk_ref, wvt_ref, query_ref, top_ref, sum_ref, wout_ref, wlat_ref,
     state_ref, latent_ref, to_pair_ref, to_other_ref,
     attended_ref,
 ):
-    rows, width = state_ref.shape
-    parts, group, lanes = query_ref.shape
-    members = lanes // rows
-    head = group // members
-    candidates = [None, pair_ref[...], inner_ref[rows : 2 * rows], inner_ref[:rows], beside_ref[...]]
+    rows = state_ref.shape[0]
+    parts, group, _ = query_ref.shape
+    candidates = [None] * 3 + [inner_ref[:rows], beside_ref[...]]
     candidates += [outer_ref[rows : 2 * rows], outer_ref[:rows], corner_ref[...]]
-    nodes = chosen(range(EARLY, choice_ref.shape[0]), rows, choice_ref, candidates)
+    entries = range(EARLY + MIDDLE, choice_ref.shape[0])
+    nodes = chosen(entries, rows, choice_ref, candidates)
     keys, values = project(nodes, gain_ref[...], wk_ref, wvt_ref)
-    ones = jnp.ones((ROWS, nodes.shape[0]), BF16)
-
-    def scored(part):
-        span = slice(part * group, (part + 1) * group)
-        return jnp.dot(keys[:, span], query_ref[part], preferred_element_type=F32)
-
-    scores = scored(0)
     for part in range(parts):
-        now = scores
-        if part + 1 < parts:
-            scores = scored(part + 1)
-        before = top_ref[part, 0, :1]
-        top = jnp.maximum(before, jnp.max(now, axis=0, keepdims=True))
-        expo = jnp.exp2(now - top).astype(BF16)
-        weights = jnp.concatenate([values[part * group : (part + 1) * group], ones], axis=0)
-        summed = jnp.dot(weights, expo, preferred_element_type=F32)
-        shrink = jnp.exp2(before - top)
-        share = 1.0 / (summed[group : group + 1] + top_ref[part, 1, :1] * shrink)
-        merged = []
-        for member, piece in enumerate(own_heads(summed[:group], rows)):
-            span = slice(member * rows, (member + 1) * rows)
-            earlier = sum_ref[part, member * head : (member + 1) * head]
-            merged.append((piece + earlier * shrink[:, span]) * share[:, span])
-        merged = jnp.concatenate(merged, axis=0)
+        _, total, sums = updated(keys, values, query_ref, top_ref, sum_ref, part)
+        share = 1.0 / total
+        sums = [one * share[:, at * rows : (at + 1) * rows] for at, one in enumerate(sums)]
+        merged = jnp.concatenate(sums, axis=0)
         attended_ref[:, part * group : (part + 1) * group] = merged.T.astype(BF16)
     state = (
         own_ref[:rows].astype(F32)
@@ -491,9 +510,21 @@
         cost_estimate=cost(3e9, 6e6),
         name="early",
     )(choice, other, pair, inner, beside, gain, wk, wvt, query, key, value)
+    top, summed = pl.pallas_call(
+        middle_kernel,
+        in_specs=[whole()] * 11,
+        out_specs=[whole()] * 2,
+        out_shape=[
+            struct(parts, 2, 8, members * rows, dtype=F32),
+            struct(parts, LANES, rows, dtype=F32),
+        ],
+        compiler_params=params(32),
+        cost_estimate=cost(3e9, 6e6),
+        name="middle",
+    )(choice, pair, inner, beside, outer, gain, wk, wvt, query, top, summed)
     state, latent, to_pair, to_other = pl.pallas_call(
         late_kernel,
-        in_specs=[whole()] * 16,
+        in_specs=[whole()] * 15,
         out_specs=[whole()] * 4,
         out_shape=[pltpu.VMEM((rows, width), BF16), struct(rows, channels)]
         + [struct(ROWS, channels)] * 2,
@@ -502,7 +533,7 @@
         cost_estimate=cost(3e9, 6e6),
         name="late",
     )(
-        choice, cells, pair, inner, beside, outer, corner,
+        choice, cells, inner, beside, outer, corner,
         own, gain, wk, wvt, query, top, summed, w_out, w_latent,
     )
 

time: 35 us -> 36.5 us (1.043)
  Pallas kernels: 13.1 us -> 14.7 us
    pallas_call x1 -> x2, Pallas kernels: 2.7 us -> 4.24 us  [the longest x1 2.2 us: shards(): pl.pallas_call(late_kernel, in_specs=[whole()] * 15, out_specs=[whole()]...]
    ppermute x6, starting transfers between devices: 11.8 us -> 12.5 us  [exchanged(): return lax.ppermute(array, 'reg', pairs + [(j, i) for i, j in pairs])]
    ppermute x4, starting transfers between devices: 6.25 us -> 5.65 us  [paired(): return lax.ppermute(array, 'lon', pairs + [(j, i) for i, j in pairs])]
  transfers between devices with their start and end apart: 10 -> 10, of which waited for: 4 -> 3; matrix products, arithmetic and copies ran while one was open for 0% -> 0% of each run, Pallas kernels for 25% -> 30%
where the time goes in v14:
time: 36.5 us; the launch traced here: 36.3 us
  starting transfers between devices  18.2 us (50%)
  Pallas kernels  14.7 us (40%)
  waiting for transfers between devices  2.48 us (7%)
  between operations  0.87 us (2%)
    ppermute x6, starting transfers between devices, exchanged(): return lax.ppermute(array, 'reg', pairs + [(j, i) for i, j in pairs])  12.5 us
    ppermute x4, starting transfers between devices, paired(): return lax.ppermute(array, 'lon', pairs + [(j, i) for i, j in pairs])  5.65 us
    pallas_call x1, Pallas kernels, shards(): pl.pallas_call(late_kernel, in_specs=[whole()] * 15, out_specs=[whole()]...  2.2 us
    pallas_call x1, Pallas kernels, shards(): pl.pallas_call(middle_kernel, in_specs=[whole()] * 11, out_specs=[whole()...  2.03 us
    pallas_call x1, Pallas kernels, shards(): pl.pallas_call(functools.partial(prepare_kernel, sectors), in_specs=[whol...  2.02 us
    pallas_call x2, Pallas kernels, mixed(): pl.pallas_call(functools.partial(mix_kernel, blocks), in_specs=[whole()]...  1.82 us
    pallas_call x1, Pallas kernels, shards(): pl.pallas_call(functools.partial(own_kernel, (rows, 2 * rows, 2 * rows)),...  1.8 us
    ppermute x4, waiting for transfers between devices, paired(): return lax.ppermute(array, 'lon', pairs + [(j, i) for i, j in pairs])  1.63 us
  transfers between devices with their start and end apart: 10, of which 3 were waited for; matrix products, arithmetic and copies ran while one was open for 0% of the time, Pallas kernels for 30%

profile of v14, /device:TPU:1, one launch (start us, length us, event | category | flops | bytes accessed | tf_op | source)
XLA Modules:
  0.0 36.3 jit_solution(12224202636938176206)
XLA Ops:
  0.6 2.1 %collective-permute-start = (bf16[128,512]{1,0:T(8,128)(2,1)}, bf16[128,512]{1,0:T(8,128)(2,1)S(1)}, u32[]{:S(2)}, u32[]{:S(2)}) collective-permute-start(bf16[128,512]{1,0:T(8,128)(2,1)} %bitcast.14), channel_id=1, source_target_pairs={{0,1},{2,3},{1,0},{3,2},{4,5},{6,7},{5,4},{7,6},{8,9},{10,11},{9,8... | collective-permute-start | bytes 393224 | tf_op jit(solution)/shard_map/ppermute | solution.py:413
  2.8 1.2 %collective-permute-start.2 = (bf16[128,512]{1,0:T(8,128)(2,1)}, bf16[128,512]{1,0:T(8,128)(2,1)S(1)}, u32[]{:S(2)}, u32[]{:S(2)}) collective-permute-start(bf16[128,512]{1,0:T(8,128)(2,1)} %bitcast.15), channel_id=1, source_target_pairs={{1,2},{3,0},{2,1},{0,3},{5,6},{7,4},{6,5},{4,7},{9,10},{11,8},{10,... | collective-permute-start | bytes 393224 | tf_op jit(solution)/shard_map/ppermute | solution.py:413
  4.0 1.0 %gather.1.own_ref = bf16[144,512]{1,0:T(8,128)(2,1)S(1)} custom-call(bf16[128,512]{1,0:T(8,128)(2,1)} %bitcast.16, s32[2,256]{1,0:T(2,128)} %assign_hbm.3), custom_call_target="tpu_custom_call" | custom-call | flops 1000 | bytes 1000 | tf_op jit(solution)/shard_map/gather/pallas_call | solution.py:449
  4.9 2.0 %prepare.1 = (bf16[4,128,512]{2,1,0:T(8,128)(2,1)S(1)}, bf16[128,512]{1,0:T(8,128)(2,1)S(1)}, bf16[512,128]{1,0:T(8,128)(2,1)S(1)}, bf16[512,512]{1,0:T(8,128)(2...) custom-call(bf16[144,512]{1,0:T(8,128)(2,1)S(1)} %gather.1.own_ref, ...), custom_call_target="tpu_custom_call" | custom-call | flops 500000000 | bytes 1000000 | tf_op jit(solution)/shard_map/prepare/pallas_call | solution.py:462
  7.0 1.3 %collective-permute-start.1 = (bf16[272,512]{1,0:T(8,128)(2,1)S(1)}, bf16[272,512]{1,0:T(8,128)(2,1)S(1)}, u32[]{:S(2)}, u32[]{:S(2)}) collective-permute-start(bf16[272,512]{1,0:T(8,128)(2,1)S(1)} %constant_dynamic-update-slice_fusion), channel_id=1, source_target_pairs={{0,4},{8,12},{16,20},{24,28},{4,0},{12,8},{20,16},{28,24},{1,5},{9... | collective-permute-start | bytes 835592 | tf_op jit(solution)/shard_map/ppermute | solution.py:418
  8.3 3.2 %collective-permute-start.4 = (bf16[272,512]{1,0:T(8,128)(2,1)S(1)}, bf16[272,512]{1,0:T(8,128)(2,1)S(1)}, u32[]{:S(2)}, u32[]{:S(2)}) collective-permute-start(bf16[272,512]{1,0:T(8,128)(2,1)S(1)} %constant_dynamic-update-slice_fusion), channel_id=1, source_target_pairs={{4,8},{12,16},{20,24},{8,4},{16,12},{24,20},{5,9},{13,17},{21,25},... | collective-permute-start | bytes 835592 | tf_op jit(solution)/shard_map/ppermute | solution.py:418
  11.5 0.0 copy-start.4
  11.5 3.1 %collective-permute-start.5 = (bf16[128,512]{1,0:T(8,128)(2,1)S(1)}, bf16[128,512]{1,0:T(8,128)(2,1)S(1)}, u32[]{:S(2)}, u32[]{:S(2)}) collective-permute-start(bf16[128,512]{1,0:T(8,128)(2,1)S(1)} %collective-permute-done.2.other_ref), channel_id=1, source_target_pairs={{4,8},{12,16},{20,24},{8,4},{16,12},{24,20},{5,9},{13,17},{21,25},... | collective-permute-start | bytes 393224 | tf_op jit(solution)/shard_map/ppermute | solution.py:418
  14.7 0.1 collective-permute-start.3
  14.8 1.0 %mix_edges.1.weights_ref = bf16[30,96,512]{2,1,0:T(8,128)(2,1)S(1)} custom-call(f32[5,5,2,9]{3,2,1,0:T(2,128)S(1)} %bitcast.8, bf16[9,84,512]{2,1,0:T(8,128)(2,1)S(1)} %bitcast.6), custom_call_target="tpu_custom_call" | custom-call | flops 2000000000 | bytes 6000000 | tf_op jit(solution)/shard_map/mix_edges/pallas_call | solution.py:434
  15.8 0.3 collective-permute-done.3.beside_ref
  16.1 1.3 %early.1 = (f32[4,2,8,512]{3,2,1,0:T(8,128)S(1)}, f32[4,128,128]{2,1,0:T(8,128)S(1)}) custom-call(bf16[4,5,16,128]{3,2,1,0:T(8,128)(2,1)S(1)} %get-tuple-element.31.choice_ref, bf16[128,512]{1,0:T(8,128)(2,1)S(1)} %collective-permute-done.2.other_ref, bf16[128,512]{1,0:T(8,128)(2,1)S(1)} %collective-permute-done.pair_ref, ...), custom_call_target="tpu_custom_call" | custom-call | flops 3000000000 | bytes 6000000 | tf_op jit(solution)/shard_map/early/pallas_call | solution.py:497
  17.4 2.0 %middle.1 = (f32[4,2,8,512]{3,2,1,0:T(8,128)S(1)}, f32[4,128,128]{2,1,0:T(8,128)S(1)}) custom-call(bf16[4,5,16,128]{3,2,1,0:T(8,128)(2,1)S(1)} %get-tuple-element.31.choice_ref, bf16[128,512]{1,0:T(8,128)(2,1)S(1)} %collective-permute-done.pair_ref, bf16[272,512]{1,0:T(8,128)(2,1)S(1)} %collective-permute-done.1.inner_ref, ...), custom_call_target="tpu_custom_call" | custom-call | flops 3000000000 | bytes 6000000 | tf_op jit(solution)/shard_map/middle/pallas_call | solution.py:513
  19.5 2.2 %late.1 = (bf16[128,512]{1,0:T(8,128)(2,1)S(1)}, bf16[128,512]{1,0:T(8,128)(2,1)S(1)}, bf16[16,512]{1,0:T(8,128)(2,1)S(1)}, bf16[16,512]{1,0:T(8,128)(2,1)S(1)}) custom-call(bf16[4,5,16,128]{3,2,1,0:T(8,128)(2,1)S(1)} %get-tuple-element.31.choice_ref, bf16[32,128]{1,0:T(8,128)(2,1)S(1)} %get-tuple-element.32.cells_ref, ...), custom_call_target="tpu_custom_call" | custom-call | flops 3000000000 | bytes 6000000 | tf_op jit(solution)/shard_map/late/pallas_call | solution.py:525
  21.7 1.3 %collective-permute-start.6 = (bf16[16,512]{1,0:T(8,128)(2,1)S(1)}, bf16[16,512]{1,0:T(8,128)(2,1)S(1)}, u32[]{:S(2)}, u32[]{:S(2)}) collective-permute-start(bf16[16,512]{1,0:T(8,128)(2,1)S(1)} %get-tuple-element.50), channel_id=1, source_target_pairs={{0,1},{2,3},{1,0},{3,2},{4,5},{6,7},{5,4},{7,6},{8,9},{10,11},{9,8... | collective-permute-start | bytes 49160 | tf_op jit(solution)/shard_map/ppermute | solution.py:413
  23.0 1.1 %collective-permute-start.7 = (bf16[16,512]{1,0:T(8,128)(2,1)S(1)}, bf16[16,512]{1,0:T(8,128)(2,1)S(1)}, u32[]{:S(2)}, u32[]{:S(2)}) collective-permute-start(bf16[16,512]{1,0:T(8,128)(2,1)S(1)} %get-tuple-element.54), channel_id=1, source_target_pairs={{1,2},{3,0},{2,1},{0,3},{5,6},{7,4},{6,5},{4,7},{9,10},{11,8},{10,... | collective-permute-start | bytes 49160 | tf_op jit(solution)/shard_map/ppermute | solution.py:413
  24.0 0.8 %mix_own.1.weights_ref = bf16[20,96,512]{2,1,0:T(8,128)(2,1)S(1)} custom-call(f32[5,5,2,9]{3,2,1,0:T(2,128)S(1)} %bitcast.9, bf16[9,84,512]{2,1,0:T(8,128)(2,1)S(1)} %bitcast.7), custom_call_target="tpu_custom_call" | custom-call | flops 2000000000 | bytes 6000000 | tf_op jit(solution)/shard_map/mix_own/pallas_call | solution.py:434
  24.8 1.6 %collective-permute-done.7 = bf16[16,512]{1,0:T(8,128)(2,1)S(1)} collective-permute-done((bf16[16,512]{1,0:T(8,128)(2,1)S(1)}, bf16[16,512]{1,0:T(8,128)(2,1)S(1)}, u32[]{:S(2)}, u32[]{:S(2)}) %collective-permute-start.7) | collective-permute-done | bytes 16416 | tf_op jit(solution)/shard_map/ppermute | solution.py:413
  26.5 1.7 %collective-permute-start.9 = (bf16[144,512]{1,0:T(8,128)(2,1)S(1)}, bf16[144,512]{1,0:T(8,128)(2,1)S(1)}, u32[]{:S(2)}, u32[]{:S(2)}) collective-permute-start(bf16[144,512]{1,0:T(8,128)(2,1)S(1)} %pad_maximum_fusion.latent_ref), channel_id=1, source_target_pairs={{0,4},{8,12},{16,20},{24,28},{4,0},{12,8},{20,16},{28,24},{1,5},{9... | collective-permute-start | bytes 442376 | tf_op jit(solution)/shard_map/ppermute | solution.py:418
  28.2 3.1 %collective-permute-start.8 = (bf16[144,512]{1,0:T(8,128)(2,1)S(1)}, bf16[144,512]{1,0:T(8,128)(2,1)S(1)}, u32[]{:S(2)}, u32[]{:S(2)}) collective-permute-start(bf16[144,512]{1,0:T(8,128)(2,1)S(1)} %pad_maximum_fusion.latent_ref), channel_id=1, source_target_pairs={{4,8},{12,16},{20,24},{8,4},{16,12},{24,20},{5,9},{13,17},{21,25},... | collective-permute-start | bytes 442376 | tf_op jit(solution)/shard_map/ppermute | solution.py:418
  31.3 1.8 %own_band.1 = (f32[2,96,256]{2,1,0:T(8,128)S(1)}, bf16[2,2,5,256,256]{4,3,2,1,0:T(8,128)(2,1)S(1)}, bf16[128,512]{1,0:T(8,128)(2,1)}) custom-call(bf16[128,512]{1,0:T(8,128)(2,1)S(1)} %get-tuple-element.47.state_ref, bf16[144,512]{1,0:T(8,128)(2,1)S(1)} %gather.1.own_ref, bf16[272,512]{1,0:T(8,128)(2,1)S(1)} %collective-permute-done.1.inner_ref, ...), custom_call_target="tpu_custom_call" | custom-call | flops 1000000000 | bytes 2500000 | tf_op jit(solution)/shard_map/own_band/pallas_call | solution.py:549
  33.1 0.9 %inner_band.1.partial_ref = f32[2,96,256]{2,1,0:T(8,128)S(1)} custom-call(bf16[144,512]{1,0:T(8,128)(2,1)S(1)} %collective-permute-done.9.latent_ref, bf16[30,96,512]{2,1,0:T(8,128)(2,1)S(1)} %mix_edges.1.weights_ref, bf16[2,2,5,256,256]{4,3,2,1,0:T(8,128)(2,1)S(1)} %get-tuple-element.58.hot_ref, f32[2,96,256]{2,1,0:T(8,128)S(1)} %get-tuple-element.59.partial_ref), custom_call_target="tpu_custom_call" | custom-call | flops 1000000000 | bytes 2500000 | tf_op jit(solution)/shard_map/inner_band/pallas_call | solution.py:566
  34.1 0.6 %collective-permute-done.8.latent_ref = bf16[144,512]{1,0:T(8,128)(2,1)S(1)} collective-permute-done((bf16[144,512]{1,0:T(8,128)(2,1)S(1)}, bf16[144,512]{1,0:T(8,128)(2,1)S(1)}, u32[]{:S(2)}, u32[]{:S(2)}) %collective-permute-start.8) | collective-permute-done | bytes 147488 | tf_op jit(solution)/shard_map/ppermute | solution.py:418
  34.7 1.6 %outer_band.1 = bf16[84,2,256]{2,1,0:T(2,128)(2,1)} custom-call(bf16[144,512]{1,0:T(8,128)(2,1)S(1)} %collective-permute-done.8.latent_ref, bf16[30,96,512]{2,1,0:T(8,128)(2,1)S(1)} %mix_edges.1.weights_ref, bf16[2,2,5,256,256]{4,3,2,1,0:T(8,128)(2,1)S(1)} %get-tuple-element.58.hot_ref, f32[2,96,256]{2,1,0:T(8,128)S(1)} %inner_band.1.partial_ref), custom_call_target="tpu_custom_call" | custom-call | flops 1000000000 | bytes 2500000 | tf_op jit(solution)/shard_map/outer_band/pallas_call | solution.py:576
  (21 shorter events, 0.1 us)
Async XLA Ops:
  0.6 14.1 %copy-start = (bf16[9,512,84]{1,2,0:T(8,128)(2,1)S(1)}, bf16[9,512,84]{1,2,0:T(8,128)(2,1)}, u32[]{:S(2)}) copy-start(bf16[9,512,84]{1,2,0:T(8,128)(2,1)} %param.17) | copy-start | bytes 2322436
  0.6 14.1 %copy-start.3 = (f32[9,2,5,5]{0,1,3,2:T(2,128)S(1)}, f32[9,2,5,5]{0,1,3,2:T(2,128)}, u32[]{:S(2)}) copy-start(f32[9,2,5,5]{0,1,3,2:T(2,128)} %param.16) | copy-start | bytes 5404
  0.6 6.3 %collective-permute-start = (bf16[128,512]{1,0:T(8,128)(2,1)}, bf16[128,512]{1,0:T(8,128)(2,1)S(1)}, u32[]{:S(2)}, u32[]{:S(2)}) collective-permute-start(bf16[128,512]{1,0:T(8,128)(2,1)} %bitcast.14), channel_id=1, source_target_pairs={{0,1},{2,3},{1,0},{3,2},{4,5},{6,7},{5,4},{7,6},{8,9},{10,11},{9,8... | collective-permute-start | bytes 393224 | tf_op jit(solution)/shard_map/ppermute | solution.py:413
  2.8 8.8 %collective-permute-start.2 = (bf16[128,512]{1,0:T(8,128)(2,1)}, bf16[128,512]{1,0:T(8,128)(2,1)S(1)}, u32[]{:S(2)}, u32[]{:S(2)}) collective-permute-start(bf16[128,512]{1,0:T(8,128)(2,1)} %bitcast.15), channel_id=1, source_target_pairs={{1,2},{3,0},{2,1},{0,3},{5,6},{7,4},{6,5},{4,7},{9,10},{11,8},{10,... | collective-permute-start | bytes 393224 | tf_op jit(solution)/shard_map/ppermute | solution.py:413
  7.0 8.8 %collective-permute-start.1 = (bf16[272,512]{1,0:T(8,128)(2,1)S(1)}, bf16[272,512]{1,0:T(8,128)(2,1)S(1)}, u32[]{:S(2)}, u32[]{:S(2)}) collective-permute-start(bf16[272,512]{1,0:T(8,128)(2,1)S(1)} %constant_dynamic-update-slice_fusion), channel_id=1, source_target_pairs={{0,4},{8,12},{16,20},{24,28},{4,0},{12,8},{20,16},{28,24},{1,5},{9... | collective-permute-start | bytes 835592 | tf_op jit(solution)/shard_map/ppermute | solution.py:418
  8.3 9.1 %collective-permute-start.4 = (bf16[272,512]{1,0:T(8,128)(2,1)S(1)}, bf16[272,512]{1,0:T(8,128)(2,1)S(1)}, u32[]{:S(2)}, u32[]{:S(2)}) collective-permute-start(bf16[272,512]{1,0:T(8,128)(2,1)S(1)} %constant_dynamic-update-slice_fusion), channel_id=1, source_target_pairs={{4,8},{12,16},{20,24},{8,4},{16,12},{24,20},{5,9},{13,17},{21,25},... | collective-permute-start | bytes 835592 | tf_op jit(solution)/shard_map/ppermute | solution.py:418
  11.5 4.5 %copy-start.4 = (f32[512]{0:T(512)S(1)}, f32[512]{0:T(512)}, u32[]{:S(2)}) copy-start(f32[512]{0:T(512)} %param.10) | copy-start | bytes 6148
  11.5 7.9 %collective-permute-start.5 = (bf16[128,512]{1,0:T(8,128)(2,1)S(1)}, bf16[128,512]{1,0:T(8,128)(2,1)S(1)}, u32[]{:S(2)}, u32[]{:S(2)}) collective-permute-start(bf16[128,512]{1,0:T(8,128)(2,1)S(1)} %collective-permute-done.2.other_ref), channel_id=1, source_target_pairs={{4,8},{12,16},{20,24},{8,4},{16,12},{24,20},{5,9},{13,17},{21,25},... | collective-permute-start | bytes 393224 | tf_op jit(solution)/shard_map/ppermute | solution.py:418
  14.7 1.4 %collective-permute-start.3 = (bf16[128,512]{1,0:T(8,128)(2,1)S(1)}, bf16[128,512]{1,0:T(8,128)(2,1)S(1)}, u32[]{:S(2)}, u32[]{:S(2)}) collective-permute-start(bf16[128,512]{1,0:T(8,128)(2,1)S(1)} %collective-permute-done.2.other_ref), channel_id=1, source_target_pairs={{0,4},{8,12},{16,20},{24,28},{4,0},{12,8},{20,16},{28,24},{1,5},{9... | collective-permute-start | bytes 393224 | tf_op jit(solution)/shard_map/ppermute | solution.py:418
  17.4 2.1 %copy-start.1 = (bf16[512,512]{1,0:T(8,128)(2,1)S(1)}, bf16[512,512]{1,0:T(8,128)(2,1)}, u32[]{:S(2)}) copy-start(bf16[512,512]{1,0:T(8,128)(2,1)} %wout_ref.1) | copy-start | bytes 1572868
  17.4 2.1 %copy-start.2 = (bf16[512,512]{1,0:T(8,128)(2,1)S(1)}, bf16[512,512]{1,0:T(8,128)(2,1)}, u32[]{:S(2)}) copy-start(bf16[512,512]{1,0:T(8,128)(2,1)} %wlat_ref.1) | copy-start | bytes 1572868
  21.7 3.1 %collective-permute-start.6 = (bf16[16,512]{1,0:T(8,128)(2,1)S(1)}, bf16[16,512]{1,0:T(8,128)(2,1)S(1)}, u32[]{:S(2)}, u32[]{:S(2)}) collective-permute-start(bf16[16,512]{1,0:T(8,128)(2,1)S(1)} %get-tuple-element.50), channel_id=1, source_target_pairs={{0,1},{2,3},{1,0},{3,2},{4,5},{6,7},{5,4},{7,6},{8,9},{10,11},{9,8... | collective-permute-start | bytes 49160 | tf_op jit(solution)/shard_map/ppermute | solution.py:413
  23.0 3.5 %collective-permute-start.7 = (bf16[16,512]{1,0:T(8,128)(2,1)S(1)}, bf16[16,512]{1,0:T(8,128)(2,1)S(1)}, u32[]{:S(2)}, u32[]{:S(2)}) collective-permute-start(bf16[16,512]{1,0:T(8,128)(2,1)S(1)} %get-tuple-element.54), channel_id=1, source_target_pairs={{1,2},{3,0},{2,1},{0,3},{5,6},{7,4},{6,5},{4,7},{9,10},{11,8},{10,... | collective-permute-start | bytes 49160 | tf_op jit(solution)/shard_map/ppermute | solution.py:413
  26.5 6.7 %collective-permute-start.9 = (bf16[144,512]{1,0:T(8,128)(2,1)S(1)}, bf16[144,512]{1,0:T(8,128)(2,1)S(1)}, u32[]{:S(2)}, u32[]{:S(2)}) collective-permute-start(bf16[144,512]{1,0:T(8,128)(2,1)S(1)} %pad_maximum_fusion.latent_ref), channel_id=1, source_target_pairs={{0,4},{8,12},{16,20},{24,28},{4,0},{12,8},{20,16},{28,24},{1,5},{9... | collective-permute-start | bytes 442376 | tf_op jit(solution)/shard_map/ppermute | solution.py:418
  28.2 6.5 %collective-permute-start.8 = (bf16[144,512]{1,0:T(8,128)(2,1)S(1)}, bf16[144,512]{1,0:T(8,128)(2,1)S(1)}, u32[]{:S(2)}, u32[]{:S(2)}) collective-permute-start(bf16[144,512]{1,0:T(8,128)(2,1)S(1)} %pad_maximum_fusion.latent_ref), channel_id=1, source_target_pairs={{4,8},{12,16},{20,24},{8,4},{16,12},{24,20},{5,9},{13,17},{21,25},... | collective-permute-start | bytes 442376 | tf_op jit(solution)/shard_map/ppermute | solution.py:418

commit v15 on v13

--- a/solution.py
+++ b/solution.py
@@ -14,7 +14,7 @@
 SIDE = 8
 ROWS = 16
 LANES = 128
-EARLY = 1
+EARLY = 2
 CANDIDATES = 5
 F32 = jnp.float32
 BF16 = jnp.bfloat16
@@ -80,9 +80,10 @@
         step_reg = (block // sectors - reg_here) * toward
         step_lon = (block % sectors - lon_here + 1 + sectors) % sectors - 1
         lean = step_lon * (1 - 2 * (lon_here % 2))
-        place = jnp.where(lean == 0, 0, jnp.where(lean > 0, 1, 2))
+        side = jnp.where(lean == 0, 0, jnp.where(lean > 0, 1, 4))
         ahead = jnp.where(lean < 0, 0, 1)
-        found.append(jnp.where(step_reg == 0, ahead, jnp.where(step_reg > 0, 2, 5) + jnp.where(step_reg == 0, 0, place)))
+        behind = jnp.where(lean < 0, 7, 4 + side)
+        found.append(jnp.where(step_reg == 0, ahead, jnp.where(step_reg > 0, 2 + side, behind)))
     for low in range(len(found)):
         for high in range(low + 1, len(found)):
             less, more = jnp.minimum(found[low], found[high]), jnp.maximum(found[low], found[high])
@@ -191,14 +192,14 @@
 
 
 def early_kernel(
-    choice_ref, other_ref, pair_ref, inner_ref, beside_ref,
+    choice_ref, other_ref, pair_ref, inner_ref, outer_ref,
     gain_ref, wk_ref, wvt_ref, query_ref, key_ref, value_ref,
     top_ref, sum_ref, keys_ref, values_ref,
 ):
     rows = key_ref.shape[0]
     parts, group, _ = query_ref.shape
     candidates = [other_ref[...], pair_ref[...]]
-    candidates += [inner_ref[rows : 2 * rows], inner_ref[:rows], beside_ref[...]]
+    candidates += [ref[rows : 2 * rows] if center else ref[:rows] for ref in (inner_ref, outer_ref) for center in (1, 0)]
     nodes = chosen(range(EARLY), rows, choice_ref, candidates)
     keys, values = project(nodes, gain_ref[...], wk_ref, wvt_ref)
     keys_ref[:rows] = key_ref[...]
@@ -209,65 +210,66 @@
         values_ref[part, :group, rows:] = values[span]
         values_ref[part, group:, :] = jnp.ones((ROWS, keys_ref.shape[0]), BF16)
 
-    def scored(part):
-        span = slice(part * group, (part + 1) * group)
-        return jnp.dot(keys_ref[:, span], query_ref[part], preferred_element_type=F32)
-
-    scores = scored(0)
-    for part in range(parts):
-        now = scores
-        if part + 1 < parts:
-            scores = scored(part + 1)
-        top = jnp.max(now, axis=0, keepdims=True)
-        expo = jnp.exp2(now - top).astype(BF16)
-        summed = jnp.dot(values_ref[part], expo, preferred_element_type=F32)
+    spans = [slice(part * group, (part + 1) * group) for part in range(parts)]
+    scores = [
+        jnp.dot(keys_ref[:, span], query_ref[part], preferred_element_type=F32)
+        for part, span in enumerate(spans)
+    ]
+    tops = [jnp.max(one, axis=0, keepdims=True) for one in scores]
+    expos = [jnp.exp2(one - top).astype(BF16) for one, top in zip(scores, tops)]
+    sums = [
+        jnp.dot(values_ref[part], expo, preferred_element_type=F32) for part, expo in enumerate(expos)
+    ]
+    for part, (top, summed) in enumerate(zip(tops, sums)):
         top_ref[part, 0] = jnp.broadcast_to(top, top_ref.shape[2:])
         top_ref[part, 1] = jnp.broadcast_to(summed[group : group + 1], top_ref.shape[2:])
         sum_ref[part] = jnp.concatenate(own_heads(summed[:group], rows), axis=0)
 
 
 def late_kernel(
-    choice_ref, cells_ref, pair_ref, inner_ref, beside_ref, outer_ref, corner_ref,
+    choice_ref, cells_ref, inner_ref, outer_ref, beside_ref, corner_ref,
     own_ref, gain_ref, wk_ref, wvt_ref, query_ref, top_ref, sum_ref, wout_ref, wlat_ref,
     state_ref, latent_ref, to_pair_ref, to_other_ref,
-    attended_ref,
 ):
     rows, width = state_ref.shape
     parts, group, lanes = query_ref.shape
     members = lanes // rows
     head = group // members
-    candidates = [None, pair_ref[...], inner_ref[rows : 2 * rows], inner_ref[:rows], beside_ref[...]]
-    candidates += [outer_ref[rows : 2 * rows], outer_ref[:rows], corner_ref[...]]
+    candidates = [None, None]
+    candidates += [ref[rows : 2 * rows] if center else ref[:rows] for ref in (inner_ref, outer_ref) for center in (1, 0)]
+    candidates += [beside_ref[...], corner_ref[...]]
     nodes = chosen(range(EARLY, choice_ref.shape[0]), rows, choice_ref, candidates)
     keys, values = project(nodes, gain_ref[...], wk_ref, wvt_ref)
     ones = jnp.ones((ROWS, nodes.shape[0]), BF16)
-
-    def scored(part):
-        span = slice(part * group, (part + 1) * group)
-        return jnp.dot(keys[:, span], query_ref[part], preferred_element_type=F32)
-
-    scores = scored(0)
-    for part in range(parts):
-        now = scores
-        if part + 1 < parts:
-            scores = scored(part + 1)
-        before = top_ref[part, 0, :1]
-        top = jnp.maximum(before, jnp.max(now, axis=0, keepdims=True))
-        expo = jnp.exp2(now - top).astype(BF16)
-        weights = jnp.concatenate([values[part * group : (part + 1) * group], ones], axis=0)
-        summed = jnp.dot(weights, expo, preferred_element_type=F32)
-        shrink = jnp.exp2(before - top)
+    spans = [slice(part * group, (part + 1) * group) for part in range(parts)]
+    scores = [
+        jnp.dot(keys[:, span], query_ref[part], preferred_element_type=F32)
+        for part, span in enumerate(spans)
+    ]
+    befores = [top_ref[part, 0, :1] for part in range(parts)]
+    tops = [
+        jnp.maximum(before, jnp.max(one, axis=0, keepdims=True))
+        for before, one in zip(befores, scores)
+    ]
+    expos = [jnp.exp2(one - top).astype(BF16) for one, top in zip(scores, tops)]
+    sums = [
+        jnp.dot(jnp.concatenate([values[span], ones], axis=0), expo, preferred_element_type=F32)
+        for span, expo in zip(spans, expos)
+    ]
+    attended = []
+    for part, summed in enumerate(sums):
+        shrink = jnp.exp2(befores[part] - tops[part])
         share = 1.0 / (summed[group : group + 1] + top_ref[part, 1, :1] * shrink)
         merged = []
         for member, piece in enumerate(own_heads(summed[:group], rows)):
             span = slice(member * rows, (member + 1) * rows)
             earlier = sum_ref[part, member * head : (member + 1) * head]
             merged.append((piece + earlier * shrink[:, span]) * share[:, span])
-        merged = jnp.concatenate(merged, axis=0)
-        attended_ref[:, part * group : (part + 1) * group] = merged.T.astype(BF16)
+        attended.append(jnp.concatenate(merged, axis=0).T.astype(BF16))
+    attended = jnp.concatenate(attended, axis=1)
     state = (
         own_ref[:rows].astype(F32)
-        + jnp.dot(attended_ref[...], wout_ref[...], preferred_element_type=F32)
+        + jnp.dot(attended, wout_ref[...], preferred_element_type=F32)
     ).astype(BF16)
     state_ref[...] = state
     value = jnp.dot(state, wlat_ref[...], preferred_element_type=F32)
@@ -490,19 +492,18 @@
         compiler_params=params(32),
         cost_estimate=cost(3e9, 6e6),
         name="early",
-    )(choice, other, pair, inner, beside, gain, wk, wvt, query, key, value)
+    )(choice, other, pair, inner, outer, gain, wk, wvt, query, key, value)
     state, latent, to_pair, to_other = pl.pallas_call(
         late_kernel,
-        in_specs=[whole()] * 16,
+        in_specs=[whole()] * 15,
         out_specs=[whole()] * 4,
         out_shape=[pltpu.VMEM((rows, width), BF16), struct(rows, channels)]
         + [struct(ROWS, channels)] * 2,
-        scratch_shapes=[pltpu.VMEM((rows, width), BF16)],
         compiler_params=params(32),
         cost_estimate=cost(3e9, 6e6),
         name="late",
     )(
-        choice, cells, pair, inner, beside, outer, corner,
+        choice, cells, inner, outer, beside, corner,
         own, gain, wk, wvt, query, top, summed, w_out, w_latent,
     )
 

time: 35 us -> 34.5 us (0.986)
  waiting for transfers between devices: 2.73 us -> 2.03 us
  starting transfers between devices: 18 us -> 18.6 us
  Pallas kernels: 13.1 us -> 12.7 us
    pallas_call x1, Pallas kernels: 2.7 us -> 1.95 us  [shards(): pl.pallas_call(late_kernel, in_specs=[whole()] * 15, out_specs=[whole()]...]
    ppermute x6, starting transfers between devices: 11.8 us -> 12.3 us  [exchanged(): return lax.ppermute(array, 'reg', pairs + [(j, i) for i, j in pairs])]
    ppermute x4, waiting for transfers between devices: 1.86 us -> 1.47 us  [paired(): return lax.ppermute(array, 'lon', pairs + [(j, i) for i, j in pairs])]
  transfers between devices with their start and end apart: 10 -> 10, of which waited for: 4 -> 4; matrix products, arithmetic and copies ran while one was open for 0% -> 0% of each run, Pallas kernels for 25% -> 27%
where the time goes in v15:
time: 34.5 us; the launch traced here: 34.2 us
  starting transfers between devices  18.6 us (54%)
  Pallas kernels  12.7 us (37%)
  waiting for transfers between devices  2.03 us (6%)
  between operations  0.82 us (2%)
    ppermute x6, starting transfers between devices, exchanged(): return lax.ppermute(array, 'reg', pairs + [(j, i) for i, j in pairs])  12.3 us
    ppermute x4, starting transfers between devices, paired(): return lax.ppermute(array, 'lon', pairs + [(j, i) for i, j in pairs])  6.35 us
    pallas_call x1, Pallas kernels, shards(): pl.pallas_call(functools.partial(prepare_kernel, sectors), in_specs=[whol...  2.02 us
    pallas_call x1, Pallas kernels, shards(): pl.pallas_call(late_kernel, in_specs=[whole()] * 15, out_specs=[whole()]...  1.95 us
    pallas_call x2, Pallas kernels, mixed(): pl.pallas_call(functools.partial(mix_kernel, blocks), in_specs=[whole()]...  1.82 us
    pallas_call x1, Pallas kernels, shards(): pl.pallas_call(functools.partial(own_kernel, (rows, 2 * rows, 2 * rows)),...  1.8 us
    pallas_call x1, Pallas kernels, shards(): pl.pallas_call(functools.partial(band_kernel, False), in_specs=[whole()]...  1.62 us
    pallas_call x1, Pallas kernels, shards(): pl.pallas_call(early_kernel, in_specs=[whole()] * 11, out_specs=[whole()]...  1.6 us
  transfers between devices with their start and end apart: 10, of which 4 were waited for; matrix products, arithmetic and copies ran while one was open for 0% of the time, Pallas kernels for 27%

profile of v15, /device:TPU:1, one launch (start us, length us, event | category | flops | bytes accessed | tf_op | source)
XLA Modules:
  0.0 34.2 jit_solution(6989927723953957074)
XLA Ops:
  0.6 2.1 %collective-permute-start = (bf16[128,512]{1,0:T(8,128)(2,1)}, bf16[128,512]{1,0:T(8,128)(2,1)S(1)}, u32[]{:S(2)}, u32[]{:S(2)}) collective-permute-start(bf16[128,512]{1,0:T(8,128)(2,1)} %bitcast.13), channel_id=1, source_target_pairs={{0,1},{2,3},{1,0},{3,2},{4,5},{6,7},{5,4},{7,6},{8,9},{10,11},{9,8... | collective-permute-start | bytes 393224 | tf_op jit(solution)/shard_map/ppermute | solution.py:396
  2.8 1.2 %collective-permute-start.2 = (bf16[128,512]{1,0:T(8,128)(2,1)}, bf16[128,512]{1,0:T(8,128)(2,1)S(1)}, u32[]{:S(2)}, u32[]{:S(2)}) collective-permute-start(bf16[128,512]{1,0:T(8,128)(2,1)} %bitcast.14), channel_id=1, source_target_pairs={{1,2},{3,0},{2,1},{0,3},{5,6},{7,4},{6,5},{4,7},{9,10},{11,8},{10,... | collective-permute-start | bytes 393224 | tf_op jit(solution)/shard_map/ppermute | solution.py:396
  4.0 1.0 %gather.1.own_ref = bf16[144,512]{1,0:T(8,128)(2,1)S(1)} custom-call(bf16[128,512]{1,0:T(8,128)(2,1)} %bitcast.15, s32[2,256]{1,0:T(2,128)} %assign_hbm.3), custom_call_target="tpu_custom_call" | custom-call | flops 1000 | bytes 1000 | tf_op jit(solution)/shard_map/gather/pallas_call | solution.py:432
  4.9 2.0 %prepare.1 = (bf16[4,128,512]{2,1,0:T(8,128)(2,1)S(1)}, bf16[128,512]{1,0:T(8,128)(2,1)S(1)}, bf16[512,128]{1,0:T(8,128)(2,1)S(1)}, bf16[512,512]{1,0:T(8,128)(2...) custom-call(bf16[144,512]{1,0:T(8,128)(2,1)S(1)} %gather.1.own_ref, ...), custom_call_target="tpu_custom_call" | custom-call | flops 500000000 | bytes 1000000 | tf_op jit(solution)/shard_map/prepare/pallas_call | solution.py:445
  7.0 1.3 %collective-permute-start.1 = (bf16[272,512]{1,0:T(8,128)(2,1)S(1)}, bf16[272,512]{1,0:T(8,128)(2,1)S(1)}, u32[]{:S(2)}, u32[]{:S(2)}) collective-permute-start(bf16[272,512]{1,0:T(8,128)(2,1)S(1)} %constant_dynamic-update-slice_fusion), channel_id=1, source_target_pairs={{0,4},{8,12},{16,20},{24,28},{4,0},{12,8},{20,16},{28,24},{1,5},{9... | collective-permute-start | bytes 835592 | tf_op jit(solution)/shard_map/ppermute | solution.py:401
  8.3 3.2 %collective-permute-start.3 = (bf16[272,512]{1,0:T(8,128)(2,1)S(1)}, bf16[272,512]{1,0:T(8,128)(2,1)S(1)}, u32[]{:S(2)}, u32[]{:S(2)}) collective-permute-start(bf16[272,512]{1,0:T(8,128)(2,1)S(1)} %constant_dynamic-update-slice_fusion), channel_id=1, source_target_pairs={{4,8},{12,16},{20,24},{8,4},{16,12},{24,20},{5,9},{13,17},{21,25},... | collective-permute-start | bytes 835592 | tf_op jit(solution)/shard_map/ppermute | solution.py:401
  11.5 0.0 copy-start.4
  11.5 3.1 %collective-permute-start.5 = (bf16[128,512]{1,0:T(8,128)(2,1)S(1)}, bf16[128,512]{1,0:T(8,128)(2,1)S(1)}, u32[]{:S(2)}, u32[]{:S(2)}) collective-permute-start(bf16[128,512]{1,0:T(8,128)(2,1)S(1)} %collective-permute-done.2.other_ref), channel_id=1, source_target_pairs={{4,8},{12,16},{20,24},{8,4},{16,12},{24,20},{5,9},{13,17},{21,25},... | collective-permute-start | bytes 393224 | tf_op jit(solution)/shard_map/ppermute | solution.py:401
  14.7 0.1 collective-permute-start.4
  14.8 1.0 %mix_edges.1.weights_ref = bf16[30,96,512]{2,1,0:T(8,128)(2,1)S(1)} custom-call(f32[5,5,2,9]{3,2,1,0:T(2,128)S(1)} %bitcast.8, bf16[9,84,512]{2,1,0:T(8,128)(2,1)S(1)} %bitcast.6), custom_call_target="tpu_custom_call" | custom-call | flops 2000000000 | bytes 6000000 | tf_op jit(solution)/shard_map/mix_edges/pallas_call | solution.py:417
  15.8 0.3 %collective-permute-done.3.outer_ref = bf16[272,512]{1,0:T(8,128)(2,1)S(1)} collective-permute-done((bf16[272,512]{1,0:T(8,128)(2,1)S(1)}, bf16[272,512]{1,0:T(8,128)(2,1)S(1)}, u32[]{:S(2)}, u32[]{:S(2)}) %collective-permute-start.3) | collective-permute-done | bytes 278560 | tf_op jit(solution)/shard_map/ppermute | solution.py:401
  16.2 1.6 %early.1 = (f32[4,2,8,512]{3,2,1,0:T(8,128)S(1)}, f32[4,128,128]{2,1,0:T(8,128)S(1)}) custom-call(bf16[4,5,16,128]{3,2,1,0:T(8,128)(2,1)S(1)} %get-tuple-element.29.choice_ref, bf16[128,512]{1,0:T(8,128)(2,1)S(1)} %collective-permute-done.2.other_ref, bf16[128,512]{1,0:T(8,128)(2,1)S(1)} %collective-permute-done.pair_ref, ...), custom_call_target="tpu_custom_call" | custom-call | flops 3000000000 | bytes 6000000 | tf_op jit(solution)/shard_map/early/pallas_call | solution.py:480
  17.8 0.1 collective-permute-done.5.corner_ref
  17.8 2.0 %late.1 = (bf16[128,512]{1,0:T(8,128)(2,1)S(1)}, bf16[128,512]{1,0:T(8,128)(2,1)S(1)}, bf16[16,512]{1,0:T(8,128)(2,1)S(1)}, bf16[16,512]{1,0:T(8,128)(2,1)S(1)}) custom-call(bf16[4,5,16,128]{3,2,1,0:T(8,128)(2,1)S(1)} %get-tuple-element.29.choice_ref, bf16[32,128]{1,0:T(8,128)(2,1)S(1)} %get-tuple-element.30.cells_ref, ...), custom_call_target="tpu_custom_call" | custom-call | flops 3000000000 | bytes 6000000 | tf_op jit(solution)/shard_map/late/pallas_call | solution.py:496
  19.8 1.8 %collective-permute-start.6 = (bf16[16,512]{1,0:T(8,128)(2,1)S(1)}, bf16[16,512]{1,0:T(8,128)(2,1)S(1)}, u32[]{:S(2)}, u32[]{:S(2)}) collective-permute-start(bf16[16,512]{1,0:T(8,128)(2,1)S(1)} %get-tuple-element.46), channel_id=1, source_target_pairs={{0,1},{2,3},{1,0},{3,2},{4,5},{6,7},{5,4},{7,6},{8,9},{10,11},{9,8... | collective-permute-start | bytes 49160 | tf_op jit(solution)/shard_map/ppermute | solution.py:396
  21.6 1.2 %collective-permute-start.7 = (bf16[16,512]{1,0:T(8,128)(2,1)S(1)}, bf16[16,512]{1,0:T(8,128)(2,1)S(1)}, u32[]{:S(2)}, u32[]{:S(2)}) collective-permute-start(bf16[16,512]{1,0:T(8,128)(2,1)S(1)} %get-tuple-element.50), channel_id=1, source_target_pairs={{1,2},{3,0},{2,1},{0,3},{5,6},{7,4},{6,5},{4,7},{9,10},{11,8},{10,... | collective-permute-start | bytes 49160 | tf_op jit(solution)/shard_map/ppermute | solution.py:396
  22.8 0.8 %mix_own.1.weights_ref = bf16[20,96,512]{2,1,0:T(8,128)(2,1)S(1)} custom-call(f32[5,5,2,9]{3,2,1,0:T(2,128)S(1)} %bitcast.9, bf16[9,84,512]{2,1,0:T(8,128)(2,1)S(1)} %bitcast.7), custom_call_target="tpu_custom_call" | custom-call | flops 2000000000 | bytes 6000000 | tf_op jit(solution)/shard_map/mix_own/pallas_call | solution.py:417
  23.6 1.5 %collective-permute-done.7 = bf16[16,512]{1,0:T(8,128)(2,1)S(1)} collective-permute-done((bf16[16,512]{1,0:T(8,128)(2,1)S(1)}, bf16[16,512]{1,0:T(8,128)(2,1)S(1)}, u32[]{:S(2)}, u32[]{:S(2)}) %collective-permute-start.7) | collective-permute-done | bytes 16416 | tf_op jit(solution)/shard_map/ppermute | solution.py:396
  25.1 1.1 %collective-permute-start.9 = (bf16[144,512]{1,0:T(8,128)(2,1)S(1)}, bf16[144,512]{1,0:T(8,128)(2,1)S(1)}, u32[]{:S(2)}, u32[]{:S(2)}) collective-permute-start(bf16[144,512]{1,0:T(8,128)(2,1)S(1)} %pad_maximum_fusion.latent_ref), channel_id=1, source_target_pairs={{0,4},{8,12},{16,20},{24,28},{4,0},{12,8},{20,16},{28,24},{1,5},{9... | collective-permute-start | bytes 442376 | tf_op jit(solution)/shard_map/ppermute | solution.py:401
  26.2 3.6 %collective-permute-start.8 = (bf16[144,512]{1,0:T(8,128)(2,1)S(1)}, bf16[144,512]{1,0:T(8,128)(2,1)S(1)}, u32[]{:S(2)}, u32[]{:S(2)}) collective-permute-start(bf16[144,512]{1,0:T(8,128)(2,1)S(1)} %pad_maximum_fusion.latent_ref), channel_id=1, source_target_pairs={{4,8},{12,16},{20,24},{8,4},{16,12},{24,20},{5,9},{13,17},{21,25},... | collective-permute-start | bytes 442376 | tf_op jit(solution)/shard_map/ppermute | solution.py:401
  29.7 1.8 %own_band.1 = (f32[2,96,256]{2,1,0:T(8,128)S(1)}, bf16[2,2,5,256,256]{4,3,2,1,0:T(8,128)(2,1)S(1)}, bf16[128,512]{1,0:T(8,128)(2,1)}) custom-call(bf16[128,512]{1,0:T(8,128)(2,1)S(1)} %get-tuple-element.43.state_ref, bf16[144,512]{1,0:T(8,128)(2,1)S(1)} %gather.1.own_ref, bf16[272,512]{1,0:T(8,128)(2,1)S(1)} %collective-permute-done.1.inner_ref, ...), custom_call_target="tpu_custom_call" | custom-call | flops 1000000000 | bytes 2500000 | tf_op jit(solution)/shard_map/own_band/pallas_call | solution.py:519
  31.5 0.9 %inner_band.1.partial_ref = f32[2,96,256]{2,1,0:T(8,128)S(1)} custom-call(bf16[144,512]{1,0:T(8,128)(2,1)S(1)} %collective-permute-done.9.latent_ref, bf16[30,96,512]{2,1,0:T(8,128)(2,1)S(1)} %mix_edges.1.weights_ref, bf16[2,2,5,256,256]{4,3,2,1,0:T(8,128)(2,1)S(1)} %get-tuple-element.54.hot_ref, f32[2,96,256]{2,1,0:T(8,128)S(1)} %get-tuple-element.55.partial_ref), custom_call_target="tpu_custom_call" | custom-call | flops 1000000000 | bytes 2500000 | tf_op jit(solution)/shard_map/inner_band/pallas_call | solution.py:536
  32.5 0.1 collective-permute-done.8.latent_ref
  32.6 1.6 %outer_band.1 = bf16[84,2,256]{2,1,0:T(2,128)(2,1)} custom-call(bf16[144,512]{1,0:T(8,128)(2,1)S(1)} %collective-permute-done.8.latent_ref, bf16[30,96,512]{2,1,0:T(8,128)(2,1)S(1)} %mix_edges.1.weights_ref, bf16[2,2,5,256,256]{4,3,2,1,0:T(8,128)(2,1)S(1)} %get-tuple-element.54.hot_ref, f32[2,96,256]{2,1,0:T(8,128)S(1)} %inner_band.1.partial_ref), custom_call_target="tpu_custom_call" | custom-call | flops 1000000000 | bytes 2500000 | tf_op jit(solution)/shard_map/outer_band/pallas_call | solution.py:546
  (20 shorter events, 0.1 us)
Async XLA Ops:
  0.6 14.1 %copy-start = (bf16[9,512,84]{1,2,0:T(8,128)(2,1)S(1)}, bf16[9,512,84]{1,2,0:T(8,128)(2,1)}, u32[]{:S(2)}) copy-start(bf16[9,512,84]{1,2,0:T(8,128)(2,1)} %param.17) | copy-start | bytes 2322436
  0.6 14.1 %copy-start.3 = (f32[9,2,5,5]{0,1,3,2:T(2,128)S(1)}, f32[9,2,5,5]{0,1,3,2:T(2,128)}, u32[]{:S(2)}) copy-start(f32[9,2,5,5]{0,1,3,2:T(2,128)} %param.16) | copy-start | bytes 5404
  0.6 6.3 %collective-permute-start = (bf16[128,512]{1,0:T(8,128)(2,1)}, bf16[128,512]{1,0:T(8,128)(2,1)S(1)}, u32[]{:S(2)}, u32[]{:S(2)}) collective-permute-start(bf16[128,512]{1,0:T(8,128)(2,1)} %bitcast.13), channel_id=1, source_target_pairs={{0,1},{2,3},{1,0},{3,2},{4,5},{6,7},{5,4},{7,6},{8,9},{10,11},{9,8... | collective-permute-start | bytes 393224 | tf_op jit(solution)/shard_map/ppermute | solution.py:396
  2.8 8.8 %collective-permute-start.2 = (bf16[128,512]{1,0:T(8,128)(2,1)}, bf16[128,512]{1,0:T(8,128)(2,1)S(1)}, u32[]{:S(2)}, u32[]{:S(2)}) collective-permute-start(bf16[128,512]{1,0:T(8,128)(2,1)} %bitcast.14), channel_id=1, source_target_pairs={{1,2},{3,0},{2,1},{0,3},{5,6},{7,4},{6,5},{4,7},{9,10},{11,8},{10,... | collective-permute-start | bytes 393224 | tf_op jit(solution)/shard_map/ppermute | solution.py:396
  7.0 8.8 %collective-permute-start.1 = (bf16[272,512]{1,0:T(8,128)(2,1)S(1)}, bf16[272,512]{1,0:T(8,128)(2,1)S(1)}, u32[]{:S(2)}, u32[]{:S(2)}) collective-permute-start(bf16[272,512]{1,0:T(8,128)(2,1)S(1)} %constant_dynamic-update-slice_fusion), channel_id=1, source_target_pairs={{0,4},{8,12},{16,20},{24,28},{4,0},{12,8},{20,16},{28,24},{1,5},{9... | collective-permute-start | bytes 835592 | tf_op jit(solution)/shard_map/ppermute | solution.py:401
  8.3 7.9 %collective-permute-start.3 = (bf16[272,512]{1,0:T(8,128)(2,1)S(1)}, bf16[272,512]{1,0:T(8,128)(2,1)S(1)}, u32[]{:S(2)}, u32[]{:S(2)}) collective-permute-start(bf16[272,512]{1,0:T(8,128)(2,1)S(1)} %constant_dynamic-update-slice_fusion), channel_id=1, source_target_pairs={{4,8},{12,16},{20,24},{8,4},{16,12},{24,20},{5,9},{13,17},{21,25},... | collective-permute-start | bytes 835592 | tf_op jit(solution)/shard_map/ppermute | solution.py:401
  11.5 4.6 %copy-start.4 = (f32[512]{0:T(512)S(1)}, f32[512]{0:T(512)}, u32[]{:S(2)}) copy-start(f32[512]{0:T(512)} %param.10) | copy-start | bytes 6148
  11.5 6.3 %collective-permute-start.5 = (bf16[128,512]{1,0:T(8,128)(2,1)S(1)}, bf16[128,512]{1,0:T(8,128)(2,1)S(1)}, u32[]{:S(2)}, u32[]{:S(2)}) collective-permute-start(bf16[128,512]{1,0:T(8,128)(2,1)S(1)} %collective-permute-done.2.other_ref), channel_id=1, source_target_pairs={{4,8},{12,16},{20,24},{8,4},{16,12},{24,20},{5,9},{13,17},{21,25},... | collective-permute-start | bytes 393224 | tf_op jit(solution)/shard_map/ppermute | solution.py:401
  14.7 3.2 %collective-permute-start.4 = (bf16[128,512]{1,0:T(8,128)(2,1)S(1)}, bf16[128,512]{1,0:T(8,128)(2,1)S(1)}, u32[]{:S(2)}, u32[]{:S(2)}) collective-permute-start(bf16[128,512]{1,0:T(8,128)(2,1)S(1)} %collective-permute-done.2.other_ref), channel_id=1, source_target_pairs={{0,4},{8,12},{16,20},{24,28},{4,0},{12,8},{20,16},{28,24},{1,5},{9... | collective-permute-start | bytes 393224 | tf_op jit(solution)/shard_map/ppermute | solution.py:401
  16.2 1.7 %copy-start.1 = (bf16[512,512]{1,0:T(8,128)(2,1)S(1)}, bf16[512,512]{1,0:T(8,128)(2,1)}, u32[]{:S(2)}) copy-start(bf16[512,512]{1,0:T(8,128)(2,1)} %wout_ref.1) | copy-start | bytes 1572868
  16.2 1.7 %copy-start.2 = (bf16[512,512]{1,0:T(8,128)(2,1)S(1)}, bf16[512,512]{1,0:T(8,128)(2,1)}, u32[]{:S(2)}) copy-start(bf16[512,512]{1,0:T(8,128)(2,1)} %wlat_ref.1) | copy-start | bytes 1572868
  19.8 3.8 %collective-permute-start.6 = (bf16[16,512]{1,0:T(8,128)(2,1)S(1)}, bf16[16,512]{1,0:T(8,128)(2,1)S(1)}, u32[]{:S(2)}, u32[]{:S(2)}) collective-permute-start(bf16[16,512]{1,0:T(8,128)(2,1)S(1)} %get-tuple-element.46), channel_id=1, source_target_pairs={{0,1},{2,3},{1,0},{3,2},{4,5},{6,7},{5,4},{7,6},{8,9},{10,11},{9,8... | collective-permute-start | bytes 49160 | tf_op jit(solution)/shard_map/ppermute | solution.py:396
  21.6 3.5 %collective-permute-start.7 = (bf16[16,512]{1,0:T(8,128)(2,1)S(1)}, bf16[16,512]{1,0:T(8,128)(2,1)S(1)}, u32[]{:S(2)}, u32[]{:S(2)}) collective-permute-start(bf16[16,512]{1,0:T(8,128)(2,1)S(1)} %get-tuple-element.50), channel_id=1, source_target_pairs={{1,2},{3,0},{2,1},{0,3},{5,6},{7,4},{6,5},{4,7},{9,10},{11,8},{10,... | collective-permute-start | bytes 49160 | tf_op jit(solution)/shard_map/ppermute | solution.py:396
  25.1 6.4 %collective-permute-start.9 = (bf16[144,512]{1,0:T(8,128)(2,1)S(1)}, bf16[144,512]{1,0:T(8,128)(2,1)S(1)}, u32[]{:S(2)}, u32[]{:S(2)}) collective-permute-start(bf16[144,512]{1,0:T(8,128)(2,1)S(1)} %pad_maximum_fusion.latent_ref), channel_id=1, source_target_pairs={{0,4},{8,12},{16,20},{24,28},{4,0},{12,8},{20,16},{28,24},{1,5},{9... | collective-permute-start | bytes 442376 | tf_op jit(solution)/shard_map/ppermute | solution.py:401
  26.2 6.5 %collective-permute-start.8 = (bf16[144,512]{1,0:T(8,128)(2,1)S(1)}, bf16[144,512]{1,0:T(8,128)(2,1)S(1)}, u32[]{:S(2)}, u32[]{:S(2)}) collective-permute-start(bf16[144,512]{1,0:T(8,128)(2,1)S(1)} %pad_maximum_fusion.latent_ref), channel_id=1, source_target_pairs={{4,8},{12,16},{20,24},{8,4},{16,12},{24,20},{5,9},{13,17},{21,25},... | collective-permute-start | bytes 442376 | tf_op jit(solution)/shard_map/ppermute | solution.py:401

commit v16 on v15

--- a/solution.py
+++ b/solution.py
@@ -338,7 +338,9 @@
                 hot_ref[band, at, off, nodes:] = jnp.zeros((hot_ref.shape[3] - nodes, cols), BF16)
 
 
-def band_kernel(from_inner, latent_ref, weights_ref, hot_ref, partial_ref, out_ref, one_ref, two_ref):
+def band_kernel(
+    from_inner, latent_ref, weights_ref, hot_ref, partial_ref, out_ref, one_ref, two_ref, paired_ref
+):
     odd = lax.axis_index("reg") % 2
     band = 1 - odd if from_inner else odd
     latent = latent_ref[...]
@@ -362,7 +364,13 @@
         if from_inner:
             out_ref[row] = total
         else:
-            out_ref[:, row, :] = total[: out_ref.shape[0]].astype(BF16)
+            for tile in range(cols // LANES):
+                part = total[:, tile * LANES : (tile + 1) * LANES]
+                paired_ref[tile, pl.ds(row, outputs, stride=2), :] = part
+    if not from_inner:
+        out_ch = out_ref.shape[0]
+        tiles = [paired_ref[tile, : 2 * out_ch, :] for tile in range(cols // LANES)]
+        out_ref[...] = jnp.concatenate(tiles, axis=1).astype(BF16).reshape(out_ref.shape)
 
 
 def whole(memory=pltpu.VMEM):
@@ -532,6 +540,7 @@
     band_scratch = [
         pltpu.VMEM((outputs, TAPS * lanes), BF16),
         pltpu.VMEM((2 * outputs, TAPS * lanes), BF16),
+        pltpu.VMEM((lon_cols // LANES, 2 * outputs, LANES), F32),
     ]
     partial = pl.pallas_call(
         functools.partial(band_kernel, True),

time: 34.5 us -> 34.4 us (level)
  no operation moved by 1% of the time
where the time goes in v16:
time: 34.4 us; the launch traced here: 34.2 us
  starting transfers between devices  18.6 us (54%)
  Pallas kernels  12.7 us (37%)
  waiting for transfers between devices  2.03 us (6%)
  between operations  0.82 us (2%)
    ppermute x6, starting transfers between devices, exchanged(): return lax.ppermute(array, 'reg', pairs + [(j, i) for i, j in pairs])  12.3 us
    ppermute x4, starting transfers between devices, paired(): return lax.ppermute(array, 'lon', pairs + [(j, i) for i, j in pairs])  6.35 us
    pallas_call x1, Pallas kernels, shards(): pl.pallas_call(functools.partial(prepare_kernel, sectors), in_specs=[whol...  2.02 us
    pallas_call x1, Pallas kernels, shards(): pl.pallas_call(late_kernel, in_specs=[whole()] * 15, out_specs=[whole()]...  1.95 us
    pallas_call x2, Pallas kernels, mixed(): pl.pallas_call(functools.partial(mix_kernel, blocks), in_specs=[whole()]...  1.82 us
    pallas_call x1, Pallas kernels, shards(): pl.pallas_call(functools.partial(own_kernel, (rows, 2 * rows, 2 * rows)),...  1.8 us
    pallas_call x1, Pallas kernels, shards(): pl.pallas_call(early_kernel, in_specs=[whole()] * 11, out_specs=[whole()]...  1.6 us
    pallas_call x1, Pallas kernels, shards(): pl.pallas_call(functools.partial(band_kernel, False), in_specs=[whole()]...  1.6 us
  transfers between devices with their start and end apart: 10, of which 4 were waited for; matrix products, arithmetic and copies ran while one was open for 0% of the time, Pallas kernels for 27%

profile of v16, /device:TPU:1, one launch (start us, length us, event | category | flops | bytes accessed | tf_op | source)
XLA Modules:
  0.0 34.2 jit_solution(8162678113205017902)
XLA Ops:
  0.6 2.1 %collective-permute-start = (bf16[128,512]{1,0:T(8,128)(2,1)}, bf16[128,512]{1,0:T(8,128)(2,1)S(1)}, u32[]{:S(2)}, u32[]{:S(2)}) collective-permute-start(bf16[128,512]{1,0:T(8,128)(2,1)} %bitcast.13), channel_id=1, source_target_pairs={{0,1},{2,3},{1,0},{3,2},{4,5},{6,7},{5,4},{7,6},{8,9},{10,11},{9,8... | collective-permute-start | bytes 393224 | tf_op jit(solution)/shard_map/ppermute | solution.py:404
  2.8 1.2 %collective-permute-start.2 = (bf16[128,512]{1,0:T(8,128)(2,1)}, bf16[128,512]{1,0:T(8,128)(2,1)S(1)}, u32[]{:S(2)}, u32[]{:S(2)}) collective-permute-start(bf16[128,512]{1,0:T(8,128)(2,1)} %bitcast.14), channel_id=1, source_target_pairs={{1,2},{3,0},{2,1},{0,3},{5,6},{7,4},{6,5},{4,7},{9,10},{11,8},{10,... | collective-permute-start | bytes 393224 | tf_op jit(solution)/shard_map/ppermute | solution.py:404
  4.0 1.0 %gather.1.own_ref = bf16[144,512]{1,0:T(8,128)(2,1)S(1)} custom-call(bf16[128,512]{1,0:T(8,128)(2,1)} %bitcast.15, s32[2,256]{1,0:T(2,128)} %assign_hbm.3), custom_call_target="tpu_custom_call" | custom-call | flops 1000 | bytes 1000 | tf_op jit(solution)/shard_map/gather/pallas_call | solution.py:440
  4.9 2.0 %prepare.1 = (bf16[4,128,512]{2,1,0:T(8,128)(2,1)S(1)}, bf16[128,512]{1,0:T(8,128)(2,1)S(1)}, bf16[512,128]{1,0:T(8,128)(2,1)S(1)}, bf16[512,512]{1,0:T(8,128)(2...) custom-call(bf16[144,512]{1,0:T(8,128)(2,1)S(1)} %gather.1.own_ref, ...), custom_call_target="tpu_custom_call" | custom-call | flops 500000000 | bytes 1000000 | tf_op jit(solution)/shard_map/prepare/pallas_call | solution.py:453
  7.0 1.3 %collective-permute-start.1 = (bf16[272,512]{1,0:T(8,128)(2,1)S(1)}, bf16[272,512]{1,0:T(8,128)(2,1)S(1)}, u32[]{:S(2)}, u32[]{:S(2)}) collective-permute-start(bf16[272,512]{1,0:T(8,128)(2,1)S(1)} %constant_dynamic-update-slice_fusion), channel_id=1, source_target_pairs={{0,4},{8,12},{16,20},{24,28},{4,0},{12,8},{20,16},{28,24},{1,5},{9... | collective-permute-start | bytes 835592 | tf_op jit(solution)/shard_map/ppermute | solution.py:409
  8.3 3.2 %collective-permute-start.3 = (bf16[272,512]{1,0:T(8,128)(2,1)S(1)}, bf16[272,512]{1,0:T(8,128)(2,1)S(1)}, u32[]{:S(2)}, u32[]{:S(2)}) collective-permute-start(bf16[272,512]{1,0:T(8,128)(2,1)S(1)} %constant_dynamic-update-slice_fusion), channel_id=1, source_target_pairs={{4,8},{12,16},{20,24},{8,4},{16,12},{24,20},{5,9},{13,17},{21,25},... | collective-permute-start | bytes 835592 | tf_op jit(solution)/shard_map/ppermute | solution.py:409
  11.5 0.0 copy-start.4
  11.5 3.1 %collective-permute-start.5 = (bf16[128,512]{1,0:T(8,128)(2,1)S(1)}, bf16[128,512]{1,0:T(8,128)(2,1)S(1)}, u32[]{:S(2)}, u32[]{:S(2)}) collective-permute-start(bf16[128,512]{1,0:T(8,128)(2,1)S(1)} %collective-permute-done.2.other_ref), channel_id=1, source_target_pairs={{4,8},{12,16},{20,24},{8,4},{16,12},{24,20},{5,9},{13,17},{21,25},... | collective-permute-start | bytes 393224 | tf_op jit(solution)/shard_map/ppermute | solution.py:409
  14.7 0.1 collective-permute-start.4
  14.8 1.0 %mix_edges.1.weights_ref = bf16[30,96,512]{2,1,0:T(8,128)(2,1)S(1)} custom-call(f32[5,5,2,9]{3,2,1,0:T(2,128)S(1)} %bitcast.8, bf16[9,84,512]{2,1,0:T(8,128)(2,1)S(1)} %bitcast.6), custom_call_target="tpu_custom_call" | custom-call | flops 2000000000 | bytes 6000000 | tf_op jit(solution)/shard_map/mix_edges/pallas_call | solution.py:425
  15.8 0.3 %collective-permute-done.3.outer_ref = bf16[272,512]{1,0:T(8,128)(2,1)S(1)} collective-permute-done((bf16[272,512]{1,0:T(8,128)(2,1)S(1)}, bf16[272,512]{1,0:T(8,128)(2,1)S(1)}, u32[]{:S(2)}, u32[]{:S(2)}) %collective-permute-start.3) | collective-permute-done | bytes 278560 | tf_op jit(solution)/shard_map/ppermute | solution.py:409
  16.2 1.6 %early.1 = (f32[4,2,8,512]{3,2,1,0:T(8,128)S(1)}, f32[4,128,128]{2,1,0:T(8,128)S(1)}) custom-call(bf16[4,5,16,128]{3,2,1,0:T(8,128)(2,1)S(1)} %get-tuple-element.29.choice_ref, bf16[128,512]{1,0:T(8,128)(2,1)S(1)} %collective-permute-done.2.other_ref, bf16[128,512]{1,0:T(8,128)(2,1)S(1)} %collective-permute-done.pair_ref, ...), custom_call_target="tpu_custom_call" | custom-call | flops 3000000000 | bytes 6000000 | tf_op jit(solution)/shard_map/early/pallas_call | solution.py:488
  17.8 0.1 collective-permute-done.5.corner_ref
  17.8 2.0 %late.1 = (bf16[128,512]{1,0:T(8,128)(2,1)S(1)}, bf16[128,512]{1,0:T(8,128)(2,1)S(1)}, bf16[16,512]{1,0:T(8,128)(2,1)S(1)}, bf16[16,512]{1,0:T(8,128)(2,1)S(1)}) custom-call(bf16[4,5,16,128]{3,2,1,0:T(8,128)(2,1)S(1)} %get-tuple-element.29.choice_ref, bf16[32,128]{1,0:T(8,128)(2,1)S(1)} %get-tuple-element.30.cells_ref, ...), custom_call_target="tpu_custom_call" | custom-call | flops 3000000000 | bytes 6000000 | tf_op jit(solution)/shard_map/late/pallas_call | solution.py:504
  19.8 1.8 %collective-permute-start.6 = (bf16[16,512]{1,0:T(8,128)(2,1)S(1)}, bf16[16,512]{1,0:T(8,128)(2,1)S(1)}, u32[]{:S(2)}, u32[]{:S(2)}) collective-permute-start(bf16[16,512]{1,0:T(8,128)(2,1)S(1)} %get-tuple-element.46), channel_id=1, source_target_pairs={{0,1},{2,3},{1,0},{3,2},{4,5},{6,7},{5,4},{7,6},{8,9},{10,11},{9,8... | collective-permute-start | bytes 49160 | tf_op jit(solution)/shard_map/ppermute | solution.py:404
  21.6 1.2 %collective-permute-start.7 = (bf16[16,512]{1,0:T(8,128)(2,1)S(1)}, bf16[16,512]{1,0:T(8,128)(2,1)S(1)}, u32[]{:S(2)}, u32[]{:S(2)}) collective-permute-start(bf16[16,512]{1,0:T(8,128)(2,1)S(1)} %get-tuple-element.50), channel_id=1, source_target_pairs={{1,2},{3,0},{2,1},{0,3},{5,6},{7,4},{6,5},{4,7},{9,10},{11,8},{10,... | collective-permute-start | bytes 49160 | tf_op jit(solution)/shard_map/ppermute | solution.py:404
  22.8 0.8 %mix_own.1.weights_ref = bf16[20,96,512]{2,1,0:T(8,128)(2,1)S(1)} custom-call(f32[5,5,2,9]{3,2,1,0:T(2,128)S(1)} %bitcast.9, bf16[9,84,512]{2,1,0:T(8,128)(2,1)S(1)} %bitcast.7), custom_call_target="tpu_custom_call" | custom-call | flops 2000000000 | bytes 6000000 | tf_op jit(solution)/shard_map/mix_own/pallas_call | solution.py:425
  23.6 1.5 %collective-permute-done.7 = bf16[16,512]{1,0:T(8,128)(2,1)S(1)} collective-permute-done((bf16[16,512]{1,0:T(8,128)(2,1)S(1)}, bf16[16,512]{1,0:T(8,128)(2,1)S(1)}, u32[]{:S(2)}, u32[]{:S(2)}) %collective-permute-start.7) | collective-permute-done | bytes 16416 | tf_op jit(solution)/shard_map/ppermute | solution.py:404
  25.1 1.1 %collective-permute-start.9 = (bf16[144,512]{1,0:T(8,128)(2,1)S(1)}, bf16[144,512]{1,0:T(8,128)(2,1)S(1)}, u32[]{:S(2)}, u32[]{:S(2)}) collective-permute-start(bf16[144,512]{1,0:T(8,128)(2,1)S(1)} %pad_maximum_fusion.latent_ref), channel_id=1, source_target_pairs={{0,4},{8,12},{16,20},{24,28},{4,0},{12,8},{20,16},{28,24},{1,5},{9... | collective-permute-start | bytes 442376 | tf_op jit(solution)/shard_map/ppermute | solution.py:409
  26.2 3.6 %collective-permute-start.8 = (bf16[144,512]{1,0:T(8,128)(2,1)S(1)}, bf16[144,512]{1,0:T(8,128)(2,1)S(1)}, u32[]{:S(2)}, u32[]{:S(2)}) collective-permute-start(bf16[144,512]{1,0:T(8,128)(2,1)S(1)} %pad_maximum_fusion.latent_ref), channel_id=1, source_target_pairs={{4,8},{12,16},{20,24},{8,4},{16,12},{24,20},{5,9},{13,17},{21,25},... | collective-permute-start | bytes 442376 | tf_op jit(solution)/shard_map/ppermute | solution.py:409
  29.7 1.8 %own_band.1 = (f32[2,96,256]{2,1,0:T(8,128)S(1)}, bf16[2,2,5,256,256]{4,3,2,1,0:T(8,128)(2,1)S(1)}, bf16[128,512]{1,0:T(8,128)(2,1)}) custom-call(bf16[128,512]{1,0:T(8,128)(2,1)S(1)} %get-tuple-element.43.state_ref, bf16[144,512]{1,0:T(8,128)(2,1)S(1)} %gather.1.own_ref, bf16[272,512]{1,0:T(8,128)(2,1)S(1)} %collective-permute-done.1.inner_ref, ...), custom_call_target="tpu_custom_call" | custom-call | flops 1000000000 | bytes 2500000 | tf_op jit(solution)/shard_map/own_band/pallas_call | solution.py:527
  31.5 0.9 %inner_band.1.partial_ref = f32[2,96,256]{2,1,0:T(8,128)S(1)} custom-call(bf16[144,512]{1,0:T(8,128)(2,1)S(1)} %collective-permute-done.9.latent_ref, bf16[30,96,512]{2,1,0:T(8,128)(2,1)S(1)} %mix_edges.1.weights_ref, bf16[2,2,5,256,256]{4,3,2,1,0:T(8,128)(2,1)S(1)} %get-tuple-element.54.hot_ref, f32[2,96,256]{2,1,0:T(8,128)S(1)} %get-tuple-element.55.partial_ref), custom_call_target="tpu_custom_call" | custom-call | flops 1000000000 | bytes 2500000 | tf_op jit(solution)/shard_map/inner_band/pallas_call | solution.py:545
  32.5 0.1 collective-permute-done.8.latent_ref
  32.6 1.6 %outer_band.1 = bf16[84,2,256]{2,1,0:T(2,128)(2,1)} custom-call(bf16[144,512]{1,0:T(8,128)(2,1)S(1)} %collective-permute-done.8.latent_ref, bf16[30,96,512]{2,1,0:T(8,128)(2,1)S(1)} %mix_edges.1.weights_ref, bf16[2,2,5,256,256]{4,3,2,1,0:T(8,128)(2,1)S(1)} %get-tuple-element.54.hot_ref, f32[2,96,256]{2,1,0:T(8,128)S(1)} %inner_band.1.partial_ref), custom_call_target="tpu_custom_call" | custom-call | flops 1000000000 | bytes 2500000 | tf_op jit(solution)/shard_map/outer_band/pallas_call | solution.py:555
  (20 shorter events, 0.1 us)
Async XLA Ops:
  0.6 14.1 %copy-start = (bf16[9,512,84]{1,2,0:T(8,128)(2,1)S(1)}, bf16[9,512,84]{1,2,0:T(8,128)(2,1)}, u32[]{:S(2)}) copy-start(bf16[9,512,84]{1,2,0:T(8,128)(2,1)} %param.17) | copy-start | bytes 2322436
  0.6 14.1 %copy-start.3 = (f32[9,2,5,5]{0,1,3,2:T(2,128)S(1)}, f32[9,2,5,5]{0,1,3,2:T(2,128)}, u32[]{:S(2)}) copy-start(f32[9,2,5,5]{0,1,3,2:T(2,128)} %param.16) | copy-start | bytes 5404
  0.6 6.3 %collective-permute-start = (bf16[128,512]{1,0:T(8,128)(2,1)}, bf16[128,512]{1,0:T(8,128)(2,1)S(1)}, u32[]{:S(2)}, u32[]{:S(2)}) collective-permute-start(bf16[128,512]{1,0:T(8,128)(2,1)} %bitcast.13), channel_id=1, source_target_pairs={{0,1},{2,3},{1,0},{3,2},{4,5},{6,7},{5,4},{7,6},{8,9},{10,11},{9,8... | collective-permute-start | bytes 393224 | tf_op jit(solution)/shard_map/ppermute | solution.py:404
  2.8 8.8 %collective-permute-start.2 = (bf16[128,512]{1,0:T(8,128)(2,1)}, bf16[128,512]{1,0:T(8,128)(2,1)S(1)}, u32[]{:S(2)}, u32[]{:S(2)}) collective-permute-start(bf16[128,512]{1,0:T(8,128)(2,1)} %bitcast.14), channel_id=1, source_target_pairs={{1,2},{3,0},{2,1},{0,3},{5,6},{7,4},{6,5},{4,7},{9,10},{11,8},{10,... | collective-permute-start | bytes 393224 | tf_op jit(solution)/shard_map/ppermute | solution.py:404
  7.0 8.8 %collective-permute-start.1 = (bf16[272,512]{1,0:T(8,128)(2,1)S(1)}, bf16[272,512]{1,0:T(8,128)(2,1)S(1)}, u32[]{:S(2)}, u32[]{:S(2)}) collective-permute-start(bf16[272,512]{1,0:T(8,128)(2,1)S(1)} %constant_dynamic-update-slice_fusion), channel_id=1, source_target_pairs={{0,4},{8,12},{16,20},{24,28},{4,0},{12,8},{20,16},{28,24},{1,5},{9... | collective-permute-start | bytes 835592 | tf_op jit(solution)/shard_map/ppermute | solution.py:409
  8.3 7.9 %collective-permute-start.3 = (bf16[272,512]{1,0:T(8,128)(2,1)S(1)}, bf16[272,512]{1,0:T(8,128)(2,1)S(1)}, u32[]{:S(2)}, u32[]{:S(2)}) collective-permute-start(bf16[272,512]{1,0:T(8,128)(2,1)S(1)} %constant_dynamic-update-slice_fusion), channel_id=1, source_target_pairs={{4,8},{12,16},{20,24},{8,4},{16,12},{24,20},{5,9},{13,17},{21,25},... | collective-permute-start | bytes 835592 | tf_op jit(solution)/shard_map/ppermute | solution.py:409
  11.5 4.6 %copy-start.4 = (f32[512]{0:T(512)S(1)}, f32[512]{0:T(512)}, u32[]{:S(2)}) copy-start(f32[512]{0:T(512)} %param.10) | copy-start | bytes 6148
  11.5 6.3 %collective-permute-start.5 = (bf16[128,512]{1,0:T(8,128)(2,1)S(1)}, bf16[128,512]{1,0:T(8,128)(2,1)S(1)}, u32[]{:S(2)}, u32[]{:S(2)}) collective-permute-start(bf16[128,512]{1,0:T(8,128)(2,1)S(1)} %collective-permute-done.2.other_ref), channel_id=1, source_target_pairs={{4,8},{12,16},{20,24},{8,4},{16,12},{24,20},{5,9},{13,17},{21,25},... | collective-permute-start | bytes 393224 | tf_op jit(solution)/shard_map/ppermute | solution.py:409
  14.7 3.2 %collective-permute-start.4 = (bf16[128,512]{1,0:T(8,128)(2,1)S(1)}, bf16[128,512]{1,0:T(8,128)(2,1)S(1)}, u32[]{:S(2)}, u32[]{:S(2)}) collective-permute-start(bf16[128,512]{1,0:T(8,128)(2,1)S(1)} %collective-permute-done.2.other_ref), channel_id=1, source_target_pairs={{0,4},{8,12},{16,20},{24,28},{4,0},{12,8},{20,16},{28,24},{1,5},{9... | collective-permute-start | bytes 393224 | tf_op jit(solution)/shard_map/ppermute | solution.py:409
  16.2 1.7 %copy-start.1 = (bf16[512,512]{1,0:T(8,128)(2,1)S(1)}, bf16[512,512]{1,0:T(8,128)(2,1)}, u32[]{:S(2)}) copy-start(bf16[512,512]{1,0:T(8,128)(2,1)} %wout_ref.1) | copy-start | bytes 1572868
  16.2 1.7 %copy-start.2 = (bf16[512,512]{1,0:T(8,128)(2,1)S(1)}, bf16[512,512]{1,0:T(8,128)(2,1)}, u32[]{:S(2)}) copy-start(bf16[512,512]{1,0:T(8,128)(2,1)} %wlat_ref.1) | copy-start | bytes 1572868
  19.8 3.8 %collective-permute-start.6 = (bf16[16,512]{1,0:T(8,128)(2,1)S(1)}, bf16[16,512]{1,0:T(8,128)(2,1)S(1)}, u32[]{:S(2)}, u32[]{:S(2)}) collective-permute-start(bf16[16,512]{1,0:T(8,128)(2,1)S(1)} %get-tuple-element.46), channel_id=1, source_target_pairs={{0,1},{2,3},{1,0},{3,2},{4,5},{6,7},{5,4},{7,6},{8,9},{10,11},{9,8... | collective-permute-start | bytes 49160 | tf_op jit(solution)/shard_map/ppermute | solution.py:404
  21.6 3.5 %collective-permute-start.7 = (bf16[16,512]{1,0:T(8,128)(2,1)S(1)}, bf16[16,512]{1,0:T(8,128)(2,1)S(1)}, u32[]{:S(2)}, u32[]{:S(2)}) collective-permute-start(bf16[16,512]{1,0:T(8,128)(2,1)S(1)} %get-tuple-element.50), channel_id=1, source_target_pairs={{1,2},{3,0},{2,1},{0,3},{5,6},{7,4},{6,5},{4,7},{9,10},{11,8},{10,... | collective-permute-start | bytes 49160 | tf_op jit(solution)/shard_map/ppermute | solution.py:404
  25.1 6.4 %collective-permute-start.9 = (bf16[144,512]{1,0:T(8,128)(2,1)S(1)}, bf16[144,512]{1,0:T(8,128)(2,1)S(1)}, u32[]{:S(2)}, u32[]{:S(2)}) collective-permute-start(bf16[144,512]{1,0:T(8,128)(2,1)S(1)} %pad_maximum_fusion.latent_ref), channel_id=1, source_target_pairs={{0,4},{8,12},{16,20},{24,28},{4,0},{12,8},{20,16},{28,24},{1,5},{9... | collective-permute-start | bytes 442376 | tf_op jit(solution)/shard_map/ppermute | solution.py:409
  26.2 6.5 %collective-permute-start.8 = (bf16[144,512]{1,0:T(8,128)(2,1)S(1)}, bf16[144,512]{1,0:T(8,128)(2,1)S(1)}, u32[]{:S(2)}, u32[]{:S(2)}) collective-permute-start(bf16[144,512]{1,0:T(8,128)(2,1)S(1)} %pad_maximum_fusion.latent_ref), channel_id=1, source_target_pairs={{4,8},{12,16},{20,24},{8,4},{16,12},{24,20},{5,9},{13,17},{21,25},... | collective-permute-start | bytes 442376 | tf_op jit(solution)/shard_map/ppermute | solution.py:409

commit v17 on v16

--- a/solution.py
+++ b/solution.py
@@ -518,7 +518,7 @@
     from_pair = paired(to_pair, 0)
     from_other = paired(to_other, 1)
     middle, latent = mixed(blocks_of(OWN), "mix_own", latent)
-    from_pair, middle = lax.optimization_barrier((from_pair, middle))
+    from_other, from_pair, middle = lax.optimization_barrier((from_other, from_pair, middle))
     extended = jnp.concatenate([latent, from_pair[:SIDE], from_other[:SIDE]], axis=0)
     far = exchanged(extended, 1)
     near = exchanged(extended, 0)

time: 34.4 us -> 34.4 us (level)
    ppermute x4, waiting for transfers between devices: 1.47 us -> 1.87 us  [paired(): return lax.ppermute(array, 'lon', pairs + [(j, i) for i, j in pairs])]
  transfers between devices with their start and end apart: 10 -> 10, of which waited for: 4 -> 5; matrix products, arithmetic and copies ran while one was open for 0% -> 0% of each run, Pallas kernels for 27% -> 27%
where the time goes in v17:
time: 34.4 us; the launch traced here: 34.2 us
  starting transfers between devices  18.3 us (53%)
  Pallas kernels  12.7 us (37%)
  waiting for transfers between devices  2.35 us (7%)
  between operations  0.8 us (2%)
    ppermute x6, starting transfers between devices, exchanged(): return lax.ppermute(array, 'reg', pairs + [(j, i) for i, j in pairs])  12 us
    ppermute x4, starting transfers between devices, paired(): return lax.ppermute(array, 'lon', pairs + [(j, i) for i, j in pairs])  6.35 us
    pallas_call x1, Pallas kernels, shards(): pl.pallas_call(functools.partial(prepare_kernel, sectors), in_specs=[whol...  2.02 us
    pallas_call x1, Pallas kernels, shards(): pl.pallas_call(late_kernel, in_specs=[whole()] * 15, out_specs=[whole()]...  1.95 us
    ppermute x4, waiting for transfers between devices, paired(): return lax.ppermute(array, 'lon', pairs + [(j, i) for i, j in pairs])  1.87 us
    pallas_call x2, Pallas kernels, mixed(): pl.pallas_call(functools.partial(mix_kernel, blocks), in_specs=[whole()]...  1.82 us
    pallas_call x1, Pallas kernels, shards(): pl.pallas_call(functools.partial(own_kernel, (rows, 2 * rows, 2 * rows)),...  1.8 us
    pallas_call x1, Pallas kernels, shards(): pl.pallas_call(early_kernel, in_specs=[whole()] * 11, out_specs=[whole()]...  1.6 us
  transfers between devices with their start and end apart: 10, of which 5 were waited for; matrix products, arithmetic and copies ran while one was open for 0% of the time, Pallas kernels for 27%

profile of v17, /device:TPU:1, one launch (start us, length us, event | category | flops | bytes accessed | tf_op | source)
XLA Modules:
  0.0 34.2 jit_solution(573130992622621208)
XLA Ops:
  0.6 2.1 %collective-permute-start = (bf16[128,512]{1,0:T(8,128)(2,1)}, bf16[128,512]{1,0:T(8,128)(2,1)S(1)}, u32[]{:S(2)}, u32[]{:S(2)}) collective-permute-start(bf16[128,512]{1,0:T(8,128)(2,1)} %bitcast.13), channel_id=1, source_target_pairs={{0,1},{2,3},{1,0},{3,2},{4,5},{6,7},{5,4},{7,6},{8,9},{10,11},{9,8... | collective-permute-start | bytes 393224 | tf_op jit(solution)/shard_map/ppermute | solution.py:404
  2.8 1.2 %collective-permute-start.2 = (bf16[128,512]{1,0:T(8,128)(2,1)}, bf16[128,512]{1,0:T(8,128)(2,1)S(1)}, u32[]{:S(2)}, u32[]{:S(2)}) collective-permute-start(bf16[128,512]{1,0:T(8,128)(2,1)} %bitcast.14), channel_id=1, source_target_pairs={{1,2},{3,0},{2,1},{0,3},{5,6},{7,4},{6,5},{4,7},{9,10},{11,8},{10,... | collective-permute-start | bytes 393224 | tf_op jit(solution)/shard_map/ppermute | solution.py:404
  4.0 1.0 %gather.1.own_ref = bf16[144,512]{1,0:T(8,128)(2,1)S(1)} custom-call(bf16[128,512]{1,0:T(8,128)(2,1)} %bitcast.15, s32[2,256]{1,0:T(2,128)} %assign_hbm.3), custom_call_target="tpu_custom_call" | custom-call | flops 1000 | bytes 1000 | tf_op jit(solution)/shard_map/gather/pallas_call | solution.py:440
  4.9 2.0 %prepare.1 = (bf16[4,128,512]{2,1,0:T(8,128)(2,1)S(1)}, bf16[128,512]{1,0:T(8,128)(2,1)S(1)}, bf16[512,128]{1,0:T(8,128)(2,1)S(1)}, bf16[512,512]{1,0:T(8,128)(2...) custom-call(bf16[144,512]{1,0:T(8,128)(2,1)S(1)} %gather.1.own_ref, ...), custom_call_target="tpu_custom_call" | custom-call | flops 500000000 | bytes 1000000 | tf_op jit(solution)/shard_map/prepare/pallas_call | solution.py:453
  7.0 1.3 %collective-permute-start.1 = (bf16[272,512]{1,0:T(8,128)(2,1)S(1)}, bf16[272,512]{1,0:T(8,128)(2,1)S(1)}, u32[]{:S(2)}, u32[]{:S(2)}) collective-permute-start(bf16[272,512]{1,0:T(8,128)(2,1)S(1)} %constant_dynamic-update-slice_fusion), channel_id=1, source_target_pairs={{0,4},{8,12},{16,20},{24,28},{4,0},{12,8},{20,16},{28,24},{1,5},{9... | collective-permute-start | bytes 835592 | tf_op jit(solution)/shard_map/ppermute | solution.py:409
  8.3 3.2 %collective-permute-start.3 = (bf16[272,512]{1,0:T(8,128)(2,1)S(1)}, bf16[272,512]{1,0:T(8,128)(2,1)S(1)}, u32[]{:S(2)}, u32[]{:S(2)}) collective-permute-start(bf16[272,512]{1,0:T(8,128)(2,1)S(1)} %constant_dynamic-update-slice_fusion), channel_id=1, source_target_pairs={{4,8},{12,16},{20,24},{8,4},{16,12},{24,20},{5,9},{13,17},{21,25},... | collective-permute-start | bytes 835592 | tf_op jit(solution)/shard_map/ppermute | solution.py:409
  11.5 3.1 %collective-permute-start.5 = (bf16[128,512]{1,0:T(8,128)(2,1)S(1)}, bf16[128,512]{1,0:T(8,128)(2,1)S(1)}, u32[]{:S(2)}, u32[]{:S(2)}) collective-permute-start(bf16[128,512]{1,0:T(8,128)(2,1)S(1)} %collective-permute-done.2.other_ref), channel_id=1, source_target_pairs={{4,8},{12,16},{20,24},{8,4},{16,12},{24,20},{5,9},{13,17},{21,25},... | collective-permute-start | bytes 393224 | tf_op jit(solution)/shard_map/ppermute | solution.py:409
  14.7 0.1 collective-permute-start.4
  14.8 1.0 %mix_edges.1.weights_ref = bf16[30,96,512]{2,1,0:T(8,128)(2,1)S(1)} custom-call(f32[5,5,2,9]{3,2,1,0:T(2,128)S(1)} %bitcast.8, bf16[9,84,512]{2,1,0:T(8,128)(2,1)S(1)} %bitcast.6), custom_call_target="tpu_custom_call" | custom-call | flops 2000000000 | bytes 6000000 | tf_op jit(solution)/shard_map/mix_edges/pallas_call | solution.py:425
  15.8 0.3 %collective-permute-done.3.outer_ref = bf16[272,512]{1,0:T(8,128)(2,1)S(1)} collective-permute-done((bf16[272,512]{1,0:T(8,128)(2,1)S(1)}, bf16[272,512]{1,0:T(8,128)(2,1)S(1)}, u32[]{:S(2)}, u32[]{:S(2)}) %collective-permute-start.3) | collective-permute-done | bytes 278560 | tf_op jit(solution)/shard_map/ppermute | solution.py:409
  16.2 1.6 %early.1 = (f32[4,2,8,512]{3,2,1,0:T(8,128)S(1)}, f32[4,128,128]{2,1,0:T(8,128)S(1)}) custom-call(bf16[4,5,16,128]{3,2,1,0:T(8,128)(2,1)S(1)} %get-tuple-element.30.choice_ref, bf16[128,512]{1,0:T(8,128)(2,1)S(1)} %collective-permute-done.2.other_ref, bf16[128,512]{1,0:T(8,128)(2,1)S(1)} %collective-permute-done.pair_ref, ...), custom_call_target="tpu_custom_call" | custom-call | flops 3000000000 | bytes 6000000 | tf_op jit(solution)/shard_map/early/pallas_call | solution.py:488
  17.8 0.1 collective-permute-done.5.corner_ref
  17.8 2.0 %late.1 = (bf16[128,512]{1,0:T(8,128)(2,1)S(1)}, bf16[128,512]{1,0:T(8,128)(2,1)S(1)}, bf16[16,512]{1,0:T(8,128)(2,1)S(1)}, bf16[16,512]{1,0:T(8,128)(2,1)S(1)}) custom-call(bf16[4,5,16,128]{3,2,1,0:T(8,128)(2,1)S(1)} %get-tuple-element.30.choice_ref, bf16[32,128]{1,0:T(8,128)(2,1)S(1)} %get-tuple-element.31.cells_ref, ...), custom_call_target="tpu_custom_call" | custom-call | flops 3000000000 | bytes 6000000 | tf_op jit(solution)/shard_map/late/pallas_call | solution.py:504
  19.8 2.8 %collective-permute-start.6 = (bf16[16,512]{1,0:T(8,128)(2,1)S(1)}, bf16[16,512]{1,0:T(8,128)(2,1)S(1)}, u32[]{:S(2)}, u32[]{:S(2)}) collective-permute-start(bf16[16,512]{1,0:T(8,128)(2,1)S(1)} %get-tuple-element.47), channel_id=1, source_target_pairs={{1,2},{3,0},{2,1},{0,3},{5,6},{7,4},{6,5},{4,7},{9,10},{11,8},{10,... | collective-permute-start | bytes 49160 | tf_op jit(solution)/shard_map/ppermute | solution.py:404
  22.6 0.3 collective-permute-start.7
  22.8 0.8 %mix_own.1.weights_ref = bf16[20,96,512]{2,1,0:T(8,128)(2,1)S(1)} custom-call(f32[5,5,2,9]{3,2,1,0:T(2,128)S(1)} %bitcast.9, bf16[9,84,512]{2,1,0:T(8,128)(2,1)S(1)} %bitcast.7), custom_call_target="tpu_custom_call" | custom-call | flops 2000000000 | bytes 6000000 | tf_op jit(solution)/shard_map/mix_own/pallas_call | solution.py:425
  23.6 0.1 collective-permute-done.6
  23.7 1.8 %collective-permute-done.7 = bf16[16,512]{1,0:T(8,128)(2,1)S(1)} collective-permute-done((bf16[16,512]{1,0:T(8,128)(2,1)S(1)}, bf16[16,512]{1,0:T(8,128)(2,1)S(1)}, u32[]{:S(2)}, u32[]{:S(2)}) %collective-permute-start.7) | collective-permute-done | bytes 16416 | tf_op jit(solution)/shard_map/ppermute | solution.py:404
  25.5 0.6 %collective-permute-start.9 = (bf16[144,512]{1,0:T(8,128)(2,1)S(1)}, bf16[144,512]{1,0:T(8,128)(2,1)S(1)}, u32[]{:S(2)}, u32[]{:S(2)}) collective-permute-start(bf16[144,512]{1,0:T(8,128)(2,1)S(1)} %pad_maximum_fusion.latent_ref), channel_id=1, source_target_pairs={{0,4},{8,12},{16,20},{24,28},{4,0},{12,8},{20,16},{28,24},{1,5},{9... | collective-permute-start | bytes 442376 | tf_op jit(solution)/shard_map/ppermute | solution.py:409
  26.1 3.7 %collective-permute-start.8 = (bf16[144,512]{1,0:T(8,128)(2,1)S(1)}, bf16[144,512]{1,0:T(8,128)(2,1)S(1)}, u32[]{:S(2)}, u32[]{:S(2)}) collective-permute-start(bf16[144,512]{1,0:T(8,128)(2,1)S(1)} %pad_maximum_fusion.latent_ref), channel_id=1, source_target_pairs={{4,8},{12,16},{20,24},{8,4},{16,12},{24,20},{5,9},{13,17},{21,25},... | collective-permute-start | bytes 442376 | tf_op jit(solution)/shard_map/ppermute | solution.py:409
  29.8 1.8 %own_band.1 = (f32[2,96,256]{2,1,0:T(8,128)S(1)}, bf16[2,2,5,256,256]{4,3,2,1,0:T(8,128)(2,1)S(1)}, bf16[128,512]{1,0:T(8,128)(2,1)}) custom-call(bf16[128,512]{1,0:T(8,128)(2,1)S(1)} %get-tuple-element.44.state_ref, bf16[144,512]{1,0:T(8,128)(2,1)S(1)} %gather.1.own_ref, bf16[272,512]{1,0:T(8,128)(2,1)S(1)} %collective-permute-done.1.inner_ref, ...), custom_call_target="tpu_custom_call" | custom-call | flops 1000000000 | bytes 2500000 | tf_op jit(solution)/shard_map/own_band/pallas_call | solution.py:527
  31.6 0.9 %inner_band.1.partial_ref = f32[2,96,256]{2,1,0:T(8,128)S(1)} custom-call(bf16[144,512]{1,0:T(8,128)(2,1)S(1)} %collective-permute-done.9.latent_ref, bf16[30,96,512]{2,1,0:T(8,128)(2,1)S(1)} %mix_edges.1.weights_ref, bf16[2,2,5,256,256]{4,3,2,1,0:T(8,128)(2,1)S(1)} %get-tuple-element.56.hot_ref, f32[2,96,256]{2,1,0:T(8,128)S(1)} %get-tuple-element.57.partial_ref), custom_call_target="tpu_custom_call" | custom-call | flops 1000000000 | bytes 2500000 | tf_op jit(solution)/shard_map/inner_band/pallas_call | solution.py:545
  32.5 0.1 collective-permute-done.8.latent_ref
  32.6 1.6 %outer_band.1 = bf16[84,2,256]{2,1,0:T(2,128)(2,1)} custom-call(bf16[144,512]{1,0:T(8,128)(2,1)S(1)} %collective-permute-done.8.latent_ref, bf16[30,96,512]{2,1,0:T(8,128)(2,1)S(1)} %mix_edges.1.weights_ref, bf16[2,2,5,256,256]{4,3,2,1,0:T(8,128)(2,1)S(1)} %get-tuple-element.56.hot_ref, f32[2,96,256]{2,1,0:T(8,128)S(1)} %inner_band.1.partial_ref), custom_call_target="tpu_custom_call" | custom-call | flops 1000000000 | bytes 2500000 | tf_op jit(solution)/shard_map/outer_band/pallas_call | solution.py:555
  (20 shorter events, 0.1 us)
Async XLA Ops:
  0.6 14.1 %copy-start = (bf16[9,512,84]{1,2,0:T(8,128)(2,1)S(1)}, bf16[9,512,84]{1,2,0:T(8,128)(2,1)}, u32[]{:S(2)}) copy-start(bf16[9,512,84]{1,2,0:T(8,128)(2,1)} %param.17) | copy-start | bytes 2322436
  0.6 14.1 %copy-start.3 = (f32[9,2,5,5]{0,1,3,2:T(2,128)S(1)}, f32[9,2,5,5]{0,1,3,2:T(2,128)}, u32[]{:S(2)}) copy-start(f32[9,2,5,5]{0,1,3,2:T(2,128)} %param.16) | copy-start | bytes 5404
  0.6 6.3 %collective-permute-start = (bf16[128,512]{1,0:T(8,128)(2,1)}, bf16[128,512]{1,0:T(8,128)(2,1)S(1)}, u32[]{:S(2)}, u32[]{:S(2)}) collective-permute-start(bf16[128,512]{1,0:T(8,128)(2,1)} %bitcast.13), channel_id=1, source_target_pairs={{0,1},{2,3},{1,0},{3,2},{4,5},{6,7},{5,4},{7,6},{8,9},{10,11},{9,8... | collective-permute-start | bytes 393224 | tf_op jit(solution)/shard_map/ppermute | solution.py:404
  2.8 8.8 %collective-permute-start.2 = (bf16[128,512]{1,0:T(8,128)(2,1)}, bf16[128,512]{1,0:T(8,128)(2,1)S(1)}, u32[]{:S(2)}, u32[]{:S(2)}) collective-permute-start(bf16[128,512]{1,0:T(8,128)(2,1)} %bitcast.14), channel_id=1, source_target_pairs={{1,2},{3,0},{2,1},{0,3},{5,6},{7,4},{6,5},{4,7},{9,10},{11,8},{10,... | collective-permute-start | bytes 393224 | tf_op jit(solution)/shard_map/ppermute | solution.py:404
  7.0 8.8 %collective-permute-start.1 = (bf16[272,512]{1,0:T(8,128)(2,1)S(1)}, bf16[272,512]{1,0:T(8,128)(2,1)S(1)}, u32[]{:S(2)}, u32[]{:S(2)}) collective-permute-start(bf16[272,512]{1,0:T(8,128)(2,1)S(1)} %constant_dynamic-update-slice_fusion), channel_id=1, source_target_pairs={{0,4},{8,12},{16,20},{24,28},{4,0},{12,8},{20,16},{28,24},{1,5},{9... | collective-permute-start | bytes 835592 | tf_op jit(solution)/shard_map/ppermute | solution.py:409
  8.3 7.9 %collective-permute-start.3 = (bf16[272,512]{1,0:T(8,128)(2,1)S(1)}, bf16[272,512]{1,0:T(8,128)(2,1)S(1)}, u32[]{:S(2)}, u32[]{:S(2)}) collective-permute-start(bf16[272,512]{1,0:T(8,128)(2,1)S(1)} %constant_dynamic-update-slice_fusion), channel_id=1, source_target_pairs={{4,8},{12,16},{20,24},{8,4},{16,12},{24,20},{5,9},{13,17},{21,25},... | collective-permute-start | bytes 835592 | tf_op jit(solution)/shard_map/ppermute | solution.py:409
  11.5 4.6 %copy-start.4 = (f32[512]{0:T(512)S(1)}, f32[512]{0:T(512)}, u32[]{:S(2)}) copy-start(f32[512]{0:T(512)} %param.10) | copy-start | bytes 6148
  11.5 6.3 %collective-permute-start.5 = (bf16[128,512]{1,0:T(8,128)(2,1)S(1)}, bf16[128,512]{1,0:T(8,128)(2,1)S(1)}, u32[]{:S(2)}, u32[]{:S(2)}) collective-permute-start(bf16[128,512]{1,0:T(8,128)(2,1)S(1)} %collective-permute-done.2.other_ref), channel_id=1, source_target_pairs={{4,8},{12,16},{20,24},{8,4},{16,12},{24,20},{5,9},{13,17},{21,25},... | collective-permute-start | bytes 393224 | tf_op jit(solution)/shard_map/ppermute | solution.py:409
  14.7 3.2 %collective-permute-start.4 = (bf16[128,512]{1,0:T(8,128)(2,1)S(1)}, bf16[128,512]{1,0:T(8,128)(2,1)S(1)}, u32[]{:S(2)}, u32[]{:S(2)}) collective-permute-start(bf16[128,512]{1,0:T(8,128)(2,1)S(1)} %collective-permute-done.2.other_ref), channel_id=1, source_target_pairs={{0,4},{8,12},{16,20},{24,28},{4,0},{12,8},{20,16},{28,24},{1,5},{9... | collective-permute-start | bytes 393224 | tf_op jit(solution)/shard_map/ppermute | solution.py:409
  16.2 1.7 %copy-start.1 = (bf16[512,512]{1,0:T(8,128)(2,1)S(1)}, bf16[512,512]{1,0:T(8,128)(2,1)}, u32[]{:S(2)}) copy-start(bf16[512,512]{1,0:T(8,128)(2,1)} %wout_ref.1) | copy-start | bytes 1572868
  16.2 1.7 %copy-start.2 = (bf16[512,512]{1,0:T(8,128)(2,1)S(1)}, bf16[512,512]{1,0:T(8,128)(2,1)}, u32[]{:S(2)}) copy-start(bf16[512,512]{1,0:T(8,128)(2,1)} %wlat_ref.1) | copy-start | bytes 1572868
  19.8 3.9 %collective-permute-start.6 = (bf16[16,512]{1,0:T(8,128)(2,1)S(1)}, bf16[16,512]{1,0:T(8,128)(2,1)S(1)}, u32[]{:S(2)}, u32[]{:S(2)}) collective-permute-start(bf16[16,512]{1,0:T(8,128)(2,1)S(1)} %get-tuple-element.47), channel_id=1, source_target_pairs={{1,2},{3,0},{2,1},{0,3},{5,6},{7,4},{6,5},{4,7},{9,10},{11,8},{10,... | collective-permute-start | bytes 49160 | tf_op jit(solution)/shard_map/ppermute | solution.py:404
  22.6 2.9 %collective-permute-start.7 = (bf16[16,512]{1,0:T(8,128)(2,1)S(1)}, bf16[16,512]{1,0:T(8,128)(2,1)S(1)}, u32[]{:S(2)}, u32[]{:S(2)}) collective-permute-start(bf16[16,512]{1,0:T(8,128)(2,1)S(1)} %get-tuple-element.48), channel_id=1, source_target_pairs={{0,1},{2,3},{1,0},{3,2},{4,5},{6,7},{5,4},{7,6},{8,9},{10,11},{9,8... | collective-permute-start | bytes 49160 | tf_op jit(solution)/shard_map/ppermute | solution.py:404
  25.5 6.1 %collective-permute-start.9 = (bf16[144,512]{1,0:T(8,128)(2,1)S(1)}, bf16[144,512]{1,0:T(8,128)(2,1)S(1)}, u32[]{:S(2)}, u32[]{:S(2)}) collective-permute-start(bf16[144,512]{1,0:T(8,128)(2,1)S(1)} %pad_maximum_fusion.latent_ref), channel_id=1, source_target_pairs={{0,4},{8,12},{16,20},{24,28},{4,0},{12,8},{20,16},{28,24},{1,5},{9... | collective-permute-start | bytes 442376 | tf_op jit(solution)/shard_map/ppermute | solution.py:409
  26.1 6.5 %collective-permute-start.8 = (bf16[144,512]{1,0:T(8,128)(2,1)S(1)}, bf16[144,512]{1,0:T(8,128)(2,1)S(1)}, u32[]{:S(2)}, u32[]{:S(2)}) collective-permute-start(bf16[144,512]{1,0:T(8,128)(2,1)S(1)} %pad_maximum_fusion.latent_ref), channel_id=1, source_target_pairs={{4,8},{12,16},{20,24},{8,4},{16,12},{24,20},{5,9},{13,17},{21,25},... | collective-permute-start | bytes 442376 | tf_op jit(solution)/shard_map/ppermute | solution.py:409

commit v18 on v16

--- a/solution.py
+++ b/solution.py
@@ -45,7 +45,11 @@
     return (center * lax.rsqrt(spread + 1e-05) * gain).astype(BF16)
 
 
-def mix_kernel(blocks, psi_ref, dec_ref, mixed_ref, psi_rows_ref, taps_ref):
+def mix_kernel(blocks, psi_ref, dec_ref, *refs):
+    if len(refs) > 3:
+        refs[2][...] = refs[0][...]
+        refs = (refs[1], *refs[3:])
+    mixed_ref, psi_rows_ref, taps_ref = refs
     basis, out_ch, channels = dec_ref.shape
     depth = basis * ROWS
     for tap in range(TAPS):
@@ -310,10 +314,8 @@
 
 
 def own_kernel(
-    begin, state_ref, own_ref, inner_ref, outer_ref, latent_ref, weights_ref,
-    out_ref, hot_ref, kept_ref,
+    begin, own_ref, inner_ref, outer_ref, latent_ref, weights_ref, out_ref, hot_ref
 ):
-    kept_ref[...] = state_ref[...]
     cols = out_ref.shape[2]
     rows = latent_ref.shape[0] - 2 * SIDE
     own = lines_of(own_ref, begin[0], cols)
@@ -418,15 +420,16 @@
     head = width // HEADS
     members = LANES // head
     parts = HEADS // members
-    def mixed(blocks, name, after):
+    def mixed(blocks, name, after, kept=()):
         taps = psi.transpose(2, 3, 1, 0)
         mixing = w_dec.transpose(0, 2, 1)
         taps, mixing, after = lax.optimization_barrier((taps, mixing, after))
         weights = pl.pallas_call(
             functools.partial(mix_kernel, blocks),
-            in_specs=[whole()] * 2,
-            out_specs=whole(),
-            out_shape=struct(len(blocks), outputs, channels),
+            in_specs=[whole()] * (2 + len(kept)),
+            out_specs=[whole()] * (1 + len(kept)),
+            out_shape=[struct(len(blocks), outputs, channels)]
+            + [struct(*array.shape) for array in kept],
             scratch_shapes=[
                 pltpu.VMEM((2 * TAPS * TAPS, basis), F32),
                 pltpu.VMEM((len(blocks) * ROWS, basis * ROWS), BF16),
@@ -434,8 +437,8 @@
             compiler_params=params(32),
             cost_estimate=cost(2e9, 6e6),
             name=name,
-        )(taps, mixing)
-        return weights, after
+        )(taps, mixing, *kept)
+        return *weights, after
 
     own = pl.pallas_call(
         gather_kernel,
@@ -517,26 +520,27 @@
 
     from_pair = paired(to_pair, 0)
     from_other = paired(to_other, 1)
-    middle, latent = mixed(blocks_of(OWN), "mix_own", latent)
+    middle, state, latent = mixed(blocks_of(OWN), "mix_own", latent, (state,))
     from_pair, middle = lax.optimization_barrier((from_pair, middle))
     extended = jnp.concatenate([latent, from_pair[:SIDE], from_other[:SIDE]], axis=0)
     far = exchanged(extended, 1)
-    near = exchanged(extended, 0)
+    cut = rows // 2
+    near = [exchanged(latent[:cut], 0), exchanged(extended[cut:], 0)]
+    near = jnp.concatenate(near, axis=0)
 
     lanes = -(-(rows + 2 * SIDE) // 256) * 256
-    partial, hots, state = pl.pallas_call(
+    partial, hots = pl.pallas_call(
         functools.partial(own_kernel, (rows, 2 * rows, 2 * rows)),
-        in_specs=[whole()] * 6,
-        out_specs=[whole()] * 3,
+        in_specs=[whole()] * 5,
+        out_specs=[whole()] * 2,
         out_shape=[
             struct(lat_rows, outputs, lon_cols, dtype=F32),
             struct(2, 2, TAPS, lanes, lon_cols),
-            struct(rows, width),
         ],
         compiler_params=params(32),
         cost_estimate=cost(1e9, 2.5e6),
         name="own_band",
-    )(state, own, inner, outer, extended, middle)
+    )(own, inner, outer, extended, middle)
     band_scratch = [
         pltpu.VMEM((outputs, TAPS * lanes), BF16),
         pltpu.VMEM((2 * outputs, TAPS * lanes), BF16),

time: 34.4 us -> 34.3 us (level)
    pallas_call x2, Pallas kernels: 1.82 us -> 2.41 us  [mixed(): pl.pallas_call(functools.partial(mix_kernel, blocks), in_specs=[whole()]...]
    ppermute x4, waiting for transfers between devices: 1.47 us -> 0.9 us  [paired(): return lax.ppermute(array, 'lon', pairs + [(j, i) for i, j in pairs])]
    pallas_call x1, Pallas kernels: 1.8 us -> 1.27 us  [shards(): pl.pallas_call(functools.partial(own_kernel, (rows, 2 * rows, 2 * rows)),...]
    ppermute x6 -> x7, waiting for transfers between devices: 0.55 us -> 0.89 us  [exchanged(): return lax.ppermute(array, 'reg', pairs + [(j, i) for i, j in pairs])]
    ppermute x6 -> x7, starting transfers between devices: 12.3 us -> 12.3 us  [exchanged(): return lax.ppermute(array, 'reg', pairs + [(j, i) for i, j in pairs])]
  transfers between devices with their start and end apart: 10 -> 11, of which waited for: 4 -> 4; matrix products, arithmetic and copies ran while one was open for 0% -> 0% of each run, Pallas kernels for 27% -> 27%
where the time goes in v18:
time: 34.3 us; the launch traced here: 34.1 us
  starting transfers between devices  18.6 us (54%)
  Pallas kernels  12.7 us (37%)
  waiting for transfers between devices  1.79 us (5%)
  between operations  0.85 us (2%)
    ppermute x7, starting transfers between devices, exchanged(): return lax.ppermute(array, 'reg', pairs + [(j, i) for i, j in pairs])  12.3 us
    ppermute x4, starting transfers between devices, paired(): return lax.ppermute(array, 'lon', pairs + [(j, i) for i, j in pairs])  6.34 us
    pallas_call x2, Pallas kernels, mixed(): pl.pallas_call(functools.partial(mix_kernel, blocks), in_specs=[whole()]...  2.41 us
    pallas_call x1, Pallas kernels, shards(): pl.pallas_call(functools.partial(prepare_kernel, sectors), in_specs=[whol...  2.02 us
    pallas_call x1, Pallas kernels, shards(): pl.pallas_call(late_kernel, in_specs=[whole()] * 15, out_specs=[whole()]...  1.94 us
    pallas_call x1, Pallas kernels, shards(): pl.pallas_call(early_kernel, in_specs=[whole()] * 11, out_specs=[whole()]...  1.6 us
    pallas_call x1, Pallas kernels, shards(): pl.pallas_call(functools.partial(band_kernel, False), in_specs=[whole()]...  1.59 us
    pallas_call x1, Pallas kernels, shards(): pl.pallas_call(functools.partial(own_kernel, (rows, 2 * rows, 2 * rows)),...  1.27 us
  transfers between devices with their start and end apart: 11, of which 4 were waited for; matrix products, arithmetic and copies ran while one was open for 0% of the time, Pallas kernels for 27%

profile of v18, /device:TPU:1, one launch (start us, length us, event | category | flops | bytes accessed | tf_op | source)
XLA Modules:
  0.0 34.1 jit_solution(5806889543806711997)
XLA Ops:
  0.6 2.1 %collective-permute-start = (bf16[128,512]{1,0:T(8,128)(2,1)}, bf16[128,512]{1,0:T(8,128)(2,1)S(1)}, u32[]{:S(2)}, u32[]{:S(2)}) collective-permute-start(bf16[128,512]{1,0:T(8,128)(2,1)} %bitcast.13), channel_id=1, source_target_pairs={{0,1},{2,3},{1,0},{3,2},{4,5},{6,7},{5,4},{7,6},{8,9},{10,11},{9,8... | collective-permute-start | bytes 393224 | tf_op jit(solution)/shard_map/ppermute | solution.py:406
  2.8 1.2 %collective-permute-start.2 = (bf16[128,512]{1,0:T(8,128)(2,1)}, bf16[128,512]{1,0:T(8,128)(2,1)S(1)}, u32[]{:S(2)}, u32[]{:S(2)}) collective-permute-start(bf16[128,512]{1,0:T(8,128)(2,1)} %bitcast.14), channel_id=1, source_target_pairs={{1,2},{3,0},{2,1},{0,3},{5,6},{7,4},{6,5},{4,7},{9,10},{11,8},{10,... | collective-permute-start | bytes 393224 | tf_op jit(solution)/shard_map/ppermute | solution.py:406
  4.0 1.0 %gather.1.own_ref = bf16[144,512]{1,0:T(8,128)(2,1)S(1)} custom-call(bf16[128,512]{1,0:T(8,128)(2,1)} %bitcast.15, s32[2,256]{1,0:T(2,128)} %assign_hbm.3), custom_call_target="tpu_custom_call" | custom-call | flops 1000 | bytes 1000 | tf_op jit(solution)/shard_map/gather/pallas_call | solution.py:443
  4.9 2.0 %prepare.1 = (bf16[4,128,512]{2,1,0:T(8,128)(2,1)S(1)}, bf16[128,512]{1,0:T(8,128)(2,1)S(1)}, bf16[512,128]{1,0:T(8,128)(2,1)S(1)}, bf16[512,512]{1,0:T(8,128)(2...) custom-call(bf16[144,512]{1,0:T(8,128)(2,1)S(1)} %gather.1.own_ref, ...), custom_call_target="tpu_custom_call" | custom-call | flops 500000000 | bytes 1000000 | tf_op jit(solution)/shard_map/prepare/pallas_call | solution.py:456
  7.0 1.3 %collective-permute-start.1 = (bf16[272,512]{1,0:T(8,128)(2,1)S(1)}, bf16[272,512]{1,0:T(8,128)(2,1)S(1)}, u32[]{:S(2)}, u32[]{:S(2)}) collective-permute-start(bf16[272,512]{1,0:T(8,128)(2,1)S(1)} %constant_dynamic-update-slice_fusion), channel_id=1, source_target_pairs={{0,4},{8,12},{16,20},{24,28},{4,0},{12,8},{20,16},{28,24},{1,5},{9... | collective-permute-start | bytes 835592 | tf_op jit(solution)/shard_map/ppermute | solution.py:411
  8.3 3.2 %collective-permute-start.3 = (bf16[272,512]{1,0:T(8,128)(2,1)S(1)}, bf16[272,512]{1,0:T(8,128)(2,1)S(1)}, u32[]{:S(2)}, u32[]{:S(2)}) collective-permute-start(bf16[272,512]{1,0:T(8,128)(2,1)S(1)} %constant_dynamic-update-slice_fusion), channel_id=1, source_target_pairs={{4,8},{12,16},{20,24},{8,4},{16,12},{24,20},{5,9},{13,17},{21,25},... | collective-permute-start | bytes 835592 | tf_op jit(solution)/shard_map/ppermute | solution.py:411
  11.5 0.0 copy-start.4
  11.5 3.1 %collective-permute-start.5 = (bf16[128,512]{1,0:T(8,128)(2,1)S(1)}, bf16[128,512]{1,0:T(8,128)(2,1)S(1)}, u32[]{:S(2)}, u32[]{:S(2)}) collective-permute-start(bf16[128,512]{1,0:T(8,128)(2,1)S(1)} %collective-permute-done.2.other_ref), channel_id=1, source_target_pairs={{4,8},{12,16},{20,24},{8,4},{16,12},{24,20},{5,9},{13,17},{21,25},... | collective-permute-start | bytes 393224 | tf_op jit(solution)/shard_map/ppermute | solution.py:411
  14.7 0.1 collective-permute-start.4
  14.8 1.0 %mix_edges.1.weights_ref = bf16[30,96,512]{2,1,0:T(8,128)(2,1)S(1)} custom-call(f32[5,5,2,9]{3,2,1,0:T(2,128)S(1)} %bitcast.8, bf16[9,84,512]{2,1,0:T(8,128)(2,1)S(1)} %bitcast.6), custom_call_target="tpu_custom_call" | custom-call | flops 2000000000 | bytes 6000000 | tf_op jit(solution)/shard_map/mix_edges/pallas_call | solution.py:427
  15.8 0.3 %collective-permute-done.3.outer_ref = bf16[272,512]{1,0:T(8,128)(2,1)S(1)} collective-permute-done((bf16[272,512]{1,0:T(8,128)(2,1)S(1)}, bf16[272,512]{1,0:T(8,128)(2,1)S(1)}, u32[]{:S(2)}, u32[]{:S(2)}) %collective-permute-start.3) | collective-permute-done | bytes 278560 | tf_op jit(solution)/shard_map/ppermute | solution.py:411
  16.2 1.6 %early.1 = (f32[4,2,8,512]{3,2,1,0:T(8,128)S(1)}, f32[4,128,128]{2,1,0:T(8,128)S(1)}) custom-call(bf16[4,5,16,128]{3,2,1,0:T(8,128)(2,1)S(1)} %get-tuple-element.30.choice_ref, bf16[128,512]{1,0:T(8,128)(2,1)S(1)} %collective-permute-done.2.other_ref, bf16[128,512]{1,0:T(8,128)(2,1)S(1)} %collective-permute-done.pair_ref, ...), custom_call_target="tpu_custom_call" | custom-call | flops 3000000000 | bytes 6000000 | tf_op jit(solution)/shard_map/early/pallas_call | solution.py:491
  17.8 0.1 collective-permute-done.5.corner_ref
  17.8 1.9 %late.1 = (bf16[128,512]{1,0:T(8,128)(2,1)S(1)}, bf16[128,512]{1,0:T(8,128)(2,1)S(1)}, bf16[16,512]{1,0:T(8,128)(2,1)S(1)}, bf16[16,512]{1,0:T(8,128)(2,1)S(1)}) custom-call(bf16[4,5,16,128]{3,2,1,0:T(8,128)(2,1)S(1)} %get-tuple-element.30.choice_ref, bf16[32,128]{1,0:T(8,128)(2,1)S(1)} %get-tuple-element.31.cells_ref, ...), custom_call_target="tpu_custom_call" | custom-call | flops 3000000000 | bytes 6000000 | tf_op jit(solution)/shard_map/late/pallas_call | solution.py:507
  19.8 1.8 %collective-permute-start.6 = (bf16[16,512]{1,0:T(8,128)(2,1)S(1)}, bf16[16,512]{1,0:T(8,128)(2,1)S(1)}, u32[]{:S(2)}, u32[]{:S(2)}) collective-permute-start(bf16[16,512]{1,0:T(8,128)(2,1)S(1)} %get-tuple-element.50), channel_id=1, source_target_pairs={{0,1},{2,3},{1,0},{3,2},{4,5},{6,7},{5,4},{7,6},{8,9},{10,11},{9,8... | collective-permute-start | bytes 49160 | tf_op jit(solution)/shard_map/ppermute | solution.py:406
  21.6 1.2 %collective-permute-start.7 = (bf16[16,512]{1,0:T(8,128)(2,1)S(1)}, bf16[16,512]{1,0:T(8,128)(2,1)S(1)}, u32[]{:S(2)}, u32[]{:S(2)}) collective-permute-start(bf16[16,512]{1,0:T(8,128)(2,1)S(1)} %get-tuple-element.53), channel_id=1, source_target_pairs={{1,2},{3,0},{2,1},{0,3},{5,6},{7,4},{6,5},{4,7},{9,10},{11,8},{10,... | collective-permute-start | bytes 49160 | tf_op jit(solution)/shard_map/ppermute | solution.py:406
  22.8 1.4 %mix_own.1 = (bf16[20,96,512]{2,1,0:T(8,128)(2,1)S(1)}, bf16[128,512]{1,0:T(8,128)(2,1)}) custom-call(f32[5,5,2,9]{3,2,1,0:T(2,128)S(1)} %bitcast.9, bf16[9,84,512]{2,1,0:T(8,128)(2,1)S(1)} %bitcast.7, bf16[128,512]{1,0:T(8,128)(2,1)S(1)} %get-tuple-element.47.refs_0_), custom_call_target="tpu_custom_call" | custom-call | flops 2000000000 | bytes 6000000 | tf_op jit(solution)/shard_map/mix_own/pallas_call | solution.py:427
  24.2 0.9 %collective-permute-done.7 = bf16[16,512]{1,0:T(8,128)(2,1)S(1)} collective-permute-done((bf16[16,512]{1,0:T(8,128)(2,1)S(1)}, bf16[16,512]{1,0:T(8,128)(2,1)S(1)}, u32[]{:S(2)}, u32[]{:S(2)}) %collective-permute-start.7) | collective-permute-done | bytes 16416 | tf_op jit(solution)/shard_map/ppermute | solution.py:406
  25.1 4.5 %collective-permute-start.8 = (bf16[144,512]{1,0:T(8,128)(2,1)S(1)}, bf16[144,512]{1,0:T(8,128)(2,1)S(1)}, u32[]{:S(2)}, u32[]{:S(2)}) collective-permute-start(bf16[144,512]{1,0:T(8,128)(2,1)S(1)} %pad_maximum_fusion.latent_ref), channel_id=1, source_target_pairs={{4,8},{12,16},{20,24},{8,4},{16,12},{24,20},{5,9},{13,17},{21,25},... | collective-permute-start | bytes 442376 | tf_op jit(solution)/shard_map/ppermute | solution.py:411
  29.7 0.1 collective-permute-start.10
  29.7 1.3 %own_band.1 = (f32[2,96,256]{2,1,0:T(8,128)S(1)}, bf16[2,2,5,256,256]{4,3,2,1,0:T(8,128)(2,1)S(1)}) custom-call(bf16[144,512]{1,0:T(8,128)(2,1)S(1)} %gather.1.own_ref, bf16[272,512]{1,0:T(8,128)(2,1)S(1)} %collective-permute-done.1.inner_ref, bf16[272,512]{1,0:T(8,128)(2,1)S(1)} %collective-permute-done.3.outer_ref, ...), custom_call_target="tpu_custom_call" | custom-call | flops 1000000000 | bytes 2500000 | tf_op jit(solution)/shard_map/own_band/pallas_call | solution.py:532
  31.1 0.9 %inner_band.1.partial_ref = f32[2,96,256]{2,1,0:T(8,128)S(1)} custom-call(bf16[144,512]{1,0:T(8,128)(2,1)S(1)} %pad_maximum_fusion.1.latent_ref, bf16[30,96,512]{2,1,0:T(8,128)(2,1)S(1)} %mix_edges.1.weights_ref, bf16[2,2,5,256,256]{4,3,2,1,0:T(8,128)(2,1)S(1)} %get-tuple-element.56.hot_ref, f32[2,96,256]{2,1,0:T(8,128)S(1)} %get-tuple-element.57.partial_ref), custom_call_target="tpu_custom_call" | custom-call | flops 1000000000 | bytes 2500000 | tf_op jit(solution)/shard_map/inner_band/pallas_call | solution.py:549
  32.0 0.5 %collective-permute-done.8.latent_ref = bf16[144,512]{1,0:T(8,128)(2,1)S(1)} collective-permute-done((bf16[144,512]{1,0:T(8,128)(2,1)S(1)}, bf16[144,512]{1,0:T(8,128)(2,1)S(1)}, u32[]{:S(2)}, u32[]{:S(2)}) %collective-permute-start.8) | collective-permute-done | bytes 147488 | tf_op jit(solution)/shard_map/ppermute | solution.py:411
  32.5 1.6 %outer_band.1 = bf16[84,2,256]{2,1,0:T(2,128)(2,1)} custom-call(bf16[144,512]{1,0:T(8,128)(2,1)S(1)} %collective-permute-done.8.latent_ref, bf16[30,96,512]{2,1,0:T(8,128)(2,1)S(1)} %mix_edges.1.weights_ref, bf16[2,2,5,256,256]{4,3,2,1,0:T(8,128)(2,1)S(1)} %get-tuple-element.56.hot_ref, f32[2,96,256]{2,1,0:T(8,128)S(1)} %inner_band.1.partial_ref), custom_call_target="tpu_custom_call" | custom-call | flops 1000000000 | bytes 2500000 | tf_op jit(solution)/shard_map/outer_band/pallas_call | solution.py:559
  (25 shorter events, 0.1 us)
Async XLA Ops:
  0.6 14.1 %copy-start = (bf16[9,512,84]{1,2,0:T(8,128)(2,1)S(1)}, bf16[9,512,84]{1,2,0:T(8,128)(2,1)}, u32[]{:S(2)}) copy-start(bf16[9,512,84]{1,2,0:T(8,128)(2,1)} %param.17) | copy-start | bytes 2322436
  0.6 14.1 %copy-start.3 = (f32[9,2,5,5]{0,1,3,2:T(2,128)S(1)}, f32[9,2,5,5]{0,1,3,2:T(2,128)}, u32[]{:S(2)}) copy-start(f32[9,2,5,5]{0,1,3,2:T(2,128)} %param.16) | copy-start | bytes 5404
  0.6 6.3 %collective-permute-start = (bf16[128,512]{1,0:T(8,128)(2,1)}, bf16[128,512]{1,0:T(8,128)(2,1)S(1)}, u32[]{:S(2)}, u32[]{:S(2)}) collective-permute-start(bf16[128,512]{1,0:T(8,128)(2,1)} %bitcast.13), channel_id=1, source_target_pairs={{0,1},{2,3},{1,0},{3,2},{4,5},{6,7},{5,4},{7,6},{8,9},{10,11},{9,8... | collective-permute-start | bytes 393224 | tf_op jit(solution)/shard_map/ppermute | solution.py:406
  2.8 8.8 %collective-permute-start.2 = (bf16[128,512]{1,0:T(8,128)(2,1)}, bf16[128,512]{1,0:T(8,128)(2,1)S(1)}, u32[]{:S(2)}, u32[]{:S(2)}) collective-permute-start(bf16[128,512]{1,0:T(8,128)(2,1)} %bitcast.14), channel_id=1, source_target_pairs={{1,2},{3,0},{2,1},{0,3},{5,6},{7,4},{6,5},{4,7},{9,10},{11,8},{10,... | collective-permute-start | bytes 393224 | tf_op jit(solution)/shard_map/ppermute | solution.py:406
  7.0 8.8 %collective-permute-start.1 = (bf16[272,512]{1,0:T(8,128)(2,1)S(1)}, bf16[272,512]{1,0:T(8,128)(2,1)S(1)}, u32[]{:S(2)}, u32[]{:S(2)}) collective-permute-start(bf16[272,512]{1,0:T(8,128)(2,1)S(1)} %constant_dynamic-update-slice_fusion), channel_id=1, source_target_pairs={{0,4},{8,12},{16,20},{24,28},{4,0},{12,8},{20,16},{28,24},{1,5},{9... | collective-permute-start | bytes 835592 | tf_op jit(solution)/shard_map/ppermute | solution.py:411
  8.3 7.9 %collective-permute-start.3 = (bf16[272,512]{1,0:T(8,128)(2,1)S(1)}, bf16[272,512]{1,0:T(8,128)(2,1)S(1)}, u32[]{:S(2)}, u32[]{:S(2)}) collective-permute-start(bf16[272,512]{1,0:T(8,128)(2,1)S(1)} %constant_dynamic-update-slice_fusion), channel_id=1, source_target_pairs={{4,8},{12,16},{20,24},{8,4},{16,12},{24,20},{5,9},{13,17},{21,25},... | collective-permute-start | bytes 835592 | tf_op jit(solution)/shard_map/ppermute | solution.py:411
  11.5 4.6 %copy-start.4 = (f32[512]{0:T(512)S(1)}, f32[512]{0:T(512)}, u32[]{:S(2)}) copy-start(f32[512]{0:T(512)} %param.10) | copy-start | bytes 6148
  11.5 6.3 %collective-permute-start.5 = (bf16[128,512]{1,0:T(8,128)(2,1)S(1)}, bf16[128,512]{1,0:T(8,128)(2,1)S(1)}, u32[]{:S(2)}, u32[]{:S(2)}) collective-permute-start(bf16[128,512]{1,0:T(8,128)(2,1)S(1)} %collective-permute-done.2.other_ref), channel_id=1, source_target_pairs={{4,8},{12,16},{20,24},{8,4},{16,12},{24,20},{5,9},{13,17},{21,25},... | collective-permute-start | bytes 393224 | tf_op jit(solution)/shard_map/ppermute | solution.py:411
  14.7 3.2 %collective-permute-start.4 = (bf16[128,512]{1,0:T(8,128)(2,1)S(1)}, bf16[128,512]{1,0:T(8,128)(2,1)S(1)}, u32[]{:S(2)}, u32[]{:S(2)}) collective-permute-start(bf16[128,512]{1,0:T(8,128)(2,1)S(1)} %collective-permute-done.2.other_ref), channel_id=1, source_target_pairs={{0,4},{8,12},{16,20},{24,28},{4,0},{12,8},{20,16},{28,24},{1,5},{9... | collective-permute-start | bytes 393224 | tf_op jit(solution)/shard_map/ppermute | solution.py:411
  16.2 1.7 %copy-start.1 = (bf16[512,512]{1,0:T(8,128)(2,1)S(1)}, bf16[512,512]{1,0:T(8,128)(2,1)}, u32[]{:S(2)}) copy-start(bf16[512,512]{1,0:T(8,128)(2,1)} %wout_ref.1) | copy-start | bytes 1572868
  16.2 1.7 %copy-start.2 = (bf16[512,512]{1,0:T(8,128)(2,1)S(1)}, bf16[512,512]{1,0:T(8,128)(2,1)}, u32[]{:S(2)}) copy-start(bf16[512,512]{1,0:T(8,128)(2,1)} %wlat_ref.1) | copy-start | bytes 1572868
  19.8 4.4 %collective-permute-start.6 = (bf16[16,512]{1,0:T(8,128)(2,1)S(1)}, bf16[16,512]{1,0:T(8,128)(2,1)S(1)}, u32[]{:S(2)}, u32[]{:S(2)}) collective-permute-start(bf16[16,512]{1,0:T(8,128)(2,1)S(1)} %get-tuple-element.50), channel_id=1, source_target_pairs={{0,1},{2,3},{1,0},{3,2},{4,5},{6,7},{5,4},{7,6},{8,9},{10,11},{9,8... | collective-permute-start | bytes 49160 | tf_op jit(solution)/shard_map/ppermute | solution.py:406
  21.6 3.5 %collective-permute-start.7 = (bf16[16,512]{1,0:T(8,128)(2,1)S(1)}, bf16[16,512]{1,0:T(8,128)(2,1)S(1)}, u32[]{:S(2)}, u32[]{:S(2)}) collective-permute-start(bf16[16,512]{1,0:T(8,128)(2,1)S(1)} %get-tuple-element.53), channel_id=1, source_target_pairs={{1,2},{3,0},{2,1},{0,3},{5,6},{7,4},{6,5},{4,7},{9,10},{11,8},{10,... | collective-permute-start | bytes 49160 | tf_op jit(solution)/shard_map/ppermute | solution.py:406
  22.8 8.2 %collective-permute-start.9 = (bf16[64,512]{1,0:T(8,128)(2,1)S(1)}, bf16[64,512]{1,0:T(8,128)(2,1)S(1)}, u32[]{:S(2)}, u32[]{:S(2)}) collective-permute-start(bf16[64,512]{1,0:T(8,128)(2,1)S(1)} %slice.14), channel_id=1, source_target_pairs={{0,4},{8,12},{16,20},{24,28},{4,0},{12,8},{20,16},{28,24},{1,5},{9... | collective-permute-start | bytes 196616 | tf_op jit(solution)/shard_map/ppermute | solution.py:411
  25.1 7.4 %collective-permute-start.8 = (bf16[144,512]{1,0:T(8,128)(2,1)S(1)}, bf16[144,512]{1,0:T(8,128)(2,1)S(1)}, u32[]{:S(2)}, u32[]{:S(2)}) collective-permute-start(bf16[144,512]{1,0:T(8,128)(2,1)S(1)} %pad_maximum_fusion.latent_ref), channel_id=1, source_target_pairs={{4,8},{12,16},{20,24},{8,4},{16,12},{24,20},{5,9},{13,17},{21,25},... | collective-permute-start | bytes 442376 | tf_op jit(solution)/shard_map/ppermute | solution.py:411
  29.7 1.4 %collective-permute-start.10 = (bf16[80,512]{1,0:T(8,128)(2,1)S(1)}, bf16[80,512]{1,0:T(8,128)(2,1)S(1)}, u32[]{:S(2)}, u32[]{:S(2)}) collective-permute-start(bf16[80,512]{1,0:T(8,128)(2,1)S(1)} %slice.17), channel_id=1, source_target_pairs={{0,4},{8,12},{16,20},{24,28},{4,0},{12,8},{20,16},{28,24},{1,5},{9... | collective-permute-start | bytes 245768 | tf_op jit(solution)/shard_map/ppermute | solution.py:411

commit v19 on v16

--- a/solution.py
+++ b/solution.py
@@ -521,7 +521,9 @@
     from_pair, middle = lax.optimization_barrier((from_pair, middle))
     extended = jnp.concatenate([latent, from_pair[:SIDE], from_other[:SIDE]], axis=0)
     far = exchanged(extended, 1)
-    near = exchanged(extended, 0)
+    cut = rows // 2
+    near = [exchanged(latent[:cut], 0), exchanged(extended[cut:], 0)]
+    near = jnp.concatenate(near, axis=0)
 
     lanes = -(-(rows + 2 * SIDE) // 256) * 256
     partial, hots, state = pl.pallas_call(

time: 34.4 us -> 35.3 us (1.026); the launches traced: 34.2 us -> 34.6 us
  starting transfers between devices: 18.6 us -> 19.4 us
  waiting for transfers between devices: 2.03 us -> 1.57 us
    ppermute x6 -> x7, starting transfers between devices: 12.3 us -> 13.1 us  [exchanged(): return lax.ppermute(array, 'reg', pairs + [(j, i) for i, j in pairs])]
    ppermute x6 -> x7, waiting for transfers between devices: 0.55 us -> 0.02 us  [exchanged(): return lax.ppermute(array, 'reg', pairs + [(j, i) for i, j in pairs])]
  transfers between devices with their start and end apart: 10 -> 11, of which waited for: 4 -> 1; matrix products, arithmetic and copies ran while one was open for 0% -> 0% of each run, Pallas kernels for 27% -> 26%
where the time goes in v19:
time: 35.3 us; the launch traced here: 34.6 us
  starting transfers between devices  19.4 us (55%)
  Pallas kernels  12.7 us (36%)
  waiting for transfers between devices  1.57 us (4%)
  between operations  0.89 us (3%)
    ppermute x7, starting transfers between devices, exchanged(): return lax.ppermute(array, 'reg', pairs + [(j, i) for i, j in pairs])  13.1 us
    ppermute x4, starting transfers between devices, paired(): return lax.ppermute(array, 'lon', pairs + [(j, i) for i, j in pairs])  6.26 us
    pallas_call x1, Pallas kernels, shards(): pl.pallas_call(functools.partial(prepare_kernel, sectors), in_specs=[whol...  2.02 us
    pallas_call x1, Pallas kernels, shards(): pl.pallas_call(late_kernel, in_specs=[whole()] * 15, out_specs=[whole()]...  1.96 us
    pallas_call x2, Pallas kernels, mixed(): pl.pallas_call(functools.partial(mix_kernel, blocks), in_specs=[whole()]...  1.83 us
    pallas_call x1, Pallas kernels, shards(): pl.pallas_call(functools.partial(own_kernel, (rows, 2 * rows, 2 * rows)),...  1.8 us
    pallas_call x1, Pallas kernels, shards(): pl.pallas_call(early_kernel, in_specs=[whole()] * 11, out_specs=[whole()]...  1.6 us
    pallas_call x1, Pallas kernels, shards(): pl.pallas_call(functools.partial(band_kernel, False), in_specs=[whole()]...  1.6 us
  transfers between devices with their start and end apart: 11, of which 1 were waited for; matrix products, arithmetic and copies ran while one was open for 0% of the time, Pallas kernels for 26%

profile of v19, /device:TPU:1, one launch (start us, length us, event | category | flops | bytes accessed | tf_op | source)
XLA Modules:
  0.0 34.6 jit_solution(9288648952521197547)
XLA Ops:
  0.6 2.1 %collective-permute-start = (bf16[128,512]{1,0:T(8,128)(2,1)}, bf16[128,512]{1,0:T(8,128)(2,1)S(1)}, u32[]{:S(2)}, u32[]{:S(2)}) collective-permute-start(bf16[128,512]{1,0:T(8,128)(2,1)} %bitcast.13), channel_id=1, source_target_pairs={{0,1},{2,3},{1,0},{3,2},{4,5},{6,7},{5,4},{7,6},{8,9},{10,11},{9,8... | collective-permute-start | bytes 393224 | tf_op jit(solution)/shard_map/ppermute | solution.py:404
  2.8 1.2 %collective-permute-start.2 = (bf16[128,512]{1,0:T(8,128)(2,1)}, bf16[128,512]{1,0:T(8,128)(2,1)S(1)}, u32[]{:S(2)}, u32[]{:S(2)}) collective-permute-start(bf16[128,512]{1,0:T(8,128)(2,1)} %bitcast.14), channel_id=1, source_target_pairs={{1,2},{3,0},{2,1},{0,3},{5,6},{7,4},{6,5},{4,7},{9,10},{11,8},{10,... | collective-permute-start | bytes 393224 | tf_op jit(solution)/shard_map/ppermute | solution.py:404
  4.0 1.0 %gather.1.own_ref = bf16[144,512]{1,0:T(8,128)(2,1)S(1)} custom-call(bf16[128,512]{1,0:T(8,128)(2,1)} %bitcast.15, s32[2,256]{1,0:T(2,128)} %assign_hbm.3), custom_call_target="tpu_custom_call" | custom-call | flops 1000 | bytes 1000 | tf_op jit(solution)/shard_map/gather/pallas_call | solution.py:440
  4.9 2.0 %prepare.1 = (bf16[4,128,512]{2,1,0:T(8,128)(2,1)S(1)}, bf16[128,512]{1,0:T(8,128)(2,1)S(1)}, bf16[512,128]{1,0:T(8,128)(2,1)S(1)}, bf16[512,512]{1,0:T(8,128)(2...) custom-call(bf16[144,512]{1,0:T(8,128)(2,1)S(1)} %gather.1.own_ref, ...), custom_call_target="tpu_custom_call" | custom-call | flops 500000000 | bytes 1000000 | tf_op jit(solution)/shard_map/prepare/pallas_call | solution.py:453
  7.0 0.0 collective-permute-done.pair_ref
  7.0 1.3 %collective-permute-start.1 = (bf16[272,512]{1,0:T(8,128)(2,1)S(1)}, bf16[272,512]{1,0:T(8,128)(2,1)S(1)}, u32[]{:S(2)}, u32[]{:S(2)}) collective-permute-start(bf16[272,512]{1,0:T(8,128)(2,1)S(1)} %constant_dynamic-update-slice_fusion), channel_id=1, source_target_pairs={{0,4},{8,12},{16,20},{24,28},{4,0},{12,8},{20,16},{28,24},{1,5},{9... | collective-permute-start | bytes 835592 | tf_op jit(solution)/shard_map/ppermute | solution.py:409
  8.3 3.2 %collective-permute-start.3 = (bf16[272,512]{1,0:T(8,128)(2,1)S(1)}, bf16[272,512]{1,0:T(8,128)(2,1)S(1)}, u32[]{:S(2)}, u32[]{:S(2)}) collective-permute-start(bf16[272,512]{1,0:T(8,128)(2,1)S(1)} %constant_dynamic-update-slice_fusion), channel_id=1, source_target_pairs={{4,8},{12,16},{20,24},{8,4},{16,12},{24,20},{5,9},{13,17},{21,25},... | collective-permute-start | bytes 835592 | tf_op jit(solution)/shard_map/ppermute | solution.py:409
  11.5 0.0 copy-start.4
  11.5 0.1 collective-permute-start.4
  11.6 3.6 %collective-permute-start.5 = (bf16[128,512]{1,0:T(8,128)(2,1)S(1)}, bf16[128,512]{1,0:T(8,128)(2,1)S(1)}, u32[]{:S(2)}, u32[]{:S(2)}) collective-permute-start(bf16[128,512]{1,0:T(8,128)(2,1)S(1)} %collective-permute-done.2.other_ref), channel_id=1, source_target_pairs={{4,8},{12,16},{20,24},{8,4},{16,12},{24,20},{5,9},{13,17},{21,25},... | collective-permute-start | bytes 393224 | tf_op jit(solution)/shard_map/ppermute | solution.py:409
  15.2 1.0 %mix_edges.1.weights_ref = bf16[30,96,512]{2,1,0:T(8,128)(2,1)S(1)} custom-call(f32[5,5,2,9]{3,2,1,0:T(2,128)S(1)} %bitcast.8, bf16[9,84,512]{2,1,0:T(8,128)(2,1)S(1)} %bitcast.6), custom_call_target="tpu_custom_call" | custom-call | flops 2000000000 | bytes 6000000 | tf_op jit(solution)/shard_map/mix_edges/pallas_call | solution.py:425
  16.3 0.0 copy-start.1
  16.3 0.0 copy-start.2
  16.3 1.6 %early.1 = (f32[4,2,8,512]{3,2,1,0:T(8,128)S(1)}, f32[4,128,128]{2,1,0:T(8,128)S(1)}) custom-call(bf16[4,5,16,128]{3,2,1,0:T(8,128)(2,1)S(1)} %get-tuple-element.29.choice_ref, bf16[128,512]{1,0:T(8,128)(2,1)S(1)} %collective-permute-done.2.other_ref, bf16[128,512]{1,0:T(8,128)(2,1)S(1)} %collective-permute-done.pair_ref, ...), custom_call_target="tpu_custom_call" | custom-call | flops 3000000000 | bytes 6000000 | tf_op jit(solution)/shard_map/early/pallas_call | solution.py:488
  18.0 2.0 %late.1 = (bf16[128,512]{1,0:T(8,128)(2,1)S(1)}, bf16[128,512]{1,0:T(8,128)(2,1)S(1)}, bf16[16,512]{1,0:T(8,128)(2,1)S(1)}, bf16[16,512]{1,0:T(8,128)(2,1)S(1)}) custom-call(bf16[4,5,16,128]{3,2,1,0:T(8,128)(2,1)S(1)} %get-tuple-element.29.choice_ref, bf16[32,128]{1,0:T(8,128)(2,1)S(1)} %get-tuple-element.30.cells_ref, ...), custom_call_target="tpu_custom_call" | custom-call | flops 3000000000 | bytes 6000000 | tf_op jit(solution)/shard_map/late/pallas_call | solution.py:504
  19.9 2.7 %collective-permute-start.7 = (bf16[16,512]{1,0:T(8,128)(2,1)S(1)}, bf16[16,512]{1,0:T(8,128)(2,1)S(1)}, u32[]{:S(2)}, u32[]{:S(2)}) collective-permute-start(bf16[16,512]{1,0:T(8,128)(2,1)S(1)} %get-tuple-element.50), channel_id=1, source_target_pairs={{1,2},{3,0},{2,1},{0,3},{5,6},{7,4},{6,5},{4,7},{9,10},{11,8},{10,... | collective-permute-start | bytes 49160 | tf_op jit(solution)/shard_map/ppermute | solution.py:404
  22.6 0.2 collective-permute-start.6
  22.9 0.8 %mix_own.1.weights_ref = bf16[20,96,512]{2,1,0:T(8,128)(2,1)S(1)} custom-call(f32[5,5,2,9]{3,2,1,0:T(2,128)S(1)} %bitcast.9, bf16[9,84,512]{2,1,0:T(8,128)(2,1)S(1)} %bitcast.7), custom_call_target="tpu_custom_call" | custom-call | flops 2000000000 | bytes 6000000 | tf_op jit(solution)/shard_map/mix_own/pallas_call | solution.py:425
  23.7 1.5 %collective-permute-done.6 = bf16[16,512]{1,0:T(8,128)(2,1)S(1)} collective-permute-done((bf16[16,512]{1,0:T(8,128)(2,1)S(1)}, bf16[16,512]{1,0:T(8,128)(2,1)S(1)}, u32[]{:S(2)}, u32[]{:S(2)}) %collective-permute-start.6) | collective-permute-done | bytes 16416 | tf_op jit(solution)/shard_map/ppermute | solution.py:404
  25.2 4.9 %collective-permute-start.8 = (bf16[144,512]{1,0:T(8,128)(2,1)S(1)}, bf16[144,512]{1,0:T(8,128)(2,1)S(1)}, u32[]{:S(2)}, u32[]{:S(2)}) collective-permute-start(bf16[144,512]{1,0:T(8,128)(2,1)S(1)} %pad_maximum_fusion.latent_ref), channel_id=1, source_target_pairs={{4,8},{12,16},{20,24},{8,4},{16,12},{24,20},{5,9},{13,17},{21,25},... | collective-permute-start | bytes 442376 | tf_op jit(solution)/shard_map/ppermute | solution.py:409
  30.2 0.1 collective-permute-start.10
  30.3 1.8 %own_band.1 = (f32[2,96,256]{2,1,0:T(8,128)S(1)}, bf16[2,2,5,256,256]{4,3,2,1,0:T(8,128)(2,1)S(1)}, bf16[128,512]{1,0:T(8,128)(2,1)}) custom-call(bf16[128,512]{1,0:T(8,128)(2,1)S(1)} %get-tuple-element.43.state_ref, bf16[144,512]{1,0:T(8,128)(2,1)S(1)} %gather.1.own_ref, bf16[272,512]{1,0:T(8,128)(2,1)S(1)} %collective-permute-done.1.inner_ref, ...), custom_call_target="tpu_custom_call" | custom-call | flops 1000000000 | bytes 2500000 | tf_op jit(solution)/shard_map/own_band/pallas_call | solution.py:529
  32.1 0.9 %inner_band.1.partial_ref = f32[2,96,256]{2,1,0:T(8,128)S(1)} custom-call(bf16[144,512]{1,0:T(8,128)(2,1)S(1)} %pad_maximum_fusion.1.latent_ref, bf16[30,96,512]{2,1,0:T(8,128)(2,1)S(1)} %mix_edges.1.weights_ref, bf16[2,2,5,256,256]{4,3,2,1,0:T(8,128)(2,1)S(1)} %get-tuple-element.54.hot_ref, f32[2,96,256]{2,1,0:T(8,128)S(1)} %get-tuple-element.55.partial_ref), custom_call_target="tpu_custom_call" | custom-call | flops 1000000000 | bytes 2500000 | tf_op jit(solution)/shard_map/inner_band/pallas_call | solution.py:547
  33.0 1.6 %outer_band.1 = bf16[84,2,256]{2,1,0:T(2,128)(2,1)} custom-call(bf16[144,512]{1,0:T(8,128)(2,1)S(1)} %collective-permute-done.8.latent_ref, bf16[30,96,512]{2,1,0:T(8,128)(2,1)S(1)} %mix_edges.1.weights_ref, bf16[2,2,5,256,256]{4,3,2,1,0:T(8,128)(2,1)S(1)} %get-tuple-element.54.hot_ref, f32[2,96,256]{2,1,0:T(8,128)S(1)} %inner_band.1.partial_ref), custom_call_target="tpu_custom_call" | custom-call | flops 1000000000 | bytes 2500000 | tf_op jit(solution)/shard_map/outer_band/pallas_call | solution.py:557
  (25 shorter events, 0.1 us)
Async XLA Ops:
  0.6 14.6 %copy-start.3 = (f32[9,2,5,5]{0,1,3,2:T(2,128)S(1)}, f32[9,2,5,5]{0,1,3,2:T(2,128)}, u32[]{:S(2)}) copy-start(f32[9,2,5,5]{0,1,3,2:T(2,128)} %param.16) | copy-start | bytes 5404
  0.6 14.6 %copy-start = (bf16[9,512,84]{1,2,0:T(8,128)(2,1)S(1)}, bf16[9,512,84]{1,2,0:T(8,128)(2,1)}, u32[]{:S(2)}) copy-start(bf16[9,512,84]{1,2,0:T(8,128)(2,1)} %param.17) | copy-start | bytes 2322436
  0.6 6.3 %collective-permute-start = (bf16[128,512]{1,0:T(8,128)(2,1)}, bf16[128,512]{1,0:T(8,128)(2,1)S(1)}, u32[]{:S(2)}, u32[]{:S(2)}) collective-permute-start(bf16[128,512]{1,0:T(8,128)(2,1)} %bitcast.13), channel_id=1, source_target_pairs={{0,1},{2,3},{1,0},{3,2},{4,5},{6,7},{5,4},{7,6},{8,9},{10,11},{9,8... | collective-permute-start | bytes 393224 | tf_op jit(solution)/shard_map/ppermute | solution.py:404
  2.8 8.8 %collective-permute-start.2 = (bf16[128,512]{1,0:T(8,128)(2,1)}, bf16[128,512]{1,0:T(8,128)(2,1)S(1)}, u32[]{:S(2)}, u32[]{:S(2)}) collective-permute-start(bf16[128,512]{1,0:T(8,128)(2,1)} %bitcast.14), channel_id=1, source_target_pairs={{1,2},{3,0},{2,1},{0,3},{5,6},{7,4},{6,5},{4,7},{9,10},{11,8},{10,... | collective-permute-start | bytes 393224 | tf_op jit(solution)/shard_map/ppermute | solution.py:404
  7.0 9.3 %collective-permute-start.1 = (bf16[272,512]{1,0:T(8,128)(2,1)S(1)}, bf16[272,512]{1,0:T(8,128)(2,1)S(1)}, u32[]{:S(2)}, u32[]{:S(2)}) collective-permute-start(bf16[272,512]{1,0:T(8,128)(2,1)S(1)} %constant_dynamic-update-slice_fusion), channel_id=1, source_target_pairs={{0,4},{8,12},{16,20},{24,28},{4,0},{12,8},{20,16},{28,24},{1,5},{9... | collective-permute-start | bytes 835592 | tf_op jit(solution)/shard_map/ppermute | solution.py:409
  8.3 8.0 %collective-permute-start.3 = (bf16[272,512]{1,0:T(8,128)(2,1)S(1)}, bf16[272,512]{1,0:T(8,128)(2,1)S(1)}, u32[]{:S(2)}, u32[]{:S(2)}) collective-permute-start(bf16[272,512]{1,0:T(8,128)(2,1)S(1)} %constant_dynamic-update-slice_fusion), channel_id=1, source_target_pairs={{4,8},{12,16},{20,24},{8,4},{16,12},{24,20},{5,9},{13,17},{21,25},... | collective-permute-start | bytes 835592 | tf_op jit(solution)/shard_map/ppermute | solution.py:409
  11.5 4.8 %copy-start.4 = (f32[512]{0:T(512)S(1)}, f32[512]{0:T(512)}, u32[]{:S(2)}) copy-start(f32[512]{0:T(512)} %param.10) | copy-start | bytes 6148
  11.5 6.4 %collective-permute-start.4 = (bf16[128,512]{1,0:T(8,128)(2,1)S(1)}, bf16[128,512]{1,0:T(8,128)(2,1)S(1)}, u32[]{:S(2)}, u32[]{:S(2)}) collective-permute-start(bf16[128,512]{1,0:T(8,128)(2,1)S(1)} %collective-permute-done.2.other_ref), channel_id=1, source_target_pairs={{0,4},{8,12},{16,20},{24,28},{4,0},{12,8},{20,16},{28,24},{1,5},{9... | collective-permute-start | bytes 393224 | tf_op jit(solution)/shard_map/ppermute | solution.py:409
  11.6 6.3 %collective-permute-start.5 = (bf16[128,512]{1,0:T(8,128)(2,1)S(1)}, bf16[128,512]{1,0:T(8,128)(2,1)S(1)}, u32[]{:S(2)}, u32[]{:S(2)}) collective-permute-start(bf16[128,512]{1,0:T(8,128)(2,1)S(1)} %collective-permute-done.2.other_ref), channel_id=1, source_target_pairs={{4,8},{12,16},{20,24},{8,4},{16,12},{24,20},{5,9},{13,17},{21,25},... | collective-permute-start | bytes 393224 | tf_op jit(solution)/shard_map/ppermute | solution.py:409
  16.3 1.7 %copy-start.1 = (bf16[512,512]{1,0:T(8,128)(2,1)S(1)}, bf16[512,512]{1,0:T(8,128)(2,1)}, u32[]{:S(2)}) copy-start(bf16[512,512]{1,0:T(8,128)(2,1)} %wout_ref.1) | copy-start | bytes 1572868
  16.3 1.7 %copy-start.2 = (bf16[512,512]{1,0:T(8,128)(2,1)S(1)}, bf16[512,512]{1,0:T(8,128)(2,1)}, u32[]{:S(2)}) copy-start(bf16[512,512]{1,0:T(8,128)(2,1)} %wlat_ref.1) | copy-start | bytes 1572868
  19.9 5.3 %collective-permute-start.7 = (bf16[16,512]{1,0:T(8,128)(2,1)S(1)}, bf16[16,512]{1,0:T(8,128)(2,1)S(1)}, u32[]{:S(2)}, u32[]{:S(2)}) collective-permute-start(bf16[16,512]{1,0:T(8,128)(2,1)S(1)} %get-tuple-element.50), channel_id=1, source_target_pairs={{1,2},{3,0},{2,1},{0,3},{5,6},{7,4},{6,5},{4,7},{9,10},{11,8},{10,... | collective-permute-start | bytes 49160 | tf_op jit(solution)/shard_map/ppermute | solution.py:404
  22.6 2.6 %collective-permute-start.6 = (bf16[16,512]{1,0:T(8,128)(2,1)S(1)}, bf16[16,512]{1,0:T(8,128)(2,1)S(1)}, u32[]{:S(2)}, u32[]{:S(2)}) collective-permute-start(bf16[16,512]{1,0:T(8,128)(2,1)S(1)} %get-tuple-element.46), channel_id=1, source_target_pairs={{0,1},{2,3},{1,0},{3,2},{4,5},{6,7},{5,4},{7,6},{8,9},{10,11},{9,8... | collective-permute-start | bytes 49160 | tf_op jit(solution)/shard_map/ppermute | solution.py:404
  22.9 9.2 %collective-permute-start.9 = (bf16[64,512]{1,0:T(8,128)(2,1)S(1)}, bf16[64,512]{1,0:T(8,128)(2,1)S(1)}, u32[]{:S(2)}, u32[]{:S(2)}) collective-permute-start(bf16[64,512]{1,0:T(8,128)(2,1)S(1)} %slice.14), channel_id=1, source_target_pairs={{0,4},{8,12},{16,20},{24,28},{4,0},{12,8},{20,16},{28,24},{1,5},{9... | collective-permute-start | bytes 196616 | tf_op jit(solution)/shard_map/ppermute | solution.py:409
  25.2 7.8 %collective-permute-start.8 = (bf16[144,512]{1,0:T(8,128)(2,1)S(1)}, bf16[144,512]{1,0:T(8,128)(2,1)S(1)}, u32[]{:S(2)}, u32[]{:S(2)}) collective-permute-start(bf16[144,512]{1,0:T(8,128)(2,1)S(1)} %pad_maximum_fusion.latent_ref), channel_id=1, source_target_pairs={{4,8},{12,16},{20,24},{8,4},{16,12},{24,20},{5,9},{13,17},{21,25},... | collective-permute-start | bytes 442376 | tf_op jit(solution)/shard_map/ppermute | solution.py:409
  30.2 1.9 %collective-permute-start.10 = (bf16[80,512]{1,0:T(8,128)(2,1)S(1)}, bf16[80,512]{1,0:T(8,128)(2,1)S(1)}, u32[]{:S(2)}, u32[]{:S(2)}) collective-permute-start(bf16[80,512]{1,0:T(8,128)(2,1)S(1)} %slice.17), channel_id=1, source_target_pairs={{0,4},{8,12},{16,20},{24,28},{4,0},{12,8},{20,16},{28,24},{1,5},{9... | collective-permute-start | bytes 245768 | tf_op jit(solution)/shard_map/ppermute | solution.py:409

commit v20 on v16

--- a/solution.py
+++ b/solution.py
@@ -179,7 +179,7 @@
 def project(nodes, gain, wk_ref, wvt_ref):
     normed = normalise(nodes, gain)
     keys = jnp.dot(normed, wk_ref[...], preferred_element_type=F32).astype(BF16)
-    values = lax.dot_general(wvt_ref[...], normed, NT, preferred_element_type=F32).astype(BF16)
+    values = jnp.dot(wvt_ref[...], normed.T, preferred_element_type=F32).astype(BF16)
     return keys, values
 
 
@@ -298,8 +298,8 @@
 
 def shares_of(latent, weights):
     blocks, outputs, channels = weights.shape
-    shares = lax.dot_general(
-        weights.reshape(blocks * outputs, channels), latent, NT, preferred_element_type=F32
+    shares = jnp.dot(
+        weights.reshape(blocks * outputs, channels), latent.T, preferred_element_type=F32
     ).astype(BF16)
     return [shares[at * outputs : (at + 1) * outputs] for at in range(blocks)]
 

time: 34.4 us -> 34.4 us (level)
  no operation moved by 1% of the time
where the time goes in v20:
time: 34.4 us; the launch traced here: 34.2 us
  starting transfers between devices  18.6 us (54%)
  Pallas kernels  12.7 us (37%)
  waiting for transfers between devices  2.03 us (6%)
  between operations  0.82 us (2%)
    ppermute x6, starting transfers between devices, exchanged(): return lax.ppermute(array, 'reg', pairs + [(j, i) for i, j in pairs])  12.3 us
    ppermute x4, starting transfers between devices, paired(): return lax.ppermute(array, 'lon', pairs + [(j, i) for i, j in pairs])  6.35 us
    pallas_call x1, Pallas kernels, shards(): pl.pallas_call(functools.partial(prepare_kernel, sectors), in_specs=[whol...  2.02 us
    pallas_call x1, Pallas kernels, shards(): pl.pallas_call(late_kernel, in_specs=[whole()] * 15, out_specs=[whole()]...  1.95 us
    pallas_call x2, Pallas kernels, mixed(): pl.pallas_call(functools.partial(mix_kernel, blocks), in_specs=[whole()]...  1.82 us
    pallas_call x1, Pallas kernels, shards(): pl.pallas_call(functools.partial(own_kernel, (rows, 2 * rows, 2 * rows)),...  1.8 us
    pallas_call x1, Pallas kernels, shards(): pl.pallas_call(early_kernel, in_specs=[whole()] * 11, out_specs=[whole()]...  1.6 us
    pallas_call x1, Pallas kernels, shards(): pl.pallas_call(functools.partial(band_kernel, False), in_specs=[whole()]...  1.6 us
  transfers between devices with their start and end apart: 10, of which 4 were waited for; matrix products, arithmetic and copies ran while one was open for 0% of the time, Pallas kernels for 27%

profile of v20, /device:TPU:1, one launch (start us, length us, event | category | flops | bytes accessed | tf_op | source)
XLA Modules:
  0.0 34.2 jit_solution(8162678113205017902)
XLA Ops:
  0.6 2.1 %collective-permute-start = (bf16[128,512]{1,0:T(8,128)(2,1)}, bf16[128,512]{1,0:T(8,128)(2,1)S(1)}, u32[]{:S(2)}, u32[]{:S(2)}) collective-permute-start(bf16[128,512]{1,0:T(8,128)(2,1)} %bitcast.13), channel_id=1, source_target_pairs={{0,1},{2,3},{1,0},{3,2},{4,5},{6,7},{5,4},{7,6},{8,9},{10,11},{9,8... | collective-permute-start | bytes 393224 | tf_op jit(solution)/shard_map/ppermute | solution.py:404
  2.8 1.2 %collective-permute-start.2 = (bf16[128,512]{1,0:T(8,128)(2,1)}, bf16[128,512]{1,0:T(8,128)(2,1)S(1)}, u32[]{:S(2)}, u32[]{:S(2)}) collective-permute-start(bf16[128,512]{1,0:T(8,128)(2,1)} %bitcast.14), channel_id=1, source_target_pairs={{1,2},{3,0},{2,1},{0,3},{5,6},{7,4},{6,5},{4,7},{9,10},{11,8},{10,... | collective-permute-start | bytes 393224 | tf_op jit(solution)/shard_map/ppermute | solution.py:404
  4.0 1.0 %gather.1.own_ref = bf16[144,512]{1,0:T(8,128)(2,1)S(1)} custom-call(bf16[128,512]{1,0:T(8,128)(2,1)} %bitcast.15, s32[2,256]{1,0:T(2,128)} %assign_hbm.3), custom_call_target="tpu_custom_call" | custom-call | flops 1000 | bytes 1000 | tf_op jit(solution)/shard_map/gather/pallas_call | solution.py:440
  4.9 2.0 %prepare.1 = (bf16[4,128,512]{2,1,0:T(8,128)(2,1)S(1)}, bf16[128,512]{1,0:T(8,128)(2,1)S(1)}, bf16[512,128]{1,0:T(8,128)(2,1)S(1)}, bf16[512,512]{1,0:T(8,128)(2...) custom-call(bf16[144,512]{1,0:T(8,128)(2,1)S(1)} %gather.1.own_ref, ...), custom_call_target="tpu_custom_call" | custom-call | flops 500000000 | bytes 1000000 | tf_op jit(solution)/shard_map/prepare/pallas_call | solution.py:453
  7.0 1.3 %collective-permute-start.1 = (bf16[272,512]{1,0:T(8,128)(2,1)S(1)}, bf16[272,512]{1,0:T(8,128)(2,1)S(1)}, u32[]{:S(2)}, u32[]{:S(2)}) collective-permute-start(bf16[272,512]{1,0:T(8,128)(2,1)S(1)} %constant_dynamic-update-slice_fusion), channel_id=1, source_target_pairs={{0,4},{8,12},{16,20},{24,28},{4,0},{12,8},{20,16},{28,24},{1,5},{9... | collective-permute-start | bytes 835592 | tf_op jit(solution)/shard_map/ppermute | solution.py:409
  8.3 3.2 %collective-permute-start.3 = (bf16[272,512]{1,0:T(8,128)(2,1)S(1)}, bf16[272,512]{1,0:T(8,128)(2,1)S(1)}, u32[]{:S(2)}, u32[]{:S(2)}) collective-permute-start(bf16[272,512]{1,0:T(8,128)(2,1)S(1)} %constant_dynamic-update-slice_fusion), channel_id=1, source_target_pairs={{4,8},{12,16},{20,24},{8,4},{16,12},{24,20},{5,9},{13,17},{21,25},... | collective-permute-start | bytes 835592 | tf_op jit(solution)/shard_map/ppermute | solution.py:409
  11.5 0.0 copy-start.4
  11.5 3.1 %collective-permute-start.5 = (bf16[128,512]{1,0:T(8,128)(2,1)S(1)}, bf16[128,512]{1,0:T(8,128)(2,1)S(1)}, u32[]{:S(2)}, u32[]{:S(2)}) collective-permute-start(bf16[128,512]{1,0:T(8,128)(2,1)S(1)} %collective-permute-done.2.other_ref), channel_id=1, source_target_pairs={{4,8},{12,16},{20,24},{8,4},{16,12},{24,20},{5,9},{13,17},{21,25},... | collective-permute-start | bytes 393224 | tf_op jit(solution)/shard_map/ppermute | solution.py:409
  14.7 0.1 collective-permute-start.4
  14.8 1.0 %mix_edges.1.weights_ref = bf16[30,96,512]{2,1,0:T(8,128)(2,1)S(1)} custom-call(f32[5,5,2,9]{3,2,1,0:T(2,128)S(1)} %bitcast.8, bf16[9,84,512]{2,1,0:T(8,128)(2,1)S(1)} %bitcast.6), custom_call_target="tpu_custom_call" | custom-call | flops 2000000000 | bytes 6000000 | tf_op jit(solution)/shard_map/mix_edges/pallas_call | solution.py:425
  15.8 0.3 %collective-permute-done.3.outer_ref = bf16[272,512]{1,0:T(8,128)(2,1)S(1)} collective-permute-done((bf16[272,512]{1,0:T(8,128)(2,1)S(1)}, bf16[272,512]{1,0:T(8,128)(2,1)S(1)}, u32[]{:S(2)}, u32[]{:S(2)}) %collective-permute-start.3) | collective-permute-done | bytes 278560 | tf_op jit(solution)/shard_map/ppermute | solution.py:409
  16.2 1.6 %early.1 = (f32[4,2,8,512]{3,2,1,0:T(8,128)S(1)}, f32[4,128,128]{2,1,0:T(8,128)S(1)}) custom-call(bf16[4,5,16,128]{3,2,1,0:T(8,128)(2,1)S(1)} %get-tuple-element.29.choice_ref, bf16[128,512]{1,0:T(8,128)(2,1)S(1)} %collective-permute-done.2.other_ref, bf16[128,512]{1,0:T(8,128)(2,1)S(1)} %collective-permute-done.pair_ref, ...), custom_call_target="tpu_custom_call" | custom-call | flops 3000000000 | bytes 6000000 | tf_op jit(solution)/shard_map/early/pallas_call | solution.py:488
  17.8 0.1 collective-permute-done.5.corner_ref
  17.8 2.0 %late.1 = (bf16[128,512]{1,0:T(8,128)(2,1)S(1)}, bf16[128,512]{1,0:T(8,128)(2,1)S(1)}, bf16[16,512]{1,0:T(8,128)(2,1)S(1)}, bf16[16,512]{1,0:T(8,128)(2,1)S(1)}) custom-call(bf16[4,5,16,128]{3,2,1,0:T(8,128)(2,1)S(1)} %get-tuple-element.29.choice_ref, bf16[32,128]{1,0:T(8,128)(2,1)S(1)} %get-tuple-element.30.cells_ref, ...), custom_call_target="tpu_custom_call" | custom-call | flops 3000000000 | bytes 6000000 | tf_op jit(solution)/shard_map/late/pallas_call | solution.py:504
  19.8 1.8 %collective-permute-start.6 = (bf16[16,512]{1,0:T(8,128)(2,1)S(1)}, bf16[16,512]{1,0:T(8,128)(2,1)S(1)}, u32[]{:S(2)}, u32[]{:S(2)}) collective-permute-start(bf16[16,512]{1,0:T(8,128)(2,1)S(1)} %get-tuple-element.46), channel_id=1, source_target_pairs={{0,1},{2,3},{1,0},{3,2},{4,5},{6,7},{5,4},{7,6},{8,9},{10,11},{9,8... | collective-permute-start | bytes 49160 | tf_op jit(solution)/shard_map/ppermute | solution.py:404
  21.6 1.2 %collective-permute-start.7 = (bf16[16,512]{1,0:T(8,128)(2,1)S(1)}, bf16[16,512]{1,0:T(8,128)(2,1)S(1)}, u32[]{:S(2)}, u32[]{:S(2)}) collective-permute-start(bf16[16,512]{1,0:T(8,128)(2,1)S(1)} %get-tuple-element.50), channel_id=1, source_target_pairs={{1,2},{3,0},{2,1},{0,3},{5,6},{7,4},{6,5},{4,7},{9,10},{11,8},{10,... | collective-permute-start | bytes 49160 | tf_op jit(solution)/shard_map/ppermute | solution.py:404
  22.8 0.8 %mix_own.1.weights_ref = bf16[20,96,512]{2,1,0:T(8,128)(2,1)S(1)} custom-call(f32[5,5,2,9]{3,2,1,0:T(2,128)S(1)} %bitcast.9, bf16[9,84,512]{2,1,0:T(8,128)(2,1)S(1)} %bitcast.7), custom_call_target="tpu_custom_call" | custom-call | flops 2000000000 | bytes 6000000 | tf_op jit(solution)/shard_map/mix_own/pallas_call | solution.py:425
  23.6 1.5 %collective-permute-done.7 = bf16[16,512]{1,0:T(8,128)(2,1)S(1)} collective-permute-done((bf16[16,512]{1,0:T(8,128)(2,1)S(1)}, bf16[16,512]{1,0:T(8,128)(2,1)S(1)}, u32[]{:S(2)}, u32[]{:S(2)}) %collective-permute-start.7) | collective-permute-done | bytes 16416 | tf_op jit(solution)/shard_map/ppermute | solution.py:404
  25.1 1.1 %collective-permute-start.9 = (bf16[144,512]{1,0:T(8,128)(2,1)S(1)}, bf16[144,512]{1,0:T(8,128)(2,1)S(1)}, u32[]{:S(2)}, u32[]{:S(2)}) collective-permute-start(bf16[144,512]{1,0:T(8,128)(2,1)S(1)} %pad_maximum_fusion.latent_ref), channel_id=1, source_target_pairs={{0,4},{8,12},{16,20},{24,28},{4,0},{12,8},{20,16},{28,24},{1,5},{9... | collective-permute-start | bytes 442376 | tf_op jit(solution)/shard_map/ppermute | solution.py:409
  26.2 3.6 %collective-permute-start.8 = (bf16[144,512]{1,0:T(8,128)(2,1)S(1)}, bf16[144,512]{1,0:T(8,128)(2,1)S(1)}, u32[]{:S(2)}, u32[]{:S(2)}) collective-permute-start(bf16[144,512]{1,0:T(8,128)(2,1)S(1)} %pad_maximum_fusion.latent_ref), channel_id=1, source_target_pairs={{4,8},{12,16},{20,24},{8,4},{16,12},{24,20},{5,9},{13,17},{21,25},... | collective-permute-start | bytes 442376 | tf_op jit(solution)/shard_map/ppermute | solution.py:409
  29.7 1.8 %own_band.1 = (f32[2,96,256]{2,1,0:T(8,128)S(1)}, bf16[2,2,5,256,256]{4,3,2,1,0:T(8,128)(2,1)S(1)}, bf16[128,512]{1,0:T(8,128)(2,1)}) custom-call(bf16[128,512]{1,0:T(8,128)(2,1)S(1)} %get-tuple-element.43.state_ref, bf16[144,512]{1,0:T(8,128)(2,1)S(1)} %gather.1.own_ref, bf16[272,512]{1,0:T(8,128)(2,1)S(1)} %collective-permute-done.1.inner_ref, ...), custom_call_target="tpu_custom_call" | custom-call | flops 1000000000 | bytes 2500000 | tf_op jit(solution)/shard_map/own_band/pallas_call | solution.py:527
  31.5 0.9 %inner_band.1.partial_ref = f32[2,96,256]{2,1,0:T(8,128)S(1)} custom-call(bf16[144,512]{1,0:T(8,128)(2,1)S(1)} %collective-permute-done.9.latent_ref, bf16[30,96,512]{2,1,0:T(8,128)(2,1)S(1)} %mix_edges.1.weights_ref, bf16[2,2,5,256,256]{4,3,2,1,0:T(8,128)(2,1)S(1)} %get-tuple-element.54.hot_ref, f32[2,96,256]{2,1,0:T(8,128)S(1)} %get-tuple-element.55.partial_ref), custom_call_target="tpu_custom_call" | custom-call | flops 1000000000 | bytes 2500000 | tf_op jit(solution)/shard_map/inner_band/pallas_call | solution.py:545
  32.5 0.1 collective-permute-done.8.latent_ref
  32.6 1.6 %outer_band.1 = bf16[84,2,256]{2,1,0:T(2,128)(2,1)} custom-call(bf16[144,512]{1,0:T(8,128)(2,1)S(1)} %collective-permute-done.8.latent_ref, bf16[30,96,512]{2,1,0:T(8,128)(2,1)S(1)} %mix_edges.1.weights_ref, bf16[2,2,5,256,256]{4,3,2,1,0:T(8,128)(2,1)S(1)} %get-tuple-element.54.hot_ref, f32[2,96,256]{2,1,0:T(8,128)S(1)} %inner_band.1.partial_ref), custom_call_target="tpu_custom_call" | custom-call | flops 1000000000 | bytes 2500000 | tf_op jit(solution)/shard_map/outer_band/pallas_call | solution.py:555
  (20 shorter events, 0.1 us)
Async XLA Ops:
  0.6 14.1 %copy-start = (bf16[9,512,84]{1,2,0:T(8,128)(2,1)S(1)}, bf16[9,512,84]{1,2,0:T(8,128)(2,1)}, u32[]{:S(2)}) copy-start(bf16[9,512,84]{1,2,0:T(8,128)(2,1)} %param.17) | copy-start | bytes 2322436
  0.6 14.1 %copy-start.3 = (f32[9,2,5,5]{0,1,3,2:T(2,128)S(1)}, f32[9,2,5,5]{0,1,3,2:T(2,128)}, u32[]{:S(2)}) copy-start(f32[9,2,5,5]{0,1,3,2:T(2,128)} %param.16) | copy-start | bytes 5404
  0.6 6.3 %collective-permute-start = (bf16[128,512]{1,0:T(8,128)(2,1)}, bf16[128,512]{1,0:T(8,128)(2,1)S(1)}, u32[]{:S(2)}, u32[]{:S(2)}) collective-permute-start(bf16[128,512]{1,0:T(8,128)(2,1)} %bitcast.13), channel_id=1, source_target_pairs={{0,1},{2,3},{1,0},{3,2},{4,5},{6,7},{5,4},{7,6},{8,9},{10,11},{9,8... | collective-permute-start | bytes 393224 | tf_op jit(solution)/shard_map/ppermute | solution.py:404
  2.8 8.8 %collective-permute-start.2 = (bf16[128,512]{1,0:T(8,128)(2,1)}, bf16[128,512]{1,0:T(8,128)(2,1)S(1)}, u32[]{:S(2)}, u32[]{:S(2)}) collective-permute-start(bf16[128,512]{1,0:T(8,128)(2,1)} %bitcast.14), channel_id=1, source_target_pairs={{1,2},{3,0},{2,1},{0,3},{5,6},{7,4},{6,5},{4,7},{9,10},{11,8},{10,... | collective-permute-start | bytes 393224 | tf_op jit(solution)/shard_map/ppermute | solution.py:404
  7.0 8.8 %collective-permute-start.1 = (bf16[272,512]{1,0:T(8,128)(2,1)S(1)}, bf16[272,512]{1,0:T(8,128)(2,1)S(1)}, u32[]{:S(2)}, u32[]{:S(2)}) collective-permute-start(bf16[272,512]{1,0:T(8,128)(2,1)S(1)} %constant_dynamic-update-slice_fusion), channel_id=1, source_target_pairs={{0,4},{8,12},{16,20},{24,28},{4,0},{12,8},{20,16},{28,24},{1,5},{9... | collective-permute-start | bytes 835592 | tf_op jit(solution)/shard_map/ppermute | solution.py:409
  8.3 7.9 %collective-permute-start.3 = (bf16[272,512]{1,0:T(8,128)(2,1)S(1)}, bf16[272,512]{1,0:T(8,128)(2,1)S(1)}, u32[]{:S(2)}, u32[]{:S(2)}) collective-permute-start(bf16[272,512]{1,0:T(8,128)(2,1)S(1)} %constant_dynamic-update-slice_fusion), channel_id=1, source_target_pairs={{4,8},{12,16},{20,24},{8,4},{16,12},{24,20},{5,9},{13,17},{21,25},... | collective-permute-start | bytes 835592 | tf_op jit(solution)/shard_map/ppermute | solution.py:409
  11.5 4.6 %copy-start.4 = (f32[512]{0:T(512)S(1)}, f32[512]{0:T(512)}, u32[]{:S(2)}) copy-start(f32[512]{0:T(512)} %param.10) | copy-start | bytes 6148
  11.5 6.3 %collective-permute-start.5 = (bf16[128,512]{1,0:T(8,128)(2,1)S(1)}, bf16[128,512]{1,0:T(8,128)(2,1)S(1)}, u32[]{:S(2)}, u32[]{:S(2)}) collective-permute-start(bf16[128,512]{1,0:T(8,128)(2,1)S(1)} %collective-permute-done.2.other_ref), channel_id=1, source_target_pairs={{4,8},{12,16},{20,24},{8,4},{16,12},{24,20},{5,9},{13,17},{21,25},... | collective-permute-start | bytes 393224 | tf_op jit(solution)/shard_map/ppermute | solution.py:409
  14.7 3.2 %collective-permute-start.4 = (bf16[128,512]{1,0:T(8,128)(2,1)S(1)}, bf16[128,512]{1,0:T(8,128)(2,1)S(1)}, u32[]{:S(2)}, u32[]{:S(2)}) collective-permute-start(bf16[128,512]{1,0:T(8,128)(2,1)S(1)} %collective-permute-done.2.other_ref), channel_id=1, source_target_pairs={{0,4},{8,12},{16,20},{24,28},{4,0},{12,8},{20,16},{28,24},{1,5},{9... | collective-permute-start | bytes 393224 | tf_op jit(solution)/shard_map/ppermute | solution.py:409
  16.2 1.7 %copy-start.1 = (bf16[512,512]{1,0:T(8,128)(2,1)S(1)}, bf16[512,512]{1,0:T(8,128)(2,1)}, u32[]{:S(2)}) copy-start(bf16[512,512]{1,0:T(8,128)(2,1)} %wout_ref.1) | copy-start | bytes 1572868
  16.2 1.7 %copy-start.2 = (bf16[512,512]{1,0:T(8,128)(2,1)S(1)}, bf16[512,512]{1,0:T(8,128)(2,1)}, u32[]{:S(2)}) copy-start(bf16[512,512]{1,0:T(8,128)(2,1)} %wlat_ref.1) | copy-start | bytes 1572868
  19.8 3.8 %collective-permute-start.6 = (bf16[16,512]{1,0:T(8,128)(2,1)S(1)}, bf16[16,512]{1,0:T(8,128)(2,1)S(1)}, u32[]{:S(2)}, u32[]{:S(2)}) collective-permute-start(bf16[16,512]{1,0:T(8,128)(2,1)S(1)} %get-tuple-element.46), channel_id=1, source_target_pairs={{0,1},{2,3},{1,0},{3,2},{4,5},{6,7},{5,4},{7,6},{8,9},{10,11},{9,8... | collective-permute-start | bytes 49160 | tf_op jit(solution)/shard_map/ppermute | solution.py:404
  21.6 3.5 %collective-permute-start.7 = (bf16[16,512]{1,0:T(8,128)(2,1)S(1)}, bf16[16,512]{1,0:T(8,128)(2,1)S(1)}, u32[]{:S(2)}, u32[]{:S(2)}) collective-permute-start(bf16[16,512]{1,0:T(8,128)(2,1)S(1)} %get-tuple-element.50), channel_id=1, source_target_pairs={{1,2},{3,0},{2,1},{0,3},{5,6},{7,4},{6,5},{4,7},{9,10},{11,8},{10,... | collective-permute-start | bytes 49160 | tf_op jit(solution)/shard_map/ppermute | solution.py:404
  25.1 6.4 %collective-permute-start.9 = (bf16[144,512]{1,0:T(8,128)(2,1)S(1)}, bf16[144,512]{1,0:T(8,128)(2,1)S(1)}, u32[]{:S(2)}, u32[]{:S(2)}) collective-permute-start(bf16[144,512]{1,0:T(8,128)(2,1)S(1)} %pad_maximum_fusion.latent_ref), channel_id=1, source_target_pairs={{0,4},{8,12},{16,20},{24,28},{4,0},{12,8},{20,16},{28,24},{1,5},{9... | collective-permute-start | bytes 442376 | tf_op jit(solution)/shard_map/ppermute | solution.py:409
  26.2 6.5 %collective-permute-start.8 = (bf16[144,512]{1,0:T(8,128)(2,1)S(1)}, bf16[144,512]{1,0:T(8,128)(2,1)S(1)}, u32[]{:S(2)}, u32[]{:S(2)}) collective-permute-start(bf16[144,512]{1,0:T(8,128)(2,1)S(1)} %pad_maximum_fusion.latent_ref), channel_id=1, source_target_pairs={{4,8},{12,16},{20,24},{8,4},{16,12},{24,20},{5,9},{13,17},{21,25},... | collective-permute-start | bytes 442376 | tf_op jit(solution)/shard_map/ppermute | solution.py:409

commit v21 on v16

--- a/solution.py
+++ b/solution.py
@@ -110,7 +110,7 @@
 def prepare_kernel(
     sectors,
     own_ref, gain_hbm, wqkv_hbm, assign_hbm, listed_hbm,
-    query_ref, key_ref, value_ref, wk_ref, wvt_ref, choice_ref, cells_ref,
+    query_ref, key_ref, value_ref, wk_ref, wvt_ref, choice_ref, cells_ref, wide_ref,
     gain_ref, wqkv_ref, cell_ref, listed_ref, sems,
 ):
     copies = [
@@ -144,7 +144,9 @@
             for col in range(REACH):
                 cell = cell_ref[row, first + col] % rows
                 hit = jnp.where((place == row * REACH + col) & (node == cell), 1.0, hit)
-        cells_ref[side * ROWS : (side + 1) * ROWS] = hit.astype(BF16)
+        cells_ref[rows + side * ROWS : rows + (side + 1) * ROWS] = hit.astype(BF16)
+    cells_ref[:rows] = (iota((rows, rows), 0) == iota((rows, rows), 1)).astype(F32).astype(BF16)
+    wide_ref[...] = jnp.dot(cells_ref[...], own_ref[:rows], preferred_element_type=F32).astype(BF16)
     copies[0].wait()
     normed = normalise(own_ref[:rows], gain_ref[...])
     copies[1].wait()
@@ -228,7 +230,7 @@
 
 def late_kernel(
     choice_ref, cells_ref, inner_ref, outer_ref, beside_ref, corner_ref,
-    own_ref, gain_ref, wk_ref, wvt_ref, query_ref, top_ref, sum_ref, wout_ref, wlat_ref,
+    wide_ref, gain_ref, wk_ref, wvt_ref, query_ref, top_ref, sum_ref, wout_ref, wlat_ref,
     state_ref, latent_ref, to_pair_ref, to_other_ref,
 ):
     rows, width = state_ref.shape
@@ -265,19 +267,19 @@
             span = slice(member * rows, (member + 1) * rows)
             earlier = sum_ref[part, member * head : (member + 1) * head]
             merged.append((piece + earlier * shrink[:, span]) * share[:, span])
-        attended.append(jnp.concatenate(merged, axis=0).T.astype(BF16))
+        merged = jnp.concatenate(merged, axis=0).astype(BF16)
+        turned = lax.dot_general(cells_ref[...], merged, NT, preferred_element_type=F32)
+        attended.append(turned.astype(BF16))
     attended = jnp.concatenate(attended, axis=1)
     state = (
-        own_ref[:rows].astype(F32)
-        + jnp.dot(attended, wout_ref[...], preferred_element_type=F32)
+        wide_ref[...].astype(F32) + jnp.dot(attended, wout_ref[...], preferred_element_type=F32)
     ).astype(BF16)
-    state_ref[...] = state
+    state_ref[...] = state[:rows]
     value = jnp.dot(state, wlat_ref[...], preferred_element_type=F32)
     latent = (value / (1.0 + jnp.exp(-value))).astype(BF16)
-    latent_ref[...] = latent
-    cells = jnp.dot(cells_ref[...], latent, preferred_element_type=F32).astype(BF16)
-    to_pair_ref[...] = cells[:ROWS]
-    to_other_ref[...] = cells[ROWS:]
+    latent_ref[...] = latent[:rows]
+    to_pair_ref[...] = latent[rows : rows + ROWS]
+    to_other_ref[...] = latent[rows + ROWS :]
 
 
 def hot_rows(values, rows, cols, line):
@@ -450,10 +452,10 @@
         cost_estimate=cost(1e3, 1e3),
         name="gather",
     )(*in_hbm(x, assignment))
-    query, key, value, wk, wvt, choice, cells = pl.pallas_call(
+    query, key, value, wk, wvt, choice, cells, wide = pl.pallas_call(
         functools.partial(prepare_kernel, sectors),
         in_specs=[whole()] + [whole(pltpu.HBM)] * 4,
-        out_specs=[whole()] * 7,
+        out_specs=[whole()] * 8,
         out_shape=[
             struct(parts, LANES, members * rows),
             struct(rows, width),
@@ -461,7 +463,8 @@
             struct(width, width),
             struct(width, width),
             struct(count - 1, CANDIDATES, ROWS, LANES),
-            struct(2 * ROWS, rows),
+            struct(rows + 2 * ROWS, rows),
+            struct(rows + 2 * ROWS, width),
         ],
         scratch_shapes=[
             pltpu.VMEM((1, width), F32),
@@ -512,7 +515,7 @@
         name="late",
     )(
         choice, cells, inner, outer, beside, corner,
-        own, gain, wk, wvt, query, top, summed, w_out, w_latent,
+        wide, gain, wk, wvt, query, top, summed, w_out, w_latent,
     )
 
     from_pair = paired(to_pair, 0)

time: 34.4 us -> 34.5 us (level)
  no operation moved by 1% of the time
where the time goes in v21:
time: 34.5 us; the launch traced here: 34.3 us
  starting transfers between devices  18.7 us (54%)
  Pallas kernels  12.6 us (37%)
  waiting for transfers between devices  2.04 us (6%)
  between operations  0.83 us (2%)
    ppermute x6, starting transfers between devices, exchanged(): return lax.ppermute(array, 'reg', pairs + [(j, i) for i, j in pairs])  12.3 us
    ppermute x4, starting transfers between devices, paired(): return lax.ppermute(array, 'lon', pairs + [(j, i) for i, j in pairs])  6.38 us
    pallas_call x1, Pallas kernels, shards(): pl.pallas_call(functools.partial(prepare_kernel, sectors), in_specs=[whol...  2.02 us
    pallas_call x1, Pallas kernels, shards(): pl.pallas_call(late_kernel, in_specs=[whole()] * 15, out_specs=[whole()]...  1.94 us
    pallas_call x2, Pallas kernels, mixed(): pl.pallas_call(functools.partial(mix_kernel, blocks), in_specs=[whole()]...  1.82 us
    pallas_call x1, Pallas kernels, shards(): pl.pallas_call(functools.partial(own_kernel, (rows, 2 * rows, 2 * rows)),...  1.8 us
    pallas_call x1, Pallas kernels, shards(): pl.pallas_call(functools.partial(band_kernel, False), in_specs=[whole()]...  1.6 us
    pallas_call x1, Pallas kernels, shards(): pl.pallas_call(early_kernel, in_specs=[whole()] * 11, out_specs=[whole()]...  1.59 us
  transfers between devices with their start and end apart: 10, of which 4 were waited for; matrix products, arithmetic and copies ran while one was open for 0% of the time, Pallas kernels for 27%

profile of v21, /device:TPU:1, one launch (start us, length us, event | category | flops | bytes accessed | tf_op | source)
XLA Modules:
  0.0 34.3 jit_solution(12492838221747260274)
XLA Ops:
  0.6 2.1 %collective-permute-start = (bf16[128,512]{1,0:T(8,128)(2,1)}, bf16[128,512]{1,0:T(8,128)(2,1)S(1)}, u32[]{:S(2)}, u32[]{:S(2)}) collective-permute-start(bf16[128,512]{1,0:T(8,128)(2,1)} %bitcast.13), channel_id=1, source_target_pairs={{0,1},{2,3},{1,0},{3,2},{4,5},{6,7},{5,4},{7,6},{8,9},{10,11},{9,8... | collective-permute-start | bytes 393224 | tf_op jit(solution)/shard_map/ppermute | solution.py:406
  2.8 1.2 %collective-permute-start.2 = (bf16[128,512]{1,0:T(8,128)(2,1)}, bf16[128,512]{1,0:T(8,128)(2,1)S(1)}, u32[]{:S(2)}, u32[]{:S(2)}) collective-permute-start(bf16[128,512]{1,0:T(8,128)(2,1)} %bitcast.14), channel_id=1, source_target_pairs={{1,2},{3,0},{2,1},{0,3},{5,6},{7,4},{6,5},{4,7},{9,10},{11,8},{10,... | collective-permute-start | bytes 393224 | tf_op jit(solution)/shard_map/ppermute | solution.py:406
  4.0 1.0 %gather.1.own_ref = bf16[144,512]{1,0:T(8,128)(2,1)S(1)} custom-call(bf16[128,512]{1,0:T(8,128)(2,1)} %bitcast.15, s32[2,256]{1,0:T(2,128)} %assign_hbm.3), custom_call_target="tpu_custom_call" | custom-call | flops 1000 | bytes 1000 | tf_op jit(solution)/shard_map/gather/pallas_call | solution.py:442
  4.9 2.0 %prepare.1 = (bf16[4,128,512]{2,1,0:T(8,128)(2,1)S(1)}, bf16[128,512]{1,0:T(8,128)(2,1)S(1)}, bf16[512,128]{1,0:T(8,128)(2,1)S(1)}, bf16[512,512]{1,0:T(8,128)(2...) custom-call(bf16[144,512]{1,0:T(8,128)(2,1)S(1)} %gather.1.own_ref, ...), custom_call_target="tpu_custom_call" | custom-call | flops 500000000 | bytes 1000000 | tf_op jit(solution)/shard_map/prepare/pallas_call | solution.py:455
  7.0 1.3 %collective-permute-start.1 = (bf16[272,512]{1,0:T(8,128)(2,1)S(1)}, bf16[272,512]{1,0:T(8,128)(2,1)S(1)}, u32[]{:S(2)}, u32[]{:S(2)}) collective-permute-start(bf16[272,512]{1,0:T(8,128)(2,1)S(1)} %constant_dynamic-update-slice_fusion), channel_id=1, source_target_pairs={{0,4},{8,12},{16,20},{24,28},{4,0},{12,8},{20,16},{28,24},{1,5},{9... | collective-permute-start | bytes 835592 | tf_op jit(solution)/shard_map/ppermute | solution.py:411
  8.3 3.2 %collective-permute-start.3 = (bf16[272,512]{1,0:T(8,128)(2,1)S(1)}, bf16[272,512]{1,0:T(8,128)(2,1)S(1)}, u32[]{:S(2)}, u32[]{:S(2)}) collective-permute-start(bf16[272,512]{1,0:T(8,128)(2,1)S(1)} %constant_dynamic-update-slice_fusion), channel_id=1, source_target_pairs={{4,8},{12,16},{20,24},{8,4},{16,12},{24,20},{5,9},{13,17},{21,25},... | collective-permute-start | bytes 835592 | tf_op jit(solution)/shard_map/ppermute | solution.py:411
  11.5 0.0 copy-start.4
  11.5 3.1 %collective-permute-start.5 = (bf16[128,512]{1,0:T(8,128)(2,1)S(1)}, bf16[128,512]{1,0:T(8,128)(2,1)S(1)}, u32[]{:S(2)}, u32[]{:S(2)}) collective-permute-start(bf16[128,512]{1,0:T(8,128)(2,1)S(1)} %collective-permute-done.2.other_ref), channel_id=1, source_target_pairs={{4,8},{12,16},{20,24},{8,4},{16,12},{24,20},{5,9},{13,17},{21,25},... | collective-permute-start | bytes 393224 | tf_op jit(solution)/shard_map/ppermute | solution.py:411
  14.7 0.1 collective-permute-start.4
  14.8 1.0 %mix_edges.1.weights_ref = bf16[30,96,512]{2,1,0:T(8,128)(2,1)S(1)} custom-call(f32[5,5,2,9]{3,2,1,0:T(2,128)S(1)} %bitcast.8, bf16[9,84,512]{2,1,0:T(8,128)(2,1)S(1)} %bitcast.6), custom_call_target="tpu_custom_call" | custom-call | flops 2000000000 | bytes 6000000 | tf_op jit(solution)/shard_map/mix_edges/pallas_call | solution.py:427
  15.8 0.3 %collective-permute-done.3.outer_ref = bf16[272,512]{1,0:T(8,128)(2,1)S(1)} collective-permute-done((bf16[272,512]{1,0:T(8,128)(2,1)S(1)}, bf16[272,512]{1,0:T(8,128)(2,1)S(1)}, u32[]{:S(2)}, u32[]{:S(2)}) %collective-permute-start.3) | collective-permute-done | bytes 278560 | tf_op jit(solution)/shard_map/ppermute | solution.py:411
  16.2 1.6 %early.1 = (f32[4,2,8,512]{3,2,1,0:T(8,128)S(1)}, f32[4,128,128]{2,1,0:T(8,128)S(1)}) custom-call(bf16[4,5,16,128]{3,2,1,0:T(8,128)(2,1)S(1)} %get-tuple-element.30.choice_ref, bf16[128,512]{1,0:T(8,128)(2,1)S(1)} %collective-permute-done.2.other_ref, bf16[128,512]{1,0:T(8,128)(2,1)S(1)} %collective-permute-done.pair_ref, ...), custom_call_target="tpu_custom_call" | custom-call | flops 3000000000 | bytes 6000000 | tf_op jit(solution)/shard_map/early/pallas_call | solution.py:491
  17.8 0.1 collective-permute-done.5.corner_ref
  17.8 1.9 %late.1 = (bf16[128,512]{1,0:T(8,128)(2,1)S(1)}, bf16[128,512]{1,0:T(8,128)(2,1)S(1)}, bf16[16,512]{1,0:T(8,128)(2,1)S(1)}, bf16[16,512]{1,0:T(8,128)(2,1)S(1)}) custom-call(bf16[4,5,16,128]{3,2,1,0:T(8,128)(2,1)S(1)} %get-tuple-element.30.choice_ref, bf16[160,128]{1,0:T(8,128)(2,1)S(1)} %get-tuple-element.31.cells_ref, ...), custom_call_target="tpu_custom_call" | custom-call | flops 3000000000 | bytes 6000000 | tf_op jit(solution)/shard_map/late/pallas_call | solution.py:507
  19.8 1.9 %collective-permute-start.6 = (bf16[16,512]{1,0:T(8,128)(2,1)S(1)}, bf16[16,512]{1,0:T(8,128)(2,1)S(1)}, u32[]{:S(2)}, u32[]{:S(2)}) collective-permute-start(bf16[16,512]{1,0:T(8,128)(2,1)S(1)} %get-tuple-element.48), channel_id=1, source_target_pairs={{0,1},{2,3},{1,0},{3,2},{4,5},{6,7},{5,4},{7,6},{8,9},{10,11},{9,8... | collective-permute-start | bytes 49160 | tf_op jit(solution)/shard_map/ppermute | solution.py:406
  21.6 1.2 %collective-permute-start.7 = (bf16[16,512]{1,0:T(8,128)(2,1)S(1)}, bf16[16,512]{1,0:T(8,128)(2,1)S(1)}, u32[]{:S(2)}, u32[]{:S(2)}) collective-permute-start(bf16[16,512]{1,0:T(8,128)(2,1)S(1)} %get-tuple-element.52), channel_id=1, source_target_pairs={{1,2},{3,0},{2,1},{0,3},{5,6},{7,4},{6,5},{4,7},{9,10},{11,8},{10,... | collective-permute-start | bytes 49160 | tf_op jit(solution)/shard_map/ppermute | solution.py:406
  22.9 0.8 %mix_own.1.weights_ref = bf16[20,96,512]{2,1,0:T(8,128)(2,1)S(1)} custom-call(f32[5,5,2,9]{3,2,1,0:T(2,128)S(1)} %bitcast.9, bf16[9,84,512]{2,1,0:T(8,128)(2,1)S(1)} %bitcast.7), custom_call_target="tpu_custom_call" | custom-call | flops 2000000000 | bytes 6000000 | tf_op jit(solution)/shard_map/mix_own/pallas_call | solution.py:427
  23.7 1.5 %collective-permute-done.7 = bf16[16,512]{1,0:T(8,128)(2,1)S(1)} collective-permute-done((bf16[16,512]{1,0:T(8,128)(2,1)S(1)}, bf16[16,512]{1,0:T(8,128)(2,1)S(1)}, u32[]{:S(2)}, u32[]{:S(2)}) %collective-permute-start.7) | collective-permute-done | bytes 16416 | tf_op jit(solution)/shard_map/ppermute | solution.py:406
  25.1 1.1 %collective-permute-start.9 = (bf16[144,512]{1,0:T(8,128)(2,1)S(1)}, bf16[144,512]{1,0:T(8,128)(2,1)S(1)}, u32[]{:S(2)}, u32[]{:S(2)}) collective-permute-start(bf16[144,512]{1,0:T(8,128)(2,1)S(1)} %pad_maximum_fusion.latent_ref), channel_id=1, source_target_pairs={{0,4},{8,12},{16,20},{24,28},{4,0},{12,8},{20,16},{28,24},{1,5},{9... | collective-permute-start | bytes 442376 | tf_op jit(solution)/shard_map/ppermute | solution.py:411
  26.2 3.6 %collective-permute-start.8 = (bf16[144,512]{1,0:T(8,128)(2,1)S(1)}, bf16[144,512]{1,0:T(8,128)(2,1)S(1)}, u32[]{:S(2)}, u32[]{:S(2)}) collective-permute-start(bf16[144,512]{1,0:T(8,128)(2,1)S(1)} %pad_maximum_fusion.latent_ref), channel_id=1, source_target_pairs={{4,8},{12,16},{20,24},{8,4},{16,12},{24,20},{5,9},{13,17},{21,25},... | collective-permute-start | bytes 442376 | tf_op jit(solution)/shard_map/ppermute | solution.py:411
  29.8 1.8 %own_band.1 = (f32[2,96,256]{2,1,0:T(8,128)S(1)}, bf16[2,2,5,256,256]{4,3,2,1,0:T(8,128)(2,1)S(1)}, bf16[128,512]{1,0:T(8,128)(2,1)}) custom-call(bf16[128,512]{1,0:T(8,128)(2,1)S(1)} %get-tuple-element.45.state_ref, bf16[144,512]{1,0:T(8,128)(2,1)S(1)} %gather.1.own_ref, bf16[272,512]{1,0:T(8,128)(2,1)S(1)} %collective-permute-done.1.inner_ref, ...), custom_call_target="tpu_custom_call" | custom-call | flops 1000000000 | bytes 2500000 | tf_op jit(solution)/shard_map/own_band/pallas_call | solution.py:530
  31.6 0.9 %inner_band.1.partial_ref = f32[2,96,256]{2,1,0:T(8,128)S(1)} custom-call(bf16[144,512]{1,0:T(8,128)(2,1)S(1)} %collective-permute-done.9.latent_ref, bf16[30,96,512]{2,1,0:T(8,128)(2,1)S(1)} %mix_edges.1.weights_ref, bf16[2,2,5,256,256]{4,3,2,1,0:T(8,128)(2,1)S(1)} %get-tuple-element.56.hot_ref, f32[2,96,256]{2,1,0:T(8,128)S(1)} %get-tuple-element.57.partial_ref), custom_call_target="tpu_custom_call" | custom-call | flops 1000000000 | bytes 2500000 | tf_op jit(solution)/shard_map/inner_band/pallas_call | solution.py:548
  32.5 0.1 collective-permute-done.8.latent_ref
  32.7 1.6 %outer_band.1 = bf16[84,2,256]{2,1,0:T(2,128)(2,1)} custom-call(bf16[144,512]{1,0:T(8,128)(2,1)S(1)} %collective-permute-done.8.latent_ref, bf16[30,96,512]{2,1,0:T(8,128)(2,1)S(1)} %mix_edges.1.weights_ref, bf16[2,2,5,256,256]{4,3,2,1,0:T(8,128)(2,1)S(1)} %get-tuple-element.56.hot_ref, f32[2,96,256]{2,1,0:T(8,128)S(1)} %inner_band.1.partial_ref), custom_call_target="tpu_custom_call" | custom-call | flops 1000000000 | bytes 2500000 | tf_op jit(solution)/shard_map/outer_band/pallas_call | solution.py:558
  (20 shorter events, 0.1 us)
Async XLA Ops:
  0.6 14.1 %copy-start = (bf16[9,512,84]{1,2,0:T(8,128)(2,1)S(1)}, bf16[9,512,84]{1,2,0:T(8,128)(2,1)}, u32[]{:S(2)}) copy-start(bf16[9,512,84]{1,2,0:T(8,128)(2,1)} %param.17) | copy-start | bytes 2322436
  0.6 14.1 %copy-start.3 = (f32[9,2,5,5]{0,1,3,2:T(2,128)S(1)}, f32[9,2,5,5]{0,1,3,2:T(2,128)}, u32[]{:S(2)}) copy-start(f32[9,2,5,5]{0,1,3,2:T(2,128)} %param.16) | copy-start | bytes 5404
  0.6 6.3 %collective-permute-start = (bf16[128,512]{1,0:T(8,128)(2,1)}, bf16[128,512]{1,0:T(8,128)(2,1)S(1)}, u32[]{:S(2)}, u32[]{:S(2)}) collective-permute-start(bf16[128,512]{1,0:T(8,128)(2,1)} %bitcast.13), channel_id=1, source_target_pairs={{0,1},{2,3},{1,0},{3,2},{4,5},{6,7},{5,4},{7,6},{8,9},{10,11},{9,8... | collective-permute-start | bytes 393224 | tf_op jit(solution)/shard_map/ppermute | solution.py:406
  2.8 8.8 %collective-permute-start.2 = (bf16[128,512]{1,0:T(8,128)(2,1)}, bf16[128,512]{1,0:T(8,128)(2,1)S(1)}, u32[]{:S(2)}, u32[]{:S(2)}) collective-permute-start(bf16[128,512]{1,0:T(8,128)(2,1)} %bitcast.14), channel_id=1, source_target_pairs={{1,2},{3,0},{2,1},{0,3},{5,6},{7,4},{6,5},{4,7},{9,10},{11,8},{10,... | collective-permute-start | bytes 393224 | tf_op jit(solution)/shard_map/ppermute | solution.py:406
  7.0 8.8 %collective-permute-start.1 = (bf16[272,512]{1,0:T(8,128)(2,1)S(1)}, bf16[272,512]{1,0:T(8,128)(2,1)S(1)}, u32[]{:S(2)}, u32[]{:S(2)}) collective-permute-start(bf16[272,512]{1,0:T(8,128)(2,1)S(1)} %constant_dynamic-update-slice_fusion), channel_id=1, source_target_pairs={{0,4},{8,12},{16,20},{24,28},{4,0},{12,8},{20,16},{28,24},{1,5},{9... | collective-permute-start | bytes 835592 | tf_op jit(solution)/shard_map/ppermute | solution.py:411
  8.3 7.9 %collective-permute-start.3 = (bf16[272,512]{1,0:T(8,128)(2,1)S(1)}, bf16[272,512]{1,0:T(8,128)(2,1)S(1)}, u32[]{:S(2)}, u32[]{:S(2)}) collective-permute-start(bf16[272,512]{1,0:T(8,128)(2,1)S(1)} %constant_dynamic-update-slice_fusion), channel_id=1, source_target_pairs={{4,8},{12,16},{20,24},{8,4},{16,12},{24,20},{5,9},{13,17},{21,25},... | collective-permute-start | bytes 835592 | tf_op jit(solution)/shard_map/ppermute | solution.py:411
  11.5 4.6 %copy-start.4 = (f32[512]{0:T(512)S(1)}, f32[512]{0:T(512)}, u32[]{:S(2)}) copy-start(f32[512]{0:T(512)} %param.10) | copy-start | bytes 6148
  11.5 6.3 %collective-permute-start.5 = (bf16[128,512]{1,0:T(8,128)(2,1)S(1)}, bf16[128,512]{1,0:T(8,128)(2,1)S(1)}, u32[]{:S(2)}, u32[]{:S(2)}) collective-permute-start(bf16[128,512]{1,0:T(8,128)(2,1)S(1)} %collective-permute-done.2.other_ref), channel_id=1, source_target_pairs={{4,8},{12,16},{20,24},{8,4},{16,12},{24,20},{5,9},{13,17},{21,25},... | collective-permute-start | bytes 393224 | tf_op jit(solution)/shard_map/ppermute | solution.py:411
  14.7 3.2 %collective-permute-start.4 = (bf16[128,512]{1,0:T(8,128)(2,1)S(1)}, bf16[128,512]{1,0:T(8,128)(2,1)S(1)}, u32[]{:S(2)}, u32[]{:S(2)}) collective-permute-start(bf16[128,512]{1,0:T(8,128)(2,1)S(1)} %collective-permute-done.2.other_ref), channel_id=1, source_target_pairs={{0,4},{8,12},{16,20},{24,28},{4,0},{12,8},{20,16},{28,24},{1,5},{9... | collective-permute-start | bytes 393224 | tf_op jit(solution)/shard_map/ppermute | solution.py:411
  16.2 1.7 %copy-start.1 = (bf16[512,512]{1,0:T(8,128)(2,1)S(1)}, bf16[512,512]{1,0:T(8,128)(2,1)}, u32[]{:S(2)}) copy-start(bf16[512,512]{1,0:T(8,128)(2,1)} %wout_ref.1) | copy-start | bytes 1572868
  16.2 1.7 %copy-start.2 = (bf16[512,512]{1,0:T(8,128)(2,1)S(1)}, bf16[512,512]{1,0:T(8,128)(2,1)}, u32[]{:S(2)}) copy-start(bf16[512,512]{1,0:T(8,128)(2,1)} %wlat_ref.1) | copy-start | bytes 1572868
  19.8 3.9 %collective-permute-start.6 = (bf16[16,512]{1,0:T(8,128)(2,1)S(1)}, bf16[16,512]{1,0:T(8,128)(2,1)S(1)}, u32[]{:S(2)}, u32[]{:S(2)}) collective-permute-start(bf16[16,512]{1,0:T(8,128)(2,1)S(1)} %get-tuple-element.48), channel_id=1, source_target_pairs={{0,1},{2,3},{1,0},{3,2},{4,5},{6,7},{5,4},{7,6},{8,9},{10,11},{9,8... | collective-permute-start | bytes 49160 | tf_op jit(solution)/shard_map/ppermute | solution.py:406
  21.6 3.5 %collective-permute-start.7 = (bf16[16,512]{1,0:T(8,128)(2,1)S(1)}, bf16[16,512]{1,0:T(8,128)(2,1)S(1)}, u32[]{:S(2)}, u32[]{:S(2)}) collective-permute-start(bf16[16,512]{1,0:T(8,128)(2,1)S(1)} %get-tuple-element.52), channel_id=1, source_target_pairs={{1,2},{3,0},{2,1},{0,3},{5,6},{7,4},{6,5},{4,7},{9,10},{11,8},{10,... | collective-permute-start | bytes 49160 | tf_op jit(solution)/shard_map/ppermute | solution.py:406
  25.1 6.4 %collective-permute-start.9 = (bf16[144,512]{1,0:T(8,128)(2,1)S(1)}, bf16[144,512]{1,0:T(8,128)(2,1)S(1)}, u32[]{:S(2)}, u32[]{:S(2)}) collective-permute-start(bf16[144,512]{1,0:T(8,128)(2,1)S(1)} %pad_maximum_fusion.latent_ref), channel_id=1, source_target_pairs={{0,4},{8,12},{16,20},{24,28},{4,0},{12,8},{20,16},{28,24},{1,5},{9... | collective-permute-start | bytes 442376 | tf_op jit(solution)/shard_map/ppermute | solution.py:411
  26.2 6.5 %collective-permute-start.8 = (bf16[144,512]{1,0:T(8,128)(2,1)S(1)}, bf16[144,512]{1,0:T(8,128)(2,1)S(1)}, u32[]{:S(2)}, u32[]{:S(2)}) collective-permute-start(bf16[144,512]{1,0:T(8,128)(2,1)S(1)} %pad_maximum_fusion.latent_ref), channel_id=1, source_target_pairs={{4,8},{12,16},{20,24},{8,4},{16,12},{24,20},{5,9},{13,17},{21,25},... | collective-permute-start | bytes 442376 | tf_op jit(solution)/shard_map/ppermute | solution.py:411

commit v22 on v16

--- a/solution.py
+++ b/solution.py
@@ -167,11 +167,11 @@
     tall, wide = rows // ROWS, candidates[-1].shape[1] // LANES
     near = []
     for entry in entries:
-        total = None
-        for at in range(CANDIDATES):
+        total = candidates[entry]
+        for at in range(1, CANDIDATES):
             weight = jnp.concatenate([choice_ref[entry, at]] * wide, axis=1)
-            part = candidates[entry + at] * jnp.concatenate([weight] * tall, axis=0)
-            total = part if total is None else total + part
+            weight = jnp.concatenate([weight] * tall, axis=0)
+            total = jnp.where(weight > 0, candidates[entry + at], total)
         near.append(total)
     return jnp.concatenate(near, axis=0)
 

time: 34.4 us -> 34.3 us (level)
  no operation moved by 1% of the time
where the time goes in v22:
time: 34.3 us; the launch traced here: 34.1 us
  starting transfers between devices  18.6 us (54%)
  Pallas kernels  12.6 us (37%)
  waiting for transfers between devices  2.08 us (6%)
  between operations  0.82 us (2%)
    ppermute x6, starting transfers between devices, exchanged(): return lax.ppermute(array, 'reg', pairs + [(j, i) for i, j in pairs])  12.3 us
    ppermute x4, starting transfers between devices, paired(): return lax.ppermute(array, 'lon', pairs + [(j, i) for i, j in pairs])  6.29 us
    pallas_call x1, Pallas kernels, shards(): pl.pallas_call(functools.partial(prepare_kernel, sectors), in_specs=[whol...  2.02 us
    pallas_call x1, Pallas kernels, shards(): pl.pallas_call(late_kernel, in_specs=[whole()] * 15, out_specs=[whole()]...  1.91 us
    pallas_call x2, Pallas kernels, mixed(): pl.pallas_call(functools.partial(mix_kernel, blocks), in_specs=[whole()]...  1.82 us
    pallas_call x1, Pallas kernels, shards(): pl.pallas_call(functools.partial(own_kernel, (rows, 2 * rows, 2 * rows)),...  1.8 us
    pallas_call x1, Pallas kernels, shards(): pl.pallas_call(functools.partial(band_kernel, False), in_specs=[whole()]...  1.6 us
    pallas_call x1, Pallas kernels, shards(): pl.pallas_call(early_kernel, in_specs=[whole()] * 11, out_specs=[whole()]...  1.55 us
  transfers between devices with their start and end apart: 10, of which 4 were waited for; matrix products, arithmetic and copies ran while one was open for 0% of the time, Pallas kernels for 27%

profile of v22, /device:TPU:1, one launch (start us, length us, event | category | flops | bytes accessed | tf_op | source)
XLA Modules:
  0.0 34.1 jit_solution(3402934496633559901)
XLA Ops:
  0.6 2.1 %collective-permute-start = (bf16[128,512]{1,0:T(8,128)(2,1)}, bf16[128,512]{1,0:T(8,128)(2,1)S(1)}, u32[]{:S(2)}, u32[]{:S(2)}) collective-permute-start(bf16[128,512]{1,0:T(8,128)(2,1)} %bitcast.13), channel_id=1, source_target_pairs={{0,1},{2,3},{1,0},{3,2},{4,5},{6,7},{5,4},{7,6},{8,9},{10,11},{9,8... | collective-permute-start | bytes 393224 | tf_op jit(solution)/shard_map/ppermute | solution.py:404
  2.8 1.2 %collective-permute-start.2 = (bf16[128,512]{1,0:T(8,128)(2,1)}, bf16[128,512]{1,0:T(8,128)(2,1)S(1)}, u32[]{:S(2)}, u32[]{:S(2)}) collective-permute-start(bf16[128,512]{1,0:T(8,128)(2,1)} %bitcast.14), channel_id=1, source_target_pairs={{1,2},{3,0},{2,1},{0,3},{5,6},{7,4},{6,5},{4,7},{9,10},{11,8},{10,... | collective-permute-start | bytes 393224 | tf_op jit(solution)/shard_map/ppermute | solution.py:404
  4.0 1.0 %gather.1.own_ref = bf16[144,512]{1,0:T(8,128)(2,1)S(1)} custom-call(bf16[128,512]{1,0:T(8,128)(2,1)} %bitcast.15, s32[2,256]{1,0:T(2,128)} %assign_hbm.3), custom_call_target="tpu_custom_call" | custom-call | flops 1000 | bytes 1000 | tf_op jit(solution)/shard_map/gather/pallas_call | solution.py:440
  4.9 2.0 %prepare.1 = (bf16[4,128,512]{2,1,0:T(8,128)(2,1)S(1)}, bf16[128,512]{1,0:T(8,128)(2,1)S(1)}, bf16[512,128]{1,0:T(8,128)(2,1)S(1)}, bf16[512,512]{1,0:T(8,128)(2...) custom-call(bf16[144,512]{1,0:T(8,128)(2,1)S(1)} %gather.1.own_ref, ...), custom_call_target="tpu_custom_call" | custom-call | flops 500000000 | bytes 1000000 | tf_op jit(solution)/shard_map/prepare/pallas_call | solution.py:453
  7.0 1.3 %collective-permute-start.1 = (bf16[272,512]{1,0:T(8,128)(2,1)S(1)}, bf16[272,512]{1,0:T(8,128)(2,1)S(1)}, u32[]{:S(2)}, u32[]{:S(2)}) collective-permute-start(bf16[272,512]{1,0:T(8,128)(2,1)S(1)} %constant_dynamic-update-slice_fusion), channel_id=1, source_target_pairs={{0,4},{8,12},{16,20},{24,28},{4,0},{12,8},{20,16},{28,24},{1,5},{9... | collective-permute-start | bytes 835592 | tf_op jit(solution)/shard_map/ppermute | solution.py:409
  8.3 3.2 %collective-permute-start.3 = (bf16[272,512]{1,0:T(8,128)(2,1)S(1)}, bf16[272,512]{1,0:T(8,128)(2,1)S(1)}, u32[]{:S(2)}, u32[]{:S(2)}) collective-permute-start(bf16[272,512]{1,0:T(8,128)(2,1)S(1)} %constant_dynamic-update-slice_fusion), channel_id=1, source_target_pairs={{4,8},{12,16},{20,24},{8,4},{16,12},{24,20},{5,9},{13,17},{21,25},... | collective-permute-start | bytes 835592 | tf_op jit(solution)/shard_map/ppermute | solution.py:409
  11.5 0.0 copy-start.4
  11.5 3.1 %collective-permute-start.5 = (bf16[128,512]{1,0:T(8,128)(2,1)S(1)}, bf16[128,512]{1,0:T(8,128)(2,1)S(1)}, u32[]{:S(2)}, u32[]{:S(2)}) collective-permute-start(bf16[128,512]{1,0:T(8,128)(2,1)S(1)} %collective-permute-done.2.other_ref), channel_id=1, source_target_pairs={{4,8},{12,16},{20,24},{8,4},{16,12},{24,20},{5,9},{13,17},{21,25},... | collective-permute-start | bytes 393224 | tf_op jit(solution)/shard_map/ppermute | solution.py:409
  14.7 0.1 collective-permute-start.4
  14.8 1.0 %mix_edges.1.weights_ref = bf16[30,96,512]{2,1,0:T(8,128)(2,1)S(1)} custom-call(f32[5,5,2,9]{3,2,1,0:T(2,128)S(1)} %bitcast.8, bf16[9,84,512]{2,1,0:T(8,128)(2,1)S(1)} %bitcast.6), custom_call_target="tpu_custom_call" | custom-call | flops 2000000000 | bytes 6000000 | tf_op jit(solution)/shard_map/mix_edges/pallas_call | solution.py:425
  15.8 0.3 %collective-permute-done.3.outer_ref = bf16[272,512]{1,0:T(8,128)(2,1)S(1)} collective-permute-done((bf16[272,512]{1,0:T(8,128)(2,1)S(1)}, bf16[272,512]{1,0:T(8,128)(2,1)S(1)}, u32[]{:S(2)}, u32[]{:S(2)}) %collective-permute-start.3) | collective-permute-done | bytes 278560 | tf_op jit(solution)/shard_map/ppermute | solution.py:409
  16.2 1.6 %early.1 = (f32[4,2,8,512]{3,2,1,0:T(8,128)S(1)}, f32[4,128,128]{2,1,0:T(8,128)S(1)}) custom-call(bf16[4,5,16,128]{3,2,1,0:T(8,128)(2,1)S(1)} %get-tuple-element.29.choice_ref, bf16[128,512]{1,0:T(8,128)(2,1)S(1)} %collective-permute-done.2.other_ref, bf16[128,512]{1,0:T(8,128)(2,1)S(1)} %collective-permute-done.pair_ref, ...), custom_call_target="tpu_custom_call" | custom-call | flops 3000000000 | bytes 6000000 | tf_op jit(solution)/shard_map/early/pallas_call | solution.py:488
  17.7 0.1 collective-permute-done.5.corner_ref
  17.8 1.9 %late.1 = (bf16[128,512]{1,0:T(8,128)(2,1)S(1)}, bf16[128,512]{1,0:T(8,128)(2,1)S(1)}, bf16[16,512]{1,0:T(8,128)(2,1)S(1)}, bf16[16,512]{1,0:T(8,128)(2,1)S(1)}) custom-call(bf16[4,5,16,128]{3,2,1,0:T(8,128)(2,1)S(1)} %get-tuple-element.29.choice_ref, bf16[32,128]{1,0:T(8,128)(2,1)S(1)} %get-tuple-element.30.cells_ref, ...), custom_call_target="tpu_custom_call" | custom-call | flops 3000000000 | bytes 6000000 | tf_op jit(solution)/shard_map/late/pallas_call | solution.py:504
  19.7 1.8 %collective-permute-start.6 = (bf16[16,512]{1,0:T(8,128)(2,1)S(1)}, bf16[16,512]{1,0:T(8,128)(2,1)S(1)}, u32[]{:S(2)}, u32[]{:S(2)}) collective-permute-start(bf16[16,512]{1,0:T(8,128)(2,1)S(1)} %get-tuple-element.46), channel_id=1, source_target_pairs={{0,1},{2,3},{1,0},{3,2},{4,5},{6,7},{5,4},{7,6},{8,9},{10,11},{9,8... | collective-permute-start | bytes 49160 | tf_op jit(solution)/shard_map/ppermute | solution.py:404
  21.5 1.2 %collective-permute-start.7 = (bf16[16,512]{1,0:T(8,128)(2,1)S(1)}, bf16[16,512]{1,0:T(8,128)(2,1)S(1)}, u32[]{:S(2)}, u32[]{:S(2)}) collective-permute-start(bf16[16,512]{1,0:T(8,128)(2,1)S(1)} %get-tuple-element.50), channel_id=1, source_target_pairs={{1,2},{3,0},{2,1},{0,3},{5,6},{7,4},{6,5},{4,7},{9,10},{11,8},{10,... | collective-permute-start | bytes 49160 | tf_op jit(solution)/shard_map/ppermute | solution.py:404
  22.7 0.8 %mix_own.1.weights_ref = bf16[20,96,512]{2,1,0:T(8,128)(2,1)S(1)} custom-call(f32[5,5,2,9]{3,2,1,0:T(2,128)S(1)} %bitcast.9, bf16[9,84,512]{2,1,0:T(8,128)(2,1)S(1)} %bitcast.7), custom_call_target="tpu_custom_call" | custom-call | flops 2000000000 | bytes 6000000 | tf_op jit(solution)/shard_map/mix_own/pallas_call | solution.py:425
  23.5 1.5 %collective-permute-done.7 = bf16[16,512]{1,0:T(8,128)(2,1)S(1)} collective-permute-done((bf16[16,512]{1,0:T(8,128)(2,1)S(1)}, bf16[16,512]{1,0:T(8,128)(2,1)S(1)}, u32[]{:S(2)}, u32[]{:S(2)}) %collective-permute-start.7) | collective-permute-done | bytes 16416 | tf_op jit(solution)/shard_map/ppermute | solution.py:404
  25.0 1.1 %collective-permute-start.9 = (bf16[144,512]{1,0:T(8,128)(2,1)S(1)}, bf16[144,512]{1,0:T(8,128)(2,1)S(1)}, u32[]{:S(2)}, u32[]{:S(2)}) collective-permute-start(bf16[144,512]{1,0:T(8,128)(2,1)S(1)} %pad_maximum_fusion.latent_ref), channel_id=1, source_target_pairs={{0,4},{8,12},{16,20},{24,28},{4,0},{12,8},{20,16},{28,24},{1,5},{9... | collective-permute-start | bytes 442376 | tf_op jit(solution)/shard_map/ppermute | solution.py:409
  26.1 3.6 %collective-permute-start.8 = (bf16[144,512]{1,0:T(8,128)(2,1)S(1)}, bf16[144,512]{1,0:T(8,128)(2,1)S(1)}, u32[]{:S(2)}, u32[]{:S(2)}) collective-permute-start(bf16[144,512]{1,0:T(8,128)(2,1)S(1)} %pad_maximum_fusion.latent_ref), channel_id=1, source_target_pairs={{4,8},{12,16},{20,24},{8,4},{16,12},{24,20},{5,9},{13,17},{21,25},... | collective-permute-start | bytes 442376 | tf_op jit(solution)/shard_map/ppermute | solution.py:409
  29.7 1.8 %own_band.1 = (f32[2,96,256]{2,1,0:T(8,128)S(1)}, bf16[2,2,5,256,256]{4,3,2,1,0:T(8,128)(2,1)S(1)}, bf16[128,512]{1,0:T(8,128)(2,1)}) custom-call(bf16[128,512]{1,0:T(8,128)(2,1)S(1)} %get-tuple-element.43.state_ref, bf16[144,512]{1,0:T(8,128)(2,1)S(1)} %gather.1.own_ref, bf16[272,512]{1,0:T(8,128)(2,1)S(1)} %collective-permute-done.1.inner_ref, ...), custom_call_target="tpu_custom_call" | custom-call | flops 1000000000 | bytes 2500000 | tf_op jit(solution)/shard_map/own_band/pallas_call | solution.py:527
  31.5 0.9 %inner_band.1.partial_ref = f32[2,96,256]{2,1,0:T(8,128)S(1)} custom-call(bf16[144,512]{1,0:T(8,128)(2,1)S(1)} %collective-permute-done.9.latent_ref, bf16[30,96,512]{2,1,0:T(8,128)(2,1)S(1)} %mix_edges.1.weights_ref, bf16[2,2,5,256,256]{4,3,2,1,0:T(8,128)(2,1)S(1)} %get-tuple-element.54.hot_ref, f32[2,96,256]{2,1,0:T(8,128)S(1)} %get-tuple-element.55.partial_ref), custom_call_target="tpu_custom_call" | custom-call | flops 1000000000 | bytes 2500000 | tf_op jit(solution)/shard_map/inner_band/pallas_call | solution.py:545
  32.4 0.1 collective-permute-done.8.latent_ref
  32.5 1.6 %outer_band.1 = bf16[84,2,256]{2,1,0:T(2,128)(2,1)} custom-call(bf16[144,512]{1,0:T(8,128)(2,1)S(1)} %collective-permute-done.8.latent_ref, bf16[30,96,512]{2,1,0:T(8,128)(2,1)S(1)} %mix_edges.1.weights_ref, bf16[2,2,5,256,256]{4,3,2,1,0:T(8,128)(2,1)S(1)} %get-tuple-element.54.hot_ref, f32[2,96,256]{2,1,0:T(8,128)S(1)} %inner_band.1.partial_ref), custom_call_target="tpu_custom_call" | custom-call | flops 1000000000 | bytes 2500000 | tf_op jit(solution)/shard_map/outer_band/pallas_call | solution.py:555
  (20 shorter events, 0.1 us)
Async XLA Ops:
  0.6 14.1 %copy-start = (bf16[9,512,84]{1,2,0:T(8,128)(2,1)S(1)}, bf16[9,512,84]{1,2,0:T(8,128)(2,1)}, u32[]{:S(2)}) copy-start(bf16[9,512,84]{1,2,0:T(8,128)(2,1)} %param.17) | copy-start | bytes 2322436
  0.6 14.1 %copy-start.3 = (f32[9,2,5,5]{0,1,3,2:T(2,128)S(1)}, f32[9,2,5,5]{0,1,3,2:T(2,128)}, u32[]{:S(2)}) copy-start(f32[9,2,5,5]{0,1,3,2:T(2,128)} %param.16) | copy-start | bytes 5404
  0.6 6.3 %collective-permute-start = (bf16[128,512]{1,0:T(8,128)(2,1)}, bf16[128,512]{1,0:T(8,128)(2,1)S(1)}, u32[]{:S(2)}, u32[]{:S(2)}) collective-permute-start(bf16[128,512]{1,0:T(8,128)(2,1)} %bitcast.13), channel_id=1, source_target_pairs={{0,1},{2,3},{1,0},{3,2},{4,5},{6,7},{5,4},{7,6},{8,9},{10,11},{9,8... | collective-permute-start | bytes 393224 | tf_op jit(solution)/shard_map/ppermute | solution.py:404
  2.8 8.8 %collective-permute-start.2 = (bf16[128,512]{1,0:T(8,128)(2,1)}, bf16[128,512]{1,0:T(8,128)(2,1)S(1)}, u32[]{:S(2)}, u32[]{:S(2)}) collective-permute-start(bf16[128,512]{1,0:T(8,128)(2,1)} %bitcast.14), channel_id=1, source_target_pairs={{1,2},{3,0},{2,1},{0,3},{5,6},{7,4},{6,5},{4,7},{9,10},{11,8},{10,... | collective-permute-start | bytes 393224 | tf_op jit(solution)/shard_map/ppermute | solution.py:404
  7.0 8.8 %collective-permute-start.1 = (bf16[272,512]{1,0:T(8,128)(2,1)S(1)}, bf16[272,512]{1,0:T(8,128)(2,1)S(1)}, u32[]{:S(2)}, u32[]{:S(2)}) collective-permute-start(bf16[272,512]{1,0:T(8,128)(2,1)S(1)} %constant_dynamic-update-slice_fusion), channel_id=1, source_target_pairs={{0,4},{8,12},{16,20},{24,28},{4,0},{12,8},{20,16},{28,24},{1,5},{9... | collective-permute-start | bytes 835592 | tf_op jit(solution)/shard_map/ppermute | solution.py:409
  8.3 7.9 %collective-permute-start.3 = (bf16[272,512]{1,0:T(8,128)(2,1)S(1)}, bf16[272,512]{1,0:T(8,128)(2,1)S(1)}, u32[]{:S(2)}, u32[]{:S(2)}) collective-permute-start(bf16[272,512]{1,0:T(8,128)(2,1)S(1)} %constant_dynamic-update-slice_fusion), channel_id=1, source_target_pairs={{4,8},{12,16},{20,24},{8,4},{16,12},{24,20},{5,9},{13,17},{21,25},... | collective-permute-start | bytes 835592 | tf_op jit(solution)/shard_map/ppermute | solution.py:409
  11.5 4.6 %copy-start.4 = (f32[512]{0:T(512)S(1)}, f32[512]{0:T(512)}, u32[]{:S(2)}) copy-start(f32[512]{0:T(512)} %param.10) | copy-start | bytes 6148
  11.5 6.3 %collective-permute-start.5 = (bf16[128,512]{1,0:T(8,128)(2,1)S(1)}, bf16[128,512]{1,0:T(8,128)(2,1)S(1)}, u32[]{:S(2)}, u32[]{:S(2)}) collective-permute-start(bf16[128,512]{1,0:T(8,128)(2,1)S(1)} %collective-permute-done.2.other_ref), channel_id=1, source_target_pairs={{4,8},{12,16},{20,24},{8,4},{16,12},{24,20},{5,9},{13,17},{21,25},... | collective-permute-start | bytes 393224 | tf_op jit(solution)/shard_map/ppermute | solution.py:409
  14.7 3.2 %collective-permute-start.4 = (bf16[128,512]{1,0:T(8,128)(2,1)S(1)}, bf16[128,512]{1,0:T(8,128)(2,1)S(1)}, u32[]{:S(2)}, u32[]{:S(2)}) collective-permute-start(bf16[128,512]{1,0:T(8,128)(2,1)S(1)} %collective-permute-done.2.other_ref), channel_id=1, source_target_pairs={{0,4},{8,12},{16,20},{24,28},{4,0},{12,8},{20,16},{28,24},{1,5},{9... | collective-permute-start | bytes 393224 | tf_op jit(solution)/shard_map/ppermute | solution.py:409
  16.2 1.7 %copy-start.1 = (bf16[512,512]{1,0:T(8,128)(2,1)S(1)}, bf16[512,512]{1,0:T(8,128)(2,1)}, u32[]{:S(2)}) copy-start(bf16[512,512]{1,0:T(8,128)(2,1)} %wout_ref.1) | copy-start | bytes 1572868
  16.2 1.7 %copy-start.2 = (bf16[512,512]{1,0:T(8,128)(2,1)S(1)}, bf16[512,512]{1,0:T(8,128)(2,1)}, u32[]{:S(2)}) copy-start(bf16[512,512]{1,0:T(8,128)(2,1)} %wlat_ref.1) | copy-start | bytes 1572868
  19.7 3.8 %collective-permute-start.6 = (bf16[16,512]{1,0:T(8,128)(2,1)S(1)}, bf16[16,512]{1,0:T(8,128)(2,1)S(1)}, u32[]{:S(2)}, u32[]{:S(2)}) collective-permute-start(bf16[16,512]{1,0:T(8,128)(2,1)S(1)} %get-tuple-element.46), channel_id=1, source_target_pairs={{0,1},{2,3},{1,0},{3,2},{4,5},{6,7},{5,4},{7,6},{8,9},{10,11},{9,8... | collective-permute-start | bytes 49160 | tf_op jit(solution)/shard_map/ppermute | solution.py:404
  21.5 3.5 %collective-permute-start.7 = (bf16[16,512]{1,0:T(8,128)(2,1)S(1)}, bf16[16,512]{1,0:T(8,128)(2,1)S(1)}, u32[]{:S(2)}, u32[]{:S(2)}) collective-permute-start(bf16[16,512]{1,0:T(8,128)(2,1)S(1)} %get-tuple-element.50), channel_id=1, source_target_pairs={{1,2},{3,0},{2,1},{0,3},{5,6},{7,4},{6,5},{4,7},{9,10},{11,8},{10,... | collective-permute-start | bytes 49160 | tf_op jit(solution)/shard_map/ppermute | solution.py:404
  25.0 6.4 %collective-permute-start.9 = (bf16[144,512]{1,0:T(8,128)(2,1)S(1)}, bf16[144,512]{1,0:T(8,128)(2,1)S(1)}, u32[]{:S(2)}, u32[]{:S(2)}) collective-permute-start(bf16[144,512]{1,0:T(8,128)(2,1)S(1)} %pad_maximum_fusion.latent_ref), channel_id=1, source_target_pairs={{0,4},{8,12},{16,20},{24,28},{4,0},{12,8},{20,16},{28,24},{1,5},{9... | collective-permute-start | bytes 442376 | tf_op jit(solution)/shard_map/ppermute | solution.py:409
  26.1 6.5 %collective-permute-start.8 = (bf16[144,512]{1,0:T(8,128)(2,1)S(1)}, bf16[144,512]{1,0:T(8,128)(2,1)S(1)}, u32[]{:S(2)}, u32[]{:S(2)}) collective-permute-start(bf16[144,512]{1,0:T(8,128)(2,1)S(1)} %pad_maximum_fusion.latent_ref), channel_id=1, source_target_pairs={{4,8},{12,16},{20,24},{8,4},{16,12},{24,20},{5,9},{13,17},{21,25},... | collective-permute-start | bytes 442376 | tf_op jit(solution)/shard_map/ppermute | solution.py:409

commit v23 on v16

--- a/solution.py
+++ b/solution.py
@@ -349,12 +349,13 @@
     blank = jnp.zeros((lanes - latent.shape[0], latent.shape[1]), BF16)
     blocks = len(blocks_of(ABOVE))
     weights = weights_ref[pl.ds(band * blocks, blocks)]
-    shares = shares_of(jnp.concatenate([latent, blank], axis=0), weights)
+    padded = jnp.concatenate([latent, blank], axis=0)
+    single, double = shares_of(padded, weights[:TAPS]), shares_of(padded, weights[TAPS:])
     for off in range(TAPS):
         span = slice(off * lanes, (off + 1) * lanes)
-        one_ref[:, span] = shares[off]
+        one_ref[:, span] = single[off]
         for row in range(2):
-            two_ref[row * outputs : (row + 1) * outputs, span] = shares[TAPS + 2 * off + row]
+            two_ref[row * outputs : (row + 1) * outputs, span] = double[2 * off + row]
     depth = TAPS * lanes
     one = jnp.dot(one_ref[...], hot_ref[band, 0].reshape(depth, cols), preferred_element_type=F32)
     two = jnp.dot(two_ref[...], hot_ref[band, 1].reshape(depth, cols), preferred_element_type=F32)

time: 34.4 us -> 34.4 us (level)
  no operation moved by 1% of the time
where the time goes in v23:
time: 34.4 us; the launch traced here: 34.2 us
  starting transfers between devices  18.6 us (54%)
  Pallas kernels  12.6 us (37%)
  waiting for transfers between devices  2.06 us (6%)
  between operations  0.82 us (2%)
    ppermute x6, starting transfers between devices, exchanged(): return lax.ppermute(array, 'reg', pairs + [(j, i) for i, j in pairs])  12.3 us
    ppermute x4, starting transfers between devices, paired(): return lax.ppermute(array, 'lon', pairs + [(j, i) for i, j in pairs])  6.35 us
    pallas_call x1, Pallas kernels, shards(): pl.pallas_call(functools.partial(prepare_kernel, sectors), in_specs=[whol...  2.02 us
    pallas_call x1, Pallas kernels, shards(): pl.pallas_call(late_kernel, in_specs=[whole()] * 15, out_specs=[whole()]...  1.95 us
    pallas_call x2, Pallas kernels, mixed(): pl.pallas_call(functools.partial(mix_kernel, blocks), in_specs=[whole()]...  1.82 us
    pallas_call x1, Pallas kernels, shards(): pl.pallas_call(functools.partial(own_kernel, (rows, 2 * rows, 2 * rows)),...  1.8 us
    pallas_call x1, Pallas kernels, shards(): pl.pallas_call(early_kernel, in_specs=[whole()] * 11, out_specs=[whole()]...  1.6 us
    pallas_call x1, Pallas kernels, shards(): pl.pallas_call(functools.partial(band_kernel, False), in_specs=[whole()]...  1.58 us
  transfers between devices with their start and end apart: 10, of which 4 were waited for; matrix products, arithmetic and copies ran while one was open for 0% of the time, Pallas kernels for 27%

profile of v23, /device:TPU:1, one launch (start us, length us, event | category | flops | bytes accessed | tf_op | source)
XLA Modules:
  0.0 34.2 jit_solution(14370125287658325427)
XLA Ops:
  0.6 2.1 %collective-permute-start = (bf16[128,512]{1,0:T(8,128)(2,1)}, bf16[128,512]{1,0:T(8,128)(2,1)S(1)}, u32[]{:S(2)}, u32[]{:S(2)}) collective-permute-start(bf16[128,512]{1,0:T(8,128)(2,1)} %bitcast.13), channel_id=1, source_target_pairs={{0,1},{2,3},{1,0},{3,2},{4,5},{6,7},{5,4},{7,6},{8,9},{10,11},{9,8... | collective-permute-start | bytes 393224 | tf_op jit(solution)/shard_map/ppermute | solution.py:405
  2.8 1.2 %collective-permute-start.2 = (bf16[128,512]{1,0:T(8,128)(2,1)}, bf16[128,512]{1,0:T(8,128)(2,1)S(1)}, u32[]{:S(2)}, u32[]{:S(2)}) collective-permute-start(bf16[128,512]{1,0:T(8,128)(2,1)} %bitcast.14), channel_id=1, source_target_pairs={{1,2},{3,0},{2,1},{0,3},{5,6},{7,4},{6,5},{4,7},{9,10},{11,8},{10,... | collective-permute-start | bytes 393224 | tf_op jit(solution)/shard_map/ppermute | solution.py:405
  4.0 1.0 %gather.1.own_ref = bf16[144,512]{1,0:T(8,128)(2,1)S(1)} custom-call(bf16[128,512]{1,0:T(8,128)(2,1)} %bitcast.15, s32[2,256]{1,0:T(2,128)} %assign_hbm.3), custom_call_target="tpu_custom_call" | custom-call | flops 1000 | bytes 1000 | tf_op jit(solution)/shard_map/gather/pallas_call | solution.py:441
  4.9 2.0 %prepare.1 = (bf16[4,128,512]{2,1,0:T(8,128)(2,1)S(1)}, bf16[128,512]{1,0:T(8,128)(2,1)S(1)}, bf16[512,128]{1,0:T(8,128)(2,1)S(1)}, bf16[512,512]{1,0:T(8,128)(2...) custom-call(bf16[144,512]{1,0:T(8,128)(2,1)S(1)} %gather.1.own_ref, ...), custom_call_target="tpu_custom_call" | custom-call | flops 500000000 | bytes 1000000 | tf_op jit(solution)/shard_map/prepare/pallas_call | solution.py:454
  7.0 1.3 %collective-permute-start.1 = (bf16[272,512]{1,0:T(8,128)(2,1)S(1)}, bf16[272,512]{1,0:T(8,128)(2,1)S(1)}, u32[]{:S(2)}, u32[]{:S(2)}) collective-permute-start(bf16[272,512]{1,0:T(8,128)(2,1)S(1)} %constant_dynamic-update-slice_fusion), channel_id=1, source_target_pairs={{0,4},{8,12},{16,20},{24,28},{4,0},{12,8},{20,16},{28,24},{1,5},{9... | collective-permute-start | bytes 835592 | tf_op jit(solution)/shard_map/ppermute | solution.py:410
  8.3 3.2 %collective-permute-start.3 = (bf16[272,512]{1,0:T(8,128)(2,1)S(1)}, bf16[272,512]{1,0:T(8,128)(2,1)S(1)}, u32[]{:S(2)}, u32[]{:S(2)}) collective-permute-start(bf16[272,512]{1,0:T(8,128)(2,1)S(1)} %constant_dynamic-update-slice_fusion), channel_id=1, source_target_pairs={{4,8},{12,16},{20,24},{8,4},{16,12},{24,20},{5,9},{13,17},{21,25},... | collective-permute-start | bytes 835592 | tf_op jit(solution)/shard_map/ppermute | solution.py:410
  11.5 0.0 copy-start.4
  11.5 3.1 %collective-permute-start.5 = (bf16[128,512]{1,0:T(8,128)(2,1)S(1)}, bf16[128,512]{1,0:T(8,128)(2,1)S(1)}, u32[]{:S(2)}, u32[]{:S(2)}) collective-permute-start(bf16[128,512]{1,0:T(8,128)(2,1)S(1)} %collective-permute-done.2.other_ref), channel_id=1, source_target_pairs={{4,8},{12,16},{20,24},{8,4},{16,12},{24,20},{5,9},{13,17},{21,25},... | collective-permute-start | bytes 393224 | tf_op jit(solution)/shard_map/ppermute | solution.py:410
  14.7 0.1 collective-permute-start.4
  14.8 1.0 %mix_edges.1.weights_ref = bf16[30,96,512]{2,1,0:T(8,128)(2,1)S(1)} custom-call(f32[5,5,2,9]{3,2,1,0:T(2,128)S(1)} %bitcast.8, bf16[9,84,512]{2,1,0:T(8,128)(2,1)S(1)} %bitcast.6), custom_call_target="tpu_custom_call" | custom-call | flops 2000000000 | bytes 6000000 | tf_op jit(solution)/shard_map/mix_edges/pallas_call | solution.py:426
  15.8 0.3 %collective-permute-done.3.outer_ref = bf16[272,512]{1,0:T(8,128)(2,1)S(1)} collective-permute-done((bf16[272,512]{1,0:T(8,128)(2,1)S(1)}, bf16[272,512]{1,0:T(8,128)(2,1)S(1)}, u32[]{:S(2)}, u32[]{:S(2)}) %collective-permute-start.3) | collective-permute-done | bytes 278560 | tf_op jit(solution)/shard_map/ppermute | solution.py:410
  16.2 1.6 %early.1 = (f32[4,2,8,512]{3,2,1,0:T(8,128)S(1)}, f32[4,128,128]{2,1,0:T(8,128)S(1)}) custom-call(bf16[4,5,16,128]{3,2,1,0:T(8,128)(2,1)S(1)} %get-tuple-element.29.choice_ref, bf16[128,512]{1,0:T(8,128)(2,1)S(1)} %collective-permute-done.2.other_ref, bf16[128,512]{1,0:T(8,128)(2,1)S(1)} %collective-permute-done.pair_ref, ...), custom_call_target="tpu_custom_call" | custom-call | flops 3000000000 | bytes 6000000 | tf_op jit(solution)/shard_map/early/pallas_call | solution.py:489
  17.8 0.1 collective-permute-done.5.corner_ref
  17.8 2.0 %late.1 = (bf16[128,512]{1,0:T(8,128)(2,1)S(1)}, bf16[128,512]{1,0:T(8,128)(2,1)S(1)}, bf16[16,512]{1,0:T(8,128)(2,1)S(1)}, bf16[16,512]{1,0:T(8,128)(2,1)S(1)}) custom-call(bf16[4,5,16,128]{3,2,1,0:T(8,128)(2,1)S(1)} %get-tuple-element.29.choice_ref, bf16[32,128]{1,0:T(8,128)(2,1)S(1)} %get-tuple-element.30.cells_ref, ...), custom_call_target="tpu_custom_call" | custom-call | flops 3000000000 | bytes 6000000 | tf_op jit(solution)/shard_map/late/pallas_call | solution.py:505
  19.8 1.8 %collective-permute-start.6 = (bf16[16,512]{1,0:T(8,128)(2,1)S(1)}, bf16[16,512]{1,0:T(8,128)(2,1)S(1)}, u32[]{:S(2)}, u32[]{:S(2)}) collective-permute-start(bf16[16,512]{1,0:T(8,128)(2,1)S(1)} %get-tuple-element.46), channel_id=1, source_target_pairs={{0,1},{2,3},{1,0},{3,2},{4,5},{6,7},{5,4},{7,6},{8,9},{10,11},{9,8... | collective-permute-start | bytes 49160 | tf_op jit(solution)/shard_map/ppermute | solution.py:405
  21.6 1.2 %collective-permute-start.7 = (bf16[16,512]{1,0:T(8,128)(2,1)S(1)}, bf16[16,512]{1,0:T(8,128)(2,1)S(1)}, u32[]{:S(2)}, u32[]{:S(2)}) collective-permute-start(bf16[16,512]{1,0:T(8,128)(2,1)S(1)} %get-tuple-element.50), channel_id=1, source_target_pairs={{1,2},{3,0},{2,1},{0,3},{5,6},{7,4},{6,5},{4,7},{9,10},{11,8},{10,... | collective-permute-start | bytes 49160 | tf_op jit(solution)/shard_map/ppermute | solution.py:405
  22.8 0.8 %mix_own.1.weights_ref = bf16[20,96,512]{2,1,0:T(8,128)(2,1)S(1)} custom-call(f32[5,5,2,9]{3,2,1,0:T(2,128)S(1)} %bitcast.9, bf16[9,84,512]{2,1,0:T(8,128)(2,1)S(1)} %bitcast.7), custom_call_target="tpu_custom_call" | custom-call | flops 2000000000 | bytes 6000000 | tf_op jit(solution)/shard_map/mix_own/pallas_call | solution.py:426
  23.6 1.5 %collective-permute-done.7 = bf16[16,512]{1,0:T(8,128)(2,1)S(1)} collective-permute-done((bf16[16,512]{1,0:T(8,128)(2,1)S(1)}, bf16[16,512]{1,0:T(8,128)(2,1)S(1)}, u32[]{:S(2)}, u32[]{:S(2)}) %collective-permute-start.7) | collective-permute-done | bytes 16416 | tf_op jit(solution)/shard_map/ppermute | solution.py:405
  25.1 1.1 %collective-permute-start.9 = (bf16[144,512]{1,0:T(8,128)(2,1)S(1)}, bf16[144,512]{1,0:T(8,128)(2,1)S(1)}, u32[]{:S(2)}, u32[]{:S(2)}) collective-permute-start(bf16[144,512]{1,0:T(8,128)(2,1)S(1)} %pad_maximum_fusion.latent_ref), channel_id=1, source_target_pairs={{0,4},{8,12},{16,20},{24,28},{4,0},{12,8},{20,16},{28,24},{1,5},{9... | collective-permute-start | bytes 442376 | tf_op jit(solution)/shard_map/ppermute | solution.py:410
  26.2 3.6 %collective-permute-start.8 = (bf16[144,512]{1,0:T(8,128)(2,1)S(1)}, bf16[144,512]{1,0:T(8,128)(2,1)S(1)}, u32[]{:S(2)}, u32[]{:S(2)}) collective-permute-start(bf16[144,512]{1,0:T(8,128)(2,1)S(1)} %pad_maximum_fusion.latent_ref), channel_id=1, source_target_pairs={{4,8},{12,16},{20,24},{8,4},{16,12},{24,20},{5,9},{13,17},{21,25},... | collective-permute-start | bytes 442376 | tf_op jit(solution)/shard_map/ppermute | solution.py:410
  29.7 1.8 %own_band.1 = (f32[2,96,256]{2,1,0:T(8,128)S(1)}, bf16[2,2,5,256,256]{4,3,2,1,0:T(8,128)(2,1)S(1)}, bf16[128,512]{1,0:T(8,128)(2,1)}) custom-call(bf16[128,512]{1,0:T(8,128)(2,1)S(1)} %get-tuple-element.43.state_ref, bf16[144,512]{1,0:T(8,128)(2,1)S(1)} %gather.1.own_ref, bf16[272,512]{1,0:T(8,128)(2,1)S(1)} %collective-permute-done.1.inner_ref, ...), custom_call_target="tpu_custom_call" | custom-call | flops 1000000000 | bytes 2500000 | tf_op jit(solution)/shard_map/own_band/pallas_call | solution.py:528
  31.5 0.9 %inner_band.1.partial_ref = f32[2,96,256]{2,1,0:T(8,128)S(1)} custom-call(bf16[144,512]{1,0:T(8,128)(2,1)S(1)} %collective-permute-done.9.latent_ref, bf16[30,96,512]{2,1,0:T(8,128)(2,1)S(1)} %mix_edges.1.weights_ref, bf16[2,2,5,256,256]{4,3,2,1,0:T(8,128)(2,1)S(1)} %get-tuple-element.54.hot_ref, f32[2,96,256]{2,1,0:T(8,128)S(1)} %get-tuple-element.55.partial_ref), custom_call_target="tpu_custom_call" | custom-call | flops 1000000000 | bytes 2500000 | tf_op jit(solution)/shard_map/inner_band/pallas_call | solution.py:546
  32.5 0.2 collective-permute-done.8.latent_ref
  32.6 1.6 %outer_band.1 = bf16[84,2,256]{2,1,0:T(2,128)(2,1)} custom-call(bf16[144,512]{1,0:T(8,128)(2,1)S(1)} %collective-permute-done.8.latent_ref, bf16[30,96,512]{2,1,0:T(8,128)(2,1)S(1)} %mix_edges.1.weights_ref, bf16[2,2,5,256,256]{4,3,2,1,0:T(8,128)(2,1)S(1)} %get-tuple-element.54.hot_ref, f32[2,96,256]{2,1,0:T(8,128)S(1)} %inner_band.1.partial_ref), custom_call_target="tpu_custom_call" | custom-call | flops 1000000000 | bytes 2500000 | tf_op jit(solution)/shard_map/outer_band/pallas_call | solution.py:556
  (20 shorter events, 0.1 us)
Async XLA Ops:
  0.6 14.1 %copy-start = (bf16[9,512,84]{1,2,0:T(8,128)(2,1)S(1)}, bf16[9,512,84]{1,2,0:T(8,128)(2,1)}, u32[]{:S(2)}) copy-start(bf16[9,512,84]{1,2,0:T(8,128)(2,1)} %param.17) | copy-start | bytes 2322436
  0.6 14.1 %copy-start.3 = (f32[9,2,5,5]{0,1,3,2:T(2,128)S(1)}, f32[9,2,5,5]{0,1,3,2:T(2,128)}, u32[]{:S(2)}) copy-start(f32[9,2,5,5]{0,1,3,2:T(2,128)} %param.16) | copy-start | bytes 5404
  0.6 6.3 %collective-permute-start = (bf16[128,512]{1,0:T(8,128)(2,1)}, bf16[128,512]{1,0:T(8,128)(2,1)S(1)}, u32[]{:S(2)}, u32[]{:S(2)}) collective-permute-start(bf16[128,512]{1,0:T(8,128)(2,1)} %bitcast.13), channel_id=1, source_target_pairs={{0,1},{2,3},{1,0},{3,2},{4,5},{6,7},{5,4},{7,6},{8,9},{10,11},{9,8... | collective-permute-start | bytes 393224 | tf_op jit(solution)/shard_map/ppermute | solution.py:405
  2.8 8.8 %collective-permute-start.2 = (bf16[128,512]{1,0:T(8,128)(2,1)}, bf16[128,512]{1,0:T(8,128)(2,1)S(1)}, u32[]{:S(2)}, u32[]{:S(2)}) collective-permute-start(bf16[128,512]{1,0:T(8,128)(2,1)} %bitcast.14), channel_id=1, source_target_pairs={{1,2},{3,0},{2,1},{0,3},{5,6},{7,4},{6,5},{4,7},{9,10},{11,8},{10,... | collective-permute-start | bytes 393224 | tf_op jit(solution)/shard_map/ppermute | solution.py:405
  7.0 8.8 %collective-permute-start.1 = (bf16[272,512]{1,0:T(8,128)(2,1)S(1)}, bf16[272,512]{1,0:T(8,128)(2,1)S(1)}, u32[]{:S(2)}, u32[]{:S(2)}) collective-permute-start(bf16[272,512]{1,0:T(8,128)(2,1)S(1)} %constant_dynamic-update-slice_fusion), channel_id=1, source_target_pairs={{0,4},{8,12},{16,20},{24,28},{4,0},{12,8},{20,16},{28,24},{1,5},{9... | collective-permute-start | bytes 835592 | tf_op jit(solution)/shard_map/ppermute | solution.py:410
  8.3 7.9 %collective-permute-start.3 = (bf16[272,512]{1,0:T(8,128)(2,1)S(1)}, bf16[272,512]{1,0:T(8,128)(2,1)S(1)}, u32[]{:S(2)}, u32[]{:S(2)}) collective-permute-start(bf16[272,512]{1,0:T(8,128)(2,1)S(1)} %constant_dynamic-update-slice_fusion), channel_id=1, source_target_pairs={{4,8},{12,16},{20,24},{8,4},{16,12},{24,20},{5,9},{13,17},{21,25},... | collective-permute-start | bytes 835592 | tf_op jit(solution)/shard_map/ppermute | solution.py:410
  11.5 4.6 %copy-start.4 = (f32[512]{0:T(512)S(1)}, f32[512]{0:T(512)}, u32[]{:S(2)}) copy-start(f32[512]{0:T(512)} %param.10) | copy-start | bytes 6148
  11.5 6.3 %collective-permute-start.5 = (bf16[128,512]{1,0:T(8,128)(2,1)S(1)}, bf16[128,512]{1,0:T(8,128)(2,1)S(1)}, u32[]{:S(2)}, u32[]{:S(2)}) collective-permute-start(bf16[128,512]{1,0:T(8,128)(2,1)S(1)} %collective-permute-done.2.other_ref), channel_id=1, source_target_pairs={{4,8},{12,16},{20,24},{8,4},{16,12},{24,20},{5,9},{13,17},{21,25},... | collective-permute-start | bytes 393224 | tf_op jit(solution)/shard_map/ppermute | solution.py:410
  14.7 3.2 %collective-permute-start.4 = (bf16[128,512]{1,0:T(8,128)(2,1)S(1)}, bf16[128,512]{1,0:T(8,128)(2,1)S(1)}, u32[]{:S(2)}, u32[]{:S(2)}) collective-permute-start(bf16[128,512]{1,0:T(8,128)(2,1)S(1)} %collective-permute-done.2.other_ref), channel_id=1, source_target_pairs={{0,4},{8,12},{16,20},{24,28},{4,0},{12,8},{20,16},{28,24},{1,5},{9... | collective-permute-start | bytes 393224 | tf_op jit(solution)/shard_map/ppermute | solution.py:410
  16.2 1.7 %copy-start.1 = (bf16[512,512]{1,0:T(8,128)(2,1)S(1)}, bf16[512,512]{1,0:T(8,128)(2,1)}, u32[]{:S(2)}) copy-start(bf16[512,512]{1,0:T(8,128)(2,1)} %wout_ref.1) | copy-start | bytes 1572868
  16.2 1.7 %copy-start.2 = (bf16[512,512]{1,0:T(8,128)(2,1)S(1)}, bf16[512,512]{1,0:T(8,128)(2,1)}, u32[]{:S(2)}) copy-start(bf16[512,512]{1,0:T(8,128)(2,1)} %wlat_ref.1) | copy-start | bytes 1572868
  19.8 3.8 %collective-permute-start.6 = (bf16[16,512]{1,0:T(8,128)(2,1)S(1)}, bf16[16,512]{1,0:T(8,128)(2,1)S(1)}, u32[]{:S(2)}, u32[]{:S(2)}) collective-permute-start(bf16[16,512]{1,0:T(8,128)(2,1)S(1)} %get-tuple-element.46), channel_id=1, source_target_pairs={{0,1},{2,3},{1,0},{3,2},{4,5},{6,7},{5,4},{7,6},{8,9},{10,11},{9,8... | collective-permute-start | bytes 49160 | tf_op jit(solution)/shard_map/ppermute | solution.py:405
  21.6 3.5 %collective-permute-start.7 = (bf16[16,512]{1,0:T(8,128)(2,1)S(1)}, bf16[16,512]{1,0:T(8,128)(2,1)S(1)}, u32[]{:S(2)}, u32[]{:S(2)}) collective-permute-start(bf16[16,512]{1,0:T(8,128)(2,1)S(1)} %get-tuple-element.50), channel_id=1, source_target_pairs={{1,2},{3,0},{2,1},{0,3},{5,6},{7,4},{6,5},{4,7},{9,10},{11,8},{10,... | collective-permute-start | bytes 49160 | tf_op jit(solution)/shard_map/ppermute | solution.py:405
  25.1 6.4 %collective-permute-start.9 = (bf16[144,512]{1,0:T(8,128)(2,1)S(1)}, bf16[144,512]{1,0:T(8,128)(2,1)S(1)}, u32[]{:S(2)}, u32[]{:S(2)}) collective-permute-start(bf16[144,512]{1,0:T(8,128)(2,1)S(1)} %pad_maximum_fusion.latent_ref), channel_id=1, source_target_pairs={{0,4},{8,12},{16,20},{24,28},{4,0},{12,8},{20,16},{28,24},{1,5},{9... | collective-permute-start | bytes 442376 | tf_op jit(solution)/shard_map/ppermute | solution.py:410
  26.2 6.5 %collective-permute-start.8 = (bf16[144,512]{1,0:T(8,128)(2,1)S(1)}, bf16[144,512]{1,0:T(8,128)(2,1)S(1)}, u32[]{:S(2)}, u32[]{:S(2)}) collective-permute-start(bf16[144,512]{1,0:T(8,128)(2,1)S(1)} %pad_maximum_fusion.latent_ref), channel_id=1, source_target_pairs={{4,8},{12,16},{20,24},{8,4},{16,12},{24,20},{5,9},{13,17},{21,25},... | collective-permute-start | bytes 442376 | tf_op jit(solution)/shard_map/ppermute | solution.py:410

commit v24 on v16

--- a/solution.py
+++ b/solution.py
@@ -515,11 +515,11 @@
         own, gain, wk, wvt, query, top, summed, w_out, w_latent,
     )
 
-    from_pair = paired(to_pair, 0)
-    from_other = paired(to_other, 1)
+    from_pair = paired(to_pair[:SIDE], 0)
+    from_other = paired(to_other[:SIDE], 1)
     middle, latent = mixed(blocks_of(OWN), "mix_own", latent)
     from_pair, middle = lax.optimization_barrier((from_pair, middle))
-    extended = jnp.concatenate([latent, from_pair[:SIDE], from_other[:SIDE]], axis=0)
+    extended = jnp.concatenate([latent, from_pair, from_other], axis=0)
     far = exchanged(extended, 1)
     near = exchanged(extended, 0)
 

time: 34.4 us -> 34.4 us (level)
  no operation moved by 1% of the time
where the time goes in v24:
time: 34.4 us; the launch traced here: 34.2 us
  starting transfers between devices  18.7 us (54%)
  Pallas kernels  12.7 us (37%)
  waiting for transfers between devices  1.94 us (6%)
  between operations  0.82 us (2%)
    ppermute x6, starting transfers between devices, exchanged(): return lax.ppermute(array, 'reg', pairs + [(j, i) for i, j in pairs])  12.3 us
    ppermute x4, starting transfers between devices, paired(): return lax.ppermute(array, 'lon', pairs + [(j, i) for i, j in pairs])  6.39 us
    pallas_call x1, Pallas kernels, shards(): pl.pallas_call(functools.partial(prepare_kernel, sectors), in_specs=[whol...  2.02 us
    pallas_call x1, Pallas kernels, shards(): pl.pallas_call(late_kernel, in_specs=[whole()] * 15, out_specs=[whole()]...  1.94 us
    pallas_call x2, Pallas kernels, mixed(): pl.pallas_call(functools.partial(mix_kernel, blocks), in_specs=[whole()]...  1.82 us
    pallas_call x1, Pallas kernels, shards(): pl.pallas_call(functools.partial(own_kernel, (rows, 2 * rows, 2 * rows)),...  1.8 us
    pallas_call x1, Pallas kernels, shards(): pl.pallas_call(early_kernel, in_specs=[whole()] * 11, out_specs=[whole()]...  1.6 us
    pallas_call x1, Pallas kernels, shards(): pl.pallas_call(functools.partial(band_kernel, False), in_specs=[whole()]...  1.59 us
  transfers between devices with their start and end apart: 10, of which 4 were waited for; matrix products, arithmetic and copies ran while one was open for 0% of the time, Pallas kernels for 27%

profile of v24, /device:TPU:1, one launch (start us, length us, event | category | flops | bytes accessed | tf_op | source)
XLA Modules:
  0.0 34.2 jit_solution(9010884878045926474)
XLA Ops:
  0.6 2.1 %collective-permute-start = (bf16[128,512]{1,0:T(8,128)(2,1)}, bf16[128,512]{1,0:T(8,128)(2,1)S(1)}, u32[]{:S(2)}, u32[]{:S(2)}) collective-permute-start(bf16[128,512]{1,0:T(8,128)(2,1)} %bitcast.13), channel_id=1, source_target_pairs={{0,1},{2,3},{1,0},{3,2},{4,5},{6,7},{5,4},{7,6},{8,9},{10,11},{9,8... | collective-permute-start | bytes 393224 | tf_op jit(solution)/shard_map/ppermute | solution.py:404
  2.8 1.2 %collective-permute-start.2 = (bf16[128,512]{1,0:T(8,128)(2,1)}, bf16[128,512]{1,0:T(8,128)(2,1)S(1)}, u32[]{:S(2)}, u32[]{:S(2)}) collective-permute-start(bf16[128,512]{1,0:T(8,128)(2,1)} %bitcast.14), channel_id=1, source_target_pairs={{1,2},{3,0},{2,1},{0,3},{5,6},{7,4},{6,5},{4,7},{9,10},{11,8},{10,... | collective-permute-start | bytes 393224 | tf_op jit(solution)/shard_map/ppermute | solution.py:404
  4.0 1.0 %gather.1.own_ref = bf16[144,512]{1,0:T(8,128)(2,1)S(1)} custom-call(bf16[128,512]{1,0:T(8,128)(2,1)} %bitcast.15, s32[2,256]{1,0:T(2,128)} %assign_hbm.3), custom_call_target="tpu_custom_call" | custom-call | flops 1000 | bytes 1000 | tf_op jit(solution)/shard_map/gather/pallas_call | solution.py:440
  4.9 2.0 %prepare.1 = (bf16[4,128,512]{2,1,0:T(8,128)(2,1)S(1)}, bf16[128,512]{1,0:T(8,128)(2,1)S(1)}, bf16[512,128]{1,0:T(8,128)(2,1)S(1)}, bf16[512,512]{1,0:T(8,128)(2...) custom-call(bf16[144,512]{1,0:T(8,128)(2,1)S(1)} %gather.1.own_ref, ...), custom_call_target="tpu_custom_call" | custom-call | flops 500000000 | bytes 1000000 | tf_op jit(solution)/shard_map/prepare/pallas_call | solution.py:453
  7.0 1.3 %collective-permute-start.1 = (bf16[272,512]{1,0:T(8,128)(2,1)S(1)}, bf16[272,512]{1,0:T(8,128)(2,1)S(1)}, u32[]{:S(2)}, u32[]{:S(2)}) collective-permute-start(bf16[272,512]{1,0:T(8,128)(2,1)S(1)} %constant_dynamic-update-slice_fusion), channel_id=1, source_target_pairs={{0,4},{8,12},{16,20},{24,28},{4,0},{12,8},{20,16},{28,24},{1,5},{9... | collective-permute-start | bytes 835592 | tf_op jit(solution)/shard_map/ppermute | solution.py:409
  8.3 3.2 %collective-permute-start.3 = (bf16[272,512]{1,0:T(8,128)(2,1)S(1)}, bf16[272,512]{1,0:T(8,128)(2,1)S(1)}, u32[]{:S(2)}, u32[]{:S(2)}) collective-permute-start(bf16[272,512]{1,0:T(8,128)(2,1)S(1)} %constant_dynamic-update-slice_fusion), channel_id=1, source_target_pairs={{4,8},{12,16},{20,24},{8,4},{16,12},{24,20},{5,9},{13,17},{21,25},... | collective-permute-start | bytes 835592 | tf_op jit(solution)/shard_map/ppermute | solution.py:409
  11.5 0.0 copy-start.4
  11.5 3.1 %collective-permute-start.5 = (bf16[128,512]{1,0:T(8,128)(2,1)S(1)}, bf16[128,512]{1,0:T(8,128)(2,1)S(1)}, u32[]{:S(2)}, u32[]{:S(2)}) collective-permute-start(bf16[128,512]{1,0:T(8,128)(2,1)S(1)} %collective-permute-done.2.other_ref), channel_id=1, source_target_pairs={{4,8},{12,16},{20,24},{8,4},{16,12},{24,20},{5,9},{13,17},{21,25},... | collective-permute-start | bytes 393224 | tf_op jit(solution)/shard_map/ppermute | solution.py:409
  14.7 0.1 collective-permute-start.4
  14.8 1.0 %mix_edges.1.weights_ref = bf16[30,96,512]{2,1,0:T(8,128)(2,1)S(1)} custom-call(f32[5,5,2,9]{3,2,1,0:T(2,128)S(1)} %bitcast.8, bf16[9,84,512]{2,1,0:T(8,128)(2,1)S(1)} %bitcast.6), custom_call_target="tpu_custom_call" | custom-call | flops 2000000000 | bytes 6000000 | tf_op jit(solution)/shard_map/mix_edges/pallas_call | solution.py:425
  15.8 0.3 %collective-permute-done.3.outer_ref = bf16[272,512]{1,0:T(8,128)(2,1)S(1)} collective-permute-done((bf16[272,512]{1,0:T(8,128)(2,1)S(1)}, bf16[272,512]{1,0:T(8,128)(2,1)S(1)}, u32[]{:S(2)}, u32[]{:S(2)}) %collective-permute-start.3) | collective-permute-done | bytes 278560 | tf_op jit(solution)/shard_map/ppermute | solution.py:409
  16.2 1.6 %early.1 = (f32[4,2,8,512]{3,2,1,0:T(8,128)S(1)}, f32[4,128,128]{2,1,0:T(8,128)S(1)}) custom-call(bf16[4,5,16,128]{3,2,1,0:T(8,128)(2,1)S(1)} %get-tuple-element.29.choice_ref, bf16[128,512]{1,0:T(8,128)(2,1)S(1)} %collective-permute-done.2.other_ref, bf16[128,512]{1,0:T(8,128)(2,1)S(1)} %collective-permute-done.pair_ref, ...), custom_call_target="tpu_custom_call" | custom-call | flops 3000000000 | bytes 6000000 | tf_op jit(solution)/shard_map/early/pallas_call | solution.py:488
  17.8 0.1 collective-permute-done.5.corner_ref
  17.8 1.9 %late.1 = (bf16[128,512]{1,0:T(8,128)(2,1)S(1)}, bf16[128,512]{1,0:T(8,128)(2,1)S(1)}, bf16[16,512]{1,0:T(8,128)(2,1)S(1)}, bf16[16,512]{1,0:T(8,128)(2,1)S(1)}) custom-call(bf16[4,5,16,128]{3,2,1,0:T(8,128)(2,1)S(1)} %get-tuple-element.29.choice_ref, bf16[32,128]{1,0:T(8,128)(2,1)S(1)} %get-tuple-element.30.cells_ref, ...), custom_call_target="tpu_custom_call" | custom-call | flops 3000000000 | bytes 6000000 | tf_op jit(solution)/shard_map/late/pallas_call | solution.py:504
  19.8 2.8 %collective-permute-start.7 = (bf16[8,512]{1,0:T(8,128)(2,1)S(1)}, bf16[8,512]{1,0:T(8,128)(2,1)S(1)}, u32[]{:S(2)}, u32[]{:S(2)}) collective-permute-start(bf16[8,512]{1,0:T(8,128)(2,1)S(1)} %slice.7), channel_id=1, source_target_pairs={{1,2},{3,0},{2,1},{0,3},{5,6},{7,4},{6,5},{4,7},{9,10},{11,8},{10,... | collective-permute-start | bytes 24584 | tf_op jit(solution)/shard_map/ppermute | solution.py:404
  22.6 0.3 collective-permute-start.6
  22.9 0.8 %mix_own.1.weights_ref = bf16[20,96,512]{2,1,0:T(8,128)(2,1)S(1)} custom-call(f32[5,5,2,9]{3,2,1,0:T(2,128)S(1)} %bitcast.9, bf16[9,84,512]{2,1,0:T(8,128)(2,1)S(1)} %bitcast.7), custom_call_target="tpu_custom_call" | custom-call | flops 2000000000 | bytes 6000000 | tf_op jit(solution)/shard_map/mix_own/pallas_call | solution.py:425
  23.7 1.5 %collective-permute-done.6 = bf16[8,512]{1,0:T(8,128)(2,1)S(1)} collective-permute-done((bf16[8,512]{1,0:T(8,128)(2,1)S(1)}, bf16[8,512]{1,0:T(8,128)(2,1)S(1)}, u32[]{:S(2)}, u32[]{:S(2)}) %collective-permute-start.6) | collective-permute-done | bytes 8224 | tf_op jit(solution)/shard_map/ppermute | solution.py:404
  25.1 0.9 %collective-permute-start.9 = (bf16[144,512]{1,0:T(8,128)(2,1)S(1)}, bf16[144,512]{1,0:T(8,128)(2,1)S(1)}, u32[]{:S(2)}, u32[]{:S(2)}) collective-permute-start(bf16[144,512]{1,0:T(8,128)(2,1)S(1)} %constant_dynamic-update-slice_fusion.2.latent_ref), channel_id=1, source_target_pairs={{0,4},{8,12},{16,20},{24,28},{4,0},{12,8},{20,16},{28,24},{1,5},{9... | collective-permute-start | bytes 442376 | tf_op jit(solution)/shard_map/ppermute | solution.py:409
  26.1 3.7 %collective-permute-start.8 = (bf16[144,512]{1,0:T(8,128)(2,1)S(1)}, bf16[144,512]{1,0:T(8,128)(2,1)S(1)}, u32[]{:S(2)}, u32[]{:S(2)}) collective-permute-start(bf16[144,512]{1,0:T(8,128)(2,1)S(1)} %constant_dynamic-update-slice_fusion.2.latent_ref), channel_id=1, source_target_pairs={{4,8},{12,16},{20,24},{8,4},{16,12},{24,20},{5,9},{13,17},{21,25},... | collective-permute-start | bytes 442376 | tf_op jit(solution)/shard_map/ppermute | solution.py:409
  29.8 1.8 %own_band.1 = (f32[2,96,256]{2,1,0:T(8,128)S(1)}, bf16[2,2,5,256,256]{4,3,2,1,0:T(8,128)(2,1)S(1)}, bf16[128,512]{1,0:T(8,128)(2,1)}) custom-call(bf16[128,512]{1,0:T(8,128)(2,1)S(1)} %get-tuple-element.43.state_ref, bf16[144,512]{1,0:T(8,128)(2,1)S(1)} %gather.1.own_ref, bf16[272,512]{1,0:T(8,128)(2,1)S(1)} %collective-permute-done.1.inner_ref, ...), custom_call_target="tpu_custom_call" | custom-call | flops 1000000000 | bytes 2500000 | tf_op jit(solution)/shard_map/own_band/pallas_call | solution.py:527
  31.6 0.9 %inner_band.1.partial_ref = f32[2,96,256]{2,1,0:T(8,128)S(1)} custom-call(bf16[144,512]{1,0:T(8,128)(2,1)S(1)} %collective-permute-done.9.latent_ref, bf16[30,96,512]{2,1,0:T(8,128)(2,1)S(1)} %mix_edges.1.weights_ref, bf16[2,2,5,256,256]{4,3,2,1,0:T(8,128)(2,1)S(1)} %get-tuple-element.54.hot_ref, f32[2,96,256]{2,1,0:T(8,128)S(1)} %get-tuple-element.55.partial_ref), custom_call_target="tpu_custom_call" | custom-call | flops 1000000000 | bytes 2500000 | tf_op jit(solution)/shard_map/inner_band/pallas_call | solution.py:545
  32.5 0.1 collective-permute-done.8.latent_ref
  32.6 1.6 %outer_band.1 = bf16[84,2,256]{2,1,0:T(2,128)(2,1)} custom-call(bf16[144,512]{1,0:T(8,128)(2,1)S(1)} %collective-permute-done.8.latent_ref, bf16[30,96,512]{2,1,0:T(8,128)(2,1)S(1)} %mix_edges.1.weights_ref, bf16[2,2,5,256,256]{4,3,2,1,0:T(8,128)(2,1)S(1)} %get-tuple-element.54.hot_ref, f32[2,96,256]{2,1,0:T(8,128)S(1)} %inner_band.1.partial_ref), custom_call_target="tpu_custom_call" | custom-call | flops 1000000000 | bytes 2500000 | tf_op jit(solution)/shard_map/outer_band/pallas_call | solution.py:555
  (22 shorter events, 0.1 us)
Async XLA Ops:
  0.6 14.1 %copy-start = (bf16[9,512,84]{1,2,0:T(8,128)(2,1)S(1)}, bf16[9,512,84]{1,2,0:T(8,128)(2,1)}, u32[]{:S(2)}) copy-start(bf16[9,512,84]{1,2,0:T(8,128)(2,1)} %param.17) | copy-start | bytes 2322436
  0.6 14.1 %copy-start.3 = (f32[9,2,5,5]{0,1,3,2:T(2,128)S(1)}, f32[9,2,5,5]{0,1,3,2:T(2,128)}, u32[]{:S(2)}) copy-start(f32[9,2,5,5]{0,1,3,2:T(2,128)} %param.16) | copy-start | bytes 5404
  0.6 6.3 %collective-permute-start = (bf16[128,512]{1,0:T(8,128)(2,1)}, bf16[128,512]{1,0:T(8,128)(2,1)S(1)}, u32[]{:S(2)}, u32[]{:S(2)}) collective-permute-start(bf16[128,512]{1,0:T(8,128)(2,1)} %bitcast.13), channel_id=1, source_target_pairs={{0,1},{2,3},{1,0},{3,2},{4,5},{6,7},{5,4},{7,6},{8,9},{10,11},{9,8... | collective-permute-start | bytes 393224 | tf_op jit(solution)/shard_map/ppermute | solution.py:404
  2.8 8.8 %collective-permute-start.2 = (bf16[128,512]{1,0:T(8,128)(2,1)}, bf16[128,512]{1,0:T(8,128)(2,1)S(1)}, u32[]{:S(2)}, u32[]{:S(2)}) collective-permute-start(bf16[128,512]{1,0:T(8,128)(2,1)} %bitcast.14), channel_id=1, source_target_pairs={{1,2},{3,0},{2,1},{0,3},{5,6},{7,4},{6,5},{4,7},{9,10},{11,8},{10,... | collective-permute-start | bytes 393224 | tf_op jit(solution)/shard_map/ppermute | solution.py:404
  7.0 8.8 %collective-permute-start.1 = (bf16[272,512]{1,0:T(8,128)(2,1)S(1)}, bf16[272,512]{1,0:T(8,128)(2,1)S(1)}, u32[]{:S(2)}, u32[]{:S(2)}) collective-permute-start(bf16[272,512]{1,0:T(8,128)(2,1)S(1)} %constant_dynamic-update-slice_fusion), channel_id=1, source_target_pairs={{0,4},{8,12},{16,20},{24,28},{4,0},{12,8},{20,16},{28,24},{1,5},{9... | collective-permute-start | bytes 835592 | tf_op jit(solution)/shard_map/ppermute | solution.py:409
  8.3 7.9 %collective-permute-start.3 = (bf16[272,512]{1,0:T(8,128)(2,1)S(1)}, bf16[272,512]{1,0:T(8,128)(2,1)S(1)}, u32[]{:S(2)}, u32[]{:S(2)}) collective-permute-start(bf16[272,512]{1,0:T(8,128)(2,1)S(1)} %constant_dynamic-update-slice_fusion), channel_id=1, source_target_pairs={{4,8},{12,16},{20,24},{8,4},{16,12},{24,20},{5,9},{13,17},{21,25},... | collective-permute-start | bytes 835592 | tf_op jit(solution)/shard_map/ppermute | solution.py:409
  11.5 4.6 %copy-start.4 = (f32[512]{0:T(512)S(1)}, f32[512]{0:T(512)}, u32[]{:S(2)}) copy-start(f32[512]{0:T(512)} %param.10) | copy-start | bytes 6148
  11.5 6.3 %collective-permute-start.5 = (bf16[128,512]{1,0:T(8,128)(2,1)S(1)}, bf16[128,512]{1,0:T(8,128)(2,1)S(1)}, u32[]{:S(2)}, u32[]{:S(2)}) collective-permute-start(bf16[128,512]{1,0:T(8,128)(2,1)S(1)} %collective-permute-done.2.other_ref), channel_id=1, source_target_pairs={{4,8},{12,16},{20,24},{8,4},{16,12},{24,20},{5,9},{13,17},{21,25},... | collective-permute-start | bytes 393224 | tf_op jit(solution)/shard_map/ppermute | solution.py:409
  14.7 3.2 %collective-permute-start.4 = (bf16[128,512]{1,0:T(8,128)(2,1)S(1)}, bf16[128,512]{1,0:T(8,128)(2,1)S(1)}, u32[]{:S(2)}, u32[]{:S(2)}) collective-permute-start(bf16[128,512]{1,0:T(8,128)(2,1)S(1)} %collective-permute-done.2.other_ref), channel_id=1, source_target_pairs={{0,4},{8,12},{16,20},{24,28},{4,0},{12,8},{20,16},{28,24},{1,5},{9... | collective-permute-start | bytes 393224 | tf_op jit(solution)/shard_map/ppermute | solution.py:409
  16.2 1.7 %copy-start.1 = (bf16[512,512]{1,0:T(8,128)(2,1)S(1)}, bf16[512,512]{1,0:T(8,128)(2,1)}, u32[]{:S(2)}) copy-start(bf16[512,512]{1,0:T(8,128)(2,1)} %wout_ref.1) | copy-start | bytes 1572868
  16.2 1.7 %copy-start.2 = (bf16[512,512]{1,0:T(8,128)(2,1)S(1)}, bf16[512,512]{1,0:T(8,128)(2,1)}, u32[]{:S(2)}) copy-start(bf16[512,512]{1,0:T(8,128)(2,1)} %wlat_ref.1) | copy-start | bytes 1572868
  19.8 5.3 %collective-permute-start.7 = (bf16[8,512]{1,0:T(8,128)(2,1)S(1)}, bf16[8,512]{1,0:T(8,128)(2,1)S(1)}, u32[]{:S(2)}, u32[]{:S(2)}) collective-permute-start(bf16[8,512]{1,0:T(8,128)(2,1)S(1)} %slice.7), channel_id=1, source_target_pairs={{1,2},{3,0},{2,1},{0,3},{5,6},{7,4},{6,5},{4,7},{9,10},{11,8},{10,... | collective-permute-start | bytes 24584 | tf_op jit(solution)/shard_map/ppermute | solution.py:404
  22.6 2.5 %collective-permute-start.6 = (bf16[8,512]{1,0:T(8,128)(2,1)S(1)}, bf16[8,512]{1,0:T(8,128)(2,1)S(1)}, u32[]{:S(2)}, u32[]{:S(2)}) collective-permute-start(bf16[8,512]{1,0:T(8,128)(2,1)S(1)} %slice.6), channel_id=1, source_target_pairs={{0,1},{2,3},{1,0},{3,2},{4,5},{6,7},{5,4},{7,6},{8,9},{10,11},{9,8... | collective-permute-start | bytes 24584 | tf_op jit(solution)/shard_map/ppermute | solution.py:404
  25.1 6.4 %collective-permute-start.9 = (bf16[144,512]{1,0:T(8,128)(2,1)S(1)}, bf16[144,512]{1,0:T(8,128)(2,1)S(1)}, u32[]{:S(2)}, u32[]{:S(2)}) collective-permute-start(bf16[144,512]{1,0:T(8,128)(2,1)S(1)} %constant_dynamic-update-slice_fusion.2.latent_ref), channel_id=1, source_target_pairs={{0,4},{8,12},{16,20},{24,28},{4,0},{12,8},{20,16},{28,24},{1,5},{9... | collective-permute-start | bytes 442376 | tf_op jit(solution)/shard_map/ppermute | solution.py:409
  26.1 6.5 %collective-permute-start.8 = (bf16[144,512]{1,0:T(8,128)(2,1)S(1)}, bf16[144,512]{1,0:T(8,128)(2,1)S(1)}, u32[]{:S(2)}, u32[]{:S(2)}) collective-permute-start(bf16[144,512]{1,0:T(8,128)(2,1)S(1)} %constant_dynamic-update-slice_fusion.2.latent_ref), channel_id=1, source_target_pairs={{4,8},{12,16},{20,24},{8,4},{16,12},{24,20},{5,9},{13,17},{21,25},... | collective-permute-start | bytes 442376 | tf_op jit(solution)/shard_map/ppermute | solution.py:409
